TPU v7x, 32 devices: a whole 2x2x4 slice. The times are simulated.
32 devices in a mesh: wide: 8 (over y, x, core), narrow: 4 (over z).
Axes of the slice: x: 2, y: 2, z: 4, core: 2. Of those that a mesh axis runs over, the one named last changes fastest.
Arguments:
- decode_hidden_input: bfloat16 [256, 8192], P('wide'), may hold values from -6 to 6
- queries: bfloat16 [256, 8192], P('wide', 'narrow'), may hold values from -8 to 8
- cached_key_rows: bfloat16 [256, 256, 1024], P('wide', None, 'narrow'), may hold values from -4 to 4
- cached_value_rows: bfloat16 [256, 256, 1024], P('wide', None, 'narrow'), may hold values from -6 to 6
- lengths: int32 [256], P('wide'), may hold values from 2 to 256, as said below
- decode_adapter_index: int32 [256], P('wide'), may hold values from 0 to 127, as said below
- key_matrix: bfloat16 [8192, 1024], P(None, 'narrow'), may hold values from -0.0625 to 0.0625
- value_matrix: bfloat16 [8192, 1024], P(None, 'narrow'), may hold values from -0.0625 to 0.0625
- adapter_down_map: bfloat16 [128, 16, 8192], P('wide', None, 'narrow'), may hold values from -0.0625 to 0.0625
- adapter_up_map: bfloat16 [128, 16, 1024], P('wide', None, 'narrow'), may hold values from -0.1875 to 0.1875
- training_hidden_input: bfloat16 [8192, 8192], P('wide', 'narrow'), may hold values from -6 to 6
- cotangent: bfloat16 [8192, 1024], P('wide', 'narrow'), may hold values from -0.3984375 to 0.3984375
- training_adapter_index: int32 [8192], P('wide'), may hold values from 0 to 127, as said below
- rewards: int32 [8192], P('wide'), may hold values from -2 to 2
Outputs:
- attended: bfloat16 [256, 8192], P('wide', 'narrow')
- fresh_values: bfloat16 [256, 1024], P('wide', 'narrow')
- grad_down: float32 [128, 16, 8192], P('wide', None, 'narrow')
- grad_up: float32 [128, 16, 1024], P('wide', None, 'narrow')
Inputs may be any that keep to these rules, and one draw needn't show every extreme that they name: `decode_adapter_index`: of the 32 rows of one index of wide, at most 8 use adapters of one owner (adapters o * 16 to (o + 1) * 16 - 1); in every draw one owner gets exactly 8 rows from every index of wide. `training_adapter_index`: of the 1024 tokens of one index of wide, at most 256 use adapters of one owner (adapters o * 16 to (o + 1) * 16 - 1); in every draw one owner gets exactly 256 tokens from every index of wide. `lengths`: every block of 32 rows holds a row of length 256.
All inputs are finite; a program needn't handle non-finite values.
Results may differ from a plain program's by a relative error of at most 0.0051.
Values may be sent and summed in bfloat16 or wider, within the bound.
No kernel may reach another device: no remote copies, remote signals or barrier semaphores. Data moves between devices by JAX's collectives and lax.ppermute only.
A program may use at most 128 MiB of HBM per device.

v0:
```python
import math

import jax
import jax.numpy as jnp
from jax import lax
from jax.sharding import PartitionSpec as P

HEADS = 64
KEY_VALUE_HEADS = 8
HEAD_SIZE = 128
CACHE = 256


ADAPTER_SCALE = 2.0
NEG_FILL = -1e30


def pack_slots(adapter_ids, owners, owner_totals, capacity):
    owner_of = adapter_ids // owner_totals
    owner_match = (owner_of[:, None] == jnp.arange(owners, dtype=jnp.int32)[None, :]).astype(
        jnp.int32
    )
    earlier = jnp.cumsum(owner_match, axis=0) - owner_match
    position = jnp.sum(earlier * owner_match, axis=1)
    target = owner_of * capacity + position
    return jnp.arange(owners * capacity, dtype=jnp.int32)[:, None] == target[None, :]


def place_rows(slot_match, data, owners):
    placed = jnp.dot(
        slot_match.astype(jnp.bfloat16), data, preferred_element_type=jnp.float32
    ).astype(jnp.bfloat16)
    return placed.reshape(owners, -1, data.shape[1])


def place_codes(slot_match, values, owners):
    return jnp.sum(slot_match.astype(jnp.int32) * values[None, :], axis=1).reshape(owners, -1)


def code_match(codes, owner_totals):
    return codes[:, None] == jnp.arange(1, owner_totals + 1, dtype=jnp.int32)[None, :]


def pick_rank(codes, products, owner_totals):
    slot_count = codes.shape[0]
    chosen = code_match(codes, owner_totals).astype(jnp.float32)
    return jnp.sum(products.reshape(slot_count, owner_totals, -1) * chosen[:, :, None], axis=1)


def spread_rank(codes, factors, owner_totals):
    slot_count = codes.shape[0]
    chosen = code_match(codes, owner_totals).astype(jnp.bfloat16)
    return (chosen[:, :, None] * factors[:, None, :]).reshape(slot_count, -1)


def accumulate(codes, input_rows, incoming_gradient, scaled_rank, scaled_back, owner_totals):
    spread_back = spread_rank(codes, scaled_back, owner_totals)
    grad_down = jnp.einsum("sa,sd->ad", spread_back, input_rows, preferred_element_type=jnp.float32)
    spread_hidden = spread_rank(codes, scaled_rank, owner_totals)
    grad_up = jnp.einsum(
        "sa,sk->ak", spread_hidden, incoming_gradient, preferred_element_type=jnp.float32
    )
    return (
        grad_down.reshape(owner_totals, -1, input_rows.shape[1]),
        grad_up.reshape(owner_totals, -1, incoming_gradient.shape[1]),
    )


def owner_delta(arrived_slice, arrived_codes, flattened_down, flattened_up, owner_totals):
    source_count = arrived_codes.shape[0]
    item_count = arrived_codes.shape[1]
    down_map_width = flattened_down.shape[1]
    value_map_width = flattened_up.shape[1]
    flat_codes = arrived_codes.reshape(-1)
    products = jnp.einsum(
        "sd,ad->sa",
        arrived_slice.reshape(-1, down_map_width),
        flattened_down,
        preferred_element_type=jnp.float32,
    )
    partial_value = pick_rank(flat_codes, products, owner_totals)
    summed = lax.psum(partial_value, "narrow").astype(jnp.bfloat16)
    spread_gradient = spread_rank(flat_codes, summed, owner_totals)
    delta_slots = (
        ADAPTER_SCALE * jnp.dot(spread_gradient, flattened_up, preferred_element_type=jnp.float32)
    ).astype(jnp.bfloat16)
    return lax.all_to_all(
        delta_slots.reshape(source_count, item_count, value_map_width),
        "wide",
        split_axis=0,
        concat_axis=0,
        tiled=True,
    )


def attend(queries, cached_key_rows, cached_value_rows, lengths, fresh_keys, fresh_values):
    row_count = queries.shape[0]
    kv_local = fresh_keys.shape[1] // HEAD_SIZE
    group = HEADS // KEY_VALUE_HEADS
    query_heads = queries.reshape(row_count, kv_local, group, HEAD_SIZE)
    key_heads = cached_key_rows.reshape(row_count, CACHE, kv_local, HEAD_SIZE)
    value_heads = cached_value_rows.reshape(row_count, CACHE, kv_local, HEAD_SIZE)
    inverse = 1.0 / math.sqrt(HEAD_SIZE)
    scores = (
        jnp.einsum("bhgd,bphd->bhgp", query_heads, key_heads, preferred_element_type=jnp.float32)
        * inverse
    )
    own_score = (
        jnp.einsum(
            "bhgd,bhd->bhg",
            query_heads,
            fresh_keys.reshape(row_count, kv_local, HEAD_SIZE),
            preferred_element_type=jnp.float32,
        )
        * inverse
    )
    allowed = jnp.arange(CACHE, dtype=jnp.int32)[None, :] < lengths[:, None]
    scores = jnp.where(allowed[:, None, None, :], scores, NEG_FILL)
    highest = jnp.maximum(jnp.max(scores, axis=-1), own_score)
    cache_exp = jnp.exp(scores - highest[..., None])
    own_exp = jnp.exp(own_score - highest)
    denominator = jnp.sum(cache_exp, axis=-1) + own_exp
    cache_weight = (cache_exp / denominator[..., None]).astype(jnp.bfloat16)
    own_weight = (own_exp / denominator).astype(jnp.bfloat16)
    attended = jnp.einsum(
        "bhgp,bphd->bhgd", cache_weight, value_heads, preferred_element_type=jnp.float32
    )
    attended = attended + own_weight.astype(jnp.float32)[..., None] * fresh_values.reshape(
        row_count, kv_local, 1, HEAD_SIZE
    ).astype(jnp.float32)
    return attended.reshape(row_count, -1).astype(jnp.bfloat16)


def per_device(
    decode_hidden_input,
    queries,
    cached_key_rows,
    cached_value_rows,
    lengths,
    decode_adapter_index,
    key_matrix,
    value_matrix,
    adapter_down_map,
    adapter_up_map,
    training_hidden_input,
    cotangent,
    training_adapter_index,
    rewards,
):
    wide_count = lax.axis_size("wide")
    narrow_index = lax.axis_index("narrow")
    owner_totals = adapter_down_map.shape[0]
    down_map_width = adapter_down_map.shape[2]
    value_map_width = adapter_up_map.shape[2]
    row_count = decode_hidden_input.shape[0]
    token_count = training_hidden_input.shape[0]
    row_capacity = 2 * row_count // wide_count
    token_capacity = 2 * token_count // wide_count
    decode_slice = lax.dynamic_slice_in_dim(
        decode_hidden_input, narrow_index * down_map_width, down_map_width, 1
    )
    fresh_keys = jnp.dot(
        decode_hidden_input, key_matrix, preferred_element_type=jnp.float32
    ).astype(jnp.bfloat16)
    base_values = jnp.dot(decode_hidden_input, value_matrix, preferred_element_type=jnp.float32)
    flattened_down = adapter_down_map.reshape(-1, down_map_width)
    flattened_up = adapter_up_map.reshape(-1, value_map_width)
    decode_match = pack_slots(decode_adapter_index, wide_count, owner_totals, row_capacity)
    decode_codes = place_codes(decode_match, decode_adapter_index % owner_totals + 1, wide_count)
    decode_sent = place_rows(decode_match, decode_slice, wide_count)
    token_match = pack_slots(training_adapter_index, wide_count, owner_totals, token_capacity)
    token_codes = place_codes(token_match, training_adapter_index % owner_totals + 1, wide_count)
    token_rewards = place_codes(token_match, rewards, wide_count)
    sent_rows = place_rows(token_match, training_hidden_input, wide_count)
    sent_grads = place_rows(token_match, cotangent, wide_count)
    returned = owner_delta(
        lax.all_to_all(decode_sent, "wide", split_axis=0, concat_axis=0, tiled=True),
        lax.all_to_all(decode_codes, "wide", split_axis=0, concat_axis=0, tiled=True),
        flattened_down,
        flattened_up,
        owner_totals,
    )
    arrived_rows, arrived_grads, arrived_codes, received_rewards = (
        lax.all_to_all(sent_rows, "wide", split_axis=0, concat_axis=0, tiled=True),
        lax.all_to_all(sent_grads, "wide", split_axis=0, concat_axis=0, tiled=True),
        lax.all_to_all(token_codes, "wide", split_axis=0, concat_axis=0, tiled=True),
        lax.all_to_all(token_rewards, "wide", split_axis=0, concat_axis=0, tiled=True),
    )
    value_delta_rows = jnp.einsum(
        "sn,sk->nk",
        decode_match.astype(jnp.bfloat16),
        returned.reshape(-1, value_map_width),
        preferred_element_type=jnp.float32,
    ).astype(jnp.bfloat16)
    fresh_values = (base_values + value_delta_rows.astype(jnp.float32)).astype(jnp.bfloat16)
    attended = attend(
        queries, cached_key_rows, cached_value_rows, lengths, fresh_keys, fresh_values
    )
    flat_rows = arrived_rows.reshape(-1, down_map_width)
    flat_grads = arrived_grads.reshape(-1, value_map_width)
    flat_codes = arrived_codes.reshape(-1)
    part_hidden = pick_rank(
        flat_codes,
        jnp.einsum("sd,ad->sa", flat_rows, flattened_down, preferred_element_type=jnp.float32),
        owner_totals,
    )
    part_back = pick_rank(
        flat_codes,
        jnp.einsum("sk,ak->sa", flat_grads, flattened_up, preferred_element_type=jnp.float32),
        owner_totals,
    )
    hidden_sum, back_sum = lax.psum((part_hidden, part_back), "narrow")
    scale_factor = ADAPTER_SCALE * received_rewards.reshape(-1).astype(jnp.float32)[:, None]
    grad_down, grad_up = accumulate(
        flat_codes,
        flat_rows,
        flat_grads,
        (scale_factor * hidden_sum).astype(jnp.bfloat16),
        (scale_factor * back_sum).astype(jnp.bfloat16),
        owner_totals,
    )
    return (attended, fresh_values, grad_down, grad_up)


def solution(mesh):
    return jax.shard_map(
        per_device,
        mesh=mesh,
        in_specs=(
            P("wide", None),
            P("wide", "narrow"),
            P("wide", None, "narrow"),
            P("wide", None, "narrow"),
            P("wide"),
            P("wide"),
            P(None, "narrow"),
            P(None, "narrow"),
            P("wide", None, "narrow"),
            P("wide", None, "narrow"),
            P("wide", "narrow"),
            P("wide", "narrow"),
            P("wide"),
            P("wide"),
        ),
        out_specs=(
            P("wide", "narrow"),
            P("wide", "narrow"),
            P("wide", None, "narrow"),
            P("wide", None, "narrow"),
        ),
        check_vma=False,
    )
```

profile of v0, /device:TPU:0, one launch (start us, length us, event | category | flops | bytes accessed | tf_op | source)
XLA Modules:
  0.0 240.0 jit_solution(2139539113297709406)
XLA Ops:
  9.0 5.2 %all-to-all-start = ((s32[8,1,8]{2,1,0:T(1,128)}), s32[8,1,8]{2,1,0:T(1,128)S(1)}, u32[]{:S(2)}, u32[]{:S(2)}) async-start(s32[8,1,8]{2,1,0:T(1,128)} %bitcast.1), calls=%async_computation | async-start | bytes 8192 | tf_op jit(solution)/shard_map/all_to_all | solution.py:178
  14.9 2.3 reduce-window.6
  17.8 3.7 %select_reduce_fusion = (s32[2048]{0:T(1024)}, s32[2048]{0:T(1024)}) fusion(s32[1024]{0:T(1024)} %param.27, s32[1024]{0:T(1024)S(1)} %multiply_add_fusion, s32[1024]{0:T(1024)S(1)} %get-tuple-element.14), kind=kLoop, calls=%fused_computation | loop fusion | flops 10481664 | bytes 28672 | tf_op jit(solution)/shard_map/reduce_sum | solution.py:37
  21.4 1.9 fusion.12
  23.4 4.2 %all-to-all-start.1 = ((bf16[8,8,2048]{2,1,0:T(8,128)(2,1)}), bf16[8,8,2048]{2,1,0:T(8,128)(2,1)S(1)}, u32[]{:S(2)}, u32[]{:S(2)}) async-start(bf16[8,8,2048]{2,1,0:T(8,128)(2,1)} %fusion.12), calls=%async_computation.1 | async-start | bytes 524288 | tf_op jit(solution)/shard_map/all_to_all | solution.py:177
  29.0 5.6 %all-to-all-done.1 = bf16[8,8,2048]{2,1,0:T(8,128)(2,1)S(1)} async-done(((bf16[8,8,2048]{2,1,0:T(8,128)(2,1)}), bf16[8,8,2048]{2,1,0:T(8,128)(2,1)S(1)}, u32[]{:S(2)}, u32[]{:S(2)}) %all-to-all-start.1) | async-done | bytes 262176 | tf_op jit(solution)/shard_map/all_to_all | solution.py:177
  34.5 3.3 %all-to-all-start.3 = ((s32[8,1,256]{2,1,0:T(1,128)}), s32[8,1,256]{2,1,0:T(1,128)S(1)}, u32[]{:S(2)}, u32[]{:S(2)}) async-start(s32[8,1,256]{2,1,0:T(1,128)} %bitcast.10), calls=%async_computation.3 | async-start | bytes 16384 | tf_op jit(solution)/shard_map/all_to_all | solution.py:186
  38.3 12.1 %psum.21 = bf16[64,16]{0,1:T(8,128)(2,1)S(1)} all-reduce(f32[64,16]{0,1:T(8,128)S(1)} %fusion.27), channel_id=1, replica_groups=mesh['wide'=8,'narrow'=4] {'narrow'}, use_global_device_ids=true, to_apply=%region_6.7 | all-reduce | flops 1024 | bytes 6144 | tf_op jit(solution)/shard_map/psum | solution.py:82
  50.5 4.1 %all-to-all-start.4 = ((s32[8,1,256]{2,1,0:T(1,128)}), s32[8,1,256]{2,1,0:T(1,128)S(1)}, u32[]{:S(2)}, u32[]{:S(2)}) async-start(s32[8,1,256]{2,1,0:T(1,128)} %bitcast.12), calls=%async_computation.4 | async-start | bytes 16384 | tf_op jit(solution)/shard_map/all_to_all | solution.py:187
  56.3 3.0 %all-to-all-done.4 = s32[8,1,256]{2,1,0:T(1,128)S(1)} async-done(((s32[8,1,256]{2,1,0:T(1,128)}), s32[8,1,256]{2,1,0:T(1,128)S(1)}, u32[]{:S(2)}, u32[]{:S(2)}) %all-to-all-start.4) | async-done | bytes 8224 | tf_op jit(solution)/shard_map/all_to_all | solution.py:187
  59.3 3.3 %all-to-all-start.2 = ((bf16[8,8,256]{2,1,0:T(8,128)(2,1)}), bf16[8,8,256]{2,1,0:T(8,128)(2,1)S(1)}, u32[]{:S(2)}, u32[]{:S(2)}) async-start(bf16[8,8,256]{2,1,0:T(8,128)(2,1)} %fusion.30), calls=%async_computation.2 | async-start | bytes 65536 | tf_op jit(solution)/shard_map/all_to_all | solution.py:87
  62.6 3.6 %fusion.11 = bf16[2048,256]{1,0:T(8,128)(2,1)} fusion(bf16[1024,256]{1,0:T(8,128)(2,1)} %param.25, s32[1024]{0:T(1024)S(1)} %multiply_add_fusion), kind=kOutput, calls=%fused_computation.16 | convolution fusion | flops 1076363264 | bytes 1576960 | tf_op jit(solution)/shard_map/dot_general | solution.py:30
  67.4 3.6 %all-to-all-start.5 = ((bf16[8,256,256]{2,1,0:T(8,128)(2,1)}), bf16[8,256,256]{2,1,0:T(8,128)(2,1)S(1)}, u32[]{:S(2)}, u32[]{:S(2)}) async-start(bf16[8,256,256]{2,1,0:T(8,128)(2,1)} %bitcast.14), calls=%async_computation.5 | async-start | bytes 2097152 | tf_op jit(solution)/shard_map/all_to_all | solution.py:185
  71.0 13.0 %fusion.2 = bf16[2048,2048]{1,0:T(8,128)(2,1)} fusion(bf16[1024,2048]{1,0:T(8,128)(2,1)} %param.24, s32[1024]{0:T(1024)S(1)} %multiply_add_fusion), kind=kOutput, calls=%fused_computation.5 | convolution fusion | flops 8596226048 | bytes 12587008 | tf_op jit(solution)/shard_map/dot_general | solution.py:30
  84.0 2.4 all-to-all-done.5
  86.3 5.1 %all-to-all-start.6 = ((bf16[8,256,2048]{2,1,0:T(8,128)(2,1)}), bf16[8,256,2048]{2,1,0:T(8,128)(2,1)}, u32[]{:S(2)}, u32[]{:S(2)}) async-start(bf16[8,256,2048]{2,1,0:T(8,128)(2,1)} %bitcast.132), calls=%async_computation.6 | async-start | bytes 16777216 | tf_op jit(solution)/shard_map/all_to_all | solution.py:184
  91.7 3.0 %convolution_convert_fusion.2 = bf16[32,256]{1,0:T(8,128)(2,1)S(1)} fusion(bf16[32,8192]{1,0:T(8,128)(2,1)S(1)} %copy-done.1, bf16[8192,256]{1,0:T(8,128)(2,1)} %param.20), kind=kOutput, calls=%fused_computation.35 | convolution fusion | flops 134225920 | bytes 4734976 | tf_op jit(solution)/shard_map/dot_general | solution.py:162
  95.1 3.5 %fusion.67 = (f32[32,2,8]{2,1,0:T(2,128)S(1)}, f32[32,2,8,256]{3,2,1,0:T(8,128)S(1)}) fusion(bf16[32,2,8,128]{3,2,1,0:T(8,128)(2,1)S(1)} %bitcast.136, pred[32,256]{1,0:T(8,128)(4,1)S(1)} %iota_compare_fusion.9, bf16[32,256,256]{2,1,0:T(8,128)(2,1)} %param.16), kind=kOutput, calls=%fused_computation.107 | convolution fusion | flops 33947136 | bytes 4859904 | tf_op jit(solution)/shard_map/bhgd,bphd->bhgp/dot_general | solution.py:105
  102.1 3.0 %fusion.31 = bf16[32,256]{1,0:T(8,128)(2,1)S(1)} fusion(f32[32,256]{1,0:T(8,128)S(1)} %fusion.32, bf16[32,8192]{1,0:T(8,128)(2,1)S(1)} %copy-done.1, bf16[8192,256]{1,0:T(8,128)(2,1)} %param.21), kind=kOutput, calls=%fused_computation.32 | convolution fusion | flops 134234112 | bytes 4767744 | tf_op jit(solution)/shard_map/dot_general | solution.py:165
  106.3 79.2 %all-to-all-done.6 = bf16[8,256,2048]{2,1,0:T(8,128)(2,1)} async-done(((bf16[8,256,2048]{2,1,0:T(8,128)(2,1)}), bf16[8,256,2048]{2,1,0:T(8,128)(2,1)}, u32[]{:S(2)}, u32[]{:S(2)}) %all-to-all-start.6) | async-done | bytes 8388640 | tf_op jit(solution)/shard_map/all_to_all | solution.py:184
  185.5 6.4 %fusion.14 = f32[2048,16]{0,1:T(8,128)} fusion(bf16[2048,2048,1]{1,0,2:T(8,128)(2,1)} %bitcast.22, bf16[16,16,2048]{2,1,0:T(8,128)(2,1)S(1)} %copy-done, f32[2048,16]{0,1:T(8,128)S(1)} %get-tuple-element.11), kind=kOutput, calls=%fused_computation.20 | convolution fusion | flops 2148499456 | bytes 9699328 | tf_op jit(solution)/shard_map/sd,ad->sa/dot_general | solution.py:204
  192.0 3.0 %fusion.24 = bf16[32,2,8,128]{3,2,1,0:T(8,128)(2,1)S(1)} fusion(f32[32,2,8,256]{3,2,1,0:T(8,128)S(1)} %get-tuple-element.21, f32[32,2,8]{2,1,0:T(2,128)S(1)} %copy-done.5, f32[32,2,8]{2,1,0:T(2,128)S(1)} %copy.38, f32[32,2,128]{2,1,0:T(2,128)S(1)} %reshape.292, f32[32,2,8]{2,1,0:T(2,128)S(1)} %copy-done.6, bf16[32,256,256]{2,1,0:T(8,128)(2,1)} %param.17), kind=kOutput, calls=%fused_computation.24 | convolution fusion | flops 34144256 | bytes 4888576 | tf_op jit(solution)/shard_map/bhgp,bphd->bhgd/dot_general | solution.py:125
  195.6 28.4 %all-reduce.3.cloned.1.call-done = (f32[2048,16]{0,1:T(8,128)}, f32[2048,16]{0,1:T(8,128)}) async-done(((f32[2048,16]{0,1:T(8,128)}, f32[2048,16]{0,1:T(8,128)}), (f32[2048,16]{0,1:T(8,128)}, f32[2048,16]{0,1:T(8,128)})) %all-reduce.3.cloned.1.call-update) | async-done | bytes 262160 | tf_op jit(solution)/shard_map/psum | solution.py:212
  225.0 7.0 %fusion.35 = f32[16,16,2048]{2,1,0:T(8,128)} fusion(bf16[2048,2048,1]{1,0,2:T(8,128)(2,1)} %bitcast.22, bf16[2048,16]{0,1:T(8,128)(2,1)S(1)} %get-tuple-element.13, bf16[2048,16]{0,1:T(8,128)(2,1)S(1)} %get-tuple-element.10), kind=kOutput, calls=%fused_computation.38 | convolution fusion | flops 2148007936 | bytes 10616832 | tf_op jit(solution)/shard_map/sa,sd->ad/dot_general | solution.py:58
  (67 shorter events, 15.8 us)
Async XLA Ops:
  7.2 30.7 %copy-start = (bf16[16,16,2048]{2,1,0:T(8,128)(2,1)S(1)}, bf16[16,16,2048]{2,1,0:T(8,128)(2,1)}, u32[]{:S(2)}) copy-start(bf16[16,16,2048]{2,1,0:T(8,128)(2,1)} %param.22) | copy-start | bytes 3145732
  8.3 15.1 %copy-start.7 = (s32[32]{0:T(128)}, s32[32]{0:T(128)S(1)}, u32[]{:S(2)}) copy-start(s32[32]{0:T(128)S(1)} %multiply_add_fusion.1) | copy-start | bytes 388
  9.0 14.4 %all-to-all-start = ((s32[8,1,8]{2,1,0:T(1,128)}), s32[8,1,8]{2,1,0:T(1,128)S(1)}, u32[]{:S(2)}, u32[]{:S(2)}) async-start(s32[8,1,8]{2,1,0:T(1,128)} %bitcast.1), calls=%async_computation | async-start | bytes 8192 | tf_op jit(solution)/shard_map/all_to_all | solution.py:178
  23.4 11.1 %all-to-all-start.1 = ((bf16[8,8,2048]{2,1,0:T(8,128)(2,1)}), bf16[8,8,2048]{2,1,0:T(8,128)(2,1)S(1)}, u32[]{:S(2)}, u32[]{:S(2)}) async-start(bf16[8,8,2048]{2,1,0:T(8,128)(2,1)} %fusion.12), calls=%async_computation.1 | async-start | bytes 524288 | tf_op jit(solution)/shard_map/all_to_all | solution.py:177
  27.6 38.7 %copy-start.8 = (s32[16]{0:T(128)}, s32[16]{0:T(128)S(1)}, u32[]{:S(2)}) copy-start(s32[16]{0:T(128)S(1)} %iota_add_fusion) | copy-start | bytes 196
  34.5 15.9 %all-to-all-start.3 = ((s32[8,1,256]{2,1,0:T(1,128)}), s32[8,1,256]{2,1,0:T(1,128)S(1)}, u32[]{:S(2)}, u32[]{:S(2)}) async-start(s32[8,1,256]{2,1,0:T(1,128)} %bitcast.10), calls=%async_computation.3 | async-start | bytes 16384 | tf_op jit(solution)/shard_map/all_to_all | solution.py:186
  50.5 8.8 %all-to-all-start.4 = ((s32[8,1,256]{2,1,0:T(1,128)}), s32[8,1,256]{2,1,0:T(1,128)S(1)}, u32[]{:S(2)}, u32[]{:S(2)}) async-start(s32[8,1,256]{2,1,0:T(1,128)} %bitcast.12), calls=%async_computation.4 | async-start | bytes 16384 | tf_op jit(solution)/shard_map/all_to_all | solution.py:187
  59.3 8.1 %all-to-all-start.2 = ((bf16[8,8,256]{2,1,0:T(8,128)(2,1)}), bf16[8,8,256]{2,1,0:T(8,128)(2,1)S(1)}, u32[]{:S(2)}, u32[]{:S(2)}) async-start(bf16[8,8,256]{2,1,0:T(8,128)(2,1)} %fusion.30), calls=%async_computation.2 | async-start | bytes 65536 | tf_op jit(solution)/shard_map/all_to_all | solution.py:87
  67.4 18.9 %all-to-all-start.5 = ((bf16[8,256,256]{2,1,0:T(8,128)(2,1)}), bf16[8,256,256]{2,1,0:T(8,128)(2,1)S(1)}, u32[]{:S(2)}, u32[]{:S(2)}) async-start(bf16[8,256,256]{2,1,0:T(8,128)(2,1)} %bitcast.14), calls=%async_computation.5 | async-start | bytes 2097152 | tf_op jit(solution)/shard_map/all_to_all | solution.py:185
  86.3 5.3 %copy-start.2 = (bf16[32,2048]{1,0:T(8,128)(2,1)S(1)}, bf16[32,2048]{1,0:T(8,128)(2,1)}, u32[]{:S(2)}) copy-start(bf16[32,2048]{1,0:T(8,128)(2,1)} %param.15) | copy-start | bytes 393220
  86.3 5.4 %copy-start.1 = (bf16[32,8192]{1,0:T(8,128)(2,1)S(1)}, bf16[32,8192]{1,0:T(8,128)(2,1)}, u32[]{:S(2)}) copy-start(bf16[32,8192]{1,0:T(8,128)(2,1)} %param.14) | copy-start | bytes 1572868
  86.3 99.2 %all-to-all-start.6 = ((bf16[8,256,2048]{2,1,0:T(8,128)(2,1)}), bf16[8,256,2048]{2,1,0:T(8,128)(2,1)}, u32[]{:S(2)}, u32[]{:S(2)}) async-start(bf16[8,256,2048]{2,1,0:T(8,128)(2,1)} %bitcast.132), calls=%async_computation.6 | async-start | bytes 16777216 | tf_op jit(solution)/shard_map/all_to_all | solution.py:184
  91.4 3.6 %copy-start.9 = (s32[32]{0:T(128)S(1)}, s32[32]{0:T(128)}, u32[]{:S(2)}) copy-start(s32[32]{0:T(128)} %param.18) | copy-start | bytes 388
  91.4 132.6 %all-reduce.3.cloned.1.call-start = ((), (), s32[]{:S(2)}) async-start(), calls=%async_computation.7 | async-start | bytes 524288 | tf_op jit(solution)/shard_map/psum | solution.py:212
  98.6 6.6 %copy-start.3 = (bf16[16,16,256]{2,1,0:T(8,128)(2,1)S(1)}, bf16[16,16,256]{2,1,0:T(8,128)(2,1)}, u32[]{:S(2)}) copy-start(bf16[16,16,256]{2,1,0:T(8,128)(2,1)} %param.23) | copy-start | bytes 393220
  105.1 86.8 %copy-start.4 = (bf16[32,256]{1,0:T(8,128)(2,1)}, bf16[32,256]{1,0:T(8,128)(2,1)S(1)}, u32[]{:S(2)}) copy-start(bf16[32,256]{1,0:T(8,128)(2,1)S(1)} %fusion.31) | copy-start | bytes 49156
  185.5 6.5 %copy-start.5 = (f32[32,2,8]{2,1,0:T(2,128)S(1)}, f32[32,2,8]{2,1,0:T(2,128)}, u32[]{:S(2)}) copy-start(f32[32,2,8]{2,1,0:T(2,128)} %copy.40) | copy-start | bytes 6148
  185.5 6.5 %copy-start.6 = (f32[32,2,8]{2,1,0:T(2,128)S(1)}, f32[32,2,8]{2,1,0:T(2,128)}, u32[]{:S(2)}) copy-start(f32[32,2,8]{2,1,0:T(2,128)} %copy.42) | copy-start | bytes 6148
Sparse Core Ops, SparseCore 0:
  192.1 31.8 all-reduce.2
where the time goes:
time: 241 us; the launch traced here: 240 us
  waiting for transfers between devices  120 us (50%)
  matrix products  49.9 us (21%)
  starting transfers between devices  29.1 us (12%)
  between operations  14.3 us (6%)
  blocking collectives  12.1 us (5%)
  other arithmetic  10.9 us (5%)
  local copies, waits for them, and re-layouts  4.05 us (2%)
    all_to_all x1, waiting for transfers between devices, per_device(): lax.all_to_all(sent_rows, 'wide', split_axis=0, concat_axis=0, tiled=True)  79.2 us
    psum x1, waiting for transfers between devices, per_device(): hidden_sum, back_sum = lax.psum((part_hidden, part_back), 'narrow')  28.4 us
    dot_general x3, matrix products, place_rows(): jnp.dot(slot_match.astype(jnp.bfloat16), data, preferred_element_type=jnp...  18.6 us
    psum x1, blocking collectives, owner_delta(): summed = lax.psum(partial_value, 'narrow').astype(jnp.bfloat16)  12.1 us
    dot_general x1, matrix products, accumulate(): jnp.einsum('sa,sd->ad', spread_back, input_rows, preferred_element_type=j...  7.03 us
    dot_general x1, matrix products, per_device(): jnp.einsum('sd,ad->sa', flat_rows, flattened_down, preferred_element_type...  6.43 us
    all_to_all x1, waiting for transfers between devices, per_device(): lax.all_to_all(decode_sent, 'wide', split_axis=0, concat_axis=0, tiled=True)  5.59 us
    all_to_all x1, starting transfers between devices, per_device(): lax.all_to_all(decode_codes, 'wide', split_axis=0, concat_axis=0, tiled=T...  5.17 us
  transfers between devices with their start and end apart: 8, of which 6 were waited for; matrix products, arithmetic and copies ran while one was open for 20% of the time, Pallas kernels for 0%

commit v1 on v0

v1 whole, which is shorter than its diff:
```python
import functools
import math

import jax
import jax.numpy as jnp
from jax import lax
from jax.experimental import pallas as pl
from jax.experimental.pallas import tpu as pltpu
from jax.sharding import PartitionSpec as P

HEADS = 64
KEY_VALUE_HEADS = 8
HEAD_SIZE = 128
CACHE = 256

ADAPTER_SCALE = 2.0
NEG_FILL = -1e30
VMEM_LIMIT = 48 * 1024 * 1024


def swap(array, axis, mask):
    count = lax.axis_size(axis)
    return lax.ppermute(array, axis, [(i, i ^ mask) for i in range(count)])


def axis_bits(axis):
    count = lax.axis_size(axis)
    assert count & (count - 1) == 0, "axis size"
    return [1 << k for k in range(count.bit_length() - 1)]


def highest_in(order, mask):
    return [bit for bit in order if bit & mask][-1]


def largest_tile(length, limit):
    tile = length
    while tile > limit and tile % 2 == 0:
        tile //= 2
    return tile


def rank_kernel(chunk_bases, rank, own_tiles, with_rows, *refs):
    codes_ref, own_ref, mate_ref = refs[:3]
    rest = refs[3:]
    if with_rows:
        row_codes_ref, rows_ref = rest[:2]
        rest = rest[2:]
    maps = rest[: len(chunk_bases)]
    out_ref = rest[len(chunk_bases)]
    step = pl.program_id(0)

    def project(codes, tokens):
        total = jnp.zeros((rank, tokens.shape[0]), jnp.float32)
        for base, chunk in zip(chunk_bases, maps):
            products = lax.dot_general(
                chunk[...], tokens, (((1,), (1,)), ((), ())), preferred_element_type=jnp.float32
            )
            for j in range(chunk.shape[0] // rank):
                total += jnp.where(codes == base + j, products[j * rank : (j + 1) * rank], 0.0)
        return total

    @pl.when(step < own_tiles)
    def _():
        out_ref[...] = project(codes_ref[...], own_ref[...])

    @pl.when(step >= own_tiles)
    def _():
        out_ref[...] = project(codes_ref[...], mate_ref[...])

    if with_rows:

        @pl.when(step == 0)
        def _():
            rest[len(chunk_bases) + 1][...] = project(row_codes_ref[...], rows_ref[...])


def project_tokens(codes, own, mate, chunks, rank, row_codes=None, rows=None):
    token_count, width = own.shape
    tile = largest_tile(token_count, 512)
    own_tiles = token_count // tile
    with_rows = rows is not None
    in_specs = [
        pl.BlockSpec((1, tile), lambda i: (0, i)),
        pl.BlockSpec((tile, width), lambda i: (jnp.minimum(i, own_tiles - 1), 0)),
        pl.BlockSpec((tile, width), lambda i: (jnp.maximum(i - own_tiles, 0), 0)),
    ]
    operands = [codes, own, mate]
    out_specs = [pl.BlockSpec((rank, tile), lambda i: (0, i))]
    out_shape = [jax.ShapeDtypeStruct((rank, 2 * token_count), jnp.float32)]
    if with_rows:
        in_specs += [pl.BlockSpec(a.shape, lambda i: (0, 0)) for a in (row_codes, rows)]
        operands += [row_codes, rows]
        out_specs.append(pl.BlockSpec((rank, rows.shape[0]), lambda i: (0, 0)))
        out_shape.append(jax.ShapeDtypeStruct((rank, rows.shape[0]), jnp.float32))
    in_specs += [pl.BlockSpec(chunk.shape, lambda i: (0, 0)) for _, chunk in chunks]
    operands += [chunk for _, chunk in chunks]
    map_rows = sum(chunk.shape[0] for _, chunk in chunks)
    return pl.pallas_call(
        functools.partial(
            rank_kernel, [base for base, _ in chunks], rank, own_tiles, with_rows
        ),
        grid=(2 * own_tiles,),
        in_specs=in_specs,
        out_specs=out_specs,
        out_shape=out_shape,
        compiler_params=pltpu.CompilerParams(vmem_limit_bytes=VMEM_LIMIT),
        cost_estimate=pl.CostEstimate(
            flops=4 * token_count * width * map_rows,
            bytes_accessed=4 * token_count * width + 2 * map_rows * width,
            transcendentals=0,
        ),
    )(*operands)


def gradient_kernel(chunk_bases, rank, adapters, *refs):
    codes_ref, rewards_ref, factor_ref, own_ref, mate_ref = refs[:5]
    outs = refs[5:-1]
    spread_ref = refs[-1]
    token_count = own_ref.shape[0]
    chunk_rows = adapters * rank

    @pl.when(pl.program_id(0) == 0)
    def _():
        scale = ADAPTER_SCALE * rewards_ref[...].astype(jnp.float32)
        scaled = (scale * factor_ref[...]).astype(jnp.bfloat16).astype(jnp.float32)
        codes = codes_ref[...]
        for k, base in enumerate(chunk_bases):
            for j in range(adapters):
                first = k * chunk_rows + j * rank
                spread_ref[first : first + rank, :] = jnp.where(
                    codes == base + j, scaled, 0.0
                ).astype(jnp.bfloat16)

    for k, out_ref in enumerate(outs):
        spread = spread_ref[k * chunk_rows : (k + 1) * chunk_rows, :]
        total = jnp.dot(
            spread[:, :token_count], own_ref[...], preferred_element_type=jnp.float32
        ) + jnp.dot(spread[:, token_count:], mate_ref[...], preferred_element_type=jnp.float32)
        out_ref[...] = total.astype(out_ref.dtype)


def gradient_chunks(codes, rewards, factor, own, mate, chunks, adapters):
    rank = factor.shape[0]
    token_count, width = own.shape
    tile = largest_tile(width, 512)
    rows = adapters * rank
    whole = lambda i: (0, 0)
    return pl.pallas_call(
        functools.partial(gradient_kernel, [base for base, _ in chunks], rank, adapters),
        grid=(width // tile,),
        in_specs=[
            pl.BlockSpec(codes.shape, whole),
            pl.BlockSpec(rewards.shape, whole),
            pl.BlockSpec(factor.shape, whole),
            pl.BlockSpec((token_count, tile), lambda i: (0, i)),
            pl.BlockSpec((token_count, tile), lambda i: (0, i)),
        ],
        out_specs=[pl.BlockSpec((rows, tile), lambda i: (0, i)) for _ in chunks],
        out_shape=[jax.ShapeDtypeStruct((rows, width), dtype) for _, dtype in chunks],
        scratch_shapes=[pltpu.VMEM((len(chunks) * rows, 2 * token_count), jnp.bfloat16)],
        compiler_params=pltpu.CompilerParams(vmem_limit_bytes=VMEM_LIMIT),
        cost_estimate=pl.CostEstimate(
            flops=4 * token_count * width * rows * len(chunks),
            bytes_accessed=4 * token_count * width + 4 * rows * width * len(chunks),
            transcendentals=0,
        ),
    )(codes, rewards, factor, own, mate)


def sum_over(axis, pieces):
    bits = axis_bits(axis)
    for step in range(len(bits)):
        pieces = [
            piece + swap(piece, axis, bits[step] if k % 2 == 0 else bits[-1 - step])
            for k, piece in enumerate(pieces)
        ]
    return pieces


def attend_cached(queries, cached_key_rows, cached_value_rows, lengths, fresh_keys):
    row_count = queries.shape[0]
    kv_local = fresh_keys.shape[1] // HEAD_SIZE
    group = HEADS // KEY_VALUE_HEADS
    query_heads = queries.reshape(row_count, kv_local, group, HEAD_SIZE)
    key_heads = cached_key_rows.reshape(row_count, CACHE, kv_local, HEAD_SIZE)
    value_heads = cached_value_rows.reshape(row_count, CACHE, kv_local, HEAD_SIZE)
    inverse = 1.0 / math.sqrt(HEAD_SIZE)
    scores = (
        jnp.einsum("bhgd,bphd->bhgp", query_heads, key_heads, preferred_element_type=jnp.float32)
        * inverse
    )
    own_score = (
        jnp.einsum(
            "bhgd,bhd->bhg",
            query_heads,
            fresh_keys.reshape(row_count, kv_local, HEAD_SIZE),
            preferred_element_type=jnp.float32,
        )
        * inverse
    )
    allowed = jnp.arange(CACHE, dtype=jnp.int32)[None, :] < lengths[:, None]
    scores = jnp.where(allowed[:, None, None, :], scores, NEG_FILL)
    highest = jnp.maximum(jnp.max(scores, axis=-1), own_score)
    cache_exp = jnp.exp(scores - highest[..., None])
    own_exp = jnp.exp(own_score - highest)
    denominator = jnp.sum(cache_exp, axis=-1) + own_exp
    cache_weight = (cache_exp / denominator[..., None]).astype(jnp.bfloat16)
    own_weight = (own_exp / denominator).astype(jnp.bfloat16)
    attended = jnp.einsum(
        "bhgp,bphd->bhgd", cache_weight, value_heads, preferred_element_type=jnp.float32
    )
    return attended, own_weight


def per_device(
    decode_hidden_input,
    queries,
    cached_key_rows,
    cached_value_rows,
    lengths,
    decode_adapter_index,
    key_matrix,
    value_matrix,
    adapter_down_map,
    adapter_up_map,
    training_hidden_input,
    cotangent,
    training_adapter_index,
    rewards,
):
    core_bit, *chip_bits = axis_bits("wide")
    masks = [m for m in range(lax.axis_size("wide")) if not m & core_bit]
    me = lax.axis_index("wide")
    owner_totals, rank, down_width = adapter_down_map.shape
    up_width = adapter_up_map.shape[2]
    row_count = decode_hidden_input.shape[0]
    token_count = training_hidden_input.shape[0]
    parts = len(chip_bits) if owner_totals % len(chip_bits) == 0 else 1
    orders = [chip_bits[p:] + chip_bits[:p] for p in range(parts)]
    part_adapters = owner_totals // parts
    part_rows = part_adapters * rank

    flattened_down = adapter_down_map.reshape(-1, down_width)
    flattened_up = adapter_up_map.reshape(-1, up_width)

    up_maps = {m: swap(flattened_up, "wide", m) if m else flattened_up for m in masks}
    down_parts = {}
    for p, order in enumerate(orders):
        down_parts[0, p] = flattened_down[p * part_rows : (p + 1) * part_rows]
        held = [0]
        for bit in order:
            for m in held:
                down_parts[m | bit, p] = swap(down_parts[m, p], "wide", bit)
            held = held + [m | bit for m in held]

    numbers = jnp.concatenate([training_adapter_index, rewards, decode_adapter_index])
    mate_numbers = swap(numbers, "wide", core_bit)
    mate_rows = swap(training_hidden_input, "wide", core_bit)
    mate_cotangent = swap(cotangent, "wide", core_bit)
    decode_slice = lax.dynamic_slice_in_dim(
        decode_hidden_input, lax.axis_index("narrow") * down_width, down_width, 1
    )
    mate_slice = swap(decode_slice, "wide", core_bit)

    def codes_of(ids):
        return ((ids // owner_totals) ^ me) * owner_totals + ids % owner_totals

    token_codes = codes_of(
        jnp.concatenate([training_adapter_index, mate_numbers[:token_count]])
    )[None, :]
    token_rewards = jnp.concatenate([rewards, mate_numbers[token_count : 2 * token_count]])[
        None, :
    ]
    pad = -2 * row_count % 128
    row_codes = codes_of(
        jnp.concatenate([decode_adapter_index, mate_numbers[2 * token_count :]])
    )
    padded_codes = jnp.concatenate([row_codes, jnp.full((pad,), -1, jnp.int32)])[None, :]
    chip_slices = jnp.concatenate(
        [decode_slice, mate_slice, jnp.zeros((pad, down_width), decode_slice.dtype)]
    )

    (part_back,) = project_tokens(
        token_codes,
        cotangent,
        mate_cotangent,
        [(m * owner_totals, up_maps[m]) for m in masks],
        rank,
    )
    back = jnp.concatenate(
        sum_over("narrow", [part_back[:, :token_count], part_back[:, token_count:]]), axis=1
    )
    grads = {}

    def down_gradients(chosen):
        keys = [(m, p) for m in chosen for p in range(parts)]
        last = [m & orders[p][-1] for m, p in keys]
        results = gradient_chunks(
            token_codes,
            token_rewards,
            back,
            training_hidden_input,
            mate_rows,
            [
                (m * owner_totals + p * part_adapters, jnp.bfloat16 if sends else jnp.float32)
                for (m, p), sends in zip(keys, last)
            ],
            part_adapters,
        )
        grads.update(zip(keys, results))

    far = [m for m in masks if m.bit_count() > 1]
    near = [m for m in masks if m.bit_count() == 1]
    for chosen in (far, near, [0]):
        if chosen:
            down_gradients(chosen)
    for p, order in enumerate(orders):
        held = list(masks)
        for bit in reversed(order):
            sent = [m for m in held if m & bit]
            held = [m for m in held if not m & bit]
            for m in sorted(sent, key=lambda v: -v.bit_count()):
                arrived = swap(grads[m, p].astype(jnp.bfloat16), "wide", bit)
                grads[m ^ bit, p] = grads[m ^ bit, p] + arrived.astype(jnp.float32)
    grad_down = jnp.concatenate([grads[0, p] for p in range(parts)])

    def down_chunks(chosen):
        return [
            (m * owner_totals + p * part_adapters, down_parts[m, p])
            for m in chosen
            for p in range(parts)
        ]

    part_hidden, part_rank = project_tokens(
        token_codes,
        training_hidden_input,
        mate_rows,
        [(0, flattened_down)] + down_chunks(near),
        rank,
        padded_codes,
        chip_slices,
    )
    if far:
        more_hidden, more_rank = project_tokens(
            token_codes,
            training_hidden_input,
            mate_rows,
            down_chunks(far),
            rank,
            padded_codes,
            chip_slices,
        )
        part_hidden, part_rank = part_hidden + more_hidden, part_rank + more_rank
    first, second = sum_over(
        "narrow",
        [
            part_hidden[:, :token_count],
            jnp.concatenate([part_hidden[:, token_count:], part_rank], axis=1),
        ],
    )
    hidden = jnp.concatenate([first, second[:, :token_count]], axis=1)
    decode_rank = second[:, token_count : token_count + 2 * row_count].astype(jnp.bfloat16)
    up_results = gradient_chunks(
        token_codes,
        token_rewards,
        hidden,
        cotangent,
        mate_cotangent,
        [(m * owner_totals, jnp.bfloat16 if m else jnp.float32) for m in masks],
        owner_totals,
    )
    grad_up = up_results[0]
    for m, result in zip(masks[1:], up_results[1:]):
        grad_up = grad_up + swap(result, "wide", m).astype(jnp.float32)

    delta = jnp.zeros((2 * row_count, up_width), jnp.float32)
    for m in masks:
        codes = m * owner_totals + jnp.arange(owner_totals, dtype=jnp.int32)
        chosen = (row_codes[None, :] == codes[:, None]).astype(jnp.bfloat16)
        spread = (chosen[:, None, :] * decode_rank[None, :, :]).reshape(-1, 2 * row_count)
        delta = delta + jnp.einsum(
            "ab,ak->bk", spread, up_maps[m], preferred_element_type=jnp.float32
        )
    delta = (ADAPTER_SCALE * delta).astype(jnp.bfloat16)
    own_delta = delta[:row_count] + swap(delta[row_count:], "wide", core_bit)
    fresh_keys = jnp.dot(
        decode_hidden_input, key_matrix, preferred_element_type=jnp.float32
    ).astype(jnp.bfloat16)
    base_values = jnp.dot(decode_hidden_input, value_matrix, preferred_element_type=jnp.float32)
    cached, own_weight = attend_cached(
        queries, cached_key_rows, cached_value_rows, lengths, fresh_keys
    )
    cached, own_weight, base_values = lax.optimization_barrier((cached, own_weight, base_values))
    fresh_values = (base_values + own_delta.astype(jnp.float32)).astype(jnp.bfloat16)
    kv_local = up_width // HEAD_SIZE
    attended = cached + own_weight.astype(jnp.float32)[..., None] * fresh_values.reshape(
        row_count, kv_local, 1, HEAD_SIZE
    ).astype(jnp.float32)
    return (
        attended.reshape(row_count, -1).astype(jnp.bfloat16),
        fresh_values,
        grad_down.reshape(adapter_down_map.shape),
        grad_up.reshape(adapter_up_map.shape),
    )


def solution(mesh):
    return jax.shard_map(
        per_device,
        mesh=mesh,
        in_specs=(
            P("wide", None),
            P("wide", "narrow"),
            P("wide", None, "narrow"),
            P("wide", None, "narrow"),
            P("wide"),
            P("wide"),
            P(None, "narrow"),
            P(None, "narrow"),
            P("wide", None, "narrow"),
            P("wide", None, "narrow"),
            P("wide", "narrow"),
            P("wide", "narrow"),
            P("wide"),
            P("wide"),
        ),
        out_specs=(
            P("wide", "narrow"),
            P("wide", "narrow"),
            P("wide", None, "narrow"),
            P("wide", None, "narrow"),
        ),
        check_vma=False,
    )
```

time: 241 us -> 161 us (0.67)
  waiting for transfers between devices: 120 us -> 44.5 us
  Pallas kernels: 0 us -> 48.5 us
  matrix products: 49.9 us -> 13 us
  between operations: 14.3 us -> 1.14 us
  blocking collectives: 12.1 us -> 0 us
  other arithmetic: 10.9 us -> 14.9 us
  starting transfers between devices: 29.1 us -> 32.4 us
    all_to_all x7 -> x0, waiting for transfers between devices: 91.3 us -> none  [the longest x1 79.2 us: per_device(): lax.all_to_all(sent_rows, 'wide', split_axis=0, concat_axis=0, tiled=True)]
    pallas_call x0 -> x7, Pallas kernels: none -> 48.5 us  [the longest x3 27.5 us: project_tokens(): pl.pallas_call(functools.partial(rank_kernel, [base for base, _ in chunks...]
    ppermute x0 -> x31, waiting for transfers between devices: none -> 44.5 us  [swap(): return lax.ppermute(array, axis, [(i, i ^ mask) for i in range(count)])]
    dot_general x13 -> x7, matrix products: 43.9 us -> 6.02 us  [the longest x1 3.49 us: attend_cached(): jnp.einsum('bhgd,bphd->bhgp', query_heads, key_heads, preferred_element_t...]
    ppermute x0 -> x31, starting transfers between devices: none -> 32.4 us  [swap(): return lax.ppermute(array, axis, [(i, i ^ mask) for i in range(count)])]
    all_to_all x7 -> x0, starting transfers between devices: 28.8 us -> none  [the longest x1 5.17 us: per_device(): lax.all_to_all(decode_codes, 'wide', split_axis=0, concat_axis=0, tiled=T...]
    psum x1 -> x0, waiting for transfers between devices: 28.4 us -> none  [per_device(): hidden_sum, back_sum = lax.psum((part_hidden, part_back), 'narrow')]
    psum x1 -> x0, blocking collectives: 12.1 us -> none  [owner_delta(): summed = lax.psum(partial_value, 'narrow').astype(jnp.bfloat16)]
  transfers between devices with their start and end apart: 8 -> 31, of which waited for: 6 -> 6; matrix products, arithmetic and copies ran while one was open for 20% -> 20% of each run, Pallas kernels for 0% -> 20%
where the time goes in v1:
time: 161 us
  Pallas kernels  48.5 us (30%)
  waiting for transfers between devices  44.5 us (28%)
  starting transfers between devices  32.4 us (20%)
  other arithmetic  14.9 us (9%)
  matrix products  13 us (8%)
  local copies, waits for them, and re-layouts  6.25 us (4%)
    ppermute x31, waiting for transfers between devices, swap(): return lax.ppermute(array, axis, [(i, i ^ mask) for i in range(count)])  44.5 us
    ppermute x31, starting transfers between devices, swap(): return lax.ppermute(array, axis, [(i, i ^ mask) for i in range(count)])  32.4 us
    pallas_call x3, Pallas kernels, project_tokens(): pl.pallas_call(functools.partial(rank_kernel, [base for base, _ in chunks...  27.5 us
    pallas_call x4, Pallas kernels, gradient_chunks(): pl.pallas_call(functools.partial(gradient_kernel, [base for base, _ in ch...  21 us
    dot_general x1, matrix products, per_device(): jnp.dot(decode_hidden_input, value_matrix, preferred_element_type=jnp.flo...  3.94 us
    dot_general x1, matrix products, attend_cached(): jnp.einsum('bhgd,bphd->bhgp', query_heads, key_heads, preferred_element_t...  3.49 us
  transfers between devices with their start and end apart: 31, of which 6 were waited for; matrix products, arithmetic and copies ran while one was open for 20% of the time, Pallas kernels for 20%

profile of v1, /device:TPU:0, one launch (start us, length us, event | category | flops | bytes accessed | tf_op | source)
XLA Modules:
  0.0 160.7 jit_solution(6761411619990961760)
XLA Ops:
  0.6 3.0 %collective-permute-start.11 = (bf16[256,256]{1,0:T(8,128)(2,1)}, bf16[256,256]{1,0:T(8,128)(2,1)S(1)}, u32[]{:S(2)}, u32[]{:S(2)}) collective-permute-start(bf16[256,256]{1,0:T(8,128)(2,1)} %bitcast.61), channel_id=1, source_target_pairs={{0,8},{4,12},{8,0},{12,4},{16,24},{20,28},{24,16},{28,20},{1,9},{5... | collective-permute-start | bytes 393224 | tf_op jit(solution)/shard_map/ppermute | solution.py:23
  3.6 1.5 collective-permute-start.12
  8.7 3.0 %convolution_convert_fusion = bf16[32,256]{1,0:T(8,128)(2,1)S(1)} fusion(bf16[32,8192]{1,0:T(8,128)(2,1)S(1)} %copy-done, bf16[8192,256]{1,0:T(8,128)(2,1)} %param.20), kind=kOutput, calls=%fused_computation.15 | convolution fusion | flops 134225920 | bytes 4734976 | tf_op jit(solution)/shard_map/dot_general | solution.py:387
  11.9 3.5 %fusion.30 = (f32[32,2,8]{2,1,0:T(2,128)S(1)}, f32[32,2,8,256]{3,2,1,0:T(8,128)S(1)}) fusion(bf16[32,2,8,128]{3,2,1,0:T(8,128)(2,1)S(1)} %bitcast.71, pred[32,256]{1,0:T(8,128)(4,1)S(1)} %iota_compare_fusion, bf16[32,256,256]{2,1,0:T(8,128)(2,1)} %param.16), kind=kOutput, calls=%fused_computation.79 | convolution fusion | flops 33947136 | bytes 4859904 | tf_op jit(solution)/shard_map/bhgd,bphd->bhgp/dot_general | solution.py:190
  16.4 3.9 %fusion.32 = f32[32,256]{1,0:T(8,128)} fusion(bf16[32,8192]{1,0:T(8,128)(2,1)S(1)} %copy-done, bf16[8192,256]{1,0:T(8,128)(2,1)} %param.21), kind=kOutput, calls=%fused_computation.81 | convolution fusion | flops 134217728 | bytes 4751360 | tf_op jit(solution)/shard_map/dot_general | solution.py:390
  20.3 1.6 %fusion = f32[32,2,8,128]{3,2,1,0:T(8,128)S(1)} fusion(f32[32,2,8,256]{3,2,1,0:T(8,128)S(1)} %get-tuple-element.62, f32[32,2,8]{2,1,0:T(2,128)S(1)} %get-tuple-element.51, f32[32,2,8]{2,1,0:T(2,128)} %copy-done.13, bf16[32,256,256]{2,1,0:T(8,128)(2,1)S(1)} %copy-done.15), kind=kOutput, calls=%fused_computation | convolution fusion | flops 33947648 | bytes 4984832 | tf_op jit(solution)/shard_map/bhgp,bphd->bhgd/dot_general | solution.py:210
  27.7 2.0 %collective-permute-start.3 = (bf16[128,2048]{1,0:T(8,128)(2,1)}, bf16[128,2048]{1,0:T(8,128)(2,1)S(1)}, u32[]{:S(2)}, u32[]{:S(2)}) collective-permute-start(bf16[128,2048]{1,0:T(8,128)(2,1)} %bitcast.73), channel_id=1, source_target_pairs={{0,8},{4,12},{8,0},{12,4},{16,24},{20,28},{24,16},{28,20},{1,9},{5... | collective-permute-start | bytes 1572872 | tf_op jit(solution)/shard_map/ppermute | solution.py:23
  31.2 2.2 %shard_map.167 = f32[16,2048]{1,0:T(8,128)S(1)} custom-call(s32[1,2048]{1,0:T(1,128)S(1)} %fusion.22.refs_0_, bf16[1024,256]{1,0:T(8,128)(2,1)S(1)} %copy-done.8, bf16[1024,256]{1,0:T(8,128)(2,1)S(1)} %collective-permute-done.15.refs_2_.refs_4_, bf16[256,256]{1,0:T(8,128)(2,1)S(1)} %bitcast.64, bf16[256,256]{1,0:T(8,128)(2,1)S(1)} %collective-permute-done.11.refs_4_, ...), custom_call_target="tpu_custom_call" | custom-call | flops 1073741824 | bytes 1572864 | tf_op jit(solution)/shard_map/pallas_call | solution.py:99
  33.4 1.6 %collective-permute-start.16 = (f32[16,1024]{1,0:T(8,128)S(1)}, f32[16,1024]{1,0:T(8,128)S(1)}, u32[]{:S(2)}, u32[]{:S(2)}) collective-permute-start(f32[16,1024]{1,0:T(8,128)S(1)} %get-tuple-element.48), channel_id=1, source_target_pairs={{0,1},{1,0},{2,3},{3,2},{4,5},{5,4},{6,7},{7,6},{8,9},{9,8},{10,11... | collective-permute-start | bytes 196616 | tf_op jit(solution)/shard_map/ppermute | solution.py:23
  35.1 2.6 %collective-permute-start.18 = (f32[16,1024]{1,0:T(8,128)S(1)}, f32[16,1024]{1,0:T(8,128)S(1)}, u32[]{:S(2)}, u32[]{:S(2)}) collective-permute-start(f32[16,1024]{1,0:T(8,128)S(1)} %get-tuple-element.49), channel_id=1, source_target_pairs={{0,2},{1,3},{2,0},{3,1},{4,6},{5,7},{6,4},{7,5},{8,10},{9,11},{10,... | collective-permute-start | bytes 196616 | tf_op jit(solution)/shard_map/ppermute | solution.py:23
  38.4 2.6 %collective-permute-done.18 = f32[16,1024]{1,0:T(8,128)S(1)} collective-permute-done((f32[16,1024]{1,0:T(8,128)S(1)}, f32[16,1024]{1,0:T(8,128)S(1)}, u32[]{:S(2)}, u32[]{:S(2)}) %collective-permute-start.18) | collective-permute-done | bytes 65568 | tf_op jit(solution)/shard_map/ppermute | solution.py:23
  41.0 1.9 %collective-permute-start.17 = (f32[16,1024]{1,0:T(8,128)S(1)}, f32[16,1024]{1,0:T(8,128)S(1)}, u32[]{:S(2)}, u32[]{:S(2)}) collective-permute-start(f32[16,1024]{1,0:T(8,128)S(1)} %get-tuple-element.46), channel_id=1, source_target_pairs={{0,2},{1,3},{2,0},{3,1},{4,6},{5,7},{6,4},{7,5},{8,10},{9,11},{10,... | collective-permute-start | bytes 196616 | tf_op jit(solution)/shard_map/ppermute | solution.py:23
  48.2 20.2 %collective-permute-done.7.refs_5_ = bf16[128,2048]{1,0:T(8,128)(2,1)S(1)} collective-permute-done((bf16[128,2048]{1,0:T(8,128)(2,1)S(1)}, bf16[128,2048]{1,0:T(8,128)(2,1)S(1)}, u32[]{:S(2)}, u32[]{:S(2)}) %collective-permute-start.7) | collective-permute-done | bytes 524320 | tf_op jit(solution)/shard_map/ppermute | solution.py:23
  68.4 8.2 %shard_map.166 = (f32[16,2048]{1,0:T(8,128)S(1)}, f32[16,128]{1,0:T(8,128)S(1)}) custom-call(s32[1,2048]{1,0:T(1,128)S(1)} %fusion.22.refs_0_, bf16[1024,2048]{1,0:T(8,128)(2,1)S(1)} %copy-done.1, bf16[1024,2048]{1,0:T(8,128)(2,1)} %collective-permute-done.1.refs_2_.refs_4_, s32[1,128]{1,0:T(1,128)S(1)} %pad_bitcast_fusion.refs_3_, ...), custom_call_target="tpu_custom_call" | custom-call | flops 2147483648 | bytes 9437184 | tf_op jit(solution)/shard_map/pallas_call | solution.py:99
  76.7 17.1 %shard_map.165 = (f32[16,2048]{1,0:T(8,128)S(1)}, f32[16,128]{1,0:T(8,128)S(1)}) custom-call(s32[1,2048]{1,0:T(1,128)S(1)} %fusion.22.refs_0_, bf16[1024,2048]{1,0:T(8,128)(2,1)} %refs_3_.6, bf16[1024,2048]{1,0:T(8,128)(2,1)} %collective-permute-done.1.refs_2_.refs_4_, s32[1,128]{1,0:T(1,128)S(1)} %pad_bitcast_fusion.refs_3_, ...), custom_call_target="tpu_custom_call" | custom-call | flops 6442450944 | bytes 11534336 | tf_op jit(solution)/shard_map/pallas_call | solution.py:99
  93.8 1.6 %collective-permute-start.26 = (f32[16,1024]{1,0:T(8,128)S(1)}, f32[16,1024]{1,0:T(8,128)S(1)}, u32[]{:S(2)}, u32[]{:S(2)}) collective-permute-start(f32[16,1024]{1,0:T(8,128)S(1)} %slice.70), channel_id=1, source_target_pairs={{0,1},{1,0},{2,3},{3,2},{4,5},{5,4},{6,7},{7,6},{8,9},{9,8},{10,11... | collective-permute-start | bytes 196616 | tf_op jit(solution)/shard_map/ppermute | solution.py:23
  95.4 5.9 %shard_map.170 = (bf16[128,2048]{1,0:T(8,128)(2,1)}, bf16[128,2048]{1,0:T(8,128)(2,1)}) custom-call(s32[1,2048]{1,0:T(1,128)S(1)} %fusion.22.refs_0_, s32[1,2048]{1,0:T(1,128)S(1)} %bitcast.65, f32[16,2048]{1,0:T(8,128)S(1)} %pad_maximum_fusion.1.refs_2_, bf16[1024,2048]{1,0:T(8,128)(2,1)S(1)} %copy-done.2, ...), custom_call_target="tpu_custom_call" | custom-call | flops 2147483648 | bytes 10485760 | tf_op jit(solution)/shard_map/pallas_call | solution.py:149
  101.3 1.5 collective-permute-start.21
  102.9 2.7 %collective-permute-start.9 = (f32[16,1152]{1,0:T(8,128)S(1)}, f32[16,1152]{1,0:T(8,128)S(1)}, u32[]{:S(2)}, u32[]{:S(2)}) collective-permute-start(f32[16,1152]{1,0:T(8,128)S(1)} %pad_maximum_fusion.3), channel_id=1, source_target_pairs={{0,2},{1,3},{2,0},{3,1},{4,6},{5,7},{6,4},{7,5},{8,10},{9,11},{10,... | collective-permute-start | bytes 221192 | tf_op jit(solution)/shard_map/ppermute | solution.py:23
  105.5 8.2 %shard_map.169 = (f32[128,2048]{1,0:T(8,128)S(1)}, bf16[128,2048]{1,0:T(8,128)(2,1)S(1)}, bf16[128,2048]{1,0:T(8,128)(2,1)}, f32[128,2048]{1,0:T(8,128)S(1)}) custom-call(s32[1,2048]{1,0:T(1,128)S(1)} %fusion.22.refs_0_, s32[1,2048]{1,0:T(1,128)S(1)} %bitcast.66, f32[16,2048]{1,0:T(8,128)S(1)} %pad_maximum_fusion.1.refs_2_, bf16[1024,2048]{1,0:T(8,128)(2,1)} %refs_3_.6, ...), custom_call_target="tpu_custom_call" | custom-call | flops 4294967296 | bytes 12582912 | tf_op jit(solution)/shard_map/pallas_call | solution.py:149
  117.1 5.7 %shard_map.168 = (f32[128,2048]{1,0:T(8,128)S(1)}, f32[128,2048]{1,0:T(8,128)S(1)}) custom-call(s32[1,2048]{1,0:T(1,128)S(1)} %fusion.22.refs_0_, s32[1,2048]{1,0:T(1,128)S(1)} %bitcast.67, f32[16,2048]{1,0:T(8,128)S(1)} %pad_maximum_fusion.1.refs_2_, bf16[1024,2048]{1,0:T(8,128)(2,1)} %refs_3_.6, bf16[1024,2048]{1,0:T(8,128)(2,1)} %collective-permute-done.1.refs_2_.refs_4_), custom_call_target="tpu_custom_call" | custom-call | flops 2147483648 | bytes 10485760 | tf_op jit(solution)/shard_map/pallas_call | solution.py:149
  134.5 2.5 %collective-permute-done.30 = bf16[256,256]{1,0:T(8,128)(2,1)S(1)} collective-permute-done((bf16[256,256]{1,0:T(8,128)(2,1)S(1)}, bf16[256,256]{1,0:T(8,128)(2,1)S(1)}, u32[]{:S(2)}, u32[]{:S(2)}) %collective-permute-start.30) | collective-permute-done | bytes 131104 | tf_op jit(solution)/shard_map/ppermute | solution.py:23
  137.1 1.7 %convert_add_fusion.2 = f32[256,256]{1,0:T(8,128)} fusion(bf16[256,256]{1,0:T(8,128)(2,1)S(1)} %collective-permute-done.30, bf16[256,256]{1,0:T(8,128)(2,1)} %collective-permute-done.29, f32[256,256]{1,0:T(8,128)S(1)} %get-tuple-element.38, bf16[256,256]{1,0:T(8,128)(2,1)} %collective-permute-done.28), kind=kLoop, calls=%fused_computation.24 | loop fusion | flops 393216 | bytes 917504 | tf_op jit(solution)/shard_map/add | solution.py:375
  140.0 17.7 %collective-permute-done.22 = bf16[128,2048]{1,0:T(8,128)(2,1)S(1)} collective-permute-done((bf16[128,2048]{1,0:T(8,128)(2,1)S(1)}, bf16[128,2048]{1,0:T(8,128)(2,1)S(1)}, u32[]{:S(2)}, u32[]{:S(2)}) %collective-permute-start.22) | collective-permute-done | bytes 524320 | tf_op jit(solution)/shard_map/ppermute | solution.py:23
  (136 shorter events, 36.9 us)
Async XLA Ops:
  0.6 27.0 %collective-permute-start.11 = (bf16[256,256]{1,0:T(8,128)(2,1)}, bf16[256,256]{1,0:T(8,128)(2,1)S(1)}, u32[]{:S(2)}, u32[]{:S(2)}) collective-permute-start(bf16[256,256]{1,0:T(8,128)(2,1)} %bitcast.61), channel_id=1, source_target_pairs={{0,8},{4,12},{8,0},{12,4},{16,24},{20,28},{24,16},{28,20},{1,9},{5... | collective-permute-start | bytes 393224 | tf_op jit(solution)/shard_map/ppermute | solution.py:23
  3.6 26.0 %collective-permute-start.12 = (bf16[256,256]{1,0:T(8,128)(2,1)}, bf16[256,256]{1,0:T(8,128)(2,1)S(1)}, u32[]{:S(2)}, u32[]{:S(2)}) collective-permute-start(bf16[256,256]{1,0:T(8,128)(2,1)} %bitcast.62), channel_id=1, source_target_pairs={{0,16},{4,20},{8,24},{12,28},{16,0},{20,4},{24,8},{28,12},{1,17},{... | collective-permute-start | bytes 393224 | tf_op jit(solution)/shard_map/ppermute | solution.py:23
  5.2 26.0 %collective-permute-start.13 = (bf16[256,256]{1,0:T(8,128)(2,1)}, bf16[256,256]{1,0:T(8,128)(2,1)S(1)}, u32[]{:S(2)}, u32[]{:S(2)}) collective-permute-start(bf16[256,256]{1,0:T(8,128)(2,1)} %bitcast.63), channel_id=1, source_target_pairs={{0,24},{4,28},{8,16},{12,20},{16,8},{20,12},{24,0},{28,4},{1,25},{... | collective-permute-start | bytes 393224 | tf_op jit(solution)/shard_map/ppermute | solution.py:23
  6.5 17.2 %collective-permute-start = (s32[2080]{0:T(1024)}, s32[2080]{0:T(1024)}, u32[]{:S(2)}, u32[]{:S(2)}) collective-permute-start(s32[2080]{0:T(1024)} %pad_add_fusion), channel_id=1, source_target_pairs={{0,4},{4,0},{8,12},{12,8},{16,20},{20,16},{24,28},{28,24},{1,5},{5... | collective-permute-start | bytes 24968 | tf_op jit(solution)/shard_map/ppermute | solution.py:23
  6.5 61.9 %collective-permute-start.1 = (bf16[1024,2048]{1,0:T(8,128)(2,1)}, bf16[1024,2048]{1,0:T(8,128)(2,1)}, u32[]{:S(2)}, u32[]{:S(2)}) collective-permute-start(bf16[1024,2048]{1,0:T(8,128)(2,1)} %refs_3_.6), channel_id=1, source_target_pairs={{0,4},{4,0},{8,12},{12,8},{16,20},{20,16},{24,28},{28,24},{1,5},{5... | collective-permute-start | bytes 12582920 | tf_op jit(solution)/shard_map/ppermute | solution.py:23
  23.7 7.5 %collective-permute-start.15 = (bf16[1024,256]{1,0:T(8,128)(2,1)S(1)}, bf16[1024,256]{1,0:T(8,128)(2,1)S(1)}, u32[]{:S(2)}, u32[]{:S(2)}) collective-permute-start(bf16[1024,256]{1,0:T(8,128)(2,1)S(1)} %copy-done.8), channel_id=1, source_target_pairs={{0,4},{4,0},{8,12},{12,8},{16,20},{20,16},{24,28},{28,24},{1,5},{5... | collective-permute-start | bytes 1572872 | tf_op jit(solution)/shard_map/ppermute | solution.py:23
  27.7 15.9 %collective-permute-start.3 = (bf16[128,2048]{1,0:T(8,128)(2,1)}, bf16[128,2048]{1,0:T(8,128)(2,1)S(1)}, u32[]{:S(2)}, u32[]{:S(2)}) collective-permute-start(bf16[128,2048]{1,0:T(8,128)(2,1)} %bitcast.73), channel_id=1, source_target_pairs={{0,8},{4,12},{8,0},{12,4},{16,24},{20,28},{24,16},{28,20},{1,9},{5... | collective-permute-start | bytes 1572872 | tf_op jit(solution)/shard_map/ppermute | solution.py:23
  29.7 14.4 %collective-permute-start.6 = (bf16[128,2048]{1,0:T(8,128)(2,1)}, bf16[128,2048]{1,0:T(8,128)(2,1)S(1)}, u32[]{:S(2)}, u32[]{:S(2)}) collective-permute-start(bf16[128,2048]{1,0:T(8,128)(2,1)} %bitcast.75), channel_id=1, source_target_pairs={{0,16},{4,20},{8,24},{12,28},{16,0},{20,4},{24,8},{28,12},{1,17},{... | collective-permute-start | bytes 1572872 | tf_op jit(solution)/shard_map/ppermute | solution.py:23
  43.6 33.0 %collective-permute-start.4 = (bf16[128,2048]{1,0:T(8,128)(2,1)}, bf16[128,2048]{1,0:T(8,128)(2,1)S(1)}, u32[]{:S(2)}, u32[]{:S(2)}) collective-permute-start(bf16[128,2048]{1,0:T(8,128)(2,1)} %bitcast.76), channel_id=1, source_target_pairs={{0,8},{4,12},{8,0},{12,4},{16,24},{20,28},{24,16},{28,20},{1,9},{5... | collective-permute-start | bytes 1572872 | tf_op jit(solution)/shard_map/ppermute | solution.py:23
  44.1 32.5 %collective-permute-start.5 = (bf16[128,2048]{1,0:T(8,128)(2,1)S(1)}, bf16[128,2048]{1,0:T(8,128)(2,1)S(1)}, u32[]{:S(2)}, u32[]{:S(2)}) collective-permute-start(bf16[128,2048]{1,0:T(8,128)(2,1)S(1)} %bitcast.74), channel_id=1, source_target_pairs={{0,16},{4,20},{8,24},{12,28},{16,0},{20,4},{24,8},{28,12},{1,17},{... | collective-permute-start | bytes 1572872 | tf_op jit(solution)/shard_map/ppermute | solution.py:23
  46.8 21.6 %collective-permute-start.7 = (bf16[128,2048]{1,0:T(8,128)(2,1)S(1)}, bf16[128,2048]{1,0:T(8,128)(2,1)S(1)}, u32[]{:S(2)}, u32[]{:S(2)}) collective-permute-start(bf16[128,2048]{1,0:T(8,128)(2,1)S(1)} %collective-permute-done.3.refs_6_), channel_id=1, source_target_pairs={{0,16},{4,20},{8,24},{12,28},{16,0},{20,4},{24,8},{28,12},{1,17},{... | collective-permute-start | bytes 1572872 | tf_op jit(solution)/shard_map/ppermute | solution.py:23
  47.4 20.9 %collective-permute-start.8 = (bf16[128,2048]{1,0:T(8,128)(2,1)S(1)}, bf16[128,2048]{1,0:T(8,128)(2,1)S(1)}, u32[]{:S(2)}, u32[]{:S(2)}) collective-permute-start(bf16[128,2048]{1,0:T(8,128)(2,1)S(1)} %collective-permute-done.6.refs_9_), channel_id=1, source_target_pairs={{0,8},{4,12},{8,0},{12,4},{16,24},{20,28},{24,16},{28,20},{1,9},{5... | collective-permute-start | bytes 1572872 | tf_op jit(solution)/shard_map/ppermute | solution.py:23
  93.8 9.0 %collective-permute-start.26 = (f32[16,1024]{1,0:T(8,128)S(1)}, f32[16,1024]{1,0:T(8,128)S(1)}, u32[]{:S(2)}, u32[]{:S(2)}) collective-permute-start(f32[16,1024]{1,0:T(8,128)S(1)} %slice.70), channel_id=1, source_target_pairs={{0,1},{1,0},{2,3},{3,2},{4,5},{5,4},{6,7},{7,6},{8,9},{9,8},{10,11... | collective-permute-start | bytes 196616 | tf_op jit(solution)/shard_map/ppermute | solution.py:23
  101.3 28.7 %collective-permute-start.21 = (bf16[128,2048]{1,0:T(8,128)(2,1)}, bf16[128,2048]{1,0:T(8,128)(2,1)}, u32[]{:S(2)}, u32[]{:S(2)}) collective-permute-start(bf16[128,2048]{1,0:T(8,128)(2,1)} %get-tuple-element.33), channel_id=1, source_target_pairs={{0,16},{4,20},{8,24},{12,28},{16,0},{20,4},{24,8},{28,12},{1,17},{... | collective-permute-start | bytes 1572872 | tf_op jit(solution)/shard_map/ppermute | solution.py:23
  102.9 13.2 %collective-permute-start.9 = (f32[16,1152]{1,0:T(8,128)S(1)}, f32[16,1152]{1,0:T(8,128)S(1)}, u32[]{:S(2)}, u32[]{:S(2)}) collective-permute-start(f32[16,1152]{1,0:T(8,128)S(1)} %pad_maximum_fusion.3), channel_id=1, source_target_pairs={{0,2},{1,3},{2,0},{3,1},{4,6},{5,7},{6,4},{7,5},{8,10},{9,11},{10,... | collective-permute-start | bytes 221192 | tf_op jit(solution)/shard_map/ppermute | solution.py:23
  114.7 25.4 %collective-permute-start.20 = (bf16[128,2048]{1,0:T(8,128)(2,1)}, bf16[128,2048]{1,0:T(8,128)(2,1)}, u32[]{:S(2)}, u32[]{:S(2)}) collective-permute-start(bf16[128,2048]{1,0:T(8,128)(2,1)} %get-tuple-element.31), channel_id=1, source_target_pairs={{0,16},{4,20},{8,24},{12,28},{16,0},{20,4},{24,8},{28,12},{1,17},{... | collective-permute-start | bytes 1572872 | tf_op jit(solution)/shard_map/ppermute | solution.py:23
  115.2 23.6 %collective-permute-start.24 = (bf16[128,2048]{1,0:T(8,128)(2,1)}, bf16[128,2048]{1,0:T(8,128)(2,1)}, u32[]{:S(2)}, u32[]{:S(2)}) collective-permute-start(bf16[128,2048]{1,0:T(8,128)(2,1)} %get-tuple-element.37), channel_id=1, source_target_pairs={{0,8},{4,12},{8,0},{12,4},{16,24},{20,28},{24,16},{28,20},{1,9},{5... | collective-permute-start | bytes 1572872 | tf_op jit(solution)/shard_map/ppermute | solution.py:23
  115.7 7.1 %collective-permute-start.27 = (f32[16,1024]{1,0:T(8,128)S(1)}, f32[16,1024]{1,0:T(8,128)S(1)}, u32[]{:S(2)}, u32[]{:S(2)}) collective-permute-start(f32[16,1024]{1,0:T(8,128)S(1)} %get-tuple-element.44), channel_id=1, source_target_pairs={{0,2},{1,3},{2,0},{3,1},{4,6},{5,7},{6,4},{7,5},{8,10},{9,11},{10,... | collective-permute-start | bytes 196616 | tf_op jit(solution)/shard_map/ppermute | solution.py:23
  125.0 7.4 %collective-permute-start.28 = (bf16[256,256]{1,0:T(8,128)(2,1)S(1)}, bf16[256,256]{1,0:T(8,128)(2,1)}, u32[]{:S(2)}, u32[]{:S(2)}) collective-permute-start(bf16[256,256]{1,0:T(8,128)(2,1)S(1)} %get-tuple-element.39), channel_id=1, source_target_pairs={{0,8},{4,12},{8,0},{12,4},{16,24},{20,28},{24,16},{28,20},{1,9},{5... | collective-permute-start | bytes 393224 | tf_op jit(solution)/shard_map/ppermute | solution.py:23
  126.2 7.4 %collective-permute-start.29 = (bf16[256,256]{1,0:T(8,128)(2,1)S(1)}, bf16[256,256]{1,0:T(8,128)(2,1)}, u32[]{:S(2)}, u32[]{:S(2)}) collective-permute-start(bf16[256,256]{1,0:T(8,128)(2,1)S(1)} %get-tuple-element.40), channel_id=1, source_target_pairs={{0,16},{4,20},{8,24},{12,28},{16,0},{20,4},{24,8},{28,12},{1,17},{... | collective-permute-start | bytes 393224 | tf_op jit(solution)/shard_map/ppermute | solution.py:23
  130.0 7.0 %collective-permute-start.30 = (bf16[256,256]{1,0:T(8,128)(2,1)S(1)}, bf16[256,256]{1,0:T(8,128)(2,1)S(1)}, u32[]{:S(2)}, u32[]{:S(2)}) collective-permute-start(bf16[256,256]{1,0:T(8,128)(2,1)S(1)} %get-tuple-element.41), channel_id=1, source_target_pairs={{0,24},{4,28},{8,16},{12,20},{16,8},{20,12},{24,0},{28,4},{1,25},{... | collective-permute-start | bytes 393224 | tf_op jit(solution)/shard_map/ppermute | solution.py:23
  132.4 26.6 %collective-permute-start.23 = (bf16[128,2048]{1,0:T(8,128)(2,1)}, bf16[128,2048]{1,0:T(8,128)(2,1)S(1)}, u32[]{:S(2)}, u32[]{:S(2)}) collective-permute-start(bf16[128,2048]{1,0:T(8,128)(2,1)} %copy-done.10), channel_id=1, source_target_pairs={{0,8},{4,12},{8,0},{12,4},{16,24},{20,28},{24,16},{28,20},{1,9},{5... | collective-permute-start | bytes 1572872 | tf_op jit(solution)/shard_map/ppermute | solution.py:23
  133.6 24.2 %collective-permute-start.22 = (bf16[128,2048]{1,0:T(8,128)(2,1)S(1)}, bf16[128,2048]{1,0:T(8,128)(2,1)S(1)}, u32[]{:S(2)}, u32[]{:S(2)}) collective-permute-start(bf16[128,2048]{1,0:T(8,128)(2,1)S(1)} %add_convert_fusion.1), channel_id=1, source_target_pairs={{0,8},{4,12},{8,0},{12,4},{16,24},{20,28},{24,16},{28,20},{1,9},{5... | collective-permute-start | bytes 1572872 | tf_op jit(solution)/shard_map/ppermute | solution.py:23
  140.0 19.1 %collective-permute-start.25 = (bf16[128,2048]{1,0:T(8,128)(2,1)S(1)}, bf16[128,2048]{1,0:T(8,128)(2,1)S(1)}, u32[]{:S(2)}, u32[]{:S(2)}) collective-permute-start(bf16[128,2048]{1,0:T(8,128)(2,1)S(1)} %add_convert_fusion), channel_id=1, source_target_pairs={{0,16},{4,20},{8,24},{12,28},{16,0},{20,4},{24,8},{28,12},{1,17},{... | collective-permute-start | bytes 1572872 | tf_op jit(solution)/shard_map/ppermute | solution.py:23
  (23 other events, 218.5 us)

commit v2 on v1

v2 whole, which is shorter than its diff:
```python
import functools
import math

import jax
import jax.numpy as jnp
from jax import lax
from jax.experimental import pallas as pl
from jax.experimental.pallas import tpu as pltpu
from jax.sharding import PartitionSpec as P

HEADS = 64
KEY_VALUE_HEADS = 8
HEAD_SIZE = 128
CACHE = 256

ADAPTER_SCALE = 2.0
NEG_FILL = -1e30
VMEM_LIMIT = 60 * 1024 * 1024


def swap(array, axis, mask):
    count = lax.axis_size(axis)
    return lax.ppermute(array, axis, [(i, i ^ mask) for i in range(count)])


def axis_bits(axis):
    count = lax.axis_size(axis)
    assert count & (count - 1) == 0, "axis size"
    return [1 << k for k in range(count.bit_length() - 1)]


def highest_in(order, mask):
    return [bit for bit in order if bit & mask][-1]


def largest_tile(length, limit):
    tile = length
    while tile > limit and tile % 2 == 0:
        tile //= 2
    return tile


def pick(codes, products, chunk_bases, rank, adapters):
    total = jnp.zeros((rank, products.shape[1]), jnp.float32)
    for k, base in enumerate(chunk_bases):
        for j in range(adapters):
            first = (k * adapters + j) * rank
            total += jnp.where(codes == base + j, products[first : first + rank], 0.0)
    return total


def spread(codes, values, chunk_bases, adapters, out_ref):
    rank = values.shape[0]
    for k, base in enumerate(chunk_bases):
        for j in range(adapters):
            first = (k * adapters + j) * rank
            out_ref[first : first + rank, :] = jnp.where(codes == base + j, values, 0.0).astype(
                out_ref.dtype
            )


def join(maps, joined_ref):
    rows = maps[0].shape[0]
    for k, chunk in enumerate(maps):
        joined_ref[k * rows : (k + 1) * rows, :] = chunk[...]


def times_transposed(maps, tokens):
    return lax.dot_general(
        maps, tokens, (((1,), (1,)), ((), ())), preferred_element_type=jnp.float32
    )


def token_kernel(chunk_bases, rank, adapters, own_tiles, waits, codes_ref, own_ref, mate_ref, *refs):
    maps = refs[: len(chunk_bases)]
    out_ref, joined_ref = refs[len(chunk_bases) + waits :]
    step = pl.program_id(0)

    @pl.when(step == 0)
    def _():
        join(maps, joined_ref)

    def project(tokens_ref):
        products = times_transposed(joined_ref[...], tokens_ref[...])
        out_ref[...] = pick(codes_ref[...], products, chunk_bases, rank, adapters)

    pl.when(step < own_tiles)(lambda: project(own_ref))
    pl.when(step >= own_tiles)(lambda: project(mate_ref))


def project_tokens(codes, own, mate, mate_column, chunks, rank, after=()):
    token_count, width = own.shape
    tile = largest_tile(token_count, 512)
    own_tiles = token_count // tile
    chunk_rows = chunks[0][1].shape[0]
    map_rows = len(chunks) * chunk_rows
    return pl.pallas_call(
        functools.partial(
            token_kernel,
            [base for base, _ in chunks],
            rank,
            chunk_rows // rank,
            own_tiles,
            len(after),
        ),
        grid=(2 * own_tiles,),
        in_specs=[
            pl.BlockSpec((1, tile), lambda i: (0, i)),
            pl.BlockSpec((tile, width), lambda i: (jnp.minimum(i, own_tiles - 1), 0)),
            pl.BlockSpec((tile, width), lambda i: (jnp.maximum(i - own_tiles, 0), mate_column)),
        ]
        + [pl.BlockSpec((chunk_rows, width), lambda i: (0, 0)) for _ in chunks]
        + [pl.BlockSpec(memory_space=pl.ANY) for _ in after],
        out_specs=pl.BlockSpec((rank, tile), lambda i: (0, i)),
        out_shape=jax.ShapeDtypeStruct((rank, 2 * token_count), jnp.float32),
        scratch_shapes=[pltpu.VMEM((map_rows, width), jnp.bfloat16)],
        compiler_params=pltpu.CompilerParams(vmem_limit_bytes=VMEM_LIMIT),
        cost_estimate=pl.CostEstimate(
            flops=4 * token_count * width * map_rows,
            bytes_accessed=4 * token_count * width + 2 * map_rows * width,
            transcendentals=0,
        ),
    )(codes, own, mate, *[chunk for _, chunk in chunks], *after)


def row_kernel(chunk_bases, rank, adapters, waits, codes_ref, own_ref, mate_ref, *refs):
    maps = refs[: len(chunk_bases)]
    out_ref, rows_ref = refs[len(chunk_bases) + waits :]
    count = own_ref.shape[0]
    rows_ref[:count, :] = own_ref[...]
    rows_ref[count:, :] = mate_ref[...]
    total = jnp.zeros(out_ref.shape, jnp.float32)
    for base, chunk in zip(chunk_bases, maps):
        products = times_transposed(chunk[...], rows_ref[...])
        total += pick(codes_ref[...], products, [base], rank, adapters)
    out_ref[...] = total


def project_rows(codes, own, mate, mate_row, chunks, rank, after=()):
    row_count, width = own.shape
    chunk_rows = chunks[0][1].shape[0]
    return pl.pallas_call(
        functools.partial(
            row_kernel, [base for base, _ in chunks], rank, chunk_rows // rank, len(after)
        ),
        grid=(1,),
        in_specs=[
            pl.BlockSpec((1, 2 * row_count), lambda i: (0, 0)),
            pl.BlockSpec((row_count, width), lambda i: (0, 0)),
            pl.BlockSpec((row_count, width), lambda i: (mate_row, 0)),
        ]
        + [pl.BlockSpec((chunk_rows, width), lambda i: (0, 0)) for _ in chunks]
        + [pl.BlockSpec(memory_space=pl.ANY) for _ in after],
        out_specs=pl.BlockSpec((rank, 2 * row_count), lambda i: (0, 0)),
        out_shape=jax.ShapeDtypeStruct((rank, 2 * row_count), jnp.float32),
        scratch_shapes=[pltpu.VMEM((2 * row_count, width), jnp.bfloat16)],
        compiler_params=pltpu.CompilerParams(vmem_limit_bytes=VMEM_LIMIT),
        cost_estimate=pl.CostEstimate(
            flops=4 * row_count * width * chunk_rows * len(chunks),
            bytes_accessed=2 * width * chunk_rows * len(chunks),
            transcendentals=0,
        ),
    )(codes, own, mate, *[chunk for _, chunk in chunks], *after)


def delta_kernel(chunk_bases, adapters, codes_ref, rank_ref, *refs):
    maps = refs[: len(chunk_bases)]
    out_ref, spread_ref = refs[len(chunk_bases) :]
    values = rank_ref[...].astype(jnp.bfloat16).astype(jnp.float32)
    total = jnp.zeros(out_ref.shape, jnp.float32)
    for base, chunk in zip(chunk_bases, maps):
        spread(codes_ref[...], values, [base], adapters, spread_ref)
        total += lax.dot_general(
            spread_ref[...].T.astype(jnp.bfloat16),
            chunk[...],
            (((1,), (0,)), ((), ())),
            preferred_element_type=jnp.float32,
        )
    out_ref[...] = (ADAPTER_SCALE * total).astype(out_ref.dtype)


def row_deltas(codes, ranks, chunks):
    rank, row_count = ranks.shape
    chunk_rows, width = chunks[0][1].shape
    return pl.pallas_call(
        functools.partial(delta_kernel, [base for base, _ in chunks], chunk_rows // rank),
        out_shape=jax.ShapeDtypeStruct((row_count, width), jnp.bfloat16),
        scratch_shapes=[pltpu.VMEM((chunk_rows, row_count), jnp.float32)],
        compiler_params=pltpu.CompilerParams(vmem_limit_bytes=VMEM_LIMIT),
    )(codes, ranks, *[chunk for _, chunk in chunks])


def gradient_kernel(chunk_bases, adapters, waits, codes_ref, rewards_ref, factor_ref, *refs):
    own_ref, mate_ref = refs[:2]
    outs = refs[2 + waits : -1]
    spread_ref = refs[-1]
    token_count = own_ref.shape[0]

    @pl.when(pl.program_id(0) == 0)
    def _():
        scale = ADAPTER_SCALE * rewards_ref[...].astype(jnp.float32)
        scaled = (scale * factor_ref[...]).astype(jnp.bfloat16).astype(jnp.float32)
        spread(codes_ref[...], scaled, chunk_bases, adapters, spread_ref)

    total = jnp.dot(
        spread_ref[:, :token_count], own_ref[...], preferred_element_type=jnp.float32
    ) + jnp.dot(spread_ref[:, token_count:], mate_ref[...], preferred_element_type=jnp.float32)
    for k, out_ref in enumerate(outs):
        rows = out_ref.shape[0]
        out_ref[...] = total[k * rows : (k + 1) * rows].astype(out_ref.dtype)


def gradient_chunks(codes, rewards, factor, own, mate, mate_column, chunks, adapters, after=()):
    rank = factor.shape[0]
    token_count, width = own.shape
    tile = largest_tile(width, 512)
    rows = adapters * rank
    first_mate = mate_column * (width // tile)
    whole = lambda i: (0, 0)
    return pl.pallas_call(
        functools.partial(gradient_kernel, [base for base, _ in chunks], adapters, len(after)),
        grid=(width // tile,),
        in_specs=[
            pl.BlockSpec(codes.shape, whole),
            pl.BlockSpec(rewards.shape, whole),
            pl.BlockSpec(factor.shape, whole),
            pl.BlockSpec((token_count, tile), lambda i: (0, i)),
            pl.BlockSpec((token_count, tile), lambda i: (0, first_mate + i)),
        ]
        + [pl.BlockSpec(memory_space=pl.ANY) for _ in after],
        out_specs=[pl.BlockSpec((rows, tile), lambda i: (0, i)) for _ in chunks],
        out_shape=[jax.ShapeDtypeStruct((rows, width), dtype) for _, dtype in chunks],
        scratch_shapes=[pltpu.VMEM((len(chunks) * rows, 2 * token_count), jnp.bfloat16)],
        compiler_params=pltpu.CompilerParams(vmem_limit_bytes=VMEM_LIMIT),
        cost_estimate=pl.CostEstimate(
            flops=4 * token_count * width * rows * len(chunks),
            bytes_accessed=4 * token_count * width + 4 * rows * width * len(chunks),
            transcendentals=0,
        ),
    )(codes, rewards, factor, own, mate, *after)


def sum_over(axis, piece):
    for bit in axis_bits(axis):
        piece = piece + swap(piece, axis, bit)
    return piece


def attend_cached(queries, cached_key_rows, cached_value_rows, lengths, fresh_keys):
    row_count = queries.shape[0]
    kv_local = fresh_keys.shape[1] // HEAD_SIZE
    group = HEADS // KEY_VALUE_HEADS
    query_heads = queries.reshape(row_count, kv_local, group, HEAD_SIZE)
    key_heads = cached_key_rows.reshape(row_count, CACHE, kv_local, HEAD_SIZE)
    value_heads = cached_value_rows.reshape(row_count, CACHE, kv_local, HEAD_SIZE)
    inverse = 1.0 / math.sqrt(HEAD_SIZE)
    scores = (
        jnp.einsum("bhgd,bphd->bhgp", query_heads, key_heads, preferred_element_type=jnp.float32)
        * inverse
    )
    own_score = (
        jnp.einsum(
            "bhgd,bhd->bhg",
            query_heads,
            fresh_keys.reshape(row_count, kv_local, HEAD_SIZE),
            preferred_element_type=jnp.float32,
        )
        * inverse
    )
    allowed = jnp.arange(CACHE, dtype=jnp.int32)[None, :] < lengths[:, None]
    scores = jnp.where(allowed[:, None, None, :], scores, NEG_FILL)
    highest = jnp.maximum(jnp.max(scores, axis=-1), own_score)
    cache_exp = jnp.exp(scores - highest[..., None])
    own_exp = jnp.exp(own_score - highest)
    denominator = jnp.sum(cache_exp, axis=-1) + own_exp
    cache_weight = (cache_exp / denominator[..., None]).astype(jnp.bfloat16)
    own_weight = (own_exp / denominator).astype(jnp.bfloat16)
    attended = jnp.einsum(
        "bhgp,bphd->bhgd", cache_weight, value_heads, preferred_element_type=jnp.float32
    )
    return attended, own_weight


def per_device(
    decode_hidden_input,
    queries,
    cached_key_rows,
    cached_value_rows,
    lengths,
    decode_adapter_index,
    key_matrix,
    value_matrix,
    adapter_down_map,
    adapter_up_map,
    training_hidden_input,
    cotangent,
    training_adapter_index,
    rewards,
):
    core_bit, *chip_bits = axis_bits("wide")
    masks = [m for m in range(lax.axis_size("wide")) if not m & core_bit]
    me = lax.axis_index("wide")
    owner_totals, rank, down_width = adapter_down_map.shape
    up_width = adapter_up_map.shape[2]
    row_count = decode_hidden_input.shape[0]
    token_count = training_hidden_input.shape[0]
    parts = len(chip_bits) if owner_totals % len(chip_bits) == 0 else 1
    orders = [chip_bits[p:] + chip_bits[:p] for p in range(parts)]
    part_adapters = owner_totals // parts
    part_rows = part_adapters * rank

    flattened_down = adapter_down_map.reshape(-1, down_width)
    flattened_up = adapter_up_map.reshape(-1, up_width)

    up_maps = {m: swap(flattened_up, "wide", m) if m else flattened_up for m in masks}
    down_parts = {}
    for p, order in enumerate(orders):
        down_parts[0, p] = flattened_down[p * part_rows : (p + 1) * part_rows]
        held = [0]
        for bit in order:
            for m in held:
                down_parts[m | bit, p] = swap(down_parts[m, p], "wide", bit)
            held = held + [m | bit for m in held]

    numbers = jnp.concatenate([training_adapter_index, rewards, decode_adapter_index])
    mate_numbers = swap(numbers, "wide", core_bit)
    decode_slice = lax.dynamic_slice_in_dim(
        decode_hidden_input, lax.axis_index("narrow") * down_width, down_width, 1
    )
    own_all = jnp.concatenate(
        [
            jnp.concatenate([training_hidden_input, cotangent], axis=1),
            jnp.pad(decode_slice, ((0, 0), (0, up_width))),
        ]
    )
    mate_all = swap(own_all, "wide", core_bit)
    assert token_count % row_count == 0 and down_width % up_width == 0, "block sizes"

    def codes_of(ids):
        return (((ids // owner_totals) ^ me) * owner_totals + ids % owner_totals)[None, :]

    token_codes = codes_of(
        jnp.concatenate([training_adapter_index, mate_numbers[:token_count]])
    )
    token_rewards = jnp.concatenate([rewards, mate_numbers[token_count : 2 * token_count]])[
        None, :
    ]
    row_codes = codes_of(
        jnp.concatenate([decode_adapter_index, mate_numbers[2 * token_count :]])
    )
    up_chunks = [(m * owner_totals, up_maps[m]) for m in masks]
    up_column = down_width // up_width

    def down_chunks(chosen):
        return [
            (m * owner_totals + p * part_adapters, down_parts[m, p])
            for m in chosen
            for p in range(parts)
        ]

    part_back = project_tokens(token_codes, cotangent, mate_all, up_column, up_chunks, rank)
    back = sum_over("narrow", part_back)
    grads = {}

    def down_gradients(chosen, after):
        keys = [(m, p) for m in chosen for p in range(parts)]
        results = gradient_chunks(
            token_codes,
            token_rewards,
            back,
            training_hidden_input,
            mate_all,
            0,
            [
                (
                    m * owner_totals + p * part_adapters,
                    jnp.bfloat16 if m & orders[p][-1] else jnp.float32,
                )
                for m, p in keys
            ],
            part_adapters,
            after,
        )
        grads.update(zip(keys, results))
        return results[:1]

    far = [m for m in masks if m.bit_count() > 1]
    near = [m for m in masks if m.bit_count() == 1]
    order_token = down_gradients(far, ()) if far else ()
    order_token = down_gradients(near, order_token)

    part_hidden = project_tokens(
        token_codes,
        training_hidden_input,
        mate_all,
        0,
        down_chunks([0] + near),
        rank,
        order_token,
    )
    part_ranks = project_rows(
        row_codes,
        decode_slice,
        mate_all,
        token_count // row_count,
        down_chunks(masks),
        rank,
        (part_hidden,),
    )
    if far:
        part_hidden = part_hidden + project_tokens(
            token_codes,
            training_hidden_input,
            mate_all,
            0,
            down_chunks(far),
            rank,
            (part_ranks,),
        )
    down_gradients([0], (part_hidden,))
    hidden = sum_over("narrow", part_hidden)
    decode_ranks = sum_over("narrow", part_ranks)

    for p, order in enumerate(orders):
        held = list(masks)
        for bit in reversed(order):
            sent = [m for m in held if m & bit]
            held = [m for m in held if not m & bit]
            for m in sorted(sent, key=lambda v: -v.bit_count()):
                arrived = swap(grads[m, p].astype(jnp.bfloat16), "wide", bit)
                grads[m ^ bit, p] = grads[m ^ bit, p] + arrived.astype(jnp.float32)
    grad_down = jnp.concatenate([grads[0, p] for p in range(parts)])

    up_results = gradient_chunks(
        token_codes,
        token_rewards,
        hidden,
        cotangent,
        mate_all,
        up_column,
        [(m * owner_totals, jnp.bfloat16 if m else jnp.float32) for m in masks],
        owner_totals,
    )
    grad_up = up_results[0]
    for m, result in zip(masks[1:], up_results[1:]):
        grad_up = grad_up + swap(result, "wide", m).astype(jnp.float32)

    delta = row_deltas(row_codes, decode_ranks, up_chunks)
    own_delta = delta[:row_count] + swap(delta[row_count:], "wide", core_bit)
    decode_hidden_input, queries, part_back = lax.optimization_barrier(
        (decode_hidden_input, queries, part_back)
    )
    fresh_keys = jnp.dot(
        decode_hidden_input, key_matrix, preferred_element_type=jnp.float32
    ).astype(jnp.bfloat16)
    base_values = jnp.dot(decode_hidden_input, value_matrix, preferred_element_type=jnp.float32)
    cached, own_weight = attend_cached(
        queries, cached_key_rows, cached_value_rows, lengths, fresh_keys
    )
    cached, own_weight, base_values = lax.optimization_barrier((cached, own_weight, base_values))
    fresh_values = (base_values + own_delta.astype(jnp.float32)).astype(jnp.bfloat16)
    kv_local = up_width // HEAD_SIZE
    attended = cached + own_weight.astype(jnp.float32)[..., None] * fresh_values.reshape(
        row_count, kv_local, 1, HEAD_SIZE
    ).astype(jnp.float32)
    return (
        attended.reshape(row_count, -1).astype(jnp.bfloat16),
        fresh_values,
        grad_down.reshape(adapter_down_map.shape),
        grad_up.reshape(adapter_up_map.shape),
    )


def solution(mesh):
    return jax.shard_map(
        per_device,
        mesh=mesh,
        in_specs=(
            P("wide", None),
            P("wide", "narrow"),
            P("wide", None, "narrow"),
            P("wide", None, "narrow"),
            P("wide"),
            P("wide"),
            P(None, "narrow"),
            P(None, "narrow"),
            P("wide", None, "narrow"),
            P("wide", None, "narrow"),
            P("wide", "narrow"),
            P("wide", "narrow"),
            P("wide"),
            P("wide"),
        ),
        out_specs=(
            P("wide", "narrow"),
            P("wide", "narrow"),
            P("wide", None, "narrow"),
            P("wide", None, "narrow"),
        ),
        check_vma=False,
    )
```

time: 161 us -> 171 us (1.062)
  other arithmetic: 14.9 us -> 20.8 us
  Pallas kernels: 48.5 us -> 54.1 us
    concatenate x4 -> x1, other arithmetic: 0.16 us -> 7 us  [per_device(): jnp.concatenate([jnp.concatenate([training_hidden_input, cotangent], axis...]
    pallas_call x4, Pallas kernels: 21 us -> 24.9 us  [gradient_chunks(): pl.pallas_call(functools.partial(gradient_kernel, [base for base, _ in ch...]
    add x13 -> x9, other arithmetic: 2.14 us -> 5.17 us  [the longest x6 2.96 us: sum_over(): piece = piece + swap(piece, axis, bit)]
    unnamed x34 -> x56, local copies, waits for them, and re-layouts: 2.68 us -> 4.34 us
    pallas_call x3 -> x5, Pallas kernels: 27.5 us -> 29.1 us  [the longest x3 23 us: project_tokens(): pl.pallas_call(functools.partial(token_kernel, [base for base, _ in chunk...]
    ppermute x31 -> x27, starting transfers between devices: 32.4 us -> 33.3 us  [swap(): return lax.ppermute(array, axis, [(i, i ^ mask) for i in range(count)])]
    ppermute x31 -> x27, waiting for transfers between devices: 44.5 us -> 44 us  [swap(): return lax.ppermute(array, axis, [(i, i ^ mask) for i in range(count)])]
  transfers between devices with their start and end apart: 31 -> 27, of which waited for: 6 -> 9; matrix products, arithmetic and copies ran while one was open for 20% -> 16% of each run, Pallas kernels for 20% -> 29%
where the time goes in v2:
time: 171 us; the launch traced here: 170 us
  Pallas kernels  54.1 us (32%)
  waiting for transfers between devices  44 us (26%)
  starting transfers between devices  33.3 us (19%)
  other arithmetic  20.8 us (12%)
  matrix products  11.5 us (7%)
  local copies, waits for them, and re-layouts  5.78 us (3%)
    ppermute x27, waiting for transfers between devices, swap(): return lax.ppermute(array, axis, [(i, i ^ mask) for i in range(count)])  44 us
    ppermute x27, starting transfers between devices, swap(): return lax.ppermute(array, axis, [(i, i ^ mask) for i in range(count)])  33.3 us
    pallas_call x4, Pallas kernels, gradient_chunks(): pl.pallas_call(functools.partial(gradient_kernel, [base for base, _ in ch...  24.9 us
    pallas_call x3, Pallas kernels, project_tokens(): pl.pallas_call(functools.partial(token_kernel, [base for base, _ in chunk...  23 us
    concatenate x1, other arithmetic, per_device(): jnp.concatenate([jnp.concatenate([training_hidden_input, cotangent], axis...  7 us
    unnamed x56, local copies, waits for them, and re-layouts  4.34 us
    pallas_call x1, Pallas kernels, project_rows(): pl.pallas_call(functools.partial(row_kernel, [base for base, _ in chunks]...  4.09 us
    dot_general x1, matrix products, attend_cached(): jnp.einsum('bhgd,bphd->bhgp', query_heads, key_heads, preferred_element_t...  3.64 us
  transfers between devices with their start and end apart: 27, of which 9 were waited for; matrix products, arithmetic and copies ran while one was open for 16% of the time, Pallas kernels for 29%

profile of v2, /device:TPU:0, one launch (start us, length us, event | category | flops | bytes accessed | tf_op | source)
XLA Modules:
  0.0 170.5 jit_solution(3161092065538516916)
XLA Ops:
  1.8 7.0 %fusion.1 = bf16[1056,2304]{1,0:T(8,128)(2,1)} fusion(bf16[32,2048]{1,0:T(8,128)(2,1)S(1)} %constant_dynamic-slice_fusion.own_ref, bf16[1024,256]{1,0:T(8,128)(2,1)} %refs_0_.7, bf16[1024,2048]{1,0:T(8,128)(2,1)} %refs_0_.6), kind=kLoop, calls=%fused_computation.2 | loop fusion | flops 19464192 | bytes 9715712 | tf_op jit(solution)/shard_map/concatenate | solution.py:330
  9.2 2.6 %collective-permute-start.2 = (bf16[256,256]{1,0:T(8,128)(2,1)S(1)}, bf16[256,256]{1,0:T(8,128)(2,1)S(1)}, u32[]{:S(2)}, u32[]{:S(2)}) collective-permute-start(bf16[256,256]{1,0:T(8,128)(2,1)S(1)} %bitcast.59), channel_id=1, source_target_pairs={{0,8},{4,12},{8,0},{12,4},{16,24},{20,28},{24,16},{28,20},{1,9},{5... | collective-permute-start | bytes 393224 | tf_op jit(solution)/shard_map/ppermute | solution.py:23
  14.8 2.2 %collective-permute-done = s32[2080]{0:T(1024)S(1)} collective-permute-done((s32[2080]{0:T(1024)S(1)}, s32[2080]{0:T(1024)S(1)}, u32[]{:S(2)}, u32[]{:S(2)}) %collective-permute-start) | collective-permute-done | bytes 8352 | tf_op jit(solution)/shard_map/ppermute | solution.py:23
  17.0 2.9 %collective-permute-start.8 = (bf16[128,2048]{1,0:T(8,128)(2,1)S(1)}, bf16[128,2048]{1,0:T(8,128)(2,1)}, u32[]{:S(2)}, u32[]{:S(2)}) collective-permute-start(bf16[128,2048]{1,0:T(8,128)(2,1)S(1)} %bitcast.49), channel_id=1, source_target_pairs={{0,16},{4,20},{8,24},{12,28},{16,0},{20,4},{24,8},{28,12},{1,17},{... | collective-permute-start | bytes 1572872 | tf_op jit(solution)/shard_map/ppermute | solution.py:23
  23.3 8.4 %collective-permute-done.4.refs_3_ = bf16[256,256]{1,0:T(8,128)(2,1)S(1)} collective-permute-done((bf16[256,256]{1,0:T(8,128)(2,1)S(1)}, bf16[256,256]{1,0:T(8,128)(2,1)S(1)}, u32[]{:S(2)}, u32[]{:S(2)}) %collective-permute-start.4) | collective-permute-done | bytes 131104 | tf_op jit(solution)/shard_map/ppermute | solution.py:23
  32.6 2.9 %collective-permute-done.8.refs_5_ = bf16[128,2048]{1,0:T(8,128)(2,1)} collective-permute-done((bf16[128,2048]{1,0:T(8,128)(2,1)S(1)}, bf16[128,2048]{1,0:T(8,128)(2,1)}, u32[]{:S(2)}, u32[]{:S(2)}) %collective-permute-start.8) | collective-permute-done | bytes 524320 | tf_op jit(solution)/shard_map/ppermute | solution.py:23
  39.1 4.4 %shard_map.165 = f32[16,2048]{1,0:T(8,128)} custom-call(s32[1,2048]{1,0:T(1,128)} %fusion.17.codes_ref, bf16[1024,256]{1,0:T(8,128)(2,1)} %refs_0_.7, bf16[1056,2304]{1,0:T(8,128)(2,1)} %collective-permute-done.1.mate_ref.refs_1_, bf16[256,256]{1,0:T(8,128)(2,1)} %bitcast.57, bf16[256,256]{1,0:T(8,128)(2,1)} %copy-done.15, bf16[256,256]{1,0:T(8,128)(2,1)} %copy-done.16, ...), custom_call_target="tpu_custom_call" | custom-call | flops 1073741824 | bytes 1572864 | tf_op jit(solution)/shard_map/pallas_call | solution.py:97
  46.0 3.0 %convolution_convert_fusion = bf16[32,256]{1,0:T(8,128)(2,1)S(1)} fusion(bf16[32,8192]{1,0:T(8,128)(2,1)S(1)} %copy-done, bf16[8192,256]{1,0:T(8,128)(2,1)} %param.20), kind=kOutput, calls=%fused_computation.12 | convolution fusion | flops 134225920 | bytes 4734976 | tf_op jit(solution)/shard_map/dot_general | solution.py:453
  50.8 3.6 %fusion.22 = (f32[32,2,8]{2,1,0:T(2,128)S(1)}, f32[32,2,8,256]{3,2,1,0:T(8,128)S(1)}) fusion(bf16[32,2,8,128]{3,2,1,0:T(8,128)(2,1)S(1)} %bitcast.63, pred[32,256]{1,0:T(8,128)(4,1)} %iota_compare_fusion.1, bf16[32,256,256]{2,1,0:T(8,128)(2,1)} %param.16), kind=kOutput, calls=%fused_computation.52 | convolution fusion | flops 33947136 | bytes 4859904 | tf_op jit(solution)/shard_map/bhgd,bphd->bhgp/dot_general | solution.py:258
  54.8 2.7 %collective-permute-start.12 = (f32[16,2048]{1,0:T(8,128)S(1)}, f32[16,2048]{1,0:T(8,128)S(1)}, u32[]{:S(2)}, u32[]{:S(2)}) collective-permute-start(f32[16,2048]{1,0:T(8,128)S(1)} %add.133), channel_id=1, source_target_pairs={{0,2},{1,3},{2,0},{3,1},{4,6},{5,7},{6,4},{7,5},{8,10},{9,11},{10,... | collective-permute-start | bytes 393224 | tf_op jit(solution)/shard_map/ppermute | solution.py:23
  58.2 3.8 %collective-permute-done.12 = f32[16,2048]{1,0:T(8,128)S(1)} collective-permute-done((f32[16,2048]{1,0:T(8,128)S(1)}, f32[16,2048]{1,0:T(8,128)S(1)}, u32[]{:S(2)}, u32[]{:S(2)}) %collective-permute-start.12) | collective-permute-done | bytes 131104 | tf_op jit(solution)/shard_map/ppermute | solution.py:23
  62.7 6.4 %shard_map.166 = (bf16[128,2048]{1,0:T(8,128)(2,1)}, bf16[128,2048]{1,0:T(8,128)(2,1)}) custom-call(s32[1,2048]{1,0:T(1,128)} %fusion.17.codes_ref, s32[1,2048]{1,0:T(1,128)} %bitcast.66, f32[16,2048]{1,0:T(8,128)} %add.134.factor_ref, bf16[1024,2048]{1,0:T(8,128)(2,1)} %refs_0_.6, bf16[1056,2304]{1,0:T(8,128)(2,1)} %collective-permute-done.1.mate_ref.refs_1_), custom_call_target="tpu_custom_call" | custom-call | flops 2147483648 | bytes 10485760 | tf_op jit(solution)/shard_map/pallas_call | solution.py:220
  69.2 8.5 %shard_map.167 = (f32[128,2048]{1,0:T(8,128)}, bf16[128,2048]{1,0:T(8,128)(2,1)}, bf16[128,2048]{1,0:T(8,128)(2,1)}, f32[128,2048]{1,0:T(8,128)}) custom-call(s32[1,2048]{1,0:T(1,128)} %fusion.17.codes_ref, s32[1,2048]{1,0:T(1,128)} %bitcast.67, f32[16,2048]{1,0:T(8,128)} %add.134.factor_ref, bf16[1024,2048]{1,0:T(8,128)(2,1)} %refs_0_.6, ...), custom_call_target="tpu_custom_call" | custom-call | flops 4294967296 | bytes 12582912 | tf_op jit(solution)/shard_map/pallas_call | solution.py:220
  77.7 11.5 %shard_map.168.refs_8_ = f32[16,2048]{1,0:T(8,128)} custom-call(s32[1,2048]{1,0:T(1,128)} %fusion.17.codes_ref, bf16[1024,2048]{1,0:T(8,128)(2,1)} %refs_0_.6, bf16[1056,2304]{1,0:T(8,128)(2,1)} %collective-permute-done.1.mate_ref.refs_1_, bf16[128,2048]{1,0:T(8,128)(2,1)} %bitcast.55, bf16[128,2048]{1,0:T(8,128)(2,1)} %bitcast.51, ...), custom_call_target="tpu_custom_call" | custom-call | flops 6442450944 | bytes 11534336 | tf_op jit(solution)/shard_map/pallas_call | solution.py:97
  90.8 4.1 %shard_map.169.refs_2_ = f32[16,64]{1,0:T(8,128)} custom-call(s32[1,64]{1,0:T(1,128)} %fusion.18.codes_ref, bf16[32,2048]{1,0:T(8,128)(2,1)} %copy-done.5, bf16[1056,2304]{1,0:T(8,128)(2,1)} %collective-permute-done.1.mate_ref.refs_1_, bf16[128,2048]{1,0:T(8,128)(2,1)} %bitcast.56, bf16[128,2048]{1,0:T(8,128)(2,1)} %bitcast.52, ...), custom_call_target="tpu_custom_call" | custom-call | flops 268435456 | bytes 4194304 | tf_op jit(solution)/shard_map/pallas_call | solution.py:142
  94.9 3.0 %fusion.24 = f32[32,256]{1,0:T(8,128)S(1)} fusion(bf16[32,8192]{1,0:T(8,128)(2,1)S(1)} %copy-done, bf16[8192,256]{1,0:T(8,128)(2,1)} %param.21), kind=kOutput, calls=%fused_computation.54 | convolution fusion | flops 134217728 | bytes 4751360 | tf_op jit(solution)/shard_map/dot_general | solution.py:456
  98.7 3.0 %collective-permute-start.14 = (f32[16,64]{1,0:T(8,128)S(1)}, f32[16,64]{1,0:T(8,128)S(1)}, u32[]{:S(2)}, u32[]{:S(2)}) collective-permute-start(f32[16,64]{1,0:T(8,128)S(1)} %add.135), channel_id=1, source_target_pairs={{0,2},{1,3},{2,0},{3,1},{4,6},{5,7},{6,4},{7,5},{8,10},{9,11},{10,... | collective-permute-start | bytes 12296 | tf_op jit(solution)/shard_map/ppermute | solution.py:23
  101.7 7.1 %shard_map.171 = f32[16,2048]{1,0:T(8,128)} custom-call(s32[1,2048]{1,0:T(1,128)} %fusion.17.codes_ref, bf16[1024,2048]{1,0:T(8,128)(2,1)} %refs_0_.6, bf16[1056,2304]{1,0:T(8,128)(2,1)} %collective-permute-done.1.mate_ref.refs_1_, bf16[128,2048]{1,0:T(8,128)(2,1)} %copy-done.2, bf16[128,2048]{1,0:T(8,128)(2,1)} %copy-done.1, f32[16,64]{1,0:T(8,128)} %shard_map.169.refs_2_), custom_call_target="tpu_custom_call" | custom-call | flops 2147483648 | bytes 9437184 | tf_op jit(solution)/shard_map/pallas_call | solution.py:97
  112.7 2.0 %shard_map.170 = bf16[64,256]{1,0:T(8,128)(2,1)} custom-call(s32[1,64]{1,0:T(1,128)} %fusion.18.codes_ref, f32[16,64]{1,0:T(8,128)} %add.136.rank_ref, bf16[256,256]{1,0:T(8,128)(2,1)} %bitcast.58, bf16[256,256]{1,0:T(8,128)(2,1)} %copy-done.15, bf16[256,256]{1,0:T(8,128)(2,1)} %copy-done.16, bf16[256,256]{1,0:T(8,128)(2,1)} %copy-done.17), custom_call_target="tpu_custom_call" | custom-call | tf_op jit(solution)/shard_map/pallas_call | solution.py:185
  115.5 6.7 %shard_map.172 = (f32[128,2048]{1,0:T(8,128)}, f32[128,2048]{1,0:T(8,128)}) custom-call(s32[1,2048]{1,0:T(1,128)} %fusion.17.codes_ref, s32[1,2048]{1,0:T(1,128)} %bitcast.68, f32[16,2048]{1,0:T(8,128)} %add.134.factor_ref, bf16[1024,2048]{1,0:T(8,128)(2,1)} %refs_0_.6, bf16[1056,2304]{1,0:T(8,128)(2,1)} %collective-permute-done.1.mate_ref.refs_1_, ...), custom_call_target="tpu_custom_call" | custom-call | flops 2147483648 | bytes 10485760 | tf_op jit(solution)/shard_map/pallas_call | solution.py:220
  125.7 7.2 %collective-permute-done.23 = f32[16,2048]{1,0:T(8,128)S(1)} collective-permute-done((f32[16,2048]{1,0:T(8,128)S(1)}, f32[16,2048]{1,0:T(8,128)S(1)}, u32[]{:S(2)}, u32[]{:S(2)}) %collective-permute-start.23) | collective-permute-done | bytes 131104 | tf_op jit(solution)/shard_map/ppermute | solution.py:23
  133.6 3.3 %shard_map.173 = (f32[256,256]{1,0:T(8,128)}, bf16[256,256]{1,0:T(8,128)(2,1)}, bf16[256,256]{1,0:T(8,128)(2,1)}, bf16[256,256]{1,0:T(8,128)(2,1)}) custom-call(s32[1,2048]{1,0:T(1,128)} %fusion.17.codes_ref, s32[1,2048]{1,0:T(1,128)} %bitcast.69, f32[16,2048]{1,0:T(8,128)} %add.148.factor_ref, bf16[1024,256]{1,0:T(8,128)(2,1)} %refs_0_.7, ...), custom_call_target="tpu_custom_call" | custom-call | flops 1073741824 | bytes 2097152 | tf_op jit(solution)/shard_map/pallas_call | solution.py:220
  142.7 2.4 %collective-permute-start.19 = (bf16[128,2048]{1,0:T(8,128)(2,1)}, bf16[128,2048]{1,0:T(8,128)(2,1)S(1)}, u32[]{:S(2)}, u32[]{:S(2)}) collective-permute-start(bf16[128,2048]{1,0:T(8,128)(2,1)} %get-tuple-element.31), channel_id=1, source_target_pairs={{0,8},{4,12},{8,0},{12,4},{16,24},{20,28},{24,16},{28,20},{1,9},{5... | collective-permute-start | bytes 1572872 | tf_op jit(solution)/shard_map/ppermute | solution.py:23
  150.8 16.8 %collective-permute-done.18 = bf16[128,2048]{1,0:T(8,128)(2,1)S(1)} collective-permute-done((bf16[128,2048]{1,0:T(8,128)(2,1)S(1)}, bf16[128,2048]{1,0:T(8,128)(2,1)S(1)}, u32[]{:S(2)}, u32[]{:S(2)}) %collective-permute-start.18) | collective-permute-done | bytes 524320 | tf_op jit(solution)/shard_map/ppermute | solution.py:23
  (132 shorter events, 43.9 us)
Async XLA Ops:
  8.8 30.3 %collective-permute-start.1 = (bf16[1056,2304]{1,0:T(8,128)(2,1)}, bf16[1056,2304]{1,0:T(8,128)(2,1)}, u32[]{:S(2)}, u32[]{:S(2)}) collective-permute-start(bf16[1056,2304]{1,0:T(8,128)(2,1)} %fusion.1), channel_id=1, source_target_pairs={{0,4},{4,0},{8,12},{12,8},{16,20},{20,16},{24,28},{28,24},{1,5},{5... | collective-permute-start | bytes 14598152 | tf_op jit(solution)/shard_map/ppermute | solution.py:23
  9.2 11.3 %collective-permute-start.2 = (bf16[256,256]{1,0:T(8,128)(2,1)S(1)}, bf16[256,256]{1,0:T(8,128)(2,1)S(1)}, u32[]{:S(2)}, u32[]{:S(2)}) collective-permute-start(bf16[256,256]{1,0:T(8,128)(2,1)S(1)} %bitcast.59), channel_id=1, source_target_pairs={{0,8},{4,12},{8,0},{12,4},{16,24},{20,28},{24,16},{28,20},{1,9},{5... | collective-permute-start | bytes 393224 | tf_op jit(solution)/shard_map/ppermute | solution.py:23
  11.8 11.4 %collective-permute-start.3 = (bf16[256,256]{1,0:T(8,128)(2,1)S(1)}, bf16[256,256]{1,0:T(8,128)(2,1)S(1)}, u32[]{:S(2)}, u32[]{:S(2)}) collective-permute-start(bf16[256,256]{1,0:T(8,128)(2,1)S(1)} %bitcast.60), channel_id=1, source_target_pairs={{0,16},{4,20},{8,24},{12,28},{16,0},{20,4},{24,8},{28,12},{1,17},{... | collective-permute-start | bytes 393224 | tf_op jit(solution)/shard_map/ppermute | solution.py:23
  13.5 24.0 %collective-permute-start.5 = (bf16[128,2048]{1,0:T(8,128)(2,1)S(1)}, bf16[128,2048]{1,0:T(8,128)(2,1)S(1)}, u32[]{:S(2)}, u32[]{:S(2)}) collective-permute-start(bf16[128,2048]{1,0:T(8,128)(2,1)S(1)} %bitcast.53), channel_id=1, source_target_pairs={{0,8},{4,12},{8,0},{12,4},{16,24},{20,28},{24,16},{28,20},{1,9},{5... | collective-permute-start | bytes 1572872 | tf_op jit(solution)/shard_map/ppermute | solution.py:23
  17.0 18.5 %collective-permute-start.8 = (bf16[128,2048]{1,0:T(8,128)(2,1)S(1)}, bf16[128,2048]{1,0:T(8,128)(2,1)}, u32[]{:S(2)}, u32[]{:S(2)}) collective-permute-start(bf16[128,2048]{1,0:T(8,128)(2,1)S(1)} %bitcast.49), channel_id=1, source_target_pairs={{0,16},{4,20},{8,24},{12,28},{16,0},{20,4},{24,8},{28,12},{1,17},{... | collective-permute-start | bytes 1572872 | tf_op jit(solution)/shard_map/ppermute | solution.py:23
  20.6 11.1 %collective-permute-start.4 = (bf16[256,256]{1,0:T(8,128)(2,1)S(1)}, bf16[256,256]{1,0:T(8,128)(2,1)S(1)}, u32[]{:S(2)}, u32[]{:S(2)}) collective-permute-start(bf16[256,256]{1,0:T(8,128)(2,1)S(1)} %bitcast.61), channel_id=1, source_target_pairs={{0,24},{4,28},{8,16},{12,20},{16,8},{20,12},{24,0},{28,4},{1,25},{... | collective-permute-start | bytes 393224 | tf_op jit(solution)/shard_map/ppermute | solution.py:23
  23.2 54.4 %collective-permute-start.6 = (bf16[128,2048]{1,0:T(8,128)(2,1)S(1)}, bf16[128,2048]{1,0:T(8,128)(2,1)}, u32[]{:S(2)}, u32[]{:S(2)}) collective-permute-start(bf16[128,2048]{1,0:T(8,128)(2,1)S(1)} %bitcast.50), channel_id=1, source_target_pairs={{0,8},{4,12},{8,0},{12,4},{16,24},{20,28},{24,16},{28,20},{1,9},{5... | collective-permute-start | bytes 1572872 | tf_op jit(solution)/shard_map/ppermute | solution.py:23
  31.6 46.0 %collective-permute-start.7 = (bf16[128,2048]{1,0:T(8,128)(2,1)S(1)}, bf16[128,2048]{1,0:T(8,128)(2,1)}, u32[]{:S(2)}, u32[]{:S(2)}) collective-permute-start(bf16[128,2048]{1,0:T(8,128)(2,1)S(1)} %bitcast.54), channel_id=1, source_target_pairs={{0,16},{4,20},{8,24},{12,28},{16,0},{20,4},{24,8},{28,12},{1,17},{... | collective-permute-start | bytes 1572872 | tf_op jit(solution)/shard_map/ppermute | solution.py:23
  35.5 53.7 %collective-permute-start.10 = (bf16[128,2048]{1,0:T(8,128)(2,1)}, bf16[128,2048]{1,0:T(8,128)(2,1)S(1)}, u32[]{:S(2)}, u32[]{:S(2)}) collective-permute-start(bf16[128,2048]{1,0:T(8,128)(2,1)} %collective-permute-done.8.refs_5_), channel_id=1, source_target_pairs={{0,8},{4,12},{8,0},{12,4},{16,24},{20,28},{24,16},{28,20},{1,9},{5... | collective-permute-start | bytes 1572872 | tf_op jit(solution)/shard_map/ppermute | solution.py:23
  37.5 51.6 %collective-permute-start.9 = (bf16[128,2048]{1,0:T(8,128)(2,1)S(1)}, bf16[128,2048]{1,0:T(8,128)(2,1)S(1)}, u32[]{:S(2)}, u32[]{:S(2)}) collective-permute-start(bf16[128,2048]{1,0:T(8,128)(2,1)S(1)} %collective-permute-done.5.refs_2_), channel_id=1, source_target_pairs={{0,16},{4,20},{8,24},{12,28},{16,0},{20,4},{24,8},{28,12},{1,17},{... | collective-permute-start | bytes 1572872 | tf_op jit(solution)/shard_map/ppermute | solution.py:23
  43.5 11.3 %collective-permute-start.11 = (f32[16,2048]{1,0:T(8,128)}, f32[16,2048]{1,0:T(8,128)S(1)}, u32[]{:S(2)}, u32[]{:S(2)}) collective-permute-start(f32[16,2048]{1,0:T(8,128)} %shard_map.165), channel_id=1, source_target_pairs={{0,1},{1,0},{2,3},{3,2},{4,5},{5,4},{6,7},{7,6},{8,9},{9,8},{10,11... | collective-permute-start | bytes 393224 | tf_op jit(solution)/shard_map/ppermute | solution.py:23
  54.8 7.2 %collective-permute-start.12 = (f32[16,2048]{1,0:T(8,128)S(1)}, f32[16,2048]{1,0:T(8,128)S(1)}, u32[]{:S(2)}, u32[]{:S(2)}) collective-permute-start(f32[16,2048]{1,0:T(8,128)S(1)} %add.133), channel_id=1, source_target_pairs={{0,2},{1,3},{2,0},{3,1},{4,6},{5,7},{6,4},{7,5},{8,10},{9,11},{10,... | collective-permute-start | bytes 393224 | tf_op jit(solution)/shard_map/ppermute | solution.py:23
  97.9 41.1 %collective-permute-start.17 = (bf16[128,2048]{1,0:T(8,128)(2,1)}, bf16[128,2048]{1,0:T(8,128)(2,1)}, u32[]{:S(2)}, u32[]{:S(2)}) collective-permute-start(bf16[128,2048]{1,0:T(8,128)(2,1)} %get-tuple-element.26.refs_2_), channel_id=1, source_target_pairs={{0,16},{4,20},{8,24},{12,28},{16,0},{20,4},{24,8},{28,12},{1,17},{... | collective-permute-start | bytes 1572872 | tf_op jit(solution)/shard_map/ppermute | solution.py:23
  98.7 13.4 %collective-permute-start.14 = (f32[16,64]{1,0:T(8,128)S(1)}, f32[16,64]{1,0:T(8,128)S(1)}, u32[]{:S(2)}, u32[]{:S(2)}) collective-permute-start(f32[16,64]{1,0:T(8,128)S(1)} %add.135), channel_id=1, source_target_pairs={{0,2},{1,3},{2,0},{3,1},{4,6},{5,7},{6,4},{7,5},{8,10},{9,11},{10,... | collective-permute-start | bytes 12296 | tf_op jit(solution)/shard_map/ppermute | solution.py:23
  109.7 12.5 %collective-permute-start.22 = (f32[16,2048]{1,0:T(8,128)S(1)}, f32[16,2048]{1,0:T(8,128)S(1)}, u32[]{:S(2)}, u32[]{:S(2)}) collective-permute-start(f32[16,2048]{1,0:T(8,128)S(1)} %add.140.refs_2_), channel_id=1, source_target_pairs={{0,1},{1,0},{2,3},{3,2},{4,5},{5,4},{6,7},{7,6},{8,9},{9,8},{10,11... | collective-permute-start | bytes 393224 | tf_op jit(solution)/shard_map/ppermute | solution.py:23
  110.1 40.7 %collective-permute-start.16 = (bf16[128,2048]{1,0:T(8,128)(2,1)}, bf16[128,2048]{1,0:T(8,128)(2,1)}, u32[]{:S(2)}, u32[]{:S(2)}) collective-permute-start(bf16[128,2048]{1,0:T(8,128)(2,1)} %get-tuple-element.29), channel_id=1, source_target_pairs={{0,16},{4,20},{8,24},{12,28},{16,0},{20,4},{24,8},{28,12},{1,17},{... | collective-permute-start | bytes 1572872 | tf_op jit(solution)/shard_map/ppermute | solution.py:23
  111.6 36.4 %collective-permute-start.20 = (bf16[128,2048]{1,0:T(8,128)(2,1)}, bf16[128,2048]{1,0:T(8,128)(2,1)}, u32[]{:S(2)}, u32[]{:S(2)}) collective-permute-start(bf16[128,2048]{1,0:T(8,128)(2,1)} %get-tuple-element.33), channel_id=1, source_target_pairs={{0,8},{4,12},{8,0},{12,4},{16,24},{20,28},{24,16},{28,20},{1,9},{5... | collective-permute-start | bytes 1572872 | tf_op jit(solution)/shard_map/ppermute | solution.py:23
  115.5 6.7 %collective-permute-start.15 = (bf16[32,256]{1,0:T(8,128)(2,1)S(1)}, bf16[32,256]{1,0:T(8,128)(2,1)S(1)}, u32[]{:S(2)}, u32[]{:S(2)}) collective-permute-start(bf16[32,256]{1,0:T(8,128)(2,1)S(1)} %slice.40), channel_id=1, source_target_pairs={{0,4},{4,0},{8,12},{12,8},{16,20},{20,16},{24,28},{28,24},{1,5},{5... | collective-permute-start | bytes 49160 | tf_op jit(solution)/shard_map/ppermute | solution.py:23
  123.3 9.7 %collective-permute-start.23 = (f32[16,2048]{1,0:T(8,128)S(1)}, f32[16,2048]{1,0:T(8,128)S(1)}, u32[]{:S(2)}, u32[]{:S(2)}) collective-permute-start(f32[16,2048]{1,0:T(8,128)S(1)} %add.147), channel_id=1, source_target_pairs={{0,2},{1,3},{2,0},{3,1},{4,6},{5,7},{6,4},{7,5},{8,10},{9,11},{10,... | collective-permute-start | bytes 393224 | tf_op jit(solution)/shard_map/ppermute | solution.py:23
  138.4 7.8 %collective-permute-start.25 = (bf16[256,256]{1,0:T(8,128)(2,1)}, bf16[256,256]{1,0:T(8,128)(2,1)S(1)}, u32[]{:S(2)}, u32[]{:S(2)}) collective-permute-start(bf16[256,256]{1,0:T(8,128)(2,1)} %get-tuple-element.36), channel_id=1, source_target_pairs={{0,16},{4,20},{8,24},{12,28},{16,0},{20,4},{24,8},{28,12},{1,17},{... | collective-permute-start | bytes 393224 | tf_op jit(solution)/shard_map/ppermute | solution.py:23
  139.0 7.4 %collective-permute-start.26 = (bf16[256,256]{1,0:T(8,128)(2,1)}, bf16[256,256]{1,0:T(8,128)(2,1)S(1)}, u32[]{:S(2)}, u32[]{:S(2)}) collective-permute-start(bf16[256,256]{1,0:T(8,128)(2,1)} %get-tuple-element.37), channel_id=1, source_target_pairs={{0,24},{4,28},{8,16},{12,20},{16,8},{20,12},{24,0},{28,4},{1,25},{... | collective-permute-start | bytes 393224 | tf_op jit(solution)/shard_map/ppermute | solution.py:23
  142.7 26.1 %collective-permute-start.19 = (bf16[128,2048]{1,0:T(8,128)(2,1)}, bf16[128,2048]{1,0:T(8,128)(2,1)S(1)}, u32[]{:S(2)}, u32[]{:S(2)}) collective-permute-start(bf16[128,2048]{1,0:T(8,128)(2,1)} %get-tuple-element.31), channel_id=1, source_target_pairs={{0,8},{4,12},{8,0},{12,4},{16,24},{20,28},{24,16},{28,20},{1,9},{5... | collective-permute-start | bytes 1572872 | tf_op jit(solution)/shard_map/ppermute | solution.py:23
  146.3 21.3 %collective-permute-start.18 = (bf16[128,2048]{1,0:T(8,128)(2,1)S(1)}, bf16[128,2048]{1,0:T(8,128)(2,1)S(1)}, u32[]{:S(2)}, u32[]{:S(2)}) collective-permute-start(bf16[128,2048]{1,0:T(8,128)(2,1)S(1)} %add_convert_fusion.1), channel_id=1, source_target_pairs={{0,8},{4,12},{8,0},{12,4},{16,24},{20,28},{24,16},{28,20},{1,9},{5... | collective-permute-start | bytes 1572872 | tf_op jit(solution)/shard_map/ppermute | solution.py:23
  149.2 19.6 %collective-permute-start.21 = (bf16[128,2048]{1,0:T(8,128)(2,1)S(1)}, bf16[128,2048]{1,0:T(8,128)(2,1)S(1)}, u32[]{:S(2)}, u32[]{:S(2)}) collective-permute-start(bf16[128,2048]{1,0:T(8,128)(2,1)S(1)} %add_convert_fusion), channel_id=1, source_target_pairs={{0,16},{4,20},{8,24},{12,28},{16,0},{20,4},{24,8},{28,12},{1,17},{... | collective-permute-start | bytes 1572872 | tf_op jit(solution)/shard_map/ppermute | solution.py:23
  (30 other events, 371.5 us)

commit v3 on v2

v3 whole, which is shorter than its diff:
```python
import functools
import math

import jax
import jax.numpy as jnp
from jax import lax
from jax.experimental import pallas as pl
from jax.experimental.pallas import tpu as pltpu
from jax.sharding import PartitionSpec as P

HEADS = 64
KEY_VALUE_HEADS = 8
HEAD_SIZE = 128
CACHE = 256

ADAPTER_SCALE = 2.0
NEG_FILL = -1e30
VMEM_LIMIT = 60 * 1024 * 1024


def swap(array, axis, mask):
    count = lax.axis_size(axis)
    return lax.ppermute(array, axis, [(i, i ^ mask) for i in range(count)])


def axis_bits(axis):
    count = lax.axis_size(axis)
    assert count & (count - 1) == 0, "axis size"
    return [1 << k for k in range(count.bit_length() - 1)]


def highest_in(order, mask):
    return [bit for bit in order if bit & mask][-1]


def largest_tile(length, limit):
    tile = length
    while tile > limit and tile % 2 == 0:
        tile //= 2
    return tile


def code_list(chunks, rank):
    return [base + j for base, rows in chunks for j in range(rows // rank)]


def pick(codes, products, row_codes, rank):
    total = jnp.zeros((rank, products.shape[1]), jnp.float32)
    for k, code in enumerate(row_codes):
        total += jnp.where(codes == code, products[k * rank : (k + 1) * rank], 0.0)
    return total


def spread(codes, values, row_codes, out_ref):
    rank = values.shape[0]
    for k, code in enumerate(row_codes):
        out_ref[k * rank : (k + 1) * rank, :] = jnp.where(codes == code, values, 0.0).astype(
            out_ref.dtype
        )


def join(maps, joined_ref):
    first = 0
    for chunk in maps:
        joined_ref[first : first + chunk.shape[0], :] = chunk[...]
        first += chunk.shape[0]


def times_transposed(maps, tokens):
    return lax.dot_general(
        maps, tokens, (((1,), (1,)), ((), ())), preferred_element_type=jnp.float32
    )


def token_kernel(
    map_codes, rank, own_tiles, has_rows, map_count, codes_ref, own_ref, mate_ref, *refs
):
    refs = list(refs)
    row_refs = [refs.pop(0) for _ in range(2 * has_rows)]
    maps = refs[:map_count]
    out_ref, joined_ref, *rest = refs[-2 - has_rows :]
    step = pl.program_id(0)

    @pl.when(step == 0)
    def _():
        join(maps, joined_ref)

    def project(tokens):
        products = times_transposed(joined_ref[...], tokens)
        codes = codes_ref[:, : tokens.shape[0]]
        return pick(codes, products, map_codes, rank)

    def store(total):
        out_ref[...] = total

    pl.when(step < own_tiles)(lambda: store(project(own_ref[...])))
    pl.when((step >= own_tiles) & (step < 2 * own_tiles))(lambda: store(project(mate_ref[...])))
    if has_rows:
        rows_ref = rest[0]

        @pl.when(step == 2 * own_tiles)
        def _():
            rows_ref[...] = jnp.zeros_like(rows_ref)
            join(row_refs, rows_ref)
            store(jnp.zeros_like(out_ref))
            out_ref[:, : rows_ref.shape[0]] += project(rows_ref[...])


def token_tile(token_count):
    return largest_tile(token_count, 512)


def project_tokens(codes, own, mate, chunks, rank, rows=(), after=()):
    token_count, width = own.shape
    tile = token_tile(token_count)
    own_tiles = token_count // tile
    steps = 2 * own_tiles + bool(rows)
    map_rows = sum(chunk.shape[0] for _, chunk in chunks)
    scratch = [pltpu.VMEM((map_rows, width), jnp.bfloat16)]
    if rows:
        padded = -(-2 * rows[0].shape[0] // 128) * 128
        assert padded <= tile, "row count"
        scratch.append(pltpu.VMEM((padded, width), jnp.bfloat16))
    result_spec = pl.BlockSpec((rank, tile), lambda i: (0, i))
    whole = lambda i: (0, 0)
    last = own_tiles - 1
    return pl.pallas_call(
        functools.partial(
            token_kernel,
            code_list([(base, chunk.shape[0]) for base, chunk in chunks], rank),
            rank,
            own_tiles,
            bool(rows),
            len(chunks),
        ),
        grid=(steps,),
        in_specs=[
            pl.BlockSpec((1, tile), lambda i: (0, i)),
            pl.BlockSpec((tile, width), lambda i: (jnp.minimum(i, last), 0)),
            pl.BlockSpec((tile, width), lambda i: (jnp.clip(i - own_tiles, 0, last), 0)),
        ]
        + [pl.BlockSpec(a.shape, whole) for a in rows]
        + [pl.BlockSpec(chunk.shape, whole) for _, chunk in chunks]
        + [pl.BlockSpec(memory_space=pl.ANY) for _ in after],
        out_specs=result_spec,
        out_shape=jax.ShapeDtypeStruct((rank, steps * tile), jnp.float32),
        scratch_shapes=scratch,
        compiler_params=pltpu.CompilerParams(vmem_limit_bytes=VMEM_LIMIT),
        cost_estimate=pl.CostEstimate(flops=1, bytes_accessed=1, transcendentals=0),
    )(codes, own, mate, *rows, *[chunk for _, chunk in chunks], *after)


def delta_kernel(chunk_codes, codes_ref, rank_ref, *refs):
    maps = refs[: len(chunk_codes)]
    out_ref, spread_ref = refs[-2:]
    count = codes_ref.shape[1]
    values = rank_ref[:, :count].astype(jnp.bfloat16).astype(jnp.float32)
    total = jnp.zeros(out_ref.shape, jnp.float32)
    for map_codes, chunk in zip(chunk_codes, maps):
        spread(codes_ref[...], values, map_codes, spread_ref)
        total += lax.dot_general(
            spread_ref[...].T.astype(jnp.bfloat16),
            chunk[...],
            (((1,), (0,)), ((), ())),
            preferred_element_type=jnp.float32,
        )
    out_ref[...] = (ADAPTER_SCALE * total).astype(out_ref.dtype)


def row_deltas(codes, ranks, first, width_of_ranks, chunks, after=()):
    rank = ranks.shape[0]
    row_count = codes.shape[1]
    chunk_rows, width = chunks[0][1].shape
    whole = lambda i: (0, 0)
    return pl.pallas_call(
        functools.partial(
            delta_kernel, [code_list([(base, chunk_rows)], rank) for base, _ in chunks]
        ),
        grid=(1,),
        in_specs=[
            pl.BlockSpec(codes.shape, whole),
            pl.BlockSpec((rank, width_of_ranks), lambda i: (0, first // width_of_ranks)),
        ]
        + [pl.BlockSpec((chunk_rows, width), whole) for _ in chunks]
        + [pl.BlockSpec(memory_space=pl.ANY) for _ in after],
        out_specs=pl.BlockSpec((row_count, width), whole),
        out_shape=jax.ShapeDtypeStruct((row_count, width), jnp.bfloat16),
        scratch_shapes=[pltpu.VMEM((chunk_rows, row_count), jnp.float32)],
        compiler_params=pltpu.CompilerParams(vmem_limit_bytes=VMEM_LIMIT),
    )(codes, ranks, *[chunk for _, chunk in chunks], *after)


def gradient_kernel(row_codes, rows, arrived_counts, waits, joined, *refs):
    codes_ref, rewards_ref, factor_ref, own_ref, mate_ref = refs[:5]
    refs = list(refs[5:])
    arrived = [[refs.pop(0) for _ in range(count)] for count in arrived_counts]
    outs = refs[waits:-1]
    spread_ref = refs[-1]
    token_count = own_ref.shape[0]

    @pl.when(pl.program_id(0) == 0)
    def _():
        scale = ADAPTER_SCALE * rewards_ref[...].astype(jnp.float32)
        scaled = (scale * factor_ref[...]).astype(jnp.bfloat16).astype(jnp.float32)
        spread(codes_ref[...], scaled, row_codes, spread_ref)

    total = jnp.dot(
        spread_ref[:, :token_count], own_ref[...], preferred_element_type=jnp.float32
    ) + jnp.dot(spread_ref[:, token_count:], mate_ref[...], preferred_element_type=jnp.float32)
    for k in range(len(arrived)):
        piece = total[k * rows : (k + 1) * rows]
        for ref in arrived[k]:
            piece += ref[...].astype(jnp.float32)
        if joined:
            outs[0][k * rows : (k + 1) * rows, :] = piece
        else:
            outs[k][...] = piece.astype(outs[k].dtype)


def gradient_chunks(
    codes, rewards, factor, own, mate, chunks, adapters, joined=False, after=()
):
    rank = factor.shape[0]
    token_count, width = own.shape
    tile = largest_tile(width, 512)
    rows = adapters * rank
    out_rows = [rows * len(chunks)] if joined else [rows] * len(chunks)
    arrived = [a for _, arrays in chunks for a in arrays]
    whole = lambda i: (0, 0)
    across = lambda i: (0, i)
    return pl.pallas_call(
        functools.partial(
            gradient_kernel,
            code_list([(base, rows) for base, _ in chunks], rank),
            rows,
            [len(arrays) for _, arrays in chunks],
            len(after),
            joined,
        ),
        grid=(width // tile,),
        in_specs=[
            pl.BlockSpec((1, 2 * token_count), whole),
            pl.BlockSpec(rewards.shape, whole),
            pl.BlockSpec((rank, 2 * token_count), whole),
            pl.BlockSpec((token_count, tile), across),
            pl.BlockSpec((token_count, tile), across),
        ]
        + [pl.BlockSpec((rows, tile), across) for _ in arrived]
        + [pl.BlockSpec(memory_space=pl.ANY) for _ in after],
        out_specs=[pl.BlockSpec((r, tile), across) for r in out_rows],
        out_shape=[
            jax.ShapeDtypeStruct((r, width), jnp.bfloat16 if base else jnp.float32)
            for r, (base, _) in zip(out_rows, chunks)
        ],
        scratch_shapes=[pltpu.VMEM((len(chunks) * rows, 2 * token_count), jnp.bfloat16)],
        compiler_params=pltpu.CompilerParams(vmem_limit_bytes=VMEM_LIMIT),
        cost_estimate=pl.CostEstimate(flops=1, bytes_accessed=1, transcendentals=0),
    )(codes, rewards, factor, own, mate, *arrived, *after)


def finish_kernel(start_ref, *refs):
    arrived, out_ref = refs[:-1], refs[-1]
    rows = arrived[0].shape[0]
    for p, ref in enumerate(arrived):
        part = slice(p * rows, (p + 1) * rows)
        out_ref[part, :] = start_ref[part, :] + ref[...].astype(jnp.float32)


def finish(start, arrived):
    rows, width = start.shape
    tile = largest_tile(width, 512)
    across = lambda i: (0, i)
    return pl.pallas_call(
        finish_kernel,
        grid=(width // tile,),
        in_specs=[pl.BlockSpec((a.shape[0], tile), across) for a in (start, *arrived)],
        out_specs=pl.BlockSpec((rows, tile), across),
        out_shape=jax.ShapeDtypeStruct(start.shape, start.dtype),
        compiler_params=pltpu.CompilerParams(vmem_limit_bytes=VMEM_LIMIT),
    )(start, *arrived)


def wait_for(array, *others):
    return lax.optimization_barrier((array, *others))[0]


def sum_over(axis, piece, waits=()):
    for k, bit in enumerate(axis_bits(axis)):
        arrived = swap(piece, axis, bit)
        if k < len(waits):
            arrived = wait_for(arrived, *waits[k])
        piece = piece + arrived
    return piece


def attend_cached(queries, cached_key_rows, cached_value_rows, lengths, fresh_keys):
    row_count = queries.shape[0]
    kv_local = fresh_keys.shape[1] // HEAD_SIZE
    group = HEADS // KEY_VALUE_HEADS
    query_heads = queries.reshape(row_count, kv_local, group, HEAD_SIZE)
    key_heads = cached_key_rows.reshape(row_count, CACHE, kv_local, HEAD_SIZE)
    value_heads = cached_value_rows.reshape(row_count, CACHE, kv_local, HEAD_SIZE)
    inverse = 1.0 / math.sqrt(HEAD_SIZE)
    scores = (
        jnp.einsum("bhgd,bphd->bhgp", query_heads, key_heads, preferred_element_type=jnp.float32)
        * inverse
    )
    own_score = (
        jnp.einsum(
            "bhgd,bhd->bhg",
            query_heads,
            fresh_keys.reshape(row_count, kv_local, HEAD_SIZE),
            preferred_element_type=jnp.float32,
        )
        * inverse
    )
    allowed = jnp.arange(CACHE, dtype=jnp.int32)[None, :] < lengths[:, None]
    scores = jnp.where(allowed[:, None, None, :], scores, NEG_FILL)
    highest = jnp.maximum(jnp.max(scores, axis=-1), own_score)
    cache_exp = jnp.exp(scores - highest[..., None])
    own_exp = jnp.exp(own_score - highest)
    denominator = jnp.sum(cache_exp, axis=-1) + own_exp
    cache_weight = (cache_exp / denominator[..., None]).astype(jnp.bfloat16)
    own_weight = (own_exp / denominator).astype(jnp.bfloat16)
    attended = jnp.einsum(
        "bhgp,bphd->bhgd", cache_weight, value_heads, preferred_element_type=jnp.float32
    )
    return attended, own_weight


def per_device(
    decode_hidden_input,
    queries,
    cached_key_rows,
    cached_value_rows,
    lengths,
    decode_adapter_index,
    key_matrix,
    value_matrix,
    adapter_down_map,
    adapter_up_map,
    training_hidden_input,
    cotangent,
    training_adapter_index,
    rewards,
):
    core_bit, *chip_bits = axis_bits("wide")
    masks = [m for m in range(lax.axis_size("wide")) if not m & core_bit]
    me = lax.axis_index("wide")
    owner_totals, rank, down_width = adapter_down_map.shape
    up_width = adapter_up_map.shape[2]
    row_count = decode_hidden_input.shape[0]
    token_count = training_hidden_input.shape[0]
    parts = len(chip_bits) if owner_totals % len(chip_bits) == 0 else 1
    orders = [chip_bits[p:] + chip_bits[:p] for p in range(parts)]
    part_adapters = owner_totals // parts
    part_rows = part_adapters * rank

    flattened_down = adapter_down_map.reshape(-1, down_width)
    flattened_up = adapter_up_map.reshape(-1, up_width)

    far = [m for m in masks if m.bit_count() > 1]
    near = [m for m in masks if m.bit_count() == 1]

    numbers = jnp.concatenate([training_adapter_index, rewards, decode_adapter_index])
    mate_numbers = swap(numbers, "wide", core_bit)
    mate_cotangent = swap(wait_for(cotangent, mate_numbers), "wide", core_bit)
    up_maps = {0: flattened_up}
    for m in near:
        up_maps[m] = swap(flattened_up, "wide", m)
    for m in far:
        up_maps[m] = swap(wait_for(flattened_up, mate_numbers), "wide", m)
    mate_hidden = swap(wait_for(training_hidden_input, up_maps[near[0]]), "wide", core_bit)
    down_parts = {}
    for p, order in enumerate(orders):
        own_part = flattened_down[p * part_rows : (p + 1) * part_rows]
        held = []
        for bit in order:
            for m in held:
                down_parts[m | bit, p] = swap(down_parts[m, p], "wide", bit)
            sent = wait_for(own_part, *[down_parts[m | bit, p] for m in held[-1:]])
            down_parts[bit, p] = swap(sent, "wide", bit)
            held = held + [bit] + [m | bit for m in held]
    first_maps = [down_parts[order[0], p] for p, order in enumerate(orders)]
    decode_slice = lax.dynamic_slice_in_dim(
        decode_hidden_input, lax.axis_index("narrow") * down_width, down_width, 1
    )

    def codes_of(ids):
        return (((ids // owner_totals) ^ me) * owner_totals + ids % owner_totals)[None, :]

    token_codes = codes_of(
        jnp.concatenate([training_adapter_index, mate_numbers[:token_count]])
    )
    token_rewards = jnp.concatenate([rewards, mate_numbers[token_count : 2 * token_count]])[
        None, :
    ]
    row_codes = codes_of(
        jnp.concatenate([decode_adapter_index, mate_numbers[2 * token_count :]])
    )
    tile = token_tile(token_count)
    all_codes = jnp.concatenate(
        [token_codes, jnp.pad(row_codes, ((0, 0), (0, tile - 2 * row_count)), constant_values=-1)],
        axis=1,
    )
    up_chunks = [(m * owner_totals, up_maps[m]) for m in masks]
    down_chunks = [(0, flattened_down)] + [
        (m * owner_totals + p * part_adapters, down_parts[m, p])
        for m in near + far
        for p in range(parts)
    ]

    hidden_rows = wait_for(decode_hidden_input, mate_numbers, *[up_maps[m] for m in near])
    fresh_keys = jnp.dot(
        hidden_rows, key_matrix, preferred_element_type=jnp.float32
    ).astype(jnp.bfloat16)
    base_values = jnp.dot(hidden_rows, value_matrix, preferred_element_type=jnp.float32)

    cached, own_weight = attend_cached(
        wait_for(queries, *[up_maps[m] for m in near]),
        cached_key_rows,
        cached_value_rows,
        lengths,
        fresh_keys,
    )

    part_back = project_tokens(
        token_codes,
        cotangent,
        mate_cotangent,
        up_chunks,
        rank,
        after=(*first_maps, mate_hidden, cached, base_values),
    )
    mate_slice = swap(wait_for(decode_slice, part_back), "wide", core_bit)
    back = sum_over("narrow", part_back)
    arrived = {(m, p): [] for m in masks for p in range(parts)}

    def level_gradients(level, after):
        keys = [
            (m, p)
            for m in far + near
            for p, order in enumerate(orders)
            if m & order[level] and not any(m & bit for bit in order[level + 1 :])
        ]
        results = gradient_chunks(
            token_codes,
            token_rewards,
            back,
            training_hidden_input,
            mate_hidden,
            [(m * owner_totals + p * part_adapters, arrived[m, p]) for m, p in keys],
            part_adapters,
            after=after,
        )
        for (m, p), result in zip(keys, results):
            bit = orders[p][level]
            arrived[m ^ bit, p].append(swap(result, "wide", bit))
        return results[:1]

    levels = list(reversed(range(len(chip_bits))))
    order_token = level_gradients(levels[0], ())

    part_hidden = project_tokens(
        all_codes,
        training_hidden_input,
        mate_hidden,
        down_chunks,
        rank,
        rows=(decode_slice, mate_slice),
        after=order_token,
    )

    order_token = (part_hidden,)
    for level in levels[1:]:
        order_token = level_gradients(level, order_token)
    (own_down,) = gradient_chunks(
        token_codes,
        token_rewards,
        back,
        training_hidden_input,
        mate_hidden,
        [(p * part_adapters, arrived[0, p][:-1]) for p in range(parts)],
        part_adapters,
        joined=True,
        after=order_token,
    )
    last_down = [arrived[0, p][-1] for p in range(parts)]
    grad_down = finish(own_down, last_down)

    hidden = sum_over("narrow", part_hidden, [order_token, (own_down,)])
    up_results = gradient_chunks(
        token_codes,
        token_rewards,
        hidden,
        cotangent,
        mate_cotangent,
        [(m * owner_totals, ()) for m in masks],
        owner_totals,
        after=(own_down,),
    )
    grad_up = grad_up_own = up_results[0]
    for m, result in zip(masks[1:], up_results[1:]):
        result = wait_for(result, *last_down)
        grad_up = grad_up + swap(result, "wide", m).astype(jnp.float32)

    delta = row_deltas(row_codes, hidden, 2 * token_count, tile, up_chunks, (grad_up_own,))
    own_delta = delta[:row_count] + swap(delta[row_count:], "wide", core_bit)
    fresh_values = (base_values + own_delta.astype(jnp.float32)).astype(jnp.bfloat16)
    kv_local = up_width // HEAD_SIZE
    attended = cached + own_weight.astype(jnp.float32)[..., None] * fresh_values.reshape(
        row_count, kv_local, 1, HEAD_SIZE
    ).astype(jnp.float32)
    return (
        attended.reshape(row_count, -1).astype(jnp.bfloat16),
        fresh_values,
        grad_down.reshape(adapter_down_map.shape),
        grad_up.reshape(adapter_up_map.shape),
    )


def solution(mesh):
    return jax.shard_map(
        per_device,
        mesh=mesh,
        in_specs=(
            P("wide", None),
            P("wide", "narrow"),
            P("wide", None, "narrow"),
            P("wide", None, "narrow"),
            P("wide"),
            P("wide"),
            P(None, "narrow"),
            P(None, "narrow"),
            P("wide", None, "narrow"),
            P("wide", None, "narrow"),
            P("wide", "narrow"),
            P("wide", "narrow"),
            P("wide"),
            P("wide"),
        ),
        out_specs=(
            P("wide", "narrow"),
            P("wide", "narrow"),
            P("wide", None, "narrow"),
            P("wide", None, "narrow"),
        ),
        check_vma=False,
    )
```

time: 171 us -> 130 us (0.76)
  waiting for transfers between devices: 44 us -> 13.4 us
  other arithmetic: 20.8 us -> 8.3 us
  local copies, waits for them, and re-layouts: 5.78 us -> 9.83 us
    ppermute x27, waiting for transfers between devices: 44 us -> 13.4 us  [swap(): return lax.ppermute(array, axis, [(i, i ^ mask) for i in range(count)])]
    concatenate x2 -> x1, other arithmetic: 8.46 us -> 0.6 us  [per_device(): jnp.concatenate([token_codes, jnp.pad(row_codes, ((0, 0), (0, tile - 2 *...]
    dot_general x1, matrix products: 0.71 us -> 3.76 us  [attend_cached(): jnp.einsum('bhgp,bphd->bhgd', cache_weight, value_heads, preferred_elemen...]
    add x9 -> x4, other arithmetic: 5.25 us -> 2.29 us  [sum_over(): piece = piece + arrived]
    convert_element_type x3 -> x0, other arithmetic: 2.35 us -> none  [the longest x2 2.29 us: per_device(): arrived = swap(grads[m, p].astype(jnp.bfloat16), 'wide', bit)]
    slice x1, local copies, waits for them, and re-layouts: 0.07 us -> 2.32 us  [per_device(): own_part = flattened_down[p * part_rows:(p + 1) * part_rows]]
    pallas_call x9 -> x8, Pallas kernels: 54.1 us -> 52.6 us  [the longest x4 26.1 us: gradient_chunks(): pl.pallas_call(functools.partial(gradient_kernel, code_list([(base, rows)...]
    unnamed x56 -> x58, local copies, waits for them, and re-layouts: 4.34 us -> 5.58 us
  transfers between devices with their start and end apart: 27 -> 27, of which waited for: 9 -> 7; matrix products, arithmetic and copies ran while one was open for 16% -> 20% of each run, Pallas kernels for 29% -> 41%
where the time goes in v3:
time: 130 us; the launch traced here: 129 us
  Pallas kernels  52.6 us (40%)
  starting transfers between devices  32.3 us (25%)
  waiting for transfers between devices  13.4 us (10%)
  matrix products  11.9 us (9%)
  local copies, waits for them, and re-layouts  9.83 us (8%)
  other arithmetic  8.3 us (6%)
    ppermute x27, starting transfers between devices, swap(): return lax.ppermute(array, axis, [(i, i ^ mask) for i in range(count)])  32.3 us
    pallas_call x4, Pallas kernels, gradient_chunks(): pl.pallas_call(functools.partial(gradient_kernel, code_list([(base, rows)...  26.1 us
    pallas_call x2, Pallas kernels, project_tokens(): pl.pallas_call(functools.partial(token_kernel, code_list([(base, chunk.sh...  20.4 us
    ppermute x27, waiting for transfers between devices, swap(): return lax.ppermute(array, axis, [(i, i ^ mask) for i in range(count)])  13.4 us
    unnamed x58, local copies, waits for them, and re-layouts  5.58 us
    pallas_call x1, Pallas kernels, finish(): pl.pallas_call(finish_kernel, grid=(width // tile,), in_specs=[pl.BlockSp...  3.98 us
    dot_general x1, matrix products, attend_cached(): jnp.einsum('bhgp,bphd->bhgd', cache_weight, value_heads, preferred_elemen...  3.76 us
    dot_general x1, matrix products, attend_cached(): jnp.einsum('bhgd,bphd->bhgp', query_heads, key_heads, preferred_element_t...  3.49 us
  transfers between devices with their start and end apart: 27, of which 7 were waited for; matrix products, arithmetic and copies ran while one was open for 20% of the time, Pallas kernels for 41%

profile of v3, /device:TPU:0, one launch (start us, length us, event | category | flops | bytes accessed | tf_op | source)
XLA Modules:
  0.0 129.4 jit_solution(1218274790811031819)
XLA Ops:
  0.6 3.0 %collective-permute-start = (bf16[256,256]{1,0:T(8,128)(2,1)}, bf16[256,256]{1,0:T(8,128)(2,1)S(1)}, u32[]{:S(2)}, u32[]{:S(2)}) collective-permute-start(bf16[256,256]{1,0:T(8,128)(2,1)} %bitcast.65), channel_id=1, source_target_pairs={{0,8},{4,12},{8,0},{12,4},{16,24},{20,28},{24,16},{28,20},{1,9},{5... | collective-permute-start | bytes 393224 | tf_op jit(solution)/shard_map/ppermute | solution.py:23
  3.6 3.7 %collective-permute-done.refs_1_ = bf16[256,256]{1,0:T(8,128)(2,1)S(1)} collective-permute-done((bf16[256,256]{1,0:T(8,128)(2,1)}, bf16[256,256]{1,0:T(8,128)(2,1)S(1)}, u32[]{:S(2)}, u32[]{:S(2)}) %collective-permute-start) | collective-permute-done | bytes 131104 | tf_op jit(solution)/shard_map/ppermute | solution.py:23
  7.4 1.8 %collective-permute-start.1 = (bf16[256,256]{1,0:T(8,128)(2,1)}, bf16[256,256]{1,0:T(8,128)(2,1)S(1)}, u32[]{:S(2)}, u32[]{:S(2)}) collective-permute-start(bf16[256,256]{1,0:T(8,128)(2,1)} %bitcast.66), channel_id=1, source_target_pairs={{0,16},{4,20},{8,24},{12,28},{16,0},{20,4},{24,8},{28,12},{1,17},{... | collective-permute-start | bytes 393224 | tf_op jit(solution)/shard_map/ppermute | solution.py:23
  10.1 2.3 %fusion.21 = (bf16[8,16,2048]{2,1,0:T(8,128)(2,1)}, bf16[8,16,2048]{2,1,0:T(8,128)(2,1)}) fusion(bf16[16,16,2048]{2,1,0:T(8,128)(2,1)} %param.22), kind=kLoop, calls=%fused_computation.46 | loop fusion | bytes 2097152 | tf_op jit(solution)/shard_map/slice | solution.py:376
  16.6 2.1 %collective-permute-start.5 = (bf16[256,256]{1,0:T(8,128)(2,1)}, bf16[256,256]{1,0:T(8,128)(2,1)S(1)}, u32[]{:S(2)}, u32[]{:S(2)}) collective-permute-start(bf16[256,256]{1,0:T(8,128)(2,1)} %bitcast.67), channel_id=1, source_target_pairs={{0,24},{4,28},{8,16},{12,20},{16,8},{20,12},{24,0},{28,4},{1,25},{... | collective-permute-start | bytes 393224 | tf_op jit(solution)/shard_map/ppermute | solution.py:23
  19.7 3.0 %convolution_convert_fusion = bf16[32,256]{1,0:T(8,128)(2,1)S(1)} fusion(bf16[32,8192]{1,0:T(8,128)(2,1)S(1)} %copy-done, bf16[8192,256]{1,0:T(8,128)(2,1)} %param.20), kind=kOutput, calls=%fused_computation.8 | convolution fusion | flops 134225920 | bytes 4734976 | tf_op jit(solution)/shard_map/dot_general | solution.py:414
  23.0 3.5 %fusion.23 = (f32[32,2,8]{2,1,0:T(2,128)S(1)}, f32[32,2,8,256]{3,2,1,0:T(8,128)S(1)}) fusion(bf16[32,2,8,128]{3,2,1,0:T(8,128)(2,1)S(1)} %bitcast.71, pred[32,256]{1,0:T(8,128)(4,1)S(1)} %iota_compare_fusion, bf16[32,256,256]{2,1,0:T(8,128)(2,1)} %param.16), kind=kOutput, calls=%fused_computation.48 | convolution fusion | flops 33947136 | bytes 4859904 | tf_op jit(solution)/shard_map/bhgd,bphd->bhgp/dot_general | solution.py:305
  27.2 3.6 %collective-permute-done.7.refs_5_.refs_6_ = bf16[128,2048]{1,0:T(8,128)(2,1)S(1)} collective-permute-done((bf16[128,2048]{1,0:T(8,128)(2,1)}, bf16[128,2048]{1,0:T(8,128)(2,1)S(1)}, u32[]{:S(2)}, u32[]{:S(2)}) %collective-permute-start.7) | collective-permute-done | bytes 524320 | tf_op jit(solution)/shard_map/ppermute | solution.py:23
  31.3 3.8 %fusion.refs_7_ = f32[32,2,8,128]{3,2,1,0:T(8,128)} fusion(f32[32,2,8,256]{3,2,1,0:T(8,128)S(1)} %get-tuple-element.57, f32[32,2,8]{2,1,0:T(2,128)S(1)} %copy.29, f32[32,2,8]{2,1,0:T(2,128)S(1)} %copy.27, bf16[32,256,256]{2,1,0:T(8,128)(2,1)} %param.17), kind=kOutput, calls=%fused_computation | convolution fusion | flops 33947648 | bytes 4984832 | tf_op jit(solution)/shard_map/bhgp,bphd->bhgd/dot_general | solution.py:325
  37.4 4.4 %shard_map.165 = f32[16,2048]{1,0:T(8,128)} custom-call(s32[1,2048]{1,0:T(1,128)} %fusion.16.codes_ref.refs_0_, bf16[1024,256]{1,0:T(8,128)(2,1)} %refs_3_.7, bf16[1024,256]{1,0:T(8,128)(2,1)} %copy-done.2, bf16[256,256]{1,0:T(8,128)(2,1)} %bitcast.68, bf16[256,256]{1,0:T(8,128)(2,1)} %copy-done.8, bf16[256,256]{1,0:T(8,128)(2,1)} %copy-done.9, ...), custom_call_target="tpu_custom_call" | custom-call | flops 1 | bytes 1 | tf_op jit(solution)/shard_map/pallas_call | solution.py:127
  41.8 1.6 %collective-permute-start.13 = (f32[16,2048]{1,0:T(8,128)}, f32[16,2048]{1,0:T(8,128)S(1)}, u32[]{:S(2)}, u32[]{:S(2)}) collective-permute-start(f32[16,2048]{1,0:T(8,128)} %shard_map.165), channel_id=1, source_target_pairs={{0,1},{1,0},{2,3},{3,2},{4,5},{5,4},{6,7},{7,6},{8,9},{9,8},{10,11... | collective-permute-start | bytes 393224 | tf_op jit(solution)/shard_map/ppermute | solution.py:23
  47.9 2.7 %collective-permute-start.14 = (f32[16,2048]{1,0:T(8,128)S(1)}, f32[16,2048]{1,0:T(8,128)S(1)}, u32[]{:S(2)}, u32[]{:S(2)}) collective-permute-start(f32[16,2048]{1,0:T(8,128)S(1)} %add.106), channel_id=1, source_target_pairs={{0,2},{1,3},{2,0},{3,1},{4,6},{5,7},{6,4},{7,5},{8,10},{9,11},{10,... | collective-permute-start | bytes 393224 | tf_op jit(solution)/shard_map/ppermute | solution.py:23
  51.2 4.0 %collective-permute-done.14 = f32[16,2048]{1,0:T(8,128)S(1)} collective-permute-done((f32[16,2048]{1,0:T(8,128)S(1)}, f32[16,2048]{1,0:T(8,128)S(1)}, u32[]{:S(2)}, u32[]{:S(2)}) %collective-permute-start.14) | collective-permute-done | bytes 131104 | tf_op jit(solution)/shard_map/ppermute | solution.py:23
  55.9 8.6 %shard_map.166 = (bf16[128,2048]{1,0:T(8,128)(2,1)}, bf16[128,2048]{1,0:T(8,128)(2,1)}, bf16[128,2048]{1,0:T(8,128)(2,1)}, bf16[128,2048]{1,0:T(8,128)(2,1)}) custom-call(s32[1,2048]{1,0:T(1,128)} %fusion.16.codes_ref.refs_0_, s32[1,2048]{1,0:T(1,128)} %bitcast.74, f32[16,2048]{1,0:T(8,128)} %add.107.refs_2_, bf16[1024,2048]{1,0:T(8,128)(2,1)} %refs_3_.6, ...), custom_call_target="tpu_custom_call" | custom-call | flops 1 | bytes 1 | tf_op jit(solution)/shard_map/pallas_call | solution.py:231
  64.5 1.9 %collective-permute-start.16 = (bf16[128,2048]{1,0:T(8,128)(2,1)}, bf16[128,2048]{1,0:T(8,128)(2,1)S(1)}, u32[]{:S(2)}, u32[]{:S(2)}) collective-permute-start(bf16[128,2048]{1,0:T(8,128)(2,1)} %get-tuple-element.35.refs_9_), channel_id=1, source_target_pairs={{0,16},{4,20},{8,24},{12,28},{16,0},{20,4},{24,8},{28,12},{1,17},{... | collective-permute-start | bytes 1572872 | tf_op jit(solution)/shard_map/ppermute | solution.py:23
  70.8 16.0 %shard_map.167.refs_7_ = f32[16,2560]{1,0:T(8,128)} custom-call(s32[1,2560]{1,0:T(1,128)} %fusion.15.codes_ref, bf16[1024,2048]{1,0:T(8,128)(2,1)} %refs_3_.6, bf16[1024,2048]{1,0:T(8,128)(2,1)} %collective-permute-done.3.refs_6_.refs_4_.mate_ref, bf16[32,2048]{1,0:T(8,128)(2,1)} %copy-done.11, bf16[32,2048]{1,0:T(8,128)(2,1)} %copy-done.22, ...), custom_call_target="tpu_custom_call" | custom-call | flops 1 | bytes 1 | tf_op jit(solution)/shard_map/pallas_call | solution.py:127
  88.4 7.0 %shard_map.168 = (bf16[128,2048]{1,0:T(8,128)(2,1)}, bf16[128,2048]{1,0:T(8,128)(2,1)}) custom-call(s32[1,2048]{1,0:T(1,128)} %fusion.16.codes_ref.refs_0_, s32[1,2048]{1,0:T(1,128)} %bitcast.75, f32[16,2048]{1,0:T(8,128)} %add.107.refs_2_, bf16[1024,2048]{1,0:T(8,128)(2,1)} %refs_3_.6, bf16[1024,2048]{1,0:T(8,128)(2,1)} %collective-permute-done.3.refs_6_.refs_4_.mate_ref, ...), custom_call_target="tpu_custom_call" | custom-call | flops 1 | bytes 1 | tf_op jit(solution)/shard_map/pallas_call | solution.py:231
  95.4 1.8 %collective-permute-start.22 = (bf16[128,2048]{1,0:T(8,128)(2,1)}, bf16[128,2048]{1,0:T(8,128)(2,1)S(1)}, u32[]{:S(2)}, u32[]{:S(2)}) collective-permute-start(bf16[128,2048]{1,0:T(8,128)(2,1)} %get-tuple-element.37.refs_7_), channel_id=1, source_target_pairs={{0,8},{4,12},{8,0},{12,4},{16,24},{20,28},{24,16},{28,20},{1,9},{5... | collective-permute-start | bytes 1572872 | tf_op jit(solution)/shard_map/ppermute | solution.py:23
  98.8 3.4 %collective-permute-start.18 = (f32[16,2560]{1,0:T(8,128)S(1)}, f32[16,2560]{1,0:T(8,128)S(1)}, u32[]{:S(2)}, u32[]{:S(2)}) collective-permute-start(f32[16,2560]{1,0:T(8,128)S(1)} %add.108), channel_id=1, source_target_pairs={{0,2},{1,3},{2,0},{3,1},{4,6},{5,7},{6,4},{7,5},{8,10},{9,11},{10,... | collective-permute-start | bytes 491528 | tf_op jit(solution)/shard_map/ppermute | solution.py:23
  103.9 7.3 %shard_map.169.refs_5_.start_ref = f32[256,2048]{1,0:T(8,128)} custom-call(s32[1,2048]{1,0:T(1,128)} %fusion.16.codes_ref.refs_0_, s32[1,2048]{1,0:T(1,128)} %bitcast.76, f32[16,2048]{1,0:T(8,128)} %add.107.refs_2_, bf16[1024,2048]{1,0:T(8,128)(2,1)} %refs_3_.6, bf16[1024,2048]{1,0:T(8,128)(2,1)} %collective-permute-done.3.refs_6_.refs_4_.mate_ref, ...), custom_call_target="tpu_custom_call" | custom-call | flops 1 | bytes 1 | tf_op jit(solution)/shard_map/pallas_call | solution.py:231
  111.8 3.2 %shard_map.170 = (f32[256,256]{1,0:T(8,128)}, bf16[256,256]{1,0:T(8,128)(2,1)}, bf16[256,256]{1,0:T(8,128)(2,1)}, bf16[256,256]{1,0:T(8,128)(2,1)}) custom-call(s32[1,2048]{1,0:T(1,128)} %fusion.16.codes_ref.refs_0_, s32[1,2048]{1,0:T(1,128)} %bitcast.77, f32[16,2560]{1,0:T(8,128)} %add.109.refs_2_.rank_ref, bf16[1024,256]{1,0:T(8,128)(2,1)} %refs_3_.7, ...), custom_call_target="tpu_custom_call" | custom-call | flops 1 | bytes 1 | tf_op jit(solution)/shard_map/pallas_call | solution.py:231
  115.1 2.1 %shard_map.171 = bf16[64,256]{1,0:T(8,128)(2,1)} custom-call(s32[1,64]{1,0:T(1,128)} %copy-done.26, f32[16,2560]{1,0:T(8,128)} %add.109.refs_2_.rank_ref, bf16[256,256]{1,0:T(8,128)(2,1)} %bitcast.69, bf16[256,256]{1,0:T(8,128)(2,1)} %copy-done.8, bf16[256,256]{1,0:T(8,128)(2,1)} %copy-done.9, bf16[256,256]{1,0:T(8,128)(2,1)} %copy-done.10, ...), custom_call_target="tpu_custom_call" | custom-call | tf_op jit(solution)/shard_map/pallas_call | solution.py:175
  120.1 1.8 %collective-permute-start.25 = (bf16[256,256]{1,0:T(8,128)(2,1)}, bf16[256,256]{1,0:T(8,128)(2,1)S(1)}, u32[]{:S(2)}, u32[]{:S(2)}) collective-permute-start(bf16[256,256]{1,0:T(8,128)(2,1)} %get-tuple-element.47), channel_id=1, source_target_pairs={{0,16},{4,20},{8,24},{12,28},{16,0},{20,4},{24,8},{28,12},{1,17},{... | collective-permute-start | bytes 393224 | tf_op jit(solution)/shard_map/ppermute | solution.py:23
  124.3 4.0 %shard_map.172 = f32[256,2048]{1,0:T(8,128)} custom-call(f32[256,2048]{1,0:T(8,128)} %shard_map.169.refs_5_.start_ref, bf16[128,2048]{1,0:T(8,128)(2,1)} %copy-done.13, bf16[128,2048]{1,0:T(8,128)(2,1)} %copy-done.14), custom_call_target="tpu_custom_call" | custom-call | tf_op jit(solution)/shard_map/pallas_call | solution.py:273
  (130 shorter events, 31.8 us)
Async XLA Ops:
  0.6 6.7 %collective-permute-start = (bf16[256,256]{1,0:T(8,128)(2,1)}, bf16[256,256]{1,0:T(8,128)(2,1)S(1)}, u32[]{:S(2)}, u32[]{:S(2)}) collective-permute-start(bf16[256,256]{1,0:T(8,128)(2,1)} %bitcast.65), channel_id=1, source_target_pairs={{0,8},{4,12},{8,0},{12,4},{16,24},{20,28},{24,16},{28,20},{1,9},{5... | collective-permute-start | bytes 393224 | tf_op jit(solution)/shard_map/ppermute | solution.py:23
  7.4 29.2 %collective-permute-start.3 = (bf16[1024,2048]{1,0:T(8,128)(2,1)}, bf16[1024,2048]{1,0:T(8,128)(2,1)}, u32[]{:S(2)}, u32[]{:S(2)}) collective-permute-start(bf16[1024,2048]{1,0:T(8,128)(2,1)} %refs_3_.6), channel_id=1, source_target_pairs={{0,4},{4,0},{8,12},{12,8},{16,20},{20,16},{24,28},{28,24},{1,5},{5... | collective-permute-start | bytes 12582920 | tf_op jit(solution)/shard_map/ppermute | solution.py:23
  7.4 9.2 %collective-permute-start.1 = (bf16[256,256]{1,0:T(8,128)(2,1)}, bf16[256,256]{1,0:T(8,128)(2,1)S(1)}, u32[]{:S(2)}, u32[]{:S(2)}) collective-permute-start(bf16[256,256]{1,0:T(8,128)(2,1)} %bitcast.66), channel_id=1, source_target_pairs={{0,16},{4,20},{8,24},{12,28},{16,0},{20,4},{24,8},{28,12},{1,17},{... | collective-permute-start | bytes 393224 | tf_op jit(solution)/shard_map/ppermute | solution.py:23
  9.9 5.3 %collective-permute-start.2 = (s32[2080]{0:T(1024)S(1)}, s32[2080]{0:T(1024)S(1)}, u32[]{:S(2)}, u32[]{:S(2)}) collective-permute-start(s32[2080]{0:T(1024)S(1)} %pad_add_fusion), channel_id=1, source_target_pairs={{0,4},{4,0},{8,12},{12,8},{16,20},{20,16},{24,28},{28,24},{1,5},{5... | collective-permute-start | bytes 24968 | tf_op jit(solution)/shard_map/ppermute | solution.py:23
  12.4 18.9 %collective-permute-start.6 = (bf16[128,2048]{1,0:T(8,128)(2,1)}, bf16[128,2048]{1,0:T(8,128)(2,1)S(1)}, u32[]{:S(2)}, u32[]{:S(2)}) collective-permute-start(bf16[128,2048]{1,0:T(8,128)(2,1)} %bitcast.6), channel_id=1, source_target_pairs={{0,8},{4,12},{8,0},{12,4},{16,24},{20,28},{24,16},{28,20},{1,9},{5... | collective-permute-start | bytes 1572872 | tf_op jit(solution)/shard_map/ppermute | solution.py:23
  13.9 16.9 %collective-permute-start.7 = (bf16[128,2048]{1,0:T(8,128)(2,1)}, bf16[128,2048]{1,0:T(8,128)(2,1)S(1)}, u32[]{:S(2)}, u32[]{:S(2)}) collective-permute-start(bf16[128,2048]{1,0:T(8,128)(2,1)} %bitcast.7), channel_id=1, source_target_pairs={{0,16},{4,20},{8,24},{12,28},{16,0},{20,4},{24,8},{28,12},{1,17},{... | collective-permute-start | bytes 1572872 | tf_op jit(solution)/shard_map/ppermute | solution.py:23
  15.1 21.4 %collective-permute-start.4 = (bf16[1024,256]{1,0:T(8,128)(2,1)}, bf16[1024,256]{1,0:T(8,128)(2,1)S(1)}, u32[]{:S(2)}, u32[]{:S(2)}) collective-permute-start(bf16[1024,256]{1,0:T(8,128)(2,1)} %refs_3_.7), channel_id=1, source_target_pairs={{0,4},{4,0},{8,12},{12,8},{16,20},{20,16},{24,28},{28,24},{1,5},{5... | collective-permute-start | bytes 1572872 | tf_op jit(solution)/shard_map/ppermute | solution.py:23
  16.6 20.0 %collective-permute-start.5 = (bf16[256,256]{1,0:T(8,128)(2,1)}, bf16[256,256]{1,0:T(8,128)(2,1)S(1)}, u32[]{:S(2)}, u32[]{:S(2)}) collective-permute-start(bf16[256,256]{1,0:T(8,128)(2,1)} %bitcast.67), channel_id=1, source_target_pairs={{0,24},{4,28},{8,16},{12,20},{16,8},{20,12},{24,0},{28,4},{1,25},{... | collective-permute-start | bytes 393224 | tf_op jit(solution)/shard_map/ppermute | solution.py:23
  30.7 13.0 %collective-permute-start.9 = (bf16[128,2048]{1,0:T(8,128)(2,1)S(1)}, bf16[128,2048]{1,0:T(8,128)(2,1)S(1)}, u32[]{:S(2)}, u32[]{:S(2)}) collective-permute-start(bf16[128,2048]{1,0:T(8,128)(2,1)S(1)} %collective-permute-done.7.refs_5_.refs_6_), channel_id=1, source_target_pairs={{0,8},{4,12},{8,0},{12,4},{16,24},{20,28},{24,16},{28,20},{1,9},{5... | collective-permute-start | bytes 1572872 | tf_op jit(solution)/shard_map/ppermute | solution.py:23
  31.3 13.9 %collective-permute-start.11 = (bf16[128,2048]{1,0:T(8,128)(2,1)S(1)}, bf16[128,2048]{1,0:T(8,128)(2,1)}, u32[]{:S(2)}, u32[]{:S(2)}) collective-permute-start(bf16[128,2048]{1,0:T(8,128)(2,1)S(1)} %collective-permute-done.6.refs_4_.refs_3_), channel_id=1, source_target_pairs={{0,16},{4,20},{8,24},{12,28},{16,0},{20,4},{24,8},{28,12},{1,17},{... | collective-permute-start | bytes 1572872 | tf_op jit(solution)/shard_map/ppermute | solution.py:23
  43.7 25.0 %collective-permute-start.10 = (bf16[128,2048]{1,0:T(8,128)(2,1)}, bf16[128,2048]{1,0:T(8,128)(2,1)S(1)}, u32[]{:S(2)}, u32[]{:S(2)}) collective-permute-start(bf16[128,2048]{1,0:T(8,128)(2,1)} %bitcast.7), channel_id=1, source_target_pairs={{0,8},{4,12},{8,0},{12,4},{16,24},{20,28},{24,16},{28,20},{1,9},{5... | collective-permute-start | bytes 1572872 | tf_op jit(solution)/shard_map/ppermute | solution.py:23
  45.2 24.2 %collective-permute-start.12 = (bf16[128,2048]{1,0:T(8,128)(2,1)}, bf16[128,2048]{1,0:T(8,128)(2,1)S(1)}, u32[]{:S(2)}, u32[]{:S(2)}) collective-permute-start(bf16[128,2048]{1,0:T(8,128)(2,1)} %bitcast.6), channel_id=1, source_target_pairs={{0,16},{4,20},{8,24},{12,28},{16,0},{20,4},{24,8},{28,12},{1,17},{... | collective-permute-start | bytes 1572872 | tf_op jit(solution)/shard_map/ppermute | solution.py:23
  47.9 7.3 %collective-permute-start.14 = (f32[16,2048]{1,0:T(8,128)S(1)}, f32[16,2048]{1,0:T(8,128)S(1)}, u32[]{:S(2)}, u32[]{:S(2)}) collective-permute-start(f32[16,2048]{1,0:T(8,128)S(1)} %add.106), channel_id=1, source_target_pairs={{0,2},{1,3},{2,0},{3,1},{4,6},{5,7},{6,4},{7,5},{8,10},{9,11},{10,... | collective-permute-start | bytes 393224 | tf_op jit(solution)/shard_map/ppermute | solution.py:23
  64.5 23.1 %collective-permute-start.16 = (bf16[128,2048]{1,0:T(8,128)(2,1)}, bf16[128,2048]{1,0:T(8,128)(2,1)S(1)}, u32[]{:S(2)}, u32[]{:S(2)}) collective-permute-start(bf16[128,2048]{1,0:T(8,128)(2,1)} %get-tuple-element.35.refs_9_), channel_id=1, source_target_pairs={{0,16},{4,20},{8,24},{12,28},{16,0},{20,4},{24,8},{28,12},{1,17},{... | collective-permute-start | bytes 1572872 | tf_op jit(solution)/shard_map/ppermute | solution.py:23
  66.4 21.2 %collective-permute-start.17 = (bf16[128,2048]{1,0:T(8,128)(2,1)}, bf16[128,2048]{1,0:T(8,128)(2,1)}, u32[]{:S(2)}, u32[]{:S(2)}) collective-permute-start(bf16[128,2048]{1,0:T(8,128)(2,1)} %get-tuple-element.36), channel_id=1, source_target_pairs={{0,8},{4,12},{8,0},{12,4},{16,24},{20,28},{24,16},{28,20},{1,9},{5... | collective-permute-start | bytes 1572872 | tf_op jit(solution)/shard_map/ppermute | solution.py:23
  68.8 33.4 %collective-permute-start.19 = (bf16[128,2048]{1,0:T(8,128)(2,1)}, bf16[128,2048]{1,0:T(8,128)(2,1)S(1)}, u32[]{:S(2)}, u32[]{:S(2)}) collective-permute-start(bf16[128,2048]{1,0:T(8,128)(2,1)} %get-tuple-element.39), channel_id=1, source_target_pairs={{0,16},{4,20},{8,24},{12,28},{16,0},{20,4},{24,8},{28,12},{1,17},{... | collective-permute-start | bytes 1572872 | tf_op jit(solution)/shard_map/ppermute | solution.py:23
  69.4 32.9 %collective-permute-start.20 = (bf16[128,2048]{1,0:T(8,128)(2,1)}, bf16[128,2048]{1,0:T(8,128)(2,1)S(1)}, u32[]{:S(2)}, u32[]{:S(2)}) collective-permute-start(bf16[128,2048]{1,0:T(8,128)(2,1)} %get-tuple-element.40), channel_id=1, source_target_pairs={{0,8},{4,12},{8,0},{12,4},{16,24},{20,28},{24,16},{28,20},{1,9},{5... | collective-permute-start | bytes 1572872 | tf_op jit(solution)/shard_map/ppermute | solution.py:23
  86.9 11.9 %collective-permute-start.15 = (f32[16,2560]{1,0:T(8,128)}, f32[16,2560]{1,0:T(8,128)S(1)}, u32[]{:S(2)}, u32[]{:S(2)}) collective-permute-start(f32[16,2560]{1,0:T(8,128)} %shard_map.167.refs_7_), channel_id=1, source_target_pairs={{0,1},{1,0},{2,3},{3,2},{4,5},{5,4},{6,7},{7,6},{8,9},{9,8},{10,11... | collective-permute-start | bytes 491528 | tf_op jit(solution)/shard_map/ppermute | solution.py:23
  95.4 24.4 %collective-permute-start.22 = (bf16[128,2048]{1,0:T(8,128)(2,1)}, bf16[128,2048]{1,0:T(8,128)(2,1)S(1)}, u32[]{:S(2)}, u32[]{:S(2)}) collective-permute-start(bf16[128,2048]{1,0:T(8,128)(2,1)} %get-tuple-element.37.refs_7_), channel_id=1, source_target_pairs={{0,8},{4,12},{8,0},{12,4},{16,24},{20,28},{24,16},{28,20},{1,9},{5... | collective-permute-start | bytes 1572872 | tf_op jit(solution)/shard_map/ppermute | solution.py:23
  97.2 22.6 %collective-permute-start.23 = (bf16[128,2048]{1,0:T(8,128)(2,1)}, bf16[128,2048]{1,0:T(8,128)(2,1)S(1)}, u32[]{:S(2)}, u32[]{:S(2)}) collective-permute-start(bf16[128,2048]{1,0:T(8,128)(2,1)} %get-tuple-element.43), channel_id=1, source_target_pairs={{0,16},{4,20},{8,24},{12,28},{16,0},{20,4},{24,8},{28,12},{1,17},{... | collective-permute-start | bytes 1572872 | tf_op jit(solution)/shard_map/ppermute | solution.py:23
  98.8 12.4 %collective-permute-start.18 = (f32[16,2560]{1,0:T(8,128)S(1)}, f32[16,2560]{1,0:T(8,128)S(1)}, u32[]{:S(2)}, u32[]{:S(2)}) collective-permute-start(f32[16,2560]{1,0:T(8,128)S(1)} %add.108), channel_id=1, source_target_pairs={{0,2},{1,3},{2,0},{3,1},{4,6},{5,7},{6,4},{7,5},{8,10},{9,11},{10,... | collective-permute-start | bytes 491528 | tf_op jit(solution)/shard_map/ppermute | solution.py:23
  119.9 8.4 %collective-permute-start.26 = (bf16[256,256]{1,0:T(8,128)(2,1)}, bf16[256,256]{1,0:T(8,128)(2,1)S(1)}, u32[]{:S(2)}, u32[]{:S(2)}) collective-permute-start(bf16[256,256]{1,0:T(8,128)(2,1)} %get-tuple-element.49), channel_id=1, source_target_pairs={{0,24},{4,28},{8,16},{12,20},{16,8},{20,12},{24,0},{28,4},{1,25},{... | collective-permute-start | bytes 393224 | tf_op jit(solution)/shard_map/ppermute | solution.py:23
  120.1 8.5 %collective-permute-start.25 = (bf16[256,256]{1,0:T(8,128)(2,1)}, bf16[256,256]{1,0:T(8,128)(2,1)S(1)}, u32[]{:S(2)}, u32[]{:S(2)}) collective-permute-start(bf16[256,256]{1,0:T(8,128)(2,1)} %get-tuple-element.47), channel_id=1, source_target_pairs={{0,16},{4,20},{8,24},{12,28},{16,0},{20,4},{24,8},{28,12},{1,17},{... | collective-permute-start | bytes 393224 | tf_op jit(solution)/shard_map/ppermute | solution.py:23
  121.9 6.7 %collective-permute-start.24 = (bf16[256,256]{1,0:T(8,128)(2,1)}, bf16[256,256]{1,0:T(8,128)(2,1)S(1)}, u32[]{:S(2)}, u32[]{:S(2)}) collective-permute-start(bf16[256,256]{1,0:T(8,128)(2,1)} %get-tuple-element.45), channel_id=1, source_target_pairs={{0,8},{4,12},{8,0},{12,4},{16,24},{20,28},{24,16},{28,20},{1,9},{5... | collective-permute-start | bytes 393224 | tf_op jit(solution)/shard_map/ppermute | solution.py:23
  (31 other events, 254.6 us)

commit v4 on v3

--- a/solution.py
+++ b/solution.py
@@ -15,7 +15,7 @@
 
 ADAPTER_SCALE = 2.0
 NEG_FILL = -1e30
-VMEM_LIMIT = 60 * 1024 * 1024
+VMEM_LIMIT = 48 * 1024 * 1024
 
 
 def swap(array, axis, mask):
@@ -73,10 +73,11 @@
 
 
 def token_kernel(
-    map_codes, rank, own_tiles, has_rows, map_count, codes_ref, own_ref, mate_ref, *refs
+    map_codes, rank, own_tiles, has_rows, has_start, map_count, codes_ref, own_ref, mate_ref, *refs
 ):
     refs = list(refs)
     row_refs = [refs.pop(0) for _ in range(2 * has_rows)]
+    start_ref = refs.pop(0) if has_start else None
     maps = refs[:map_count]
     out_ref, joined_ref, *rest = refs[-2 - has_rows :]
     step = pl.program_id(0)
@@ -91,7 +92,7 @@
         return pick(codes, products, map_codes, rank)
 
     def store(total):
-        out_ref[...] = total
+        out_ref[...] = total if start_ref is None else total + start_ref[...]
 
     pl.when(step < own_tiles)(lambda: store(project(own_ref[...])))
     pl.when((step >= own_tiles) & (step < 2 * own_tiles))(lambda: store(project(mate_ref[...])))
@@ -106,13 +107,13 @@
             out_ref[:, : rows_ref.shape[0]] += project(rows_ref[...])
 
 
-def token_tile(token_count):
-    return largest_tile(token_count, 512)
-
-
-def project_tokens(codes, own, mate, chunks, rank, rows=(), after=()):
+def token_tile(token_count, width=0):
+    return largest_tile(token_count, 512 if width > 512 else 1024)
+
+
+def project_tokens(codes, own, mate, chunks, rank, rows=(), start=None, after=()):
     token_count, width = own.shape
-    tile = token_tile(token_count)
+    tile = token_tile(token_count, width)
     own_tiles = token_count // tile
     steps = 2 * own_tiles + bool(rows)
     map_rows = sum(chunk.shape[0] for _, chunk in chunks)
@@ -122,6 +123,7 @@
         assert padded <= tile, "row count"
         scratch.append(pltpu.VMEM((padded, width), jnp.bfloat16))
     result_spec = pl.BlockSpec((rank, tile), lambda i: (0, i))
+    starts = [] if start is None else [start]
     whole = lambda i: (0, 0)
     last = own_tiles - 1
     return pl.pallas_call(
@@ -131,6 +133,7 @@
             rank,
             own_tiles,
             bool(rows),
+            bool(starts),
             len(chunks),
         ),
         grid=(steps,),
@@ -140,6 +143,7 @@
             pl.BlockSpec((tile, width), lambda i: (jnp.clip(i - own_tiles, 0, last), 0)),
         ]
         + [pl.BlockSpec(a.shape, whole) for a in rows]
+        + [result_spec for _ in starts]
         + [pl.BlockSpec(chunk.shape, whole) for _, chunk in chunks]
         + [pl.BlockSpec(memory_space=pl.ANY) for _ in after],
         out_specs=result_spec,
@@ -147,15 +151,15 @@
         scratch_shapes=scratch,
         compiler_params=pltpu.CompilerParams(vmem_limit_bytes=VMEM_LIMIT),
         cost_estimate=pl.CostEstimate(flops=1, bytes_accessed=1, transcendentals=0),
-    )(codes, own, mate, *rows, *[chunk for _, chunk in chunks], *after)
+    )(codes, own, mate, *rows, *starts, *[chunk for _, chunk in chunks], *after)
 
 
 def delta_kernel(chunk_codes, codes_ref, rank_ref, *refs):
     maps = refs[: len(chunk_codes)]
-    out_ref, spread_ref = refs[-2:]
+    own_ref, mate_ref, spread_ref = refs[-3:]
     count = codes_ref.shape[1]
     values = rank_ref[:, :count].astype(jnp.bfloat16).astype(jnp.float32)
-    total = jnp.zeros(out_ref.shape, jnp.float32)
+    total = jnp.zeros((count, own_ref.shape[1]), jnp.float32)
     for map_codes, chunk in zip(chunk_codes, maps):
         spread(codes_ref[...], values, map_codes, spread_ref)
         total += lax.dot_general(
@@ -164,7 +168,9 @@
             (((1,), (0,)), ((), ())),
             preferred_element_type=jnp.float32,
         )
-    out_ref[...] = (ADAPTER_SCALE * total).astype(out_ref.dtype)
+    deltas = ADAPTER_SCALE * total
+    own_ref[...] = deltas[: count // 2].astype(own_ref.dtype)
+    mate_ref[...] = deltas[count // 2 :].astype(mate_ref.dtype)
 
 
 def row_deltas(codes, ranks, first, width_of_ranks, chunks, after=()):
@@ -183,17 +189,14 @@
         ]
         + [pl.BlockSpec((chunk_rows, width), whole) for _ in chunks]
         + [pl.BlockSpec(memory_space=pl.ANY) for _ in after],
-        out_specs=pl.BlockSpec((row_count, width), whole),
-        out_shape=jax.ShapeDtypeStruct((row_count, width), jnp.bfloat16),
+        out_specs=[pl.BlockSpec((row_count // 2, width), whole)] * 2,
+        out_shape=[jax.ShapeDtypeStruct((row_count // 2, width), jnp.bfloat16)] * 2,
         scratch_shapes=[pltpu.VMEM((chunk_rows, row_count), jnp.float32)],
         compiler_params=pltpu.CompilerParams(vmem_limit_bytes=VMEM_LIMIT),
     )(codes, ranks, *[chunk for _, chunk in chunks], *after)
 
 
-def gradient_kernel(row_codes, rows, arrived_counts, waits, joined, *refs):
-    codes_ref, rewards_ref, factor_ref, own_ref, mate_ref = refs[:5]
-    refs = list(refs[5:])
-    arrived = [[refs.pop(0) for _ in range(count)] for count in arrived_counts]
+def gradient_kernel(row_codes, waits, codes_ref, rewards_ref, factor_ref, own_ref, mate_ref, *refs):
     outs = refs[waits:-1]
     spread_ref = refs[-1]
     token_count = own_ref.shape[0]
@@ -207,35 +210,25 @@
     total = jnp.dot(
         spread_ref[:, :token_count], own_ref[...], preferred_element_type=jnp.float32
     ) + jnp.dot(spread_ref[:, token_count:], mate_ref[...], preferred_element_type=jnp.float32)
-    for k in range(len(arrived)):
-        piece = total[k * rows : (k + 1) * rows]
-        for ref in arrived[k]:
-            piece += ref[...].astype(jnp.float32)
-        if joined:
-            outs[0][k * rows : (k + 1) * rows, :] = piece
-        else:
-            outs[k][...] = piece.astype(outs[k].dtype)
-
-
-def gradient_chunks(
-    codes, rewards, factor, own, mate, chunks, adapters, joined=False, after=()
-):
+    first = 0
+    for out_ref in outs:
+        rows = out_ref.shape[0]
+        out_ref[...] = total[first : first + rows].astype(out_ref.dtype)
+        first += rows
+
+
+def gradient_chunks(codes, rewards, factor, own, mate, chunks, after=()):
     rank = factor.shape[0]
     token_count, width = own.shape
     tile = largest_tile(width, 512)
-    rows = adapters * rank
-    out_rows = [rows * len(chunks)] if joined else [rows] * len(chunks)
-    arrived = [a for _, arrays in chunks for a in arrays]
+    out_rows = [adapters * rank for _, adapters, _ in chunks]
     whole = lambda i: (0, 0)
     across = lambda i: (0, i)
     return pl.pallas_call(
         functools.partial(
             gradient_kernel,
-            code_list([(base, rows) for base, _ in chunks], rank),
-            rows,
-            [len(arrays) for _, arrays in chunks],
+            code_list([(base, rows) for (base, _, _), rows in zip(chunks, out_rows)], rank),
             len(after),
-            joined,
         ),
         grid=(width // tile,),
         in_specs=[
@@ -245,39 +238,50 @@
             pl.BlockSpec((token_count, tile), across),
             pl.BlockSpec((token_count, tile), across),
         ]
-        + [pl.BlockSpec((rows, tile), across) for _ in arrived]
         + [pl.BlockSpec(memory_space=pl.ANY) for _ in after],
-        out_specs=[pl.BlockSpec((r, tile), across) for r in out_rows],
+        out_specs=[pl.BlockSpec((rows, tile), across) for rows in out_rows],
         out_shape=[
-            jax.ShapeDtypeStruct((r, width), jnp.bfloat16 if base else jnp.float32)
-            for r, (base, _) in zip(out_rows, chunks)
+            jax.ShapeDtypeStruct((rows, width), dtype)
+            for rows, (_, _, dtype) in zip(out_rows, chunks)
         ],
-        scratch_shapes=[pltpu.VMEM((len(chunks) * rows, 2 * token_count), jnp.bfloat16)],
+        scratch_shapes=[pltpu.VMEM((sum(out_rows), 2 * token_count), jnp.bfloat16)],
         compiler_params=pltpu.CompilerParams(vmem_limit_bytes=VMEM_LIMIT),
         cost_estimate=pl.CostEstimate(flops=1, bytes_accessed=1, transcendentals=0),
-    )(codes, rewards, factor, own, mate, *arrived, *after)
-
-
-def finish_kernel(start_ref, *refs):
-    arrived, out_ref = refs[:-1], refs[-1]
-    rows = arrived[0].shape[0]
-    for p, ref in enumerate(arrived):
-        part = slice(p * rows, (p + 1) * rows)
-        out_ref[part, :] = start_ref[part, :] + ref[...].astype(jnp.float32)
-
-
-def finish(start, arrived):
-    rows, width = start.shape
-    tile = largest_tile(width, 512)
+    )(codes, rewards, factor, own, mate, *after)
+
+
+def add_kernel(groups, *refs):
+    starts, refs = refs[: len(groups)], refs[len(groups) :]
+    outs = refs[len(refs) - len(groups) :]
+    arrived = list(refs[: sum(sum(counts) for counts in groups)])
+    for counts, start_ref, out_ref in zip(groups, starts, outs):
+        rows = out_ref.shape[0] // len(counts)
+        for p, count in enumerate(counts):
+            part = slice(p * rows, (p + 1) * rows)
+            total = start_ref[part, :]
+            for _ in range(count):
+                total += arrived.pop(0)[...].astype(jnp.float32)
+            out_ref[part, :] = total.astype(out_ref.dtype)
+
+
+def add_arrived(groups, dtype, after=()):
+    width = groups[0][0].shape[1]
+    tile = largest_tile(width, 1024)
+    arrays = [start for start, _ in groups]
+    arrays += [a for _, parts in groups for arrived in parts for a in arrived]
     across = lambda i: (0, i)
     return pl.pallas_call(
-        finish_kernel,
+        functools.partial(
+            add_kernel, [[len(arrived) for arrived in parts] for _, parts in groups]
+        ),
         grid=(width // tile,),
-        in_specs=[pl.BlockSpec((a.shape[0], tile), across) for a in (start, *arrived)],
-        out_specs=pl.BlockSpec((rows, tile), across),
-        out_shape=jax.ShapeDtypeStruct(start.shape, start.dtype),
+        in_specs=[pl.BlockSpec((a.shape[0], tile), across) for a in arrays]
+        + [pl.BlockSpec(memory_space=pl.ANY) for _ in after],
+        out_specs=[pl.BlockSpec((start.shape[0], tile), across) for start, _ in groups],
+        out_shape=[jax.ShapeDtypeStruct(start.shape, dtype) for start, _ in groups],
         compiler_params=pltpu.CompilerParams(vmem_limit_bytes=VMEM_LIMIT),
-    )(start, *arrived)
+        cost_estimate=pl.CostEstimate(flops=1, bytes_accessed=1, transcendentals=0),
+    )(*arrays, *after)
 
 
 def wait_for(array, *others):
@@ -366,25 +370,26 @@
     mate_numbers = swap(numbers, "wide", core_bit)
     mate_cotangent = swap(wait_for(cotangent, mate_numbers), "wide", core_bit)
     up_maps = {0: flattened_up}
+    own_parts = [flattened_down[p * part_rows : (p + 1) * part_rows] for p in range(parts)]
     for m in near:
-        up_maps[m] = swap(flattened_up, "wide", m)
+        up_maps[m] = swap(wait_for(flattened_up, *own_parts), "wide", m)
     for m in far:
         up_maps[m] = swap(wait_for(flattened_up, mate_numbers), "wide", m)
-    mate_hidden = swap(wait_for(training_hidden_input, up_maps[near[0]]), "wide", core_bit)
+    mate_hidden = swap(wait_for(training_hidden_input, mate_numbers), "wide", core_bit)
     down_parts = {}
     for p, order in enumerate(orders):
-        own_part = flattened_down[p * part_rows : (p + 1) * part_rows]
         held = []
         for bit in order:
             for m in held:
                 down_parts[m | bit, p] = swap(down_parts[m, p], "wide", bit)
-            sent = wait_for(own_part, *[down_parts[m | bit, p] for m in held[-1:]])
+            sent = wait_for(own_parts[p], *[down_parts[m | bit, p] for m in held[-1:]])
             down_parts[bit, p] = swap(sent, "wide", bit)
             held = held + [bit] + [m | bit for m in held]
     first_maps = [down_parts[order[0], p] for p, order in enumerate(orders)]
     decode_slice = lax.dynamic_slice_in_dim(
         decode_hidden_input, lax.axis_index("narrow") * down_width, down_width, 1
     )
+    mate_slice = swap(wait_for(decode_slice, mate_cotangent), "wide", core_bit)
 
     def codes_of(ids):
         return (((ids // owner_totals) ^ me) * owner_totals + ids % owner_totals)[None, :]
@@ -398,17 +403,14 @@
     row_codes = codes_of(
         jnp.concatenate([decode_adapter_index, mate_numbers[2 * token_count :]])
     )
-    tile = token_tile(token_count)
+    tile = token_tile(token_count, down_width)
     all_codes = jnp.concatenate(
         [token_codes, jnp.pad(row_codes, ((0, 0), (0, tile - 2 * row_count)), constant_values=-1)],
         axis=1,
     )
     up_chunks = [(m * owner_totals, up_maps[m]) for m in masks]
-    down_chunks = [(0, flattened_down)] + [
-        (m * owner_totals + p * part_adapters, down_parts[m, p])
-        for m in near + far
-        for p in range(parts)
-    ]
+    def down_chunk(m, p):
+        return (m * owner_totals + p * part_adapters, down_parts[m, p])
 
     hidden_rows = wait_for(decode_hidden_input, mate_numbers, *[up_maps[m] for m in near])
     fresh_keys = jnp.dot(
@@ -425,87 +427,85 @@
     )
 
     part_back = project_tokens(
-        token_codes,
+        all_codes,
         cotangent,
         mate_cotangent,
         up_chunks,
         rank,
-        after=(*first_maps, mate_hidden, cached, base_values),
-    )
-    mate_slice = swap(wait_for(decode_slice, part_back), "wide", core_bit)
-    back = sum_over("narrow", part_back)
-    arrived = {(m, p): [] for m in masks for p in range(parts)}
-
-    def level_gradients(level, after):
-        keys = [
-            (m, p)
-            for m in far + near
-            for p, order in enumerate(orders)
-            if m & order[level] and not any(m & bit for bit in order[level + 1 :])
-        ]
-        results = gradient_chunks(
-            token_codes,
-            token_rewards,
-            back,
-            training_hidden_input,
-            mate_hidden,
-            [(m * owner_totals + p * part_adapters, arrived[m, p]) for m, p in keys],
-            part_adapters,
-            after=after,
-        )
-        for (m, p), result in zip(keys, results):
-            bit = orders[p][level]
-            arrived[m ^ bit, p].append(swap(result, "wide", bit))
-        return results[:1]
-
-    levels = list(reversed(range(len(chip_bits))))
-    order_token = level_gradients(levels[0], ())
-
-    part_hidden = project_tokens(
-        all_codes,
-        training_hidden_input,
-        mate_hidden,
-        down_chunks,
-        rank,
-        rows=(decode_slice, mate_slice),
-        after=order_token,
-    )
-
-    order_token = (part_hidden,)
-    for level in levels[1:]:
-        order_token = level_gradients(level, order_token)
-    (own_down,) = gradient_chunks(
+        after=(*first_maps, mate_hidden, own_weight),
+    )
+    back = sum_over("narrow", part_back, [(cached,), (base_values,)])
+
+    def level_of(m, p):
+        return max((k for k, bit in enumerate(orders[p]) if m & bit), default=-1)
+
+    last_level = len(chip_bits) - 1
+    keys = sorted(
+        ((m, p) for m in far + near for p in range(parts)), key=lambda key: -level_of(*key)
+    )
+    own_down, *down_results = gradient_chunks(
         token_codes,
         token_rewards,
         back,
         training_hidden_input,
         mate_hidden,
-        [(p * part_adapters, arrived[0, p][:-1]) for p in range(parts)],
-        part_adapters,
-        joined=True,
-        after=order_token,
+        [(0, owner_totals, jnp.float32)]
+        + [
+            (
+                m * owner_totals + p * part_adapters,
+                part_adapters,
+                jnp.bfloat16 if level_of(m, p) == last_level else jnp.float32,
+            )
+            for m, p in keys
+        ],
+    )
+    grads = dict(zip(keys, down_results))
+    arrived = {(m, p): [] for m in masks for p in range(parts)}
+
+    def send_level(level):
+        for m, p in keys:
+            if level_of(m, p) == level:
+                bit = orders[p][level]
+                arrived[m ^ bit, p].append(swap(grads[m, p], "wide", bit))
+
+    send_level(last_level)
+    part_hidden = project_tokens(
+        all_codes,
+        training_hidden_input,
+        mate_hidden,
+        [(0, flattened_down)] + [down_chunk(m, p) for m in near + far for p in range(parts)],
+        rank,
+        rows=(decode_slice, mate_slice),
+        after=(own_down,),
+    )
+    token = part_hidden
+    for level in reversed(range(last_level)):
+        added = [key for key in keys if level_of(*key) == level]
+        sums = add_arrived([(grads[key], [arrived[key]]) for key in added], jnp.bfloat16, (token,))
+        grads.update(zip(added, sums))
+        token = sums[0]
+        send_level(level)
+    (own_down,) = add_arrived(
+        [(own_down, [arrived[0, p][:-1] for p in range(parts)])], jnp.float32, (token,)
     )
     last_down = [arrived[0, p][-1] for p in range(parts)]
-    grad_down = finish(own_down, last_down)
-
-    hidden = sum_over("narrow", part_hidden, [order_token, (own_down,)])
-    up_results = gradient_chunks(
+    (grad_down,) = add_arrived([(own_down, [[a] for a in last_down])], jnp.float32)
+
+    hidden = sum_over("narrow", part_hidden, [(token,), (own_down,)])
+    grad_up, *up_results = gradient_chunks(
         token_codes,
         token_rewards,
         hidden,
         cotangent,
         mate_cotangent,
-        [(m * owner_totals, ()) for m in masks],
-        owner_totals,
-        after=(own_down,),
-    )
-    grad_up = grad_up_own = up_results[0]
-    for m, result in zip(masks[1:], up_results[1:]):
+        [(m * owner_totals, owner_totals, jnp.bfloat16 if m else jnp.float32) for m in masks],
+    )
+    own_delta, mate_delta = row_deltas(row_codes, hidden, 2 * token_count, tile, up_chunks, (grad_up,))
+    for m, result in zip(masks[1:], up_results):
         result = wait_for(result, *last_down)
         grad_up = grad_up + swap(result, "wide", m).astype(jnp.float32)
 
-    delta = row_deltas(row_codes, hidden, 2 * token_count, tile, up_chunks, (grad_up_own,))
-    own_delta = delta[:row_count] + swap(delta[row_count:], "wide", core_bit)
+    own_delta = own_delta + swap(mate_delta, "wide", core_bit)
     fresh_values = (base_values + own_delta.astype(jnp.float32)).astype(jnp.bfloat16)
     kv_local = up_width // HEAD_SIZE
     attended = cached + own_weight.astype(jnp.float32)[..., None] * fresh_values.reshape(

time: 130 us -> 110 us (0.85)
  Pallas kernels: 52.6 us -> 35.7 us
  waiting for transfers between devices: 13.4 us -> 22.7 us
  local copies, waits for them, and re-layouts: 9.83 us -> 3.19 us
  matrix products: 11.9 us -> 9.01 us
  starting transfers between devices: 32.3 us -> 30.2 us
    pallas_call x4 -> x2, Pallas kernels: 26.1 us -> 13.9 us  [gradient_chunks(): pl.pallas_call(functools.partial(gradient_kernel, code_list([(base, rows)...]
    ppermute x27, waiting for transfers between devices: 13.4 us -> 22.7 us  [swap(): return lax.ppermute(array, axis, [(i, i ^ mask) for i in range(count)])]
    unnamed x58 -> x44, local copies, waits for them, and re-layouts: 5.58 us -> 0.82 us
    pallas_call x2, Pallas kernels: 20.4 us -> 16.2 us  [project_tokens(): pl.pallas_call(functools.partial(token_kernel, code_list([(base, chunk.sh...]
    dot_general x1, matrix products: 3.76 us -> 1.42 us  [attend_cached(): jnp.einsum('bhgp,bphd->bhgd', cache_weight, value_heads, preferred_elemen...]
    add x4, other arithmetic: 2.29 us -> 0.08 us  [sum_over(): piece = piece + arrived]
    ppermute x27, starting transfers between devices: 32.3 us -> 30.2 us  [swap(): return lax.ppermute(array, axis, [(i, i ^ mask) for i in range(count)])]
    slice x2 -> x1, local copies, waits for them, and re-layouts: 3.04 us -> 2.33 us  [per_device(): flattened_down[p * part_rows:(p + 1) * part_rows]]
  transfers between devices with their start and end apart: 27 -> 27, of which waited for: 7 -> 9; matrix products, arithmetic and copies ran while one was open for 20% -> 16% of each run, Pallas kernels for 41% -> 33%
where the time goes in v4:
time: 110 us; the launch traced here: 109 us
  Pallas kernels  35.7 us (32%)
  starting transfers between devices  30.2 us (27%)
  waiting for transfers between devices  22.7 us (21%)
  matrix products  9.01 us (8%)
  other arithmetic  7.22 us (7%)
  local copies, waits for them, and re-layouts  3.19 us (3%)
    ppermute x27, starting transfers between devices, swap(): return lax.ppermute(array, axis, [(i, i ^ mask) for i in range(count)])  30.2 us
    ppermute x27, waiting for transfers between devices, swap(): return lax.ppermute(array, axis, [(i, i ^ mask) for i in range(count)])  22.7 us
    pallas_call x2, Pallas kernels, project_tokens(): pl.pallas_call(functools.partial(token_kernel, code_list([(base, chunk.sh...  16.2 us
    pallas_call x2, Pallas kernels, gradient_chunks(): pl.pallas_call(functools.partial(gradient_kernel, code_list([(base, rows)...  13.9 us
    pallas_call x3, Pallas kernels, add_arrived(): pl.pallas_call(functools.partial(add_kernel, [[len(arrived) for arrived i...  4.39 us
    dot_general x1, matrix products, attend_cached(): jnp.einsum('bhgd,bphd->bhgp', query_heads, key_heads, preferred_element_t...  3.53 us
    dot_general x1, matrix products, per_device(): jnp.dot(hidden_rows, key_matrix, preferred_element_type=jnp.float32)  3.04 us
    slice x1, local copies, waits for them, and re-layouts, per_device(): flattened_down[p * part_rows:(p + 1) * part_rows]  2.33 us
  transfers between devices with their start and end apart: 27, of which 9 were waited for; matrix products, arithmetic and copies ran while one was open for 16% of the time, Pallas kernels for 33%

profile of v4, /device:TPU:0, one launch (start us, length us, event | category | flops | bytes accessed | tf_op | source)
XLA Modules:
  0.0 109.1 jit_solution(15053264362576543188)
XLA Ops:
  3.1 2.3 %fusion.20 = (bf16[8,16,2048]{2,1,0:T(8,128)(2,1)}, bf16[8,16,2048]{2,1,0:T(8,128)(2,1)}) fusion(bf16[16,16,2048]{2,1,0:T(8,128)(2,1)} %param.22), kind=kLoop, calls=%fused_computation.44 | loop fusion | bytes 2097152 | tf_op jit(solution)/shard_map/slice | solution.py:373
  5.4 2.7 %collective-permute-start.1 = (bf16[256,256]{1,0:T(8,128)(2,1)}, bf16[256,256]{1,0:T(8,128)(2,1)S(1)}, u32[]{:S(2)}, u32[]{:S(2)}) collective-permute-start(bf16[256,256]{1,0:T(8,128)(2,1)} %bitcast.50), channel_id=1, source_target_pairs={{0,16},{4,20},{8,24},{12,28},{16,0},{20,4},{24,8},{28,12},{1,17},{... | collective-permute-start | bytes 393224 | tf_op jit(solution)/shard_map/ppermute | solution.py:23
  8.1 1.5 %collective-permute-start = (bf16[256,256]{1,0:T(8,128)(2,1)}, bf16[256,256]{1,0:T(8,128)(2,1)S(1)}, u32[]{:S(2)}, u32[]{:S(2)}) collective-permute-start(bf16[256,256]{1,0:T(8,128)(2,1)} %bitcast.51), channel_id=1, source_target_pairs={{0,8},{4,12},{8,0},{12,4},{16,24},{20,28},{24,16},{28,20},{1,9},{5... | collective-permute-start | bytes 393224 | tf_op jit(solution)/shard_map/ppermute | solution.py:23
  13.7 3.0 %collective-permute-start.12 = (bf16[256,256]{1,0:T(8,128)(2,1)}, bf16[256,256]{1,0:T(8,128)(2,1)}, u32[]{:S(2)}, u32[]{:S(2)}) collective-permute-start(bf16[256,256]{1,0:T(8,128)(2,1)} %bitcast.52), channel_id=1, source_target_pairs={{0,24},{4,28},{8,16},{12,20},{16,8},{20,12},{24,0},{28,4},{1,25},{... | collective-permute-start | bytes 393224 | tf_op jit(solution)/shard_map/ppermute | solution.py:23
  16.7 3.0 %convolution_convert_fusion = bf16[32,256]{1,0:T(8,128)(2,1)S(1)} fusion(bf16[32,8192]{1,0:T(8,128)(2,1)S(1)} %copy-done, bf16[8192,256]{1,0:T(8,128)(2,1)} %param.20), kind=kOutput, calls=%fused_computation.8 | convolution fusion | flops 134225920 | bytes 4734976 | tf_op jit(solution)/shard_map/dot_general | solution.py:416
  19.8 3.5 %fusion.22 = (f32[32,2,8]{2,1,0:T(2,128)S(1)}, f32[32,2,8,256]{3,2,1,0:T(8,128)S(1)}) fusion(bf16[32,2,8,128]{3,2,1,0:T(8,128)(2,1)S(1)} %bitcast.58, pred[32,256]{1,0:T(8,128)(4,1)S(1)} %iota_compare_fusion, bf16[32,256,256]{2,1,0:T(8,128)(2,1)} %param.16), kind=kOutput, calls=%fused_computation.46 | convolution fusion | flops 33947136 | bytes 4859904 | tf_op jit(solution)/shard_map/bhgd,bphd->bhgp/dot_general | solution.py:309
  23.9 1.4 %collective-permute-start.8 = (bf16[128,2048]{1,0:T(8,128)(2,1)S(1)}, bf16[128,2048]{1,0:T(8,128)(2,1)S(1)}, u32[]{:S(2)}, u32[]{:S(2)}) collective-permute-start(bf16[128,2048]{1,0:T(8,128)(2,1)S(1)} %collective-permute-done.7.refs_5_.refs_6_), channel_id=1, source_target_pairs={{0,8},{4,12},{8,0},{12,4},{16,24},{20,28},{24,16},{28,20},{1,9},{5... | collective-permute-start | bytes 1572872 | tf_op jit(solution)/shard_map/ppermute | solution.py:23
  25.9 1.5 %collective-permute-start.10 = (bf16[128,2048]{1,0:T(8,128)(2,1)S(1)}, bf16[128,2048]{1,0:T(8,128)(2,1)S(1)}, u32[]{:S(2)}, u32[]{:S(2)}) collective-permute-start(bf16[128,2048]{1,0:T(8,128)(2,1)S(1)} %collective-permute-done.6.refs_4_.refs_3_), channel_id=1, source_target_pairs={{0,16},{4,20},{8,24},{12,28},{16,0},{20,4},{24,8},{28,12},{1,17},{... | collective-permute-start | bytes 1572872 | tf_op jit(solution)/shard_map/ppermute | solution.py:23
  28.2 2.7 %shard_map.165 = f32[16,2048]{1,0:T(8,128)S(1)} custom-call(s32[1,2560]{1,0:T(1,128)S(1)} %copy-done.11, bf16[1024,256]{1,0:T(8,128)(2,1)S(1)} %copy-done.3, bf16[1024,256]{1,0:T(8,128)(2,1)S(1)} %collective-permute-done.4.mate_ref, bf16[256,256]{1,0:T(8,128)(2,1)S(1)} %bitcast.53, bf16[256,256]{1,0:T(8,128)(2,1)S(1)} %collective-permute-done.refs_1_, ...), custom_call_target="tpu_custom_call" | custom-call | flops 1 | bytes 1 | tf_op jit(solution)/shard_map/pallas_call | solution.py:129
  30.9 2.1 %collective-permute-start.13 = (f32[16,2048]{1,0:T(8,128)S(1)}, f32[16,2048]{1,0:T(8,128)S(1)}, u32[]{:S(2)}, u32[]{:S(2)}) collective-permute-start(f32[16,2048]{1,0:T(8,128)S(1)} %shard_map.165), channel_id=1, source_target_pairs={{0,1},{1,0},{2,3},{3,2},{4,5},{5,4},{6,7},{7,6},{8,9},{9,8},{10,11... | collective-permute-start | bytes 393224 | tf_op jit(solution)/shard_map/ppermute | solution.py:23
  33.0 1.4 %fusion = f32[32,2,8,128]{3,2,1,0:T(8,128)} fusion(f32[32,2,8,256]{3,2,1,0:T(8,128)S(1)} %get-tuple-element.74, f32[32,2,8]{2,1,0:T(2,128)S(1)} %get-tuple-element.70, f32[32,2,8]{2,1,0:T(2,128)S(1)} %multiply_maximum_fusion, bf16[32,256,256]{2,1,0:T(8,128)(2,1)S(1)} %copy-done.20), kind=kOutput, calls=%fused_computation | convolution fusion | flops 33947648 | bytes 4984832 | tf_op jit(solution)/shard_map/bhgp,bphd->bhgd/dot_general | solution.py:329
  34.4 4.6 %collective-permute-done.8.refs_8_ = bf16[128,2048]{1,0:T(8,128)(2,1)S(1)} collective-permute-done((bf16[128,2048]{1,0:T(8,128)(2,1)S(1)}, bf16[128,2048]{1,0:T(8,128)(2,1)S(1)}, u32[]{:S(2)}, u32[]{:S(2)}) %collective-permute-start.8) | collective-permute-done | bytes 524320 | tf_op jit(solution)/shard_map/ppermute | solution.py:23
  39.0 1.5 %collective-permute-start.9 = (bf16[128,2048]{1,0:T(8,128)(2,1)}, bf16[128,2048]{1,0:T(8,128)(2,1)S(1)}, u32[]{:S(2)}, u32[]{:S(2)}) collective-permute-start(bf16[128,2048]{1,0:T(8,128)(2,1)} %bitcast.2), channel_id=1, source_target_pairs={{0,8},{4,12},{8,0},{12,4},{16,24},{20,28},{24,16},{28,20},{1,9},{5... | collective-permute-start | bytes 1572872 | tf_op jit(solution)/shard_map/ppermute | solution.py:23
  40.6 2.7 %collective-permute-start.14 = (f32[16,2048]{1,0:T(8,128)S(1)}, f32[16,2048]{1,0:T(8,128)S(1)}, u32[]{:S(2)}, u32[]{:S(2)}) collective-permute-start(f32[16,2048]{1,0:T(8,128)S(1)} %add.106), channel_id=1, source_target_pairs={{0,2},{1,3},{2,0},{3,1},{4,6},{5,7},{6,4},{7,5},{8,10},{9,11},{10,... | collective-permute-start | bytes 393224 | tf_op jit(solution)/shard_map/ppermute | solution.py:23
  44.6 4.0 %collective-permute-done.14 = f32[16,2048]{1,0:T(8,128)S(1)} collective-permute-done((f32[16,2048]{1,0:T(8,128)S(1)}, f32[16,2048]{1,0:T(8,128)S(1)}, u32[]{:S(2)}, u32[]{:S(2)}) %collective-permute-start.14) | collective-permute-done | bytes 131104 | tf_op jit(solution)/shard_map/ppermute | solution.py:23
  48.7 12.6 %shard_map.166 = (f32[256,2048]{1,0:T(8,128)}, bf16[128,2048]{1,0:T(8,128)(2,1)S(1)}, bf16[128,2048]{1,0:T(8,128)(2,1)S(1)}, bf16[128,2048]{1,0:T(8,128)(2,1)S(1...) custom-call(s32[1,2048]{1,0:T(1,128)S(1)} %fusion.16.codes_ref, ...), custom_call_target="tpu_custom_call" | custom-call | flops 1 | bytes 1 | tf_op jit(solution)/shard_map/pallas_call | solution.py:227
  63.9 1.6 %collective-permute-start.19 = (bf16[128,2048]{1,0:T(8,128)(2,1)S(1)}, bf16[128,2048]{1,0:T(8,128)(2,1)S(1)}, u32[]{:S(2)}, u32[]{:S(2)}) collective-permute-start(bf16[128,2048]{1,0:T(8,128)(2,1)S(1)} %get-tuple-element.53), channel_id=1, source_target_pairs={{0,16},{4,20},{8,24},{12,28},{16,0},{20,4},{24,8},{28,12},{1,17},{... | collective-permute-start | bytes 1572872 | tf_op jit(solution)/shard_map/ppermute | solution.py:23
  65.4 1.4 %collective-permute-start.20 = (bf16[128,2048]{1,0:T(8,128)(2,1)S(1)}, bf16[128,2048]{1,0:T(8,128)(2,1)S(1)}, u32[]{:S(2)}, u32[]{:S(2)}) collective-permute-start(bf16[128,2048]{1,0:T(8,128)(2,1)S(1)} %get-tuple-element.54), channel_id=1, source_target_pairs={{0,8},{4,12},{8,0},{12,4},{16,24},{20,28},{24,16},{28,20},{1,9},{5... | collective-permute-start | bytes 1572872 | tf_op jit(solution)/shard_map/ppermute | solution.py:23
  66.8 13.5 %shard_map.167.refs_4_ = f32[16,2560]{1,0:T(8,128)S(1)} custom-call(s32[1,2560]{1,0:T(1,128)S(1)} %copy-done.11, bf16[1024,2048]{1,0:T(8,128)(2,1)} %own_ref.6, bf16[1024,2048]{1,0:T(8,128)(2,1)} %collective-permute-done.3.refs_6_.mate_ref, bf16[32,2048]{1,0:T(8,128)(2,1)S(1)} %constant_dynamic-slice_fusion.refs_0_, ...), custom_call_target="tpu_custom_call" | custom-call | flops 1 | bytes 1 | tf_op jit(solution)/shard_map/pallas_call | solution.py:129
  83.6 2.5 %collective-permute-done.15 = f32[16,2560]{1,0:T(8,128)S(1)} collective-permute-done((f32[16,2560]{1,0:T(8,128)S(1)}, f32[16,2560]{1,0:T(8,128)S(1)}, u32[]{:S(2)}, u32[]{:S(2)}) %collective-permute-start.15) | collective-permute-done | bytes 163872 | tf_op jit(solution)/shard_map/ppermute | solution.py:23
  86.1 2.4 %collective-permute-start.18 = (f32[16,2560]{1,0:T(8,128)S(1)}, f32[16,2560]{1,0:T(8,128)S(1)}, u32[]{:S(2)}, u32[]{:S(2)}) collective-permute-start(f32[16,2560]{1,0:T(8,128)S(1)} %add.108), channel_id=1, source_target_pairs={{0,2},{1,3},{2,0},{3,1},{4,6},{5,7},{6,4},{7,5},{8,10},{9,11},{10,... | collective-permute-start | bytes 491528 | tf_op jit(solution)/shard_map/ppermute | solution.py:23
  89.1 6.3 %collective-permute-done.18 = f32[16,2560]{1,0:T(8,128)S(1)} collective-permute-done((f32[16,2560]{1,0:T(8,128)S(1)}, f32[16,2560]{1,0:T(8,128)S(1)}, u32[]{:S(2)}, u32[]{:S(2)}) %collective-permute-start.18) | collective-permute-done | bytes 163872 | tf_op jit(solution)/shard_map/ppermute | solution.py:23
  100.1 1.5 %collective-permute-start.25 = (bf16[256,256]{1,0:T(8,128)(2,1)}, bf16[256,256]{1,0:T(8,128)(2,1)S(1)}, u32[]{:S(2)}, u32[]{:S(2)}) collective-permute-start(bf16[256,256]{1,0:T(8,128)(2,1)} %copy-done.15), channel_id=1, source_target_pairs={{0,16},{4,20},{8,24},{12,28},{16,0},{20,4},{24,8},{28,12},{1,17},{... | collective-permute-start | bytes 393224 | tf_op jit(solution)/shard_map/ppermute | solution.py:23
  104.7 2.5 %shard_map.172 = f32[256,2048]{1,0:T(8,128)} custom-call(f32[256,2048]{1,0:T(8,128)S(1)} %shard_map.169.refs_0_, bf16[128,2048]{1,0:T(8,128)(2,1)} %collective-permute-done.22.refs_1_, bf16[128,2048]{1,0:T(8,128)(2,1)} %collective-permute-done.23.refs_2_), custom_call_target="tpu_custom_call" | custom-call | flops 1 | bytes 1 | tf_op jit(solution)/shard_map/pallas_call | solution.py:273
  (109 shorter events, 26.1 us)
Async XLA Ops:
  2.7 25.4 %collective-permute-start.3 = (bf16[1024,2048]{1,0:T(8,128)(2,1)}, bf16[1024,2048]{1,0:T(8,128)(2,1)}, u32[]{:S(2)}, u32[]{:S(2)}) collective-permute-start(bf16[1024,2048]{1,0:T(8,128)(2,1)} %own_ref.6), channel_id=1, source_target_pairs={{0,4},{4,0},{8,12},{12,8},{16,20},{20,16},{24,28},{28,24},{1,5},{5... | collective-permute-start | bytes 12582920 | tf_op jit(solution)/shard_map/ppermute | solution.py:23
  5.4 8.3 %collective-permute-start.1 = (bf16[256,256]{1,0:T(8,128)(2,1)}, bf16[256,256]{1,0:T(8,128)(2,1)S(1)}, u32[]{:S(2)}, u32[]{:S(2)}) collective-permute-start(bf16[256,256]{1,0:T(8,128)(2,1)} %bitcast.50), channel_id=1, source_target_pairs={{0,16},{4,20},{8,24},{12,28},{16,0},{20,4},{24,8},{28,12},{1,17},{... | collective-permute-start | bytes 393224 | tf_op jit(solution)/shard_map/ppermute | solution.py:23
  8.1 8.5 %collective-permute-start = (bf16[256,256]{1,0:T(8,128)(2,1)}, bf16[256,256]{1,0:T(8,128)(2,1)S(1)}, u32[]{:S(2)}, u32[]{:S(2)}) collective-permute-start(bf16[256,256]{1,0:T(8,128)(2,1)} %bitcast.51), channel_id=1, source_target_pairs={{0,8},{4,12},{8,0},{12,4},{16,24},{20,28},{24,16},{28,20},{1,9},{5... | collective-permute-start | bytes 393224 | tf_op jit(solution)/shard_map/ppermute | solution.py:23
  9.6 14.3 %collective-permute-start.7 = (bf16[128,2048]{1,0:T(8,128)(2,1)}, bf16[128,2048]{1,0:T(8,128)(2,1)S(1)}, u32[]{:S(2)}, u32[]{:S(2)}) collective-permute-start(bf16[128,2048]{1,0:T(8,128)(2,1)} %bitcast.2), channel_id=1, source_target_pairs={{0,16},{4,20},{8,24},{12,28},{16,0},{20,4},{24,8},{28,12},{1,17},{... | collective-permute-start | bytes 1572872 | tf_op jit(solution)/shard_map/ppermute | solution.py:23
  10.1 15.8 %collective-permute-start.6 = (bf16[128,2048]{1,0:T(8,128)(2,1)}, bf16[128,2048]{1,0:T(8,128)(2,1)S(1)}, u32[]{:S(2)}, u32[]{:S(2)}) collective-permute-start(bf16[128,2048]{1,0:T(8,128)(2,1)} %bitcast.1), channel_id=1, source_target_pairs={{0,8},{4,12},{8,0},{12,4},{16,24},{20,28},{24,16},{28,20},{1,9},{5... | collective-permute-start | bytes 1572872 | tf_op jit(solution)/shard_map/ppermute | solution.py:23
  13.7 14.5 %collective-permute-start.12 = (bf16[256,256]{1,0:T(8,128)(2,1)}, bf16[256,256]{1,0:T(8,128)(2,1)}, u32[]{:S(2)}, u32[]{:S(2)}) collective-permute-start(bf16[256,256]{1,0:T(8,128)(2,1)} %bitcast.52), channel_id=1, source_target_pairs={{0,24},{4,28},{8,16},{12,20},{16,8},{20,12},{24,0},{28,4},{1,25},{... | collective-permute-start | bytes 393224 | tf_op jit(solution)/shard_map/ppermute | solution.py:23
  16.6 11.5 %collective-permute-start.4 = (bf16[1024,256]{1,0:T(8,128)(2,1)}, bf16[1024,256]{1,0:T(8,128)(2,1)S(1)}, u32[]{:S(2)}, u32[]{:S(2)}) collective-permute-start(bf16[1024,256]{1,0:T(8,128)(2,1)} %own_ref.7), channel_id=1, source_target_pairs={{0,4},{4,0},{8,12},{12,8},{16,20},{20,16},{24,28},{28,24},{1,5},{5... | collective-permute-start | bytes 1572872 | tf_op jit(solution)/shard_map/ppermute | solution.py:23
  23.9 15.2 %collective-permute-start.8 = (bf16[128,2048]{1,0:T(8,128)(2,1)S(1)}, bf16[128,2048]{1,0:T(8,128)(2,1)S(1)}, u32[]{:S(2)}, u32[]{:S(2)}) collective-permute-start(bf16[128,2048]{1,0:T(8,128)(2,1)S(1)} %collective-permute-done.7.refs_5_.refs_6_), channel_id=1, source_target_pairs={{0,8},{4,12},{8,0},{12,4},{16,24},{20,28},{24,16},{28,20},{1,9},{5... | collective-permute-start | bytes 1572872 | tf_op jit(solution)/shard_map/ppermute | solution.py:23
  25.9 18.1 %collective-permute-start.10 = (bf16[128,2048]{1,0:T(8,128)(2,1)S(1)}, bf16[128,2048]{1,0:T(8,128)(2,1)S(1)}, u32[]{:S(2)}, u32[]{:S(2)}) collective-permute-start(bf16[128,2048]{1,0:T(8,128)(2,1)S(1)} %collective-permute-done.6.refs_4_.refs_3_), channel_id=1, source_target_pairs={{0,16},{4,20},{8,24},{12,28},{16,0},{20,4},{24,8},{28,12},{1,17},{... | collective-permute-start | bytes 1572872 | tf_op jit(solution)/shard_map/ppermute | solution.py:23
  30.9 9.6 %collective-permute-start.13 = (f32[16,2048]{1,0:T(8,128)S(1)}, f32[16,2048]{1,0:T(8,128)S(1)}, u32[]{:S(2)}, u32[]{:S(2)}) collective-permute-start(f32[16,2048]{1,0:T(8,128)S(1)} %shard_map.165), channel_id=1, source_target_pairs={{0,1},{1,0},{2,3},{3,2},{4,5},{5,4},{6,7},{7,6},{8,9},{9,8},{10,11... | collective-permute-start | bytes 393224 | tf_op jit(solution)/shard_map/ppermute | solution.py:23
  39.0 26.4 %collective-permute-start.9 = (bf16[128,2048]{1,0:T(8,128)(2,1)}, bf16[128,2048]{1,0:T(8,128)(2,1)S(1)}, u32[]{:S(2)}, u32[]{:S(2)}) collective-permute-start(bf16[128,2048]{1,0:T(8,128)(2,1)} %bitcast.2), channel_id=1, source_target_pairs={{0,8},{4,12},{8,0},{12,4},{16,24},{20,28},{24,16},{28,20},{1,9},{5... | collective-permute-start | bytes 1572872 | tf_op jit(solution)/shard_map/ppermute | solution.py:23
  40.6 8.1 %collective-permute-start.14 = (f32[16,2048]{1,0:T(8,128)S(1)}, f32[16,2048]{1,0:T(8,128)S(1)}, u32[]{:S(2)}, u32[]{:S(2)}) collective-permute-start(f32[16,2048]{1,0:T(8,128)S(1)} %add.106), channel_id=1, source_target_pairs={{0,2},{1,3},{2,0},{3,1},{4,6},{5,7},{6,4},{7,5},{8,10},{9,11},{10,... | collective-permute-start | bytes 393224 | tf_op jit(solution)/shard_map/ppermute | solution.py:23
  44.1 22.7 %collective-permute-start.11 = (bf16[128,2048]{1,0:T(8,128)(2,1)}, bf16[128,2048]{1,0:T(8,128)(2,1)S(1)}, u32[]{:S(2)}, u32[]{:S(2)}) collective-permute-start(bf16[128,2048]{1,0:T(8,128)(2,1)} %bitcast.1), channel_id=1, source_target_pairs={{0,16},{4,20},{8,24},{12,28},{16,0},{20,4},{24,8},{28,12},{1,17},{... | collective-permute-start | bytes 1572872 | tf_op jit(solution)/shard_map/ppermute | solution.py:23
  61.3 19.7 %collective-permute-start.16 = (bf16[128,2048]{1,0:T(8,128)(2,1)S(1)}, bf16[128,2048]{1,0:T(8,128)(2,1)S(1)}, u32[]{:S(2)}, u32[]{:S(2)}) collective-permute-start(bf16[128,2048]{1,0:T(8,128)(2,1)S(1)} %get-tuple-element.49), channel_id=1, source_target_pairs={{0,16},{4,20},{8,24},{12,28},{16,0},{20,4},{24,8},{28,12},{1,17},{... | collective-permute-start | bytes 1572872 | tf_op jit(solution)/shard_map/ppermute | solution.py:23
  61.8 19.2 %collective-permute-start.17 = (bf16[128,2048]{1,0:T(8,128)(2,1)S(1)}, bf16[128,2048]{1,0:T(8,128)(2,1)S(1)}, u32[]{:S(2)}, u32[]{:S(2)}) collective-permute-start(bf16[128,2048]{1,0:T(8,128)(2,1)S(1)} %get-tuple-element.50), channel_id=1, source_target_pairs={{0,8},{4,12},{8,0},{12,4},{16,24},{20,28},{24,16},{28,20},{1,9},{5... | collective-permute-start | bytes 1572872 | tf_op jit(solution)/shard_map/ppermute | solution.py:23
  63.9 24.6 %collective-permute-start.19 = (bf16[128,2048]{1,0:T(8,128)(2,1)S(1)}, bf16[128,2048]{1,0:T(8,128)(2,1)S(1)}, u32[]{:S(2)}, u32[]{:S(2)}) collective-permute-start(bf16[128,2048]{1,0:T(8,128)(2,1)S(1)} %get-tuple-element.53), channel_id=1, source_target_pairs={{0,16},{4,20},{8,24},{12,28},{16,0},{20,4},{24,8},{28,12},{1,17},{... | collective-permute-start | bytes 1572872 | tf_op jit(solution)/shard_map/ppermute | solution.py:23
  65.4 23.0 %collective-permute-start.20 = (bf16[128,2048]{1,0:T(8,128)(2,1)S(1)}, bf16[128,2048]{1,0:T(8,128)(2,1)S(1)}, u32[]{:S(2)}, u32[]{:S(2)}) collective-permute-start(bf16[128,2048]{1,0:T(8,128)(2,1)S(1)} %get-tuple-element.54), channel_id=1, source_target_pairs={{0,8},{4,12},{8,0},{12,4},{16,24},{20,28},{24,16},{28,20},{1,9},{5... | collective-permute-start | bytes 1572872 | tf_op jit(solution)/shard_map/ppermute | solution.py:23
  80.3 5.8 %collective-permute-start.15 = (f32[16,2560]{1,0:T(8,128)S(1)}, f32[16,2560]{1,0:T(8,128)S(1)}, u32[]{:S(2)}, u32[]{:S(2)}) collective-permute-start(f32[16,2560]{1,0:T(8,128)S(1)} %shard_map.167.refs_4_), channel_id=1, source_target_pairs={{0,1},{1,0},{2,3},{3,2},{4,5},{5,4},{6,7},{7,6},{8,9},{9,8},{10,11... | collective-permute-start | bytes 491528 | tf_op jit(solution)/shard_map/ppermute | solution.py:23
  82.4 17.0 %collective-permute-start.23 = (bf16[128,2048]{1,0:T(8,128)(2,1)}, bf16[128,2048]{1,0:T(8,128)(2,1)}, u32[]{:S(2)}, u32[]{:S(2)}) collective-permute-start(bf16[128,2048]{1,0:T(8,128)(2,1)} %get-tuple-element.59), channel_id=1, source_target_pairs={{0,16},{4,20},{8,24},{12,28},{16,0},{20,4},{24,8},{28,12},{1,17},{... | collective-permute-start | bytes 1572872 | tf_op jit(solution)/shard_map/ppermute | solution.py:23
  82.9 16.4 %collective-permute-start.22 = (bf16[128,2048]{1,0:T(8,128)(2,1)}, bf16[128,2048]{1,0:T(8,128)(2,1)}, u32[]{:S(2)}, u32[]{:S(2)}) collective-permute-start(bf16[128,2048]{1,0:T(8,128)(2,1)} %get-tuple-element.51.refs_3_), channel_id=1, source_target_pairs={{0,8},{4,12},{8,0},{12,4},{16,24},{20,28},{24,16},{28,20},{1,9},{5... | collective-permute-start | bytes 1572872 | tf_op jit(solution)/shard_map/ppermute | solution.py:23
  86.1 9.3 %collective-permute-start.18 = (f32[16,2560]{1,0:T(8,128)S(1)}, f32[16,2560]{1,0:T(8,128)S(1)}, u32[]{:S(2)}, u32[]{:S(2)}) collective-permute-start(f32[16,2560]{1,0:T(8,128)S(1)} %add.108), channel_id=1, source_target_pairs={{0,2},{1,3},{2,0},{3,1},{4,6},{5,7},{6,4},{7,5},{8,10},{9,11},{10,... | collective-permute-start | bytes 491528 | tf_op jit(solution)/shard_map/ppermute | solution.py:23
  99.4 7.8 %collective-permute-start.26 = (bf16[256,256]{1,0:T(8,128)(2,1)}, bf16[256,256]{1,0:T(8,128)(2,1)S(1)}, u32[]{:S(2)}, u32[]{:S(2)}) collective-permute-start(bf16[256,256]{1,0:T(8,128)(2,1)} %copy-done.16), channel_id=1, source_target_pairs={{0,24},{4,28},{8,16},{12,20},{16,8},{20,12},{24,0},{28,4},{1,25},{... | collective-permute-start | bytes 393224 | tf_op jit(solution)/shard_map/ppermute | solution.py:23
  100.1 8.3 %collective-permute-start.25 = (bf16[256,256]{1,0:T(8,128)(2,1)}, bf16[256,256]{1,0:T(8,128)(2,1)S(1)}, u32[]{:S(2)}, u32[]{:S(2)}) collective-permute-start(bf16[256,256]{1,0:T(8,128)(2,1)} %copy-done.15), channel_id=1, source_target_pairs={{0,16},{4,20},{8,24},{12,28},{16,0},{20,4},{24,8},{28,12},{1,17},{... | collective-permute-start | bytes 393224 | tf_op jit(solution)/shard_map/ppermute | solution.py:23
  101.5 6.8 %collective-permute-start.24 = (bf16[256,256]{1,0:T(8,128)(2,1)}, bf16[256,256]{1,0:T(8,128)(2,1)S(1)}, u32[]{:S(2)}, u32[]{:S(2)}) collective-permute-start(bf16[256,256]{1,0:T(8,128)(2,1)} %copy-done.14), channel_id=1, source_target_pairs={{0,8},{4,12},{8,0},{12,4},{16,24},{20,28},{24,16},{28,20},{1,9},{5... | collective-permute-start | bytes 393224 | tf_op jit(solution)/shard_map/ppermute | solution.py:23
  (24 other events, 220.3 us)

commit v5 on v4

v5 whole, which is shorter than its diff:
```python
import functools
import math

import jax
import jax.numpy as jnp
from jax import lax
from jax.experimental import pallas as pl
from jax.experimental.pallas import tpu as pltpu
from jax.sharding import PartitionSpec as P

HEAD_SIZE = 128

ADAPTER_SCALE = 2.0
NEG_FILL = -1e30
VMEM_LIMIT = 48 * 1024 * 1024
SHORT = pl.CostEstimate(flops=1, bytes_accessed=1, transcendentals=0)


def swap(array, axis, mask):
    count = lax.axis_size(axis)
    return lax.ppermute(array, axis, [(i, i ^ mask) for i in range(count)])


def axis_bits(axis):
    count = lax.axis_size(axis)
    assert count & (count - 1) == 0, "axis size"
    return [1 << k for k in range(count.bit_length() - 1)]


def highest_in(order, mask):
    return [bit for bit in order if bit & mask][-1]


def largest_tile(length, limit):
    tile = length
    while tile > limit and tile % 2 == 0:
        tile //= 2
    return tile


def code_list(chunks, rank):
    return [
        base + j
        for bases, rows in chunks
        for base in bases
        for j in range(rows // rank // len(bases))
    ]


def pick(codes, products, row_codes, rank):
    total = jnp.zeros((rank, products.shape[1]), jnp.float32)
    for k, code in enumerate(row_codes):
        total += jnp.where(codes == code, products[k * rank : (k + 1) * rank], 0.0)
    return total


def spread(codes, values, row_codes, out_ref):
    rank = values.shape[0]
    for k, code in enumerate(row_codes):
        out_ref[k * rank : (k + 1) * rank, :] = jnp.where(codes == code, values, 0.0).astype(
            out_ref.dtype
        )


def join(maps, joined_ref):
    first = 0
    for chunk in maps:
        joined_ref[first : first + chunk.shape[0], :] = chunk[...]
        first += chunk.shape[0]


def times_transposed(maps, tokens):
    return lax.dot_general(
        maps, tokens, (((1,), (1,)), ((), ())), preferred_element_type=jnp.float32
    )


def token_kernel(map_codes, rank, tiles, source_count, has_rows, map_count, codes_ref, *refs):
    refs = list(refs)
    sources = [refs.pop(0) for _ in range(source_count)]
    row_refs = [refs.pop(0) for _ in range(2 * has_rows)]
    maps = refs[:map_count]
    out_ref, sent_ref, joined_ref, *rest = refs[-3 - has_rows :]
    step = pl.program_id(0)

    @pl.when(step == 0)
    def _():
        join(maps, joined_ref)

    def project(tokens):
        products = times_transposed(joined_ref[...], tokens)
        return pick(codes_ref[:, : tokens.shape[0]], products, map_codes, rank)

    def store(total):
        out_ref[...] = total
        sent_ref[...] = total.astype(sent_ref.dtype)

    for k, source_ref in enumerate(sources):
        pl.when(step // tiles == k)(lambda ref=source_ref: store(project(ref[...])))
    if has_rows:
        rows_ref = rest[0]

        @pl.when(step == source_count * tiles)
        def _():
            rows_ref[...] = jnp.zeros_like(rows_ref)
            join(row_refs, rows_ref)
            total = project(rows_ref[...])
            rest_shape = (total.shape[0], out_ref.shape[1] - total.shape[1])
            store(jnp.concatenate([total, jnp.zeros(rest_shape, jnp.float32)], axis=1))


def token_tile(token_count, width=0):
    return largest_tile(token_count, 512 if width > 512 else 1024)


def project_tokens(codes, sources, chunks, rank, rows=(), after=(), cost=SHORT):
    token_count, width = sources[0].shape
    tile = token_tile(token_count, width)
    tiles = token_count // tile
    map_rows = sum(chunk.shape[0] for _, chunk in chunks)
    scratch = [pltpu.VMEM((map_rows, width), jnp.bfloat16)]
    if rows:
        padded = -(-2 * rows[0].shape[0] // 128) * 128
        assert padded <= tile, "row count"
        scratch.append(pltpu.VMEM((padded, width), jnp.bfloat16))
    steps = len(sources) * tiles + bool(rows)
    across = lambda i: (0, i)
    whole = lambda i: (0, 0)
    operands = [codes, *sources, *rows, *[chunk for _, chunk in chunks], *after]
    return pl.pallas_call(
        functools.partial(
            token_kernel,
            code_list([(bases, chunk.shape[0]) for bases, chunk in chunks], rank),
            rank,
            tiles,
            len(sources),
            bool(rows),
            len(chunks),
        ),
        grid=(steps,),
        in_specs=[pl.BlockSpec((1, tile), across)]
        + [
            pl.BlockSpec((tile, width), lambda i, k=k: (jnp.clip(i - k * tiles, 0, tiles - 1), 0))
            for k in range(len(sources))
        ]
        + [pl.BlockSpec(a.shape, whole) for a in rows]
        + [pl.BlockSpec(chunk.shape, whole) for _, chunk in chunks]
        + [pl.BlockSpec(memory_space=pl.ANY) for _ in after],
        out_specs=[pl.BlockSpec((rank, tile), across)] * 2,
        out_shape=[
            jax.ShapeDtypeStruct((rank, steps * tile), dtype)
            for dtype in (jnp.float32, jnp.bfloat16)
        ],
        scratch_shapes=scratch,
        compiler_params=pltpu.CompilerParams(vmem_limit_bytes=VMEM_LIMIT),
        cost_estimate=cost,
    )(*operands)


def delta_kernel(chunk_codes, codes_ref, rank_ref, *refs):
    maps = refs[: len(chunk_codes)]
    own_ref, mate_ref, spread_ref = refs[-3:]
    count = codes_ref.shape[1]
    values = rank_ref[:, :count].astype(jnp.bfloat16).astype(jnp.float32)
    total = jnp.zeros((count, own_ref.shape[1]), jnp.float32)
    for map_codes, chunk in zip(chunk_codes, maps):
        spread(codes_ref[...], values, map_codes, spread_ref)
        total += lax.dot_general(
            spread_ref[...].T.astype(jnp.bfloat16),
            chunk[...],
            (((1,), (0,)), ((), ())),
            preferred_element_type=jnp.float32,
        )
    deltas = ADAPTER_SCALE * total
    own_ref[...] = deltas[: count // 2].astype(own_ref.dtype)
    mate_ref[...] = deltas[count // 2 :].astype(mate_ref.dtype)


def row_deltas(codes, ranks, first, width_of_ranks, chunks, after=()):
    rank = ranks.shape[0]
    row_count = codes.shape[1]
    chunk_rows, width = chunks[0][1].shape
    whole = lambda i: (0, 0)
    return pl.pallas_call(
        functools.partial(
            delta_kernel, [code_list([(bases, chunk_rows)], rank) for bases, _ in chunks]
        ),
        grid=(1,),
        in_specs=[
            pl.BlockSpec(codes.shape, whole),
            pl.BlockSpec((rank, width_of_ranks), lambda i: (0, first // width_of_ranks)),
        ]
        + [pl.BlockSpec((chunk_rows, width), whole) for _ in chunks]
        + [pl.BlockSpec(memory_space=pl.ANY) for _ in after],
        out_specs=[pl.BlockSpec((row_count // 2, width), whole)] * 2,
        out_shape=[jax.ShapeDtypeStruct((row_count // 2, width), jnp.bfloat16)] * 2,
        scratch_shapes=[pltpu.VMEM((chunk_rows, row_count), jnp.float32)],
        compiler_params=pltpu.CompilerParams(vmem_limit_bytes=VMEM_LIMIT),
    )(codes, ranks, *[chunk for _, chunk in chunks], *after)


def place_kernel(buffer_ref, piece_ref, *refs):
    refs[-1][...] = piece_ref[...]


def place(buffer, piece, k, after=()):
    return pl.pallas_call(
        place_kernel,
        grid=(1,),
        in_specs=[
            pl.BlockSpec(memory_space=pl.ANY),
            pl.BlockSpec(piece.shape, lambda i: (0, 0)),
        ]
        + [pl.BlockSpec(memory_space=pl.ANY) for _ in after],
        out_specs=pl.BlockSpec(piece.shape, lambda i: (k, 0)),
        out_shape=jax.ShapeDtypeStruct(buffer.shape, buffer.dtype),
        input_output_aliases={0: 0},
        compiler_params=pltpu.CompilerParams(vmem_limit_bytes=VMEM_LIMIT),
        cost_estimate=SHORT,
    )(buffer, piece, *after)


def finish_rows_kernel(cached_ref, weight_ref, base_ref, own_ref, mate_ref, attended_ref, fresh_ref):
    delta = own_ref[...].astype(jnp.float32) + mate_ref[...].astype(jnp.float32)
    fresh = (base_ref[...] + delta).astype(jnp.bfloat16)
    fresh_ref[...] = fresh
    heads = cached_ref.shape[1]
    group = heads * HEAD_SIZE // fresh.shape[1]
    for j in range(heads):
        value = slice(j // group * HEAD_SIZE, (j // group + 1) * HEAD_SIZE)
        attended = cached_ref[:, j, :] + weight_ref[:, j, :] * fresh[:, value].astype(jnp.float32)
        attended_ref[:, j * HEAD_SIZE : (j + 1) * HEAD_SIZE] = attended.astype(jnp.bfloat16)


def finish_rows(cached, own_weight, base_values, own_delta, mate_delta):
    row_count, heads, size = cached.shape
    return pl.pallas_call(
        finish_rows_kernel,
        out_shape=[
            jax.ShapeDtypeStruct((row_count, heads * size), jnp.bfloat16),
            jax.ShapeDtypeStruct(base_values.shape, jnp.bfloat16),
        ],
        compiler_params=pltpu.CompilerParams(vmem_limit_bytes=VMEM_LIMIT),
        cost_estimate=SHORT,
    )(cached, own_weight, base_values, own_delta, mate_delta)


def gradient_kernel(
    row_codes, arrived_counts, codes_ref, rewards_ref, factor_ref, own_ref, mate_ref, *refs
):
    arrived = list(refs[: sum(arrived_counts)])
    outs = refs[-1 - len(arrived_counts) : -1]
    spread_ref = refs[-1]
    token_count = own_ref.shape[0]

    @pl.when(pl.program_id(0) == 0)
    def _():
        scale = ADAPTER_SCALE * rewards_ref[...].astype(jnp.float32)
        scaled = (scale * factor_ref[...]).astype(jnp.bfloat16).astype(jnp.float32)
        spread(codes_ref[...], scaled, row_codes, spread_ref)

    total = jnp.dot(
        spread_ref[:, :token_count], own_ref[...], preferred_element_type=jnp.float32
    ) + jnp.dot(spread_ref[:, token_count:], mate_ref[...], preferred_element_type=jnp.float32)
    first = 0
    for out_ref, count in zip(outs, arrived_counts):
        rows = out_ref.shape[0]
        piece = total[first : first + rows]
        for _ in range(count):
            piece += arrived.pop(0)[...].astype(jnp.float32)
        out_ref[...] = piece.astype(out_ref.dtype)
        first += rows


def gradient_chunks(codes, rewards, factor, own, mate, chunks, after=(), cost=SHORT):
    rank = factor.shape[0]
    token_count, width = own.shape
    tile = largest_tile(width, 512)
    out_rows = [adapters * rank for _, adapters, _, _ in chunks]
    arrived = [(a, rows) for (_, _, _, arrays), rows in zip(chunks, out_rows) for a in arrays]
    whole = lambda i: (0, 0)
    across = lambda i: (0, i)
    return pl.pallas_call(
        functools.partial(
            gradient_kernel,
            code_list([(chunk[0], rows) for chunk, rows in zip(chunks, out_rows)], rank),
            [len(arrays) for _, _, _, arrays in chunks],
        ),
        grid=(width // tile,),
        in_specs=[
            pl.BlockSpec((1, 2 * token_count), whole),
            pl.BlockSpec(rewards.shape, whole),
            pl.BlockSpec((rank, 2 * token_count), whole),
            pl.BlockSpec((token_count, tile), across),
            pl.BlockSpec((token_count, tile), across),
        ]
        + [pl.BlockSpec((rows, tile), across) for _, rows in arrived]
        + [pl.BlockSpec(memory_space=pl.ANY) for _ in after],
        out_specs=[pl.BlockSpec((rows, tile), across) for rows in out_rows],
        out_shape=[
            jax.ShapeDtypeStruct((rows, width), dtype)
            for rows, (_, _, dtype, _) in zip(out_rows, chunks)
        ],
        scratch_shapes=[pltpu.VMEM((sum(out_rows), 2 * token_count), jnp.bfloat16)],
        compiler_params=pltpu.CompilerParams(vmem_limit_bytes=VMEM_LIMIT),
        cost_estimate=cost,
    )(codes, rewards, factor, own, mate, *[a for a, _ in arrived], *after)


def add_kernel(groups, *refs):
    starts, refs = refs[: len(groups)], refs[len(groups) :]
    outs = refs[len(refs) - len(groups) :]
    arrived = list(refs)
    for places, start_ref, out_ref in zip(groups, starts, outs):
        rows = out_ref.shape[0] // len(places)
        for p, firsts in enumerate(places):
            part = slice(p * rows, (p + 1) * rows)
            total = start_ref[part, :]
            for k in firsts:
                total += arrived.pop(0)[k * rows : (k + 1) * rows, :].astype(jnp.float32)
            out_ref[part, :] = total.astype(out_ref.dtype)


def add_arrived(groups, after=(), dtype=jnp.bfloat16):
    width = groups[0][0].shape[1]
    tile = largest_tile(width, 1024)
    arrays = [start for start, _ in groups]
    arrays += [a for _, parts in groups for arrived in parts for a, _ in arrived]
    across = lambda i: (0, i)
    return pl.pallas_call(
        functools.partial(
            add_kernel, [[[k for _, k in arrived] for arrived in parts] for _, parts in groups]
        ),
        grid=(width // tile,),
        in_specs=[pl.BlockSpec((a.shape[0], tile), across) for a in arrays]
        + [pl.BlockSpec(memory_space=pl.ANY) for _ in after],
        out_specs=[pl.BlockSpec((start.shape[0], tile), across) for start, _ in groups],
        out_shape=[jax.ShapeDtypeStruct(start.shape, dtype) for start, _ in groups],
        compiler_params=pltpu.CompilerParams(vmem_limit_bytes=VMEM_LIMIT),
        cost_estimate=SHORT,
    )(*arrays, *after)


def wait_for(array, *others):
    return lax.optimization_barrier((array, *others))[0]


def step_kernel(piece_ref, came_ref, *refs):
    out_ref, sent_ref = refs[-2:]
    total = piece_ref[...] + came_ref[...].astype(jnp.float32)
    out_ref[...] = total
    sent_ref[...] = total.astype(sent_ref.dtype)


def sum_over(axis, piece, sent, waits=()):
    for k, bit in enumerate(axis_bits(axis)):
        came = swap(sent, axis, bit)
        after = waits[k] if k < len(waits) else ()
        whole = pl.BlockSpec(piece.shape, lambda: (0, 0))
        piece, sent = pl.pallas_call(
            step_kernel,
            in_specs=[whole, whole] + [pl.BlockSpec(memory_space=pl.ANY) for _ in after],
            out_specs=[whole, whole],
            out_shape=[
                jax.ShapeDtypeStruct(piece.shape, dtype) for dtype in (jnp.float32, jnp.bfloat16)
            ],
            compiler_params=pltpu.CompilerParams(vmem_limit_bytes=VMEM_LIMIT),
            cost_estimate=SHORT,
        )(piece, came, *after)
    return piece


def attend_kernel(kv_local, lengths_ref, queries_ref, keys_ref, values_ref, fresh_ref, *refs):
    out_ref, own_ref = refs[-2:]
    block, heads, size = queries_ref.shape
    slots = keys_ref.shape[1]
    group = heads // kv_local
    first_row = pl.program_id(0) * block
    inverse = 1.0 / math.sqrt(size)
    head_of = lax.broadcasted_iota(jnp.int32, (heads, slots), 0) // group
    slot = lax.broadcasted_iota(jnp.int32, (heads, slots), 1)

    def by_head(pieces):
        chosen = pieces[0]
        for h, piece in enumerate(pieces[1:], 1):
            chosen = jnp.where(head_of[:, : piece.shape[1]] == h, piece, chosen)
        return chosen

    scores, own_scores = [], []
    for r in range(block):
        queries = queries_ref[r]
        products = by_head(
            [
                times_transposed(queries, keys_ref[r, :, h * size : (h + 1) * size])
                for h in range(kv_local)
            ]
        )
        scores.append(jnp.where(slot < lengths_ref[first_row + r], inverse * products, NEG_FILL))
        fresh = by_head(
            [
                jnp.broadcast_to(fresh_ref[r : r + 1, h * size : (h + 1) * size], (heads, size))
                for h in range(kv_local)
            ]
        )
        own_scores.append(queries.astype(jnp.float32) * fresh)
    scores = jnp.concatenate(scores)
    own_score = inverse * jnp.sum(jnp.concatenate(own_scores), axis=1, keepdims=True)
    highest = jnp.maximum(jnp.max(scores, axis=1, keepdims=True), own_score)
    cache_exp = jnp.exp(scores - highest)
    own_exp = jnp.exp(own_score - highest)
    denominator = jnp.sum(cache_exp, axis=1, keepdims=True) + own_exp
    weights = cache_exp / denominator
    own_weight = (own_exp / denominator).astype(jnp.bfloat16).astype(jnp.float32)
    for r in range(block):
        mine = slice(r * heads, (r + 1) * heads)
        row_weights = weights[mine].astype(jnp.bfloat16)
        out_ref[r] = by_head(
            [
                jnp.dot(
                    row_weights,
                    values_ref[r, :, h * size : (h + 1) * size],
                    preferred_element_type=jnp.float32,
                )
                for h in range(kv_local)
            ]
        )
        own_ref[r] = jnp.broadcast_to(own_weight[mine], (heads, size))


def attend_cached(queries, cached_key_rows, cached_value_rows, lengths, fresh_keys, after=()):
    row_count, slots, kv_width = cached_key_rows.shape
    heads = queries.shape[1] // HEAD_SIZE
    block = largest_tile(row_count, 8)
    rows_of = lambda i, *_: (i, 0, 0)
    head_spec = pl.BlockSpec((block, heads, HEAD_SIZE), rows_of)
    cache_spec = pl.BlockSpec((block, slots, kv_width), rows_of)
    shape = (row_count, heads, HEAD_SIZE)
    return pl.pallas_call(
        functools.partial(attend_kernel, kv_width // HEAD_SIZE),
        grid_spec=pltpu.PrefetchScalarGridSpec(
            num_scalar_prefetch=1,
            grid=(row_count // block,),
            in_specs=[
                head_spec,
                cache_spec,
                cache_spec,
                pl.BlockSpec((block, kv_width), lambda i, *_: (i, 0)),
            ]
            + [pl.BlockSpec(memory_space=pl.ANY) for _ in after],
            out_specs=[head_spec, head_spec],
        ),
        out_shape=[jax.ShapeDtypeStruct(shape, jnp.float32)] * 2,
        compiler_params=pltpu.CompilerParams(vmem_limit_bytes=VMEM_LIMIT),
        cost_estimate=SHORT,
    )(
        lengths,
        queries.reshape(shape),
        cached_key_rows,
        cached_value_rows,
        fresh_keys.astype(jnp.float32),
        *after,
    )


def per_device(
    decode_hidden_input,
    queries,
    cached_key_rows,
    cached_value_rows,
    lengths,
    decode_adapter_index,
    key_matrix,
    value_matrix,
    adapter_down_map,
    adapter_up_map,
    training_hidden_input,
    cotangent,
    training_adapter_index,
    rewards,
):
    core_bit, *chip_bits = axis_bits("wide")
    masks = [m for m in range(lax.axis_size("wide")) if not m & core_bit]
    me = lax.axis_index("wide")
    owner_totals, rank, down_width = adapter_down_map.shape
    up_width = adapter_up_map.shape[2]
    row_count = decode_hidden_input.shape[0]
    token_count = training_hidden_input.shape[0]
    parts = len(chip_bits) if owner_totals % len(chip_bits) == 0 else 1
    orders = [chip_bits[p:] + chip_bits[:p] for p in range(parts)]
    part_adapters = owner_totals // parts
    part_rows = part_adapters * rank

    flattened_down = adapter_down_map.reshape(-1, down_width)
    flattened_up = adapter_up_map.reshape(-1, up_width)

    far = [m for m in masks if m.bit_count() > 1]
    near = [m for m in masks if m.bit_count() == 1]

    numbers = jnp.concatenate([training_adapter_index, rewards, decode_adapter_index])
    mate_numbers = swap(numbers, "wide", core_bit)
    mate_cotangent = swap(wait_for(cotangent, mate_numbers), "wide", core_bit)
    up_maps = {0: flattened_up}
    own_parts = [flattened_down[p * part_rows : (p + 1) * part_rows] for p in range(parts)]
    for m in near:
        up_maps[m] = swap(wait_for(flattened_up, *own_parts), "wide", m)
    for m in far:
        up_maps[m] = swap(wait_for(flattened_up, mate_numbers), "wide", m)
    mate_hidden = swap(wait_for(training_hidden_input, mate_numbers), "wide", core_bit)
    decode_slice = lax.dynamic_slice_in_dim(
        decode_hidden_input, lax.axis_index("narrow") * down_width, down_width, 1
    )
    mate_slice = swap(wait_for(decode_slice, mate_cotangent), "wide", core_bit)

    def codes_of(ids):
        return (((ids // owner_totals) ^ me) * owner_totals + ids % owner_totals)[None, :]

    token_codes = codes_of(
        jnp.concatenate([training_adapter_index, mate_numbers[:token_count]])
    )
    token_rewards = jnp.concatenate([rewards, mate_numbers[token_count : 2 * token_count]])[
        None, :
    ]
    row_codes = codes_of(
        jnp.concatenate([decode_adapter_index, mate_numbers[2 * token_count :]])
    )
    tile = token_tile(token_count, down_width)
    all_codes = jnp.concatenate(
        [token_codes, jnp.pad(row_codes, ((0, 0), (0, tile - 2 * row_count)), constant_values=-1)],
        axis=1,
    )
    up_chunks = [([m * owner_totals], up_maps[m]) for m in masks]
    hidden_rows = wait_for(decode_hidden_input, mate_numbers, *[up_maps[m] for m in near])
    fresh_keys = jnp.dot(
        hidden_rows, key_matrix, preferred_element_type=jnp.float32
    ).astype(jnp.bfloat16)
    base_values = jnp.dot(hidden_rows, value_matrix, preferred_element_type=jnp.float32)

    cached, own_weight = attend_cached(
        queries, cached_key_rows, cached_value_rows, lengths, fresh_keys
    )

    stages, second_sent = [], []
    down_parts = {(0, p): own_parts[p] for p in range(parts)}
    for p, order in enumerate(orders):
        held = [0]
        for bit in order:
            sent = own_parts[p]
            if len(held) > 1:
                sent = jnp.pad(sent, ((0, (len(held) - 1) * part_rows), (0, 0)))
                for k, m in enumerate(held[1:], 1):
                    sent = place(sent, down_parts[m, p], k, (cached, base_values))
                second_sent.append(sent)
            came = swap(sent, "wide", bit)
            for k, m in enumerate(held):
                down_parts[m | bit, p] = came[k * part_rows : (k + 1) * part_rows]
            if bit == order[0]:
                down_stages = [(bit, p, [bit], came)]
            else:
                down_stages.append((bit, p, [m | bit for m in held], came))
            held = held + [m | bit for m in held]
        stages.extend(down_stages)
    last_maps = [came for bit, p, _, came in stages if bit == orders[p][-1]]
    first_maps = [came for bit, p, _, came in stages if bit == orders[p][0]]

    def down_code(m, p):
        return m * owner_totals + p * part_adapters

    down_chunks = [([0], flattened_down)] + [
        ([down_code(m, p) for m in came_from], came) for _, p, came_from, came in stages
    ]

    part_back, sent_back = project_tokens(
        all_codes,
        [cotangent, mate_cotangent],
        up_chunks,
        rank,
        after=(*first_maps, *second_sent),
    )
    back = sum_over("narrow", part_back, sent_back)

    groups = {}
    for m in far + near:
        for p, order in enumerate(orders):
            level = max(k for k, bit in enumerate(order) if m & bit)
            groups.setdefault((level, p, m == order[level]), []).append(m)
    group_keys = sorted(groups, key=lambda key: (-key[0], key[2]))
    last_level = len(chip_bits) - 1
    own_down, *results = gradient_chunks(
        token_codes,
        token_rewards,
        back,
        training_hidden_input,
        mate_hidden,
        [([0], owner_totals, jnp.float32, ())]
        + [
            (
                [down_code(m, p) for m in groups[level, p, direct]],
                part_adapters * len(groups[level, p, direct]),
                jnp.bfloat16 if level == last_level else jnp.float32,
                (),
            )
            for level, p, direct in group_keys
        ],
        (mate_slice,),
    )
    grads = dict(zip(group_keys, results))
    token = own_down
    arrived = {(m, p): [] for m in masks for p in range(parts)}

    def send_level(level):
        for key in group_keys:
            if key[0] == level:
                bit = orders[key[1]][level]
                came = swap(wait_for(grads[key], *last_maps), "wide", bit)
                for k, m in enumerate(groups[key]):
                    arrived[m ^ bit, key[1]].append((came, k))

    send_level(last_level)

    part_hidden, sent_hidden = project_tokens(
        all_codes,
        [training_hidden_input, mate_hidden],
        down_chunks,
        rank,
        rows=(decode_slice, mate_slice),
        after=(token,),
    )
    token = part_hidden
    for level in reversed(range(last_level)):
        added = [key for key in group_keys if key[0] == level]
        sums = add_arrived(
            [(grads[key], [arrived[m, key[1]] for m in groups[key]]) for key in added], (token,)
        )
        grads.update(zip(added, sums))
        send_level(level)
        token = sums[0]
    early = [[arrived[0, p][:-1] for p in range(parts)]]
    (own_down,) = add_arrived([(own_down, *early)], (token,), jnp.float32)
    last_down = [arrived[0, p][-1:] for p in range(parts)]

    hidden = sum_over(
        "narrow",
        part_hidden,
        sent_hidden,
        [(token,), (own_down,)],
    )
    own_up, *up_results = gradient_chunks(
        token_codes,
        token_rewards,
        hidden,
        cotangent,
        mate_cotangent,
        [([m * owner_totals], owner_totals, jnp.bfloat16 if m else jnp.float32, ()) for m in masks],
    )
    own_delta, mate_delta = row_deltas(
        row_codes, hidden, 2 * token_count, tile, up_chunks, (own_up,)
    )
    mate_delta = wait_for(mate_delta, *[came for part in last_down for came, _ in part])
    came_up = [(swap(result, "wide", m), 0) for m, result in zip(masks[1:], up_results)]
    (grad_up,) = add_arrived([(own_up, [came_up])], (), jnp.float32)
    (grad_down,) = add_arrived([(own_down, last_down)], (), jnp.float32)
    attended, fresh_values = finish_rows(
        cached, own_weight, base_values, own_delta, swap(mate_delta, "wide", core_bit)
    )
    return (
        attended,
        fresh_values,
        grad_down.reshape(adapter_down_map.shape),
        grad_up.reshape(adapter_up_map.shape),
    )


def solution(mesh):
    return jax.shard_map(
        per_device,
        mesh=mesh,
        in_specs=(
            P("wide", None),
            P("wide", "narrow"),
            P("wide", None, "narrow"),
            P("wide", None, "narrow"),
            P("wide"),
            P("wide"),
            P(None, "narrow"),
            P(None, "narrow"),
            P("wide", None, "narrow"),
            P("wide", None, "narrow"),
            P("wide", "narrow"),
            P("wide", "narrow"),
            P("wide"),
            P("wide"),
        ),
        out_specs=(
            P("wide", "narrow"),
            P("wide", "narrow"),
            P("wide", None, "narrow"),
            P("wide", None, "narrow"),
        ),
        check_vma=False,
    )
```

time: 110 us -> 101 us (0.918)
  waiting for transfers between devices: 22.7 us -> 14.4 us
  Pallas kernels: 35.7 us -> 43.3 us
  other arithmetic: 7.22 us -> 0.94 us
  matrix products: 9.01 us -> 6.13 us
  local copies, waits for them, and re-layouts: 3.19 us -> 5.65 us
    ppermute x27 -> x25, waiting for transfers between devices: 22.7 us -> 14.4 us  [swap(): return lax.ppermute(array, axis, [(i, i ^ mask) for i in range(count)])]
    pallas_call x8 -> x17, Pallas kernels: 35.7 us -> 43.3 us  [the longest x2 16.1 us: project_tokens(): pl.pallas_call(functools.partial(token_kernel, code_list([(bases, chunk.s...]
    dot_general x3 -> x0, matrix products: 5.14 us -> none  [the longest x1 3.53 us: attend_cached(): jnp.einsum('bhgd,bphd->bhgp', query_heads, key_heads, preferred_element_t...]
    pad x0 -> x2, local copies, waits for them, and re-layouts: none -> 2.31 us  [per_device(): sent = jnp.pad(sent, ((0, (len(held) - 1) * part_rows), (0, 0)))]
    dot_general x1, matrix products: 0.82 us -> 3.08 us  [per_device(): jnp.dot(hidden_rows, value_matrix, preferred_element_type=jnp.float32)]
    convert_element_type x3 -> x0, other arithmetic: 1.76 us -> none  [the longest x1 1.08 us: per_device(): attended.reshape(row_count, -1).astype(jnp.bfloat16)]
    add x2, other arithmetic: 1.5 us -> 0.15 us  [codes_of(): (ids // owner_totals ^ me) * owner_totals + ids % owner_totals]
    ppermute x27 -> x25, starting transfers between devices: 30.2 us -> 29.4 us  [swap(): return lax.ppermute(array, axis, [(i, i ^ mask) for i in range(count)])]
  transfers between devices with their start and end apart: 27 -> 25, of which waited for: 9 -> 8; matrix products, arithmetic and copies ran while one was open for 16% -> 12% of each run, Pallas kernels for 33% -> 42%
where the time goes in v5:
time: 101 us
  Pallas kernels  43.3 us (43%)
  starting transfers between devices  29.4 us (29%)
  waiting for transfers between devices  14.4 us (14%)
  matrix products  6.13 us (6%)
  local copies, waits for them, and re-layouts  5.65 us (6%)
    ppermute x25, starting transfers between devices, swap(): return lax.ppermute(array, axis, [(i, i ^ mask) for i in range(count)])  29.4 us
    pallas_call x2, Pallas kernels, project_tokens(): pl.pallas_call(functools.partial(token_kernel, code_list([(bases, chunk.s...  16.1 us
    ppermute x25, waiting for transfers between devices, swap(): return lax.ppermute(array, axis, [(i, i ^ mask) for i in range(count)])  14.4 us
    pallas_call x2, Pallas kernels, gradient_chunks(): pl.pallas_call(functools.partial(gradient_kernel, code_list([(chunk[0], r...  14 us
    pallas_call x1, Pallas kernels, attend_cached(): pl.pallas_call(functools.partial(attend_kernel, kv_width // HEAD_SIZE), g...  5.09 us
    pallas_call x4, Pallas kernels, add_arrived(): pl.pallas_call(functools.partial(add_kernel, [[[k for _, k in arrived] fo...  3.5 us
    dot_general x1, matrix products, per_device(): jnp.dot(hidden_rows, value_matrix, preferred_element_type=jnp.float32)  3.08 us
    dot_general x1, matrix products, per_device(): jnp.dot(hidden_rows, key_matrix, preferred_element_type=jnp.float32)  3.05 us
  transfers between devices with their start and end apart: 25, of which 8 were waited for; matrix products, arithmetic and copies ran while one was open for 12% of the time, Pallas kernels for 42%

profile of v5, /device:TPU:0, one launch (start us, length us, event | category | flops | bytes accessed | tf_op | source)
XLA Modules:
  0.0 100.8 jit_solution(16515665884264422293)
XLA Ops:
  3.1 2.3 %fusion.4 = (bf16[8,16,2048]{2,1,0:T(8,128)(2,1)}, bf16[8,16,2048]{2,1,0:T(8,128)(2,1)}) fusion(bf16[16,16,2048]{2,1,0:T(8,128)(2,1)} %param.22), kind=kLoop, calls=%fused_computation.22 | loop fusion | bytes 2097152 | tf_op jit(solution)/shard_map/slice | solution.py:503
  5.4 2.7 %collective-permute-start.2 = (bf16[256,256]{1,0:T(8,128)(2,1)}, bf16[256,256]{1,0:T(8,128)(2,1)S(1)}, u32[]{:S(2)}, u32[]{:S(2)}) collective-permute-start(bf16[256,256]{1,0:T(8,128)(2,1)} %bitcast.refs_2_.refs_0_), channel_id=1, source_target_pairs={{0,16},{4,20},{8,24},{12,28},{16,0},{20,4},{24,8},{28,12},{1,17},{... | collective-permute-start | bytes 393224 | tf_op jit(solution)/shard_map/ppermute | solution.py:21
  13.4 3.0 %collective-permute-start.10 = (bf16[256,256]{1,0:T(8,128)(2,1)}, bf16[256,256]{1,0:T(8,128)(2,1)S(1)}, u32[]{:S(2)}, u32[]{:S(2)}) collective-permute-start(bf16[256,256]{1,0:T(8,128)(2,1)} %bitcast.refs_2_.refs_0_), channel_id=1, source_target_pairs={{0,24},{4,28},{8,16},{12,20},{16,8},{20,12},{24,0},{28,4},{1,25},{... | collective-permute-start | bytes 393224 | tf_op jit(solution)/shard_map/ppermute | solution.py:21
  16.4 3.1 %fusion.fresh_ref = f32[32,256]{1,0:T(8,128)S(1)} fusion(bf16[32,8192]{1,0:T(8,128)(2,1)S(1)} %copy-done, bf16[8192,256]{1,0:T(8,128)(2,1)} %param.20), kind=kOutput, calls=%fused_computation.1 | convolution fusion | flops 134234112 | bytes 4751360 | tf_op jit(solution)/shard_map/dot_general | solution.py:533
  19.5 5.1 %shard_map.165 = (f32[32,16,128]{2,1,0:T(8,128)S(1)}, f32[32,16,128]{2,1,0:T(8,128)S(1)}) custom-call(s32[32]{0:T(128)S(1)} %copy-done.9, bf16[32,16,128]{2,1,0:T(8,128)(2,1)S(1)} %bitcast.19, bf16[32,256,256]{2,1,0:T(8,128)(2,1)S(1)} %copy-done.3, bf16[32,256,256]{2,1,0:T(8,128)(2,1)} %values_ref.1, f32[32,256]{1,0:T(8,128)S(1)} %fusion.fresh_ref), custom_call_target="tpu_custom_call" | custom-call | flops 1 | bytes 1 | tf_op jit(solution)/shard_map/pallas_call | solution.py:438
  24.7 3.1 %fusion.6.refs_1_.base_ref = f32[32,256]{1,0:T(8,128)S(1)} fusion(bf16[32,8192]{1,0:T(8,128)(2,1)S(1)} %copy-done, bf16[8192,256]{1,0:T(8,128)(2,1)} %param.21), kind=kOutput, calls=%fused_computation.24 | convolution fusion | flops 134217728 | bytes 4751360 | tf_op jit(solution)/shard_map/dot_general | solution.py:536
  30.1 2.5 %shard_map.168 = (f32[16,2048]{1,0:T(8,128)S(1)}, bf16[16,2048]{1,0:T(8,128)(2,1)S(1)}) custom-call(s32[1,2560]{1,0:T(1,128)S(1)} %fusion.1.codes_ref, bf16[1024,256]{1,0:T(8,128)(2,1)S(1)} %copy-done.4, bf16[1024,256]{1,0:T(8,128)(2,1)S(1)} %collective-permute-done.4.refs_1_.mate_ref, bf16[256,256]{1,0:T(8,128)(2,1)} %bitcast.refs_2_.refs_0_, ...), custom_call_target="tpu_custom_call" | custom-call | flops 1 | bytes 1 | tf_op jit(solution)/shard_map/pallas_call | solution.py:130
  32.6 2.2 %collective-permute-start.11 = (bf16[16,2048]{1,0:T(8,128)(2,1)S(1)}, bf16[16,2048]{1,0:T(8,128)(2,1)S(1)}, u32[]{:S(2)}, u32[]{:S(2)}) collective-permute-start(bf16[16,2048]{1,0:T(8,128)(2,1)S(1)} %get-tuple-element.55), channel_id=1, source_target_pairs={{0,1},{1,0},{2,3},{3,2},{4,5},{5,4},{6,7},{7,6},{8,9},{9,8},{10,11... | collective-permute-start | bytes 196616 | tf_op jit(solution)/shard_map/ppermute | solution.py:21
  34.9 2.2 %collective-permute-done.11.came_ref = bf16[16,2048]{1,0:T(8,128)(2,1)S(1)} collective-permute-done((bf16[16,2048]{1,0:T(8,128)(2,1)S(1)}, bf16[16,2048]{1,0:T(8,128)(2,1)S(1)}, u32[]{:S(2)}, u32[]{:S(2)}) %collective-permute-start.11) | collective-permute-done | bytes 65568 | tf_op jit(solution)/shard_map/ppermute | solution.py:21
  37.0 3.1 %collective-permute-start.12 = (bf16[16,2048]{1,0:T(8,128)(2,1)S(1)}, bf16[16,2048]{1,0:T(8,128)(2,1)S(1)}, u32[]{:S(2)}, u32[]{:S(2)}) collective-permute-start(bf16[16,2048]{1,0:T(8,128)(2,1)S(1)} %get-tuple-element.57), channel_id=1, source_target_pairs={{0,2},{1,3},{2,0},{3,1},{4,6},{5,7},{6,4},{7,5},{8,10},{9,11},{10,... | collective-permute-start | bytes 196616 | tf_op jit(solution)/shard_map/ppermute | solution.py:21
  40.2 2.2 %collective-permute-done.12.came_ref = bf16[16,2048]{1,0:T(8,128)(2,1)S(1)} collective-permute-done((bf16[16,2048]{1,0:T(8,128)(2,1)S(1)}, bf16[16,2048]{1,0:T(8,128)(2,1)S(1)}, u32[]{:S(2)}, u32[]{:S(2)}) %collective-permute-start.12) | collective-permute-done | bytes 65568 | tf_op jit(solution)/shard_map/ppermute | solution.py:21
  43.0 12.7 %shard_map.171 = (f32[256,2048]{1,0:T(8,128)}, bf16[128,2048]{1,0:T(8,128)(2,1)}, bf16[128,2048]{1,0:T(8,128)(2,1)}, bf16[128,2048]{1,0:T(8,128)(2,1)S(1)}, bf16...) custom-call(s32[1,2048]{1,0:T(1,128)S(1)} %fusion.2.codes_ref, ...), custom_call_target="tpu_custom_call" | custom-call | flops 1 | bytes 1 | tf_op jit(solution)/shard_map/pallas_call | solution.py:283
  55.8 1.5 %collective-permute-start.15 = (bf16[128,2048]{1,0:T(8,128)(2,1)}, bf16[128,2048]{1,0:T(8,128)(2,1)S(1)}, u32[]{:S(2)}, u32[]{:S(2)}) collective-permute-start(bf16[128,2048]{1,0:T(8,128)(2,1)} %get-tuple-element.67), channel_id=1, source_target_pairs={{0,8},{4,12},{8,0},{12,4},{16,24},{20,28},{24,16},{28,20},{1,9},{5... | collective-permute-start | bytes 1572872 | tf_op jit(solution)/shard_map/ppermute | solution.py:21
  57.3 1.5 %collective-permute-start.14 = (bf16[128,2048]{1,0:T(8,128)(2,1)}, bf16[128,2048]{1,0:T(8,128)(2,1)S(1)}, u32[]{:S(2)}, u32[]{:S(2)}) collective-permute-start(bf16[128,2048]{1,0:T(8,128)(2,1)} %get-tuple-element.65), channel_id=1, source_target_pairs={{0,16},{4,20},{8,24},{12,28},{16,0},{20,4},{24,8},{28,12},{1,17},{... | collective-permute-start | bytes 1572872 | tf_op jit(solution)/shard_map/ppermute | solution.py:21
  59.9 13.6 %shard_map.172 = (f32[16,2560]{1,0:T(8,128)S(1)}, bf16[16,2560]{1,0:T(8,128)(2,1)S(1)}) custom-call(s32[1,2560]{1,0:T(1,128)S(1)} %fusion.1.codes_ref, bf16[1024,2048]{1,0:T(8,128)(2,1)} %refs_0_.3, bf16[1024,2048]{1,0:T(8,128)(2,1)} %collective-permute-done.3.mate_ref.refs_1_, bf16[32,2048]{1,0:T(8,128)(2,1)S(1)} %constant_dynamic-slice_fusion.refs_2_, ...), custom_call_target="tpu_custom_call" | custom-call | flops 1 | bytes 1 | tf_op jit(solution)/shard_map/pallas_call | solution.py:130
  74.1 1.5 %collective-permute-start.19 = (bf16[128,2048]{1,0:T(8,128)(2,1)S(1)}, bf16[128,2048]{1,0:T(8,128)(2,1)S(1)}, u32[]{:S(2)}, u32[]{:S(2)}) collective-permute-start(bf16[128,2048]{1,0:T(8,128)(2,1)S(1)} %get-tuple-element.79.refs_0_.refs_3_), channel_id=1, source_target_pairs={{0,8},{4,12},{8,0},{12,4},{16,24},{20,28},{24,16},{28,20},{1,9},{5... | collective-permute-start | bytes 1572872 | tf_op jit(solution)/shard_map/ppermute | solution.py:21
  75.6 1.5 %collective-permute-start.20 = (bf16[128,2048]{1,0:T(8,128)(2,1)S(1)}, bf16[128,2048]{1,0:T(8,128)(2,1)S(1)}, u32[]{:S(2)}, u32[]{:S(2)}) collective-permute-start(bf16[128,2048]{1,0:T(8,128)(2,1)S(1)} %get-tuple-element.81), channel_id=1, source_target_pairs={{0,16},{4,20},{8,24},{12,28},{16,0},{20,4},{24,8},{28,12},{1,17},{... | collective-permute-start | bytes 1572872 | tf_op jit(solution)/shard_map/ppermute | solution.py:21
  77.1 1.6 %collective-permute-start.13 = (bf16[16,2560]{1,0:T(8,128)(2,1)S(1)}, bf16[16,2560]{1,0:T(8,128)(2,1)S(1)}, u32[]{:S(2)}, u32[]{:S(2)}) collective-permute-start(bf16[16,2560]{1,0:T(8,128)(2,1)S(1)} %get-tuple-element.61), channel_id=1, source_target_pairs={{0,1},{1,0},{2,3},{3,2},{4,5},{5,4},{6,7},{7,6},{8,9},{9,8},{10,11... | collective-permute-start | bytes 245768 | tf_op jit(solution)/shard_map/ppermute | solution.py:21
  78.7 3.7 %collective-permute-done.13.came_ref = bf16[16,2560]{1,0:T(8,128)(2,1)S(1)} collective-permute-done((bf16[16,2560]{1,0:T(8,128)(2,1)S(1)}, bf16[16,2560]{1,0:T(8,128)(2,1)S(1)}, u32[]{:S(2)}, u32[]{:S(2)}) %collective-permute-start.13) | collective-permute-done | bytes 81952 | tf_op jit(solution)/shard_map/ppermute | solution.py:21
  82.5 2.3 %collective-permute-start.16 = (bf16[16,2560]{1,0:T(8,128)(2,1)S(1)}, bf16[16,2560]{1,0:T(8,128)(2,1)S(1)}, u32[]{:S(2)}, u32[]{:S(2)}) collective-permute-start(bf16[16,2560]{1,0:T(8,128)(2,1)S(1)} %get-tuple-element.70), channel_id=1, source_target_pairs={{0,2},{1,3},{2,0},{3,1},{4,6},{5,7},{6,4},{7,5},{8,10},{9,11},{10,... | collective-permute-start | bytes 245768 | tf_op jit(solution)/shard_map/ppermute | solution.py:21
  85.4 2.5 %collective-permute-done.16.came_ref = bf16[16,2560]{1,0:T(8,128)(2,1)S(1)} collective-permute-done((bf16[16,2560]{1,0:T(8,128)(2,1)S(1)}, bf16[16,2560]{1,0:T(8,128)(2,1)S(1)}, u32[]{:S(2)}, u32[]{:S(2)}) %collective-permute-start.16) | collective-permute-done | bytes 81952 | tf_op jit(solution)/shard_map/ppermute | solution.py:21
  90.9 2.4 %collective-permute-start.24 = (bf16[256,256]{1,0:T(8,128)(2,1)S(1)}, bf16[256,256]{1,0:T(8,128)(2,1)S(1)}, u32[]{:S(2)}, u32[]{:S(2)}) collective-permute-start(bf16[256,256]{1,0:T(8,128)(2,1)S(1)} %get-tuple-element.87), channel_id=1, source_target_pairs={{0,24},{4,28},{8,16},{12,20},{16,8},{20,12},{24,0},{28,4},{1,25},{... | collective-permute-start | bytes 393224 | tf_op jit(solution)/shard_map/ppermute | solution.py:21
  94.9 2.6 %collective-permute-done.23.refs_2_ = bf16[256,256]{1,0:T(8,128)(2,1)S(1)} collective-permute-done((bf16[256,256]{1,0:T(8,128)(2,1)S(1)}, bf16[256,256]{1,0:T(8,128)(2,1)S(1)}, u32[]{:S(2)}, u32[]{:S(2)}) %collective-permute-start.23) | collective-permute-done | bytes 131104 | tf_op jit(solution)/shard_map/ppermute | solution.py:21
  98.2 1.6 %shard_map.180 = f32[256,2048]{1,0:T(8,128)} custom-call(f32[256,2048]{1,0:T(8,128)S(1)} %shard_map.175.refs_0_, bf16[128,2048]{1,0:T(8,128)(2,1)S(1)} %collective-permute-done.19.refs_1_, bf16[128,2048]{1,0:T(8,128)(2,1)S(1)} %collective-permute-done.20.refs_2_), custom_call_target="tpu_custom_call" | custom-call | flops 1 | bytes 1 | tf_op jit(solution)/shard_map/pallas_call | solution.py:330
  (83 shorter events, 19.3 us)
Async XLA Ops:
  2.7 40.3 %collective-permute-start.3 = (bf16[1024,2048]{1,0:T(8,128)(2,1)}, bf16[1024,2048]{1,0:T(8,128)(2,1)}, u32[]{:S(2)}, u32[]{:S(2)}) collective-permute-start(bf16[1024,2048]{1,0:T(8,128)(2,1)} %refs_0_.3), channel_id=1, source_target_pairs={{0,4},{4,0},{8,12},{12,8},{16,20},{20,16},{24,28},{28,24},{1,5},{5... | collective-permute-start | bytes 12582920 | tf_op jit(solution)/shard_map/ppermute | solution.py:21
  5.4 8.0 %collective-permute-start.2 = (bf16[256,256]{1,0:T(8,128)(2,1)}, bf16[256,256]{1,0:T(8,128)(2,1)S(1)}, u32[]{:S(2)}, u32[]{:S(2)}) collective-permute-start(bf16[256,256]{1,0:T(8,128)(2,1)} %bitcast.refs_2_.refs_0_), channel_id=1, source_target_pairs={{0,16},{4,20},{8,24},{12,28},{16,0},{20,4},{24,8},{28,12},{1,17},{... | collective-permute-start | bytes 393224 | tf_op jit(solution)/shard_map/ppermute | solution.py:21
  8.1 8.3 %collective-permute-start.1 = (bf16[256,256]{1,0:T(8,128)(2,1)}, bf16[256,256]{1,0:T(8,128)(2,1)S(1)}, u32[]{:S(2)}, u32[]{:S(2)}) collective-permute-start(bf16[256,256]{1,0:T(8,128)(2,1)} %bitcast.refs_2_.refs_0_), channel_id=1, source_target_pairs={{0,8},{4,12},{8,0},{12,4},{16,24},{20,28},{24,16},{28,20},{1,9},{5... | collective-permute-start | bytes 393224 | tf_op jit(solution)/shard_map/ppermute | solution.py:21
  9.5 19.9 %collective-permute-start.6 = (bf16[128,2048]{1,0:T(8,128)(2,1)}, bf16[128,2048]{1,0:T(8,128)(2,1)S(1)}, u32[]{:S(2)}, u32[]{:S(2)}) collective-permute-start(bf16[128,2048]{1,0:T(8,128)(2,1)} %bitcast.1), channel_id=1, source_target_pairs={{0,8},{4,12},{8,0},{12,4},{16,24},{20,28},{24,16},{28,20},{1,9},{5... | collective-permute-start | bytes 1572872 | tf_op jit(solution)/shard_map/ppermute | solution.py:21
  10.1 17.7 %collective-permute-start.8 = (bf16[128,2048]{1,0:T(8,128)(2,1)}, bf16[128,2048]{1,0:T(8,128)(2,1)}, u32[]{:S(2)}, u32[]{:S(2)}) collective-permute-start(bf16[128,2048]{1,0:T(8,128)(2,1)} %bitcast.2), channel_id=1, source_target_pairs={{0,16},{4,20},{8,24},{12,28},{16,0},{20,4},{24,8},{28,12},{1,17},{... | collective-permute-start | bytes 1572872 | tf_op jit(solution)/shard_map/ppermute | solution.py:21
  13.4 16.7 %collective-permute-start.10 = (bf16[256,256]{1,0:T(8,128)(2,1)}, bf16[256,256]{1,0:T(8,128)(2,1)S(1)}, u32[]{:S(2)}, u32[]{:S(2)}) collective-permute-start(bf16[256,256]{1,0:T(8,128)(2,1)} %bitcast.refs_2_.refs_0_), channel_id=1, source_target_pairs={{0,24},{4,28},{8,16},{12,20},{16,8},{20,12},{24,0},{28,4},{1,25},{... | collective-permute-start | bytes 393224 | tf_op jit(solution)/shard_map/ppermute | solution.py:21
  16.4 13.7 %collective-permute-start.4 = (bf16[1024,256]{1,0:T(8,128)(2,1)}, bf16[1024,256]{1,0:T(8,128)(2,1)S(1)}, u32[]{:S(2)}, u32[]{:S(2)}) collective-permute-start(bf16[1024,256]{1,0:T(8,128)(2,1)} %own_ref.3), channel_id=1, source_target_pairs={{0,4},{4,0},{8,12},{12,8},{16,20},{20,16},{24,28},{28,24},{1,5},{5... | collective-permute-start | bytes 1572872 | tf_op jit(solution)/shard_map/ppermute | solution.py:21
  28.9 26.9 %collective-permute-start.9 = (bf16[256,2048]{1,0:T(8,128)(2,1)S(1)}, bf16[256,2048]{1,0:T(8,128)(2,1)S(1)}, u32[]{:S(2)}, u32[]{:S(2)}) collective-permute-start(bf16[256,2048]{1,0:T(8,128)(2,1)S(1)} %shard_map.167.refs_9_), channel_id=1, source_target_pairs={{0,8},{4,12},{8,0},{12,4},{16,24},{20,28},{24,16},{28,20},{1,9},{5... | collective-permute-start | bytes 3145736 | tf_op jit(solution)/shard_map/ppermute | solution.py:21
  29.5 26.3 %collective-permute-start.7 = (bf16[256,2048]{1,0:T(8,128)(2,1)S(1)}, bf16[256,2048]{1,0:T(8,128)(2,1)S(1)}, u32[]{:S(2)}, u32[]{:S(2)}) collective-permute-start(bf16[256,2048]{1,0:T(8,128)(2,1)S(1)} %shard_map.166.refs_8_), channel_id=1, source_target_pairs={{0,16},{4,20},{8,24},{12,28},{16,0},{20,4},{24,8},{28,12},{1,17},{... | collective-permute-start | bytes 3145736 | tf_op jit(solution)/shard_map/ppermute | solution.py:21
  32.6 4.4 %collective-permute-start.11 = (bf16[16,2048]{1,0:T(8,128)(2,1)S(1)}, bf16[16,2048]{1,0:T(8,128)(2,1)S(1)}, u32[]{:S(2)}, u32[]{:S(2)}) collective-permute-start(bf16[16,2048]{1,0:T(8,128)(2,1)S(1)} %get-tuple-element.55), channel_id=1, source_target_pairs={{0,1},{1,0},{2,3},{3,2},{4,5},{5,4},{6,7},{7,6},{8,9},{9,8},{10,11... | collective-permute-start | bytes 196616 | tf_op jit(solution)/shard_map/ppermute | solution.py:21
  34.8 8.3 %collective-permute-start.5 = (bf16[32,2048]{1,0:T(8,128)(2,1)S(1)}, bf16[32,2048]{1,0:T(8,128)(2,1)S(1)}, u32[]{:S(2)}, u32[]{:S(2)}) collective-permute-start(bf16[32,2048]{1,0:T(8,128)(2,1)S(1)} %constant_dynamic-slice_fusion.refs_2_), channel_id=1, source_target_pairs={{0,4},{4,0},{8,12},{12,8},{16,20},{20,16},{24,28},{28,24},{1,5},{5... | collective-permute-start | bytes 393224 | tf_op jit(solution)/shard_map/ppermute | solution.py:21
  37.0 5.3 %collective-permute-start.12 = (bf16[16,2048]{1,0:T(8,128)(2,1)S(1)}, bf16[16,2048]{1,0:T(8,128)(2,1)S(1)}, u32[]{:S(2)}, u32[]{:S(2)}) collective-permute-start(bf16[16,2048]{1,0:T(8,128)(2,1)S(1)} %get-tuple-element.57), channel_id=1, source_target_pairs={{0,2},{1,3},{2,0},{3,1},{4,6},{5,7},{6,4},{7,5},{8,10},{9,11},{10,... | collective-permute-start | bytes 196616 | tf_op jit(solution)/shard_map/ppermute | solution.py:21
  55.8 17.8 %collective-permute-start.15 = (bf16[128,2048]{1,0:T(8,128)(2,1)}, bf16[128,2048]{1,0:T(8,128)(2,1)S(1)}, u32[]{:S(2)}, u32[]{:S(2)}) collective-permute-start(bf16[128,2048]{1,0:T(8,128)(2,1)} %get-tuple-element.67), channel_id=1, source_target_pairs={{0,8},{4,12},{8,0},{12,4},{16,24},{20,28},{24,16},{28,20},{1,9},{5... | collective-permute-start | bytes 1572872 | tf_op jit(solution)/shard_map/ppermute | solution.py:21
  57.3 16.2 %collective-permute-start.14 = (bf16[128,2048]{1,0:T(8,128)(2,1)}, bf16[128,2048]{1,0:T(8,128)(2,1)S(1)}, u32[]{:S(2)}, u32[]{:S(2)}) collective-permute-start(bf16[128,2048]{1,0:T(8,128)(2,1)} %get-tuple-element.65), channel_id=1, source_target_pairs={{0,16},{4,20},{8,24},{12,28},{16,0},{20,4},{24,8},{28,12},{1,17},{... | collective-permute-start | bytes 1572872 | tf_op jit(solution)/shard_map/ppermute | solution.py:21
  58.8 25.9 %collective-permute-start.18 = (bf16[128,2048]{1,0:T(8,128)(2,1)S(1)}, bf16[128,2048]{1,0:T(8,128)(2,1)S(1)}, u32[]{:S(2)}, u32[]{:S(2)}) collective-permute-start(bf16[128,2048]{1,0:T(8,128)(2,1)S(1)} %get-tuple-element.74), channel_id=1, source_target_pairs={{0,8},{4,12},{8,0},{12,4},{16,24},{20,28},{24,16},{28,20},{1,9},{5... | collective-permute-start | bytes 1572872 | tf_op jit(solution)/shard_map/ppermute | solution.py:21
  59.4 25.4 %collective-permute-start.17 = (bf16[128,2048]{1,0:T(8,128)(2,1)S(1)}, bf16[128,2048]{1,0:T(8,128)(2,1)S(1)}, u32[]{:S(2)}, u32[]{:S(2)}) collective-permute-start(bf16[128,2048]{1,0:T(8,128)(2,1)S(1)} %get-tuple-element.72), channel_id=1, source_target_pairs={{0,16},{4,20},{8,24},{12,28},{16,0},{20,4},{24,8},{28,12},{1,17},{... | collective-permute-start | bytes 1572872 | tf_op jit(solution)/shard_map/ppermute | solution.py:21
  74.1 20.5 %collective-permute-start.19 = (bf16[128,2048]{1,0:T(8,128)(2,1)S(1)}, bf16[128,2048]{1,0:T(8,128)(2,1)S(1)}, u32[]{:S(2)}, u32[]{:S(2)}) collective-permute-start(bf16[128,2048]{1,0:T(8,128)(2,1)S(1)} %get-tuple-element.79.refs_0_.refs_3_), channel_id=1, source_target_pairs={{0,8},{4,12},{8,0},{12,4},{16,24},{20,28},{24,16},{28,20},{1,9},{5... | collective-permute-start | bytes 1572872 | tf_op jit(solution)/shard_map/ppermute | solution.py:21
  75.6 19.1 %collective-permute-start.20 = (bf16[128,2048]{1,0:T(8,128)(2,1)S(1)}, bf16[128,2048]{1,0:T(8,128)(2,1)S(1)}, u32[]{:S(2)}, u32[]{:S(2)}) collective-permute-start(bf16[128,2048]{1,0:T(8,128)(2,1)S(1)} %get-tuple-element.81), channel_id=1, source_target_pairs={{0,16},{4,20},{8,24},{12,28},{16,0},{20,4},{24,8},{28,12},{1,17},{... | collective-permute-start | bytes 1572872 | tf_op jit(solution)/shard_map/ppermute | solution.py:21
  77.1 5.3 %collective-permute-start.13 = (bf16[16,2560]{1,0:T(8,128)(2,1)S(1)}, bf16[16,2560]{1,0:T(8,128)(2,1)S(1)}, u32[]{:S(2)}, u32[]{:S(2)}) collective-permute-start(bf16[16,2560]{1,0:T(8,128)(2,1)S(1)} %get-tuple-element.61), channel_id=1, source_target_pairs={{0,1},{1,0},{2,3},{3,2},{4,5},{5,4},{6,7},{7,6},{8,9},{9,8},{10,11... | collective-permute-start | bytes 245768 | tf_op jit(solution)/shard_map/ppermute | solution.py:21
  82.5 5.4 %collective-permute-start.16 = (bf16[16,2560]{1,0:T(8,128)(2,1)S(1)}, bf16[16,2560]{1,0:T(8,128)(2,1)S(1)}, u32[]{:S(2)}, u32[]{:S(2)}) collective-permute-start(bf16[16,2560]{1,0:T(8,128)(2,1)S(1)} %get-tuple-element.70), channel_id=1, source_target_pairs={{0,2},{1,3},{2,0},{3,1},{4,6},{5,7},{6,4},{7,5},{8,10},{9,11},{10,... | collective-permute-start | bytes 245768 | tf_op jit(solution)/shard_map/ppermute | solution.py:21
  89.8 5.1 %collective-permute-start.22 = (bf16[256,256]{1,0:T(8,128)(2,1)S(1)}, bf16[256,256]{1,0:T(8,128)(2,1)S(1)}, u32[]{:S(2)}, u32[]{:S(2)}) collective-permute-start(bf16[256,256]{1,0:T(8,128)(2,1)S(1)} %get-tuple-element.85), channel_id=1, source_target_pairs={{0,8},{4,12},{8,0},{12,4},{16,24},{20,28},{24,16},{28,20},{1,9},{5... | collective-permute-start | bytes 393224 | tf_op jit(solution)/shard_map/ppermute | solution.py:21
  90.4 7.1 %collective-permute-start.23 = (bf16[256,256]{1,0:T(8,128)(2,1)S(1)}, bf16[256,256]{1,0:T(8,128)(2,1)S(1)}, u32[]{:S(2)}, u32[]{:S(2)}) collective-permute-start(bf16[256,256]{1,0:T(8,128)(2,1)S(1)} %get-tuple-element.86), channel_id=1, source_target_pairs={{0,16},{4,20},{8,24},{12,28},{16,0},{20,4},{24,8},{28,12},{1,17},{... | collective-permute-start | bytes 393224 | tf_op jit(solution)/shard_map/ppermute | solution.py:21
  90.9 6.5 %collective-permute-start.24 = (bf16[256,256]{1,0:T(8,128)(2,1)S(1)}, bf16[256,256]{1,0:T(8,128)(2,1)S(1)}, u32[]{:S(2)}, u32[]{:S(2)}) collective-permute-start(bf16[256,256]{1,0:T(8,128)(2,1)S(1)} %get-tuple-element.87), channel_id=1, source_target_pairs={{0,24},{4,28},{8,16},{12,20},{16,8},{20,12},{24,0},{28,4},{1,25},{... | collective-permute-start | bytes 393224 | tf_op jit(solution)/shard_map/ppermute | solution.py:21
  94.7 5.2 %collective-permute-start.21 = (bf16[32,256]{1,0:T(8,128)(2,1)S(1)}, bf16[32,256]{1,0:T(8,128)(2,1)S(1)}, u32[]{:S(2)}, u32[]{:S(2)}) collective-permute-start(bf16[32,256]{1,0:T(8,128)(2,1)S(1)} %get-tuple-element.82), channel_id=1, source_target_pairs={{0,4},{4,0},{8,12},{12,8},{16,20},{20,16},{24,28},{28,24},{1,5},{5... | collective-permute-start | bytes 49160 | tf_op jit(solution)/shard_map/ppermute | solution.py:21
  (14 other events, 113.0 us)

commit v6 on v5

--- a/solution.py
+++ b/solution.py
@@ -13,6 +13,9 @@
 ADAPTER_SCALE = 2.0
 NEG_FILL = -1e30
 VMEM_LIMIT = 48 * 1024 * 1024
+TOKEN = jax.ShapeDtypeStruct((8, 128), jnp.float32)
+TOKEN_SPEC = pl.BlockSpec(TOKEN.shape, lambda *_: (0, 0))
+SENT = pltpu.HBM
 SHORT = pl.CostEstimate(flops=1, bytes_accessed=1, transcendentals=0)
 
 
@@ -199,8 +202,30 @@
     )(codes, ranks, *[chunk for _, chunk in chunks], *after)
 
 
+def cut_kernel(maps_ref, *refs):
+    half = len(refs) // 2
+    rows = refs[0].shape[0]
+    for p in range(half):
+        part = maps_ref[p * rows : (p + 1) * rows, :]
+        refs[p][...] = part
+        refs[half + p][:rows, :] = part
+
+
+def cut(maps, parts):
+    rows, width = maps.shape[0] // parts, maps.shape[1]
+    return pl.pallas_call(
+        cut_kernel,
+        out_shape=[SENT((rows, width), maps.dtype)] * parts
+        + [SENT((2 * rows, width), maps.dtype)] * parts,
+        compiler_params=pltpu.CompilerParams(vmem_limit_bytes=VMEM_LIMIT),
+        cost_estimate=SHORT,
+    )(pltpu.with_memory_space_constraint(maps, pltpu.HBM))
+
+
 def place_kernel(buffer_ref, piece_ref, *refs):
-    refs[-1][...] = piece_ref[...]
+    out_ref, token_ref = refs[-2:]
+    out_ref[...] = piece_ref[...]
+    token_ref[...] = jnp.zeros_like(token_ref)
 
 
 def place(buffer, piece, k, after=()):
@@ -212,8 +237,8 @@
             pl.BlockSpec(piece.shape, lambda i: (0, 0)),
         ]
         + [pl.BlockSpec(memory_space=pl.ANY) for _ in after],
-        out_specs=pl.BlockSpec(piece.shape, lambda i: (k, 0)),
-        out_shape=jax.ShapeDtypeStruct(buffer.shape, buffer.dtype),
+        out_specs=[pl.BlockSpec(piece.shape, lambda i: (k, 0)), TOKEN_SPEC],
+        out_shape=[SENT(buffer.shape, buffer.dtype), TOKEN],
         input_output_aliases={0: 0},
         compiler_params=pltpu.CompilerParams(vmem_limit_bytes=VMEM_LIMIT),
         cost_estimate=SHORT,
@@ -249,12 +274,12 @@
     row_codes, arrived_counts, codes_ref, rewards_ref, factor_ref, own_ref, mate_ref, *refs
 ):
     arrived = list(refs[: sum(arrived_counts)])
-    outs = refs[-1 - len(arrived_counts) : -1]
-    spread_ref = refs[-1]
+    *outs, token_ref, spread_ref = refs[-2 - len(arrived_counts) :]
     token_count = own_ref.shape[0]
 
     @pl.when(pl.program_id(0) == 0)
     def _():
+        token_ref[...] = jnp.zeros_like(token_ref)
         scale = ADAPTER_SCALE * rewards_ref[...].astype(jnp.float32)
         scaled = (scale * factor_ref[...]).astype(jnp.bfloat16).astype(jnp.float32)
         spread(codes_ref[...], scaled, row_codes, spread_ref)
@@ -296,11 +321,12 @@
         ]
         + [pl.BlockSpec((rows, tile), across) for _, rows in arrived]
         + [pl.BlockSpec(memory_space=pl.ANY) for _ in after],
-        out_specs=[pl.BlockSpec((rows, tile), across) for rows in out_rows],
+        out_specs=[pl.BlockSpec((rows, tile), across) for rows in out_rows] + [TOKEN_SPEC],
         out_shape=[
-            jax.ShapeDtypeStruct((rows, width), dtype)
+            (SENT if dtype == jnp.bfloat16 else jax.ShapeDtypeStruct)((rows, width), dtype)
             for rows, (_, _, dtype, _) in zip(out_rows, chunks)
-        ],
+        ]
+        + [TOKEN],
         scratch_shapes=[pltpu.VMEM((sum(out_rows), 2 * token_count), jnp.bfloat16)],
         compiler_params=pltpu.CompilerParams(vmem_limit_bytes=VMEM_LIMIT),
         cost_estimate=cost,
@@ -309,7 +335,8 @@
 
 def add_kernel(groups, *refs):
     starts, refs = refs[: len(groups)], refs[len(groups) :]
-    outs = refs[len(refs) - len(groups) :]
+    *outs, token_ref = refs[-1 - len(groups) :]
+    token_ref[...] = jnp.zeros_like(token_ref)
     arrived = list(refs)
     for places, start_ref, out_ref in zip(groups, starts, outs):
         rows = out_ref.shape[0] // len(places)
@@ -334,8 +361,13 @@
         grid=(width // tile,),
         in_specs=[pl.BlockSpec((a.shape[0], tile), across) for a in arrays]
         + [pl.BlockSpec(memory_space=pl.ANY) for _ in after],
-        out_specs=[pl.BlockSpec((start.shape[0], tile), across) for start, _ in groups],
-        out_shape=[jax.ShapeDtypeStruct(start.shape, dtype) for start, _ in groups],
+        out_specs=[pl.BlockSpec((start.shape[0], tile), across) for start, _ in groups]
+        + [TOKEN_SPEC],
+        out_shape=[
+            (SENT if dtype == jnp.bfloat16 else jax.ShapeDtypeStruct)(start.shape, dtype)
+            for start, _ in groups
+        ]
+        + [TOKEN],
         compiler_params=pltpu.CompilerParams(vmem_limit_bytes=VMEM_LIMIT),
         cost_estimate=SHORT,
     )(*arrays, *after)
@@ -455,8 +487,8 @@
     )(
         lengths,
         queries.reshape(shape),
-        cached_key_rows,
-        cached_value_rows,
+        pltpu.with_memory_space_constraint(cached_key_rows, pltpu.HBM),
+        pltpu.with_memory_space_constraint(cached_value_rows, pltpu.HBM),
         fresh_keys.astype(jnp.float32),
         *after,
     )
@@ -500,7 +532,8 @@
     mate_numbers = swap(numbers, "wide", core_bit)
     mate_cotangent = swap(wait_for(cotangent, mate_numbers), "wide", core_bit)
     up_maps = {0: flattened_up}
-    own_parts = [flattened_down[p * part_rows : (p + 1) * part_rows] for p in range(parts)]
+    own_parts = cut(flattened_down, parts)
+    own_parts, own_buffers = own_parts[:parts], own_parts[parts:]
     for m in near:
         up_maps[m] = swap(wait_for(flattened_up, *own_parts), "wide", m)
     for m in far:
@@ -546,10 +579,12 @@
         for bit in order:
             sent = own_parts[p]
             if len(held) > 1:
-                sent = jnp.pad(sent, ((0, (len(held) - 1) * part_rows), (0, 0)))
+                sent = own_buffers[p]
+                if len(held) > 2:
+                    sent = jnp.pad(sent, ((0, (len(held) - 2) * part_rows), (0, 0)))
                 for k, m in enumerate(held[1:], 1):
-                    sent = place(sent, down_parts[m, p], k, (cached, base_values))
-                second_sent.append(sent)
+                    sent, token = place(sent, down_parts[m, p], k, (cached, base_values))
+                    second_sent.append(token)
             came = swap(sent, "wide", bit)
             for k, m in enumerate(held):
                 down_parts[m | bit, p] = came[k * part_rows : (k + 1) * part_rows]
@@ -574,7 +609,7 @@
         [cotangent, mate_cotangent],
         up_chunks,
         rank,
-        after=(*first_maps, *second_sent),
+        after=second_sent,
     )
     back = sum_over("narrow", part_back, sent_back)
 
@@ -585,7 +620,7 @@
             groups.setdefault((level, p, m == order[level]), []).append(m)
     group_keys = sorted(groups, key=lambda key: (-key[0], key[2]))
     last_level = len(chip_bits) - 1
-    own_down, *results = gradient_chunks(
+    own_down, *results, token = gradient_chunks(
         token_codes,
         token_rewards,
         back,
@@ -604,7 +639,6 @@
         (mate_slice,),
     )
     grads = dict(zip(group_keys, results))
-    token = own_down
     arrived = {(m, p): [] for m in masks for p in range(parts)}
 
     def send_level(level):
@@ -625,26 +659,25 @@
         rows=(decode_slice, mate_slice),
         after=(token,),
     )
-    token = part_hidden
+    token = sent_hidden
     for level in reversed(range(last_level)):
         added = [key for key in group_keys if key[0] == level]
-        sums = add_arrived(
+        *sums, token = add_arrived(
             [(grads[key], [arrived[m, key[1]] for m in groups[key]]) for key in added], (token,)
         )
         grads.update(zip(added, sums))
         send_level(level)
-        token = sums[0]
     early = [[arrived[0, p][:-1] for p in range(parts)]]
-    (own_down,) = add_arrived([(own_down, *early)], (token,), jnp.float32)
+    own_down, own_token = add_arrived([(own_down, *early)], (token,), jnp.float32)
     last_down = [arrived[0, p][-1:] for p in range(parts)]
 
     hidden = sum_over(
         "narrow",
         part_hidden,
         sent_hidden,
-        [(token,), (own_down,)],
-    )
-    own_up, *up_results = gradient_chunks(
+        [(token,), (own_token,)],
+    )
+    own_up, *up_results, token = gradient_chunks(
         token_codes,
         token_rewards,
         hidden,
@@ -653,15 +686,15 @@
         [([m * owner_totals], owner_totals, jnp.bfloat16 if m else jnp.float32, ()) for m in masks],
     )
     own_delta, mate_delta = row_deltas(
-        row_codes, hidden, 2 * token_count, tile, up_chunks, (own_up,)
+        row_codes, hidden, 2 * token_count, tile, up_chunks, (token,)
     )
     mate_delta = wait_for(mate_delta, *[came for part in last_down for came, _ in part])
     came_up = [(swap(result, "wide", m), 0) for m, result in zip(masks[1:], up_results)]
-    (grad_up,) = add_arrived([(own_up, [came_up])], (), jnp.float32)
-    (grad_down,) = add_arrived([(own_down, last_down)], (), jnp.float32)
+    grad_down, token = add_arrived([(own_down, last_down)], (), jnp.float32)
     attended, fresh_values = finish_rows(
         cached, own_weight, base_values, own_delta, swap(mate_delta, "wide", core_bit)
     )
+    grad_up, _ = add_arrived([(own_up, [came_up])], (token,), jnp.float32)
     return (
         attended,
         fresh_values,

time: 101 us -> 98.9 us (0.979)
  local copies, waits for them, and re-layouts: 5.65 us -> 1.01 us
  Pallas kernels: 43.3 us -> 47.5 us
  matrix products: 6.13 us -> 3.82 us
  waiting for transfers between devices: 14.4 us -> 16.1 us
    pallas_call x0 -> x1, Pallas kernels: none -> 2.95 us  [cut(): pl.pallas_call(cut_kernel, out_shape=[SENT((rows, width), maps.dtype)] *...]
    slice x1 -> x0, local copies, waits for them, and re-layouts: 2.31 us -> none  [per_device(): flattened_down[p * part_rows:(p + 1) * part_rows]]
    pad x2 -> x0, local copies, waits for them, and re-layouts: 2.31 us -> none  [per_device(): sent = jnp.pad(sent, ((0, (len(held) - 1) * part_rows), (0, 0)))]
    dot_general x1, matrix products: 3.08 us -> 0.82 us  [per_device(): jnp.dot(hidden_rows, value_matrix, preferred_element_type=jnp.float32)]
    ppermute x25, waiting for transfers between devices: 14.4 us -> 16.1 us  [swap(): return lax.ppermute(array, axis, [(i, i ^ mask) for i in range(count)])]
  transfers between devices with their start and end apart: 25 -> 25, of which waited for: 8 -> 8; matrix products, arithmetic and copies ran while one was open for 12% -> 5% of each run, Pallas kernels for 42% -> 47%
where the time goes in v6:
time: 98.9 us; the launch traced here: 98.7 us
  Pallas kernels  47.5 us (48%)
  starting transfers between devices  28.4 us (29%)
  waiting for transfers between devices  16.1 us (16%)
  matrix products  3.82 us (4%)
  local copies, waits for them, and re-layouts  1.01 us (1%)
    ppermute x25, starting transfers between devices, swap(): return lax.ppermute(array, axis, [(i, i ^ mask) for i in range(count)])  28.4 us
    ppermute x25, waiting for transfers between devices, swap(): return lax.ppermute(array, axis, [(i, i ^ mask) for i in range(count)])  16.1 us
    pallas_call x2, Pallas kernels, project_tokens(): pl.pallas_call(functools.partial(token_kernel, code_list([(bases, chunk.s...  15.1 us
    pallas_call x2, Pallas kernels, gradient_chunks(): pl.pallas_call(functools.partial(gradient_kernel, code_list([(chunk[0], r...  14.8 us
    pallas_call x1, Pallas kernels, attend_cached(): pl.pallas_call(functools.partial(attend_kernel, kv_width // HEAD_SIZE), g...  6.09 us
    pallas_call x4, Pallas kernels, add_arrived(): pl.pallas_call(functools.partial(add_kernel, [[[k for _, k in arrived] fo...  4.29 us
    dot_general x1, matrix products, per_device(): jnp.dot(hidden_rows, key_matrix, preferred_element_type=jnp.float32)  3.01 us
    pallas_call x1, Pallas kernels, cut(): pl.pallas_call(cut_kernel, out_shape=[SENT((rows, width), maps.dtype)] *...  2.95 us
  transfers between devices with their start and end apart: 25, of which 8 were waited for; matrix products, arithmetic and copies ran while one was open for 5% of the time, Pallas kernels for 47%

profile of v6, /device:TPU:0, one launch (start us, length us, event | category | flops | bytes accessed | tf_op | source)
XLA Modules:
  0.0 98.7 jit_solution(5894210744637343140)
XLA Ops:
  3.1 3.0 %shard_map.165 = (bf16[128,2048]{1,0:T(8,128)(2,1)}, bf16[128,2048]{1,0:T(8,128)(2,1)}, bf16[256,2048]{1,0:T(8,128)(2,1)}, bf16[256,2048]{1,0:T(8,128)(2,1)}) custom-call(bf16[256,2048]{1,0:T(8,128)(2,1)} %bitcast.16), custom_call_target="tpu_custom_call" | custom-call | flops 1 | bytes 1 | tf_op jit(solution)/shard_map/pallas_call | solution.py:216
  6.0 2.7 %collective-permute-start.2 = (bf16[256,256]{1,0:T(8,128)(2,1)}, bf16[256,256]{1,0:T(8,128)(2,1)S(1)}, u32[]{:S(2)}, u32[]{:S(2)}) collective-permute-start(bf16[256,256]{1,0:T(8,128)(2,1)} %bitcast.19), channel_id=1, source_target_pairs={{0,16},{4,20},{8,24},{12,28},{16,0},{20,4},{24,8},{28,12},{1,17},{... | collective-permute-start | bytes 393224 | tf_op jit(solution)/shard_map/ppermute | solution.py:24
  8.7 1.5 %collective-permute-start.1 = (bf16[256,256]{1,0:T(8,128)(2,1)}, bf16[256,256]{1,0:T(8,128)(2,1)S(1)}, u32[]{:S(2)}, u32[]{:S(2)}) collective-permute-start(bf16[256,256]{1,0:T(8,128)(2,1)} %bitcast.20), channel_id=1, source_target_pairs={{0,8},{4,12},{8,0},{12,4},{16,24},{20,28},{24,16},{28,20},{1,9},{5... | collective-permute-start | bytes 393224 | tf_op jit(solution)/shard_map/ppermute | solution.py:24
  12.9 3.2 %collective-permute-start.10 = (bf16[256,256]{1,0:T(8,128)(2,1)}, bf16[256,256]{1,0:T(8,128)(2,1)S(1)}, u32[]{:S(2)}, u32[]{:S(2)}) collective-permute-start(bf16[256,256]{1,0:T(8,128)(2,1)} %bitcast.21), channel_id=1, source_target_pairs={{0,24},{4,28},{8,16},{12,20},{16,8},{20,12},{24,0},{28,4},{1,25},{... | collective-permute-start | bytes 393224 | tf_op jit(solution)/shard_map/ppermute | solution.py:24
  16.2 3.0 %fusion.fresh_ref = f32[32,256]{1,0:T(8,128)S(1)} fusion(bf16[32,8192]{1,0:T(8,128)(2,1)S(1)} %copy-done, bf16[8192,256]{1,0:T(8,128)(2,1)} %param.20), kind=kOutput, calls=%fused_computation.1 | convolution fusion | flops 134234112 | bytes 4751360 | tf_op jit(solution)/shard_map/dot_general | solution.py:566
  19.2 6.1 %shard_map.166 = (f32[32,16,128]{2,1,0:T(8,128)S(1)}, f32[32,16,128]{2,1,0:T(8,128)S(1)}) custom-call(s32[32]{0:T(128)S(1)} %copy-done.4, bf16[32,16,128]{2,1,0:T(8,128)(2,1)S(1)} %bitcast.18, bf16[32,256,256]{2,1,0:T(8,128)(2,1)} %keys_ref.1, bf16[32,256,256]{2,1,0:T(8,128)(2,1)} %values_ref.1, f32[32,256]{1,0:T(8,128)S(1)} %fusion.fresh_ref), custom_call_target="tpu_custom_call" | custom-call | flops 1 | bytes 1 | tf_op jit(solution)/shard_map/pallas_call | solution.py:470
  29.3 1.6 %shard_map.169 = (f32[16,2048]{1,0:T(8,128)S(1)}, bf16[16,2048]{1,0:T(8,128)(2,1)S(1)}) custom-call(s32[1,2560]{1,0:T(1,128)S(1)} %fusion.1.codes_ref, bf16[1024,256]{1,0:T(8,128)(2,1)S(1)} %copy-done.2, bf16[1024,256]{1,0:T(8,128)(2,1)S(1)} %collective-permute-done.4.refs_1_.mate_ref, bf16[256,256]{1,0:T(8,128)(2,1)S(1)} %bitcast.22, ...), custom_call_target="tpu_custom_call" | custom-call | flops 1 | bytes 1 | tf_op jit(solution)/shard_map/pallas_call | solution.py:133
  30.9 1.6 %collective-permute-start.11 = (bf16[16,2048]{1,0:T(8,128)(2,1)S(1)}, bf16[16,2048]{1,0:T(8,128)(2,1)S(1)}, u32[]{:S(2)}, u32[]{:S(2)}) collective-permute-start(bf16[16,2048]{1,0:T(8,128)(2,1)S(1)} %get-tuple-element.79), channel_id=1, source_target_pairs={{0,1},{1,0},{2,3},{3,2},{4,5},{5,4},{6,7},{7,6},{8,9},{9,8},{10,11... | collective-permute-start | bytes 196616 | tf_op jit(solution)/shard_map/ppermute | solution.py:24
  32.6 2.6 %collective-permute-done.11.came_ref = bf16[16,2048]{1,0:T(8,128)(2,1)S(1)} collective-permute-done((bf16[16,2048]{1,0:T(8,128)(2,1)S(1)}, bf16[16,2048]{1,0:T(8,128)(2,1)S(1)}, u32[]{:S(2)}, u32[]{:S(2)}) %collective-permute-start.11) | collective-permute-done | bytes 65568 | tf_op jit(solution)/shard_map/ppermute | solution.py:24
  35.2 2.7 %collective-permute-start.12 = (bf16[16,2048]{1,0:T(8,128)(2,1)S(1)}, bf16[16,2048]{1,0:T(8,128)(2,1)S(1)}, u32[]{:S(2)}, u32[]{:S(2)}) collective-permute-start(bf16[16,2048]{1,0:T(8,128)(2,1)S(1)} %get-tuple-element.81), channel_id=1, source_target_pairs={{0,2},{1,3},{2,0},{3,1},{4,6},{5,7},{6,4},{7,5},{8,10},{9,11},{10,... | collective-permute-start | bytes 196616 | tf_op jit(solution)/shard_map/ppermute | solution.py:24
  37.9 2.6 %collective-permute-done.12.came_ref = bf16[16,2048]{1,0:T(8,128)(2,1)S(1)} collective-permute-done((bf16[16,2048]{1,0:T(8,128)(2,1)S(1)}, bf16[16,2048]{1,0:T(8,128)(2,1)S(1)}, u32[]{:S(2)}, u32[]{:S(2)}) %collective-permute-start.12) | collective-permute-done | bytes 65568 | tf_op jit(solution)/shard_map/ppermute | solution.py:24
  41.1 12.9 %shard_map.172 = (f32[256,2048]{1,0:T(8,128)S(1)}, bf16[128,2048]{1,0:T(8,128)(2,1)}, bf16[128,2048]{1,0:T(8,128)(2,1)}, bf16[128,2048]{1,0:T(8,128)(2,1)}, bf16...) custom-call(s32[1,2048]{1,0:T(1,128)S(1)} %fusion.2.codes_ref, ...), custom_call_target="tpu_custom_call" | custom-call | flops 1 | bytes 1 | tf_op jit(solution)/shard_map/pallas_call | solution.py:308
  55.4 1.5 %collective-permute-start.14 = (bf16[128,2048]{1,0:T(8,128)(2,1)}, bf16[128,2048]{1,0:T(8,128)(2,1)S(1)}, u32[]{:S(2)}, u32[]{:S(2)}) collective-permute-start(bf16[128,2048]{1,0:T(8,128)(2,1)} %get-tuple-element.89), channel_id=1, source_target_pairs={{0,16},{4,20},{8,24},{12,28},{16,0},{20,4},{24,8},{28,12},{1,17},{... | collective-permute-start | bytes 1572872 | tf_op jit(solution)/shard_map/ppermute | solution.py:24
  58.1 13.5 %shard_map.173 = (f32[16,2560]{1,0:T(8,128)S(1)}, bf16[16,2560]{1,0:T(8,128)(2,1)S(1)}) custom-call(s32[1,2560]{1,0:T(1,128)S(1)} %fusion.1.codes_ref, bf16[1024,2048]{1,0:T(8,128)(2,1)} %refs_0_.3, bf16[1024,2048]{1,0:T(8,128)(2,1)} %collective-permute-done.3.mate_ref.refs_1_, bf16[32,2048]{1,0:T(8,128)(2,1)S(1)} %constant_dynamic-slice_fusion.refs_2_, ...), custom_call_target="tpu_custom_call" | custom-call | flops 1 | bytes 1 | tf_op jit(solution)/shard_map/pallas_call | solution.py:133
  73.0 1.4 %collective-permute-start.20 = (bf16[128,2048]{1,0:T(8,128)(2,1)}, bf16[128,2048]{1,0:T(8,128)(2,1)S(1)}, u32[]{:S(2)}, u32[]{:S(2)}) collective-permute-start(bf16[128,2048]{1,0:T(8,128)(2,1)} %get-tuple-element.108), channel_id=1, source_target_pairs={{0,16},{4,20},{8,24},{12,28},{16,0},{20,4},{24,8},{28,12},{1,17},{... | collective-permute-start | bytes 1572872 | tf_op jit(solution)/shard_map/ppermute | solution.py:24
  74.4 1.4 %collective-permute-start.19 = (bf16[128,2048]{1,0:T(8,128)(2,1)}, bf16[128,2048]{1,0:T(8,128)(2,1)S(1)}, u32[]{:S(2)}, u32[]{:S(2)}) collective-permute-start(bf16[128,2048]{1,0:T(8,128)(2,1)} %get-tuple-element.106), channel_id=1, source_target_pairs={{0,8},{4,12},{8,0},{12,4},{16,24},{20,28},{24,16},{28,20},{1,9},{5... | collective-permute-start | bytes 1572872 | tf_op jit(solution)/shard_map/ppermute | solution.py:24
  75.8 1.6 %collective-permute-start.13 = (bf16[16,2560]{1,0:T(8,128)(2,1)S(1)}, bf16[16,2560]{1,0:T(8,128)(2,1)S(1)}, u32[]{:S(2)}, u32[]{:S(2)}) collective-permute-start(bf16[16,2560]{1,0:T(8,128)(2,1)S(1)} %get-tuple-element.85.refs_4_), channel_id=1, source_target_pairs={{0,1},{1,0},{2,3},{3,2},{4,5},{5,4},{6,7},{7,6},{8,9},{9,8},{10,11... | collective-permute-start | bytes 245768 | tf_op jit(solution)/shard_map/ppermute | solution.py:24
  77.4 3.7 %collective-permute-done.13.came_ref = bf16[16,2560]{1,0:T(8,128)(2,1)S(1)} collective-permute-done((bf16[16,2560]{1,0:T(8,128)(2,1)S(1)}, bf16[16,2560]{1,0:T(8,128)(2,1)S(1)}, u32[]{:S(2)}, u32[]{:S(2)}) %collective-permute-start.13) | collective-permute-done | bytes 81952 | tf_op jit(solution)/shard_map/ppermute | solution.py:24
  81.2 2.1 %collective-permute-start.16 = (bf16[16,2560]{1,0:T(8,128)(2,1)S(1)}, bf16[16,2560]{1,0:T(8,128)(2,1)S(1)}, u32[]{:S(2)}, u32[]{:S(2)}) collective-permute-start(bf16[16,2560]{1,0:T(8,128)(2,1)S(1)} %get-tuple-element.94), channel_id=1, source_target_pairs={{0,2},{1,3},{2,0},{3,1},{4,6},{5,7},{6,4},{7,5},{8,10},{9,11},{10,... | collective-permute-start | bytes 245768 | tf_op jit(solution)/shard_map/ppermute | solution.py:24
  83.8 2.7 %collective-permute-done.16.came_ref = bf16[16,2560]{1,0:T(8,128)(2,1)S(1)} collective-permute-done((bf16[16,2560]{1,0:T(8,128)(2,1)S(1)}, bf16[16,2560]{1,0:T(8,128)(2,1)S(1)}, u32[]{:S(2)}, u32[]{:S(2)}) %collective-permute-start.16) | collective-permute-done | bytes 81952 | tf_op jit(solution)/shard_map/ppermute | solution.py:24
  87.2 1.9 %shard_map.178 = (f32[256,256]{1,0:T(8,128)S(1)}, bf16[256,256]{1,0:T(8,128)(2,1)}, bf16[256,256]{1,0:T(8,128)(2,1)}, bf16[256,256]{1,0:T(8,128)(2,1)}, f32[8,128]{1,0:T(8,128)S(1)}) custom-call(s32[1,2048]{1,0:T(1,128)S(1)} %fusion.2.codes_ref, s32[1,2048]{1,0:T(1,128)S(1)} %bitcast.25, f32[16,2560]{1,0:T(8,128)S(1)} %get-tuple-element.101.factor_ref.rank_ref, ...), custom_call_target="tpu_custom_call" | custom-call | flops 1 | bytes 1 | tf_op jit(solution)/shard_map/pallas_call | solution.py:308
  90.9 1.7 %collective-permute-start.24 = (bf16[256,256]{1,0:T(8,128)(2,1)}, bf16[256,256]{1,0:T(8,128)(2,1)S(1)}, u32[]{:S(2)}, u32[]{:S(2)}) collective-permute-start(bf16[256,256]{1,0:T(8,128)(2,1)} %get-tuple-element.117), channel_id=1, source_target_pairs={{0,24},{4,28},{8,16},{12,20},{16,8},{20,12},{24,0},{28,4},{1,25},{... | collective-permute-start | bytes 393224 | tf_op jit(solution)/shard_map/ppermute | solution.py:24
  93.9 1.6 %shard_map.181 = (f32[256,2048]{1,0:T(8,128)}, f32[8,128]{1,0:T(8,128)S(1)}) custom-call(f32[256,2048]{1,0:T(8,128)S(1)} %get-tuple-element.112.refs_0_, bf16[128,2048]{1,0:T(8,128)(2,1)S(1)} %collective-permute-done.19.refs_1_, bf16[128,2048]{1,0:T(8,128)(2,1)S(1)} %collective-permute-done.20.refs_2_), custom_call_target="tpu_custom_call" | custom-call | flops 1 | bytes 1 | tf_op jit(solution)/shard_map/pallas_call | solution.py:357
  95.5 1.5 %collective-permute-done.24.refs_3_ = bf16[256,256]{1,0:T(8,128)(2,1)S(1)} collective-permute-done((bf16[256,256]{1,0:T(8,128)(2,1)}, bf16[256,256]{1,0:T(8,128)(2,1)S(1)}, u32[]{:S(2)}, u32[]{:S(2)}) %collective-permute-start.24) | collective-permute-done | bytes 131104 | tf_op jit(solution)/shard_map/ppermute | solution.py:24
  (73 shorter events, 19.7 us)
Async XLA Ops:
  2.7 38.4 %collective-permute-start.3 = (bf16[1024,2048]{1,0:T(8,128)(2,1)}, bf16[1024,2048]{1,0:T(8,128)(2,1)}, u32[]{:S(2)}, u32[]{:S(2)}) collective-permute-start(bf16[1024,2048]{1,0:T(8,128)(2,1)} %refs_0_.3), channel_id=1, source_target_pairs={{0,4},{4,0},{8,12},{12,8},{16,20},{20,16},{24,28},{28,24},{1,5},{5... | collective-permute-start | bytes 12582920 | tf_op jit(solution)/shard_map/ppermute | solution.py:24
  6.0 6.9 %collective-permute-start.2 = (bf16[256,256]{1,0:T(8,128)(2,1)}, bf16[256,256]{1,0:T(8,128)(2,1)S(1)}, u32[]{:S(2)}, u32[]{:S(2)}) collective-permute-start(bf16[256,256]{1,0:T(8,128)(2,1)} %bitcast.19), channel_id=1, source_target_pairs={{0,16},{4,20},{8,24},{12,28},{16,0},{20,4},{24,8},{28,12},{1,17},{... | collective-permute-start | bytes 393224 | tf_op jit(solution)/shard_map/ppermute | solution.py:24
  8.7 7.5 %collective-permute-start.1 = (bf16[256,256]{1,0:T(8,128)(2,1)}, bf16[256,256]{1,0:T(8,128)(2,1)S(1)}, u32[]{:S(2)}, u32[]{:S(2)}) collective-permute-start(bf16[256,256]{1,0:T(8,128)(2,1)} %bitcast.20), channel_id=1, source_target_pairs={{0,8},{4,12},{8,0},{12,4},{16,24},{20,28},{24,16},{28,20},{1,9},{5... | collective-permute-start | bytes 393224 | tf_op jit(solution)/shard_map/ppermute | solution.py:24
  10.2 17.5 %collective-permute-start.6 = (bf16[128,2048]{1,0:T(8,128)(2,1)}, bf16[128,2048]{1,0:T(8,128)(2,1)S(1)}, u32[]{:S(2)}, u32[]{:S(2)}) collective-permute-start(bf16[128,2048]{1,0:T(8,128)(2,1)} %get-tuple-element.62), channel_id=1, source_target_pairs={{0,8},{4,12},{8,0},{12,4},{16,24},{20,28},{24,16},{28,20},{1,9},{5... | collective-permute-start | bytes 1572872 | tf_op jit(solution)/shard_map/ppermute | solution.py:24
  10.7 15.5 %collective-permute-start.8 = (bf16[128,2048]{1,0:T(8,128)(2,1)}, bf16[128,2048]{1,0:T(8,128)(2,1)S(1)}, u32[]{:S(2)}, u32[]{:S(2)}) collective-permute-start(bf16[128,2048]{1,0:T(8,128)(2,1)} %get-tuple-element.63), channel_id=1, source_target_pairs={{0,16},{4,20},{8,24},{12,28},{16,0},{20,4},{24,8},{28,12},{1,17},{... | collective-permute-start | bytes 1572872 | tf_op jit(solution)/shard_map/ppermute | solution.py:24
  12.9 16.3 %collective-permute-start.10 = (bf16[256,256]{1,0:T(8,128)(2,1)}, bf16[256,256]{1,0:T(8,128)(2,1)S(1)}, u32[]{:S(2)}, u32[]{:S(2)}) collective-permute-start(bf16[256,256]{1,0:T(8,128)(2,1)} %bitcast.21), channel_id=1, source_target_pairs={{0,24},{4,28},{8,16},{12,20},{16,8},{20,12},{24,0},{28,4},{1,25},{... | collective-permute-start | bytes 393224 | tf_op jit(solution)/shard_map/ppermute | solution.py:24
  16.2 13.1 %collective-permute-start.4 = (bf16[1024,256]{1,0:T(8,128)(2,1)}, bf16[1024,256]{1,0:T(8,128)(2,1)S(1)}, u32[]{:S(2)}, u32[]{:S(2)}) collective-permute-start(bf16[1024,256]{1,0:T(8,128)(2,1)} %own_ref.3), channel_id=1, source_target_pairs={{0,4},{4,0},{8,12},{12,8},{16,20},{20,16},{24,28},{28,24},{1,5},{5... | collective-permute-start | bytes 1572872 | tf_op jit(solution)/shard_map/ppermute | solution.py:24
  27.1 26.9 %collective-permute-start.9 = (bf16[256,2048]{1,0:T(8,128)(2,1)}, bf16[256,2048]{1,0:T(8,128)(2,1)S(1)}, u32[]{:S(2)}, u32[]{:S(2)}) collective-permute-start(bf16[256,2048]{1,0:T(8,128)(2,1)} %get-tuple-element.74), channel_id=1, source_target_pairs={{0,8},{4,12},{8,0},{12,4},{16,24},{20,28},{24,16},{28,20},{1,9},{5... | collective-permute-start | bytes 3145736 | tf_op jit(solution)/shard_map/ppermute | solution.py:24
  28.5 25.5 %collective-permute-start.7 = (bf16[256,2048]{1,0:T(8,128)(2,1)}, bf16[256,2048]{1,0:T(8,128)(2,1)S(1)}, u32[]{:S(2)}, u32[]{:S(2)}) collective-permute-start(bf16[256,2048]{1,0:T(8,128)(2,1)} %get-tuple-element.72), channel_id=1, source_target_pairs={{0,16},{4,20},{8,24},{12,28},{16,0},{20,4},{24,8},{28,12},{1,17},{... | collective-permute-start | bytes 3145736 | tf_op jit(solution)/shard_map/ppermute | solution.py:24
  30.9 4.3 %collective-permute-start.11 = (bf16[16,2048]{1,0:T(8,128)(2,1)S(1)}, bf16[16,2048]{1,0:T(8,128)(2,1)S(1)}, u32[]{:S(2)}, u32[]{:S(2)}) collective-permute-start(bf16[16,2048]{1,0:T(8,128)(2,1)S(1)} %get-tuple-element.79), channel_id=1, source_target_pairs={{0,1},{1,0},{2,3},{3,2},{4,5},{5,4},{6,7},{7,6},{8,9},{9,8},{10,11... | collective-permute-start | bytes 196616 | tf_op jit(solution)/shard_map/ppermute | solution.py:24
  32.5 8.6 %collective-permute-start.5 = (bf16[32,2048]{1,0:T(8,128)(2,1)S(1)}, bf16[32,2048]{1,0:T(8,128)(2,1)S(1)}, u32[]{:S(2)}, u32[]{:S(2)}) collective-permute-start(bf16[32,2048]{1,0:T(8,128)(2,1)S(1)} %constant_dynamic-slice_fusion.refs_2_), channel_id=1, source_target_pairs={{0,4},{4,0},{8,12},{12,8},{16,20},{20,16},{24,28},{28,24},{1,5},{5... | collective-permute-start | bytes 393224 | tf_op jit(solution)/shard_map/ppermute | solution.py:24
  35.2 5.2 %collective-permute-start.12 = (bf16[16,2048]{1,0:T(8,128)(2,1)S(1)}, bf16[16,2048]{1,0:T(8,128)(2,1)S(1)}, u32[]{:S(2)}, u32[]{:S(2)}) collective-permute-start(bf16[16,2048]{1,0:T(8,128)(2,1)S(1)} %get-tuple-element.81), channel_id=1, source_target_pairs={{0,2},{1,3},{2,0},{3,1},{4,6},{5,7},{6,4},{7,5},{8,10},{9,11},{10,... | collective-permute-start | bytes 196616 | tf_op jit(solution)/shard_map/ppermute | solution.py:24
  54.0 17.6 %collective-permute-start.15 = (bf16[128,2048]{1,0:T(8,128)(2,1)}, bf16[128,2048]{1,0:T(8,128)(2,1)S(1)}, u32[]{:S(2)}, u32[]{:S(2)}) collective-permute-start(bf16[128,2048]{1,0:T(8,128)(2,1)} %get-tuple-element.91), channel_id=1, source_target_pairs={{0,8},{4,12},{8,0},{12,4},{16,24},{20,28},{24,16},{28,20},{1,9},{5... | collective-permute-start | bytes 1572872 | tf_op jit(solution)/shard_map/ppermute | solution.py:24
  55.4 16.2 %collective-permute-start.14 = (bf16[128,2048]{1,0:T(8,128)(2,1)}, bf16[128,2048]{1,0:T(8,128)(2,1)S(1)}, u32[]{:S(2)}, u32[]{:S(2)}) collective-permute-start(bf16[128,2048]{1,0:T(8,128)(2,1)} %get-tuple-element.89), channel_id=1, source_target_pairs={{0,16},{4,20},{8,24},{12,28},{16,0},{20,4},{24,8},{28,12},{1,17},{... | collective-permute-start | bytes 1572872 | tf_op jit(solution)/shard_map/ppermute | solution.py:24
  56.9 26.3 %collective-permute-start.18 = (bf16[128,2048]{1,0:T(8,128)(2,1)}, bf16[128,2048]{1,0:T(8,128)(2,1)S(1)}, u32[]{:S(2)}, u32[]{:S(2)}) collective-permute-start(bf16[128,2048]{1,0:T(8,128)(2,1)} %get-tuple-element.99), channel_id=1, source_target_pairs={{0,8},{4,12},{8,0},{12,4},{16,24},{20,28},{24,16},{28,20},{1,9},{5... | collective-permute-start | bytes 1572872 | tf_op jit(solution)/shard_map/ppermute | solution.py:24
  57.5 25.7 %collective-permute-start.17 = (bf16[128,2048]{1,0:T(8,128)(2,1)}, bf16[128,2048]{1,0:T(8,128)(2,1)S(1)}, u32[]{:S(2)}, u32[]{:S(2)}) collective-permute-start(bf16[128,2048]{1,0:T(8,128)(2,1)} %get-tuple-element.97), channel_id=1, source_target_pairs={{0,16},{4,20},{8,24},{12,28},{16,0},{20,4},{24,8},{28,12},{1,17},{... | collective-permute-start | bytes 1572872 | tf_op jit(solution)/shard_map/ppermute | solution.py:24
  73.0 20.9 %collective-permute-start.20 = (bf16[128,2048]{1,0:T(8,128)(2,1)}, bf16[128,2048]{1,0:T(8,128)(2,1)S(1)}, u32[]{:S(2)}, u32[]{:S(2)}) collective-permute-start(bf16[128,2048]{1,0:T(8,128)(2,1)} %get-tuple-element.108), channel_id=1, source_target_pairs={{0,16},{4,20},{8,24},{12,28},{16,0},{20,4},{24,8},{28,12},{1,17},{... | collective-permute-start | bytes 1572872 | tf_op jit(solution)/shard_map/ppermute | solution.py:24
  74.4 19.5 %collective-permute-start.19 = (bf16[128,2048]{1,0:T(8,128)(2,1)}, bf16[128,2048]{1,0:T(8,128)(2,1)S(1)}, u32[]{:S(2)}, u32[]{:S(2)}) collective-permute-start(bf16[128,2048]{1,0:T(8,128)(2,1)} %get-tuple-element.106), channel_id=1, source_target_pairs={{0,8},{4,12},{8,0},{12,4},{16,24},{20,28},{24,16},{28,20},{1,9},{5... | collective-permute-start | bytes 1572872 | tf_op jit(solution)/shard_map/ppermute | solution.py:24
  75.8 5.3 %collective-permute-start.13 = (bf16[16,2560]{1,0:T(8,128)(2,1)S(1)}, bf16[16,2560]{1,0:T(8,128)(2,1)S(1)}, u32[]{:S(2)}, u32[]{:S(2)}) collective-permute-start(bf16[16,2560]{1,0:T(8,128)(2,1)S(1)} %get-tuple-element.85.refs_4_), channel_id=1, source_target_pairs={{0,1},{1,0},{2,3},{3,2},{4,5},{5,4},{6,7},{7,6},{8,9},{9,8},{10,11... | collective-permute-start | bytes 245768 | tf_op jit(solution)/shard_map/ppermute | solution.py:24
  81.2 5.4 %collective-permute-start.16 = (bf16[16,2560]{1,0:T(8,128)(2,1)S(1)}, bf16[16,2560]{1,0:T(8,128)(2,1)S(1)}, u32[]{:S(2)}, u32[]{:S(2)}) collective-permute-start(bf16[16,2560]{1,0:T(8,128)(2,1)S(1)} %get-tuple-element.94), channel_id=1, source_target_pairs={{0,2},{1,3},{2,0},{3,1},{4,6},{5,7},{6,4},{7,5},{8,10},{9,11},{10,... | collective-permute-start | bytes 245768 | tf_op jit(solution)/shard_map/ppermute | solution.py:24
  89.1 6.4 %collective-permute-start.22 = (bf16[256,256]{1,0:T(8,128)(2,1)}, bf16[256,256]{1,0:T(8,128)(2,1)S(1)}, u32[]{:S(2)}, u32[]{:S(2)}) collective-permute-start(bf16[256,256]{1,0:T(8,128)(2,1)} %get-tuple-element.115), channel_id=1, source_target_pairs={{0,8},{4,12},{8,0},{12,4},{16,24},{20,28},{24,16},{28,20},{1,9},{5... | collective-permute-start | bytes 393224 | tf_op jit(solution)/shard_map/ppermute | solution.py:24
  89.7 5.8 %collective-permute-start.23 = (bf16[256,256]{1,0:T(8,128)(2,1)}, bf16[256,256]{1,0:T(8,128)(2,1)S(1)}, u32[]{:S(2)}, u32[]{:S(2)}) collective-permute-start(bf16[256,256]{1,0:T(8,128)(2,1)} %get-tuple-element.116), channel_id=1, source_target_pairs={{0,16},{4,20},{8,24},{12,28},{16,0},{20,4},{24,8},{28,12},{1,17},{... | collective-permute-start | bytes 393224 | tf_op jit(solution)/shard_map/ppermute | solution.py:24
  90.9 6.1 %collective-permute-start.24 = (bf16[256,256]{1,0:T(8,128)(2,1)}, bf16[256,256]{1,0:T(8,128)(2,1)S(1)}, u32[]{:S(2)}, u32[]{:S(2)}) collective-permute-start(bf16[256,256]{1,0:T(8,128)(2,1)} %get-tuple-element.117), channel_id=1, source_target_pairs={{0,24},{4,28},{8,16},{12,20},{16,8},{20,12},{24,0},{28,4},{1,25},{... | collective-permute-start | bytes 393224 | tf_op jit(solution)/shard_map/ppermute | solution.py:24
  93.9 3.9 %collective-permute-start.21 = (bf16[32,256]{1,0:T(8,128)(2,1)S(1)}, bf16[32,256]{1,0:T(8,128)(2,1)S(1)}, u32[]{:S(2)}, u32[]{:S(2)}) collective-permute-start(bf16[32,256]{1,0:T(8,128)(2,1)S(1)} %get-tuple-element.109), channel_id=1, source_target_pairs={{0,4},{4,0},{8,12},{12,8},{16,20},{20,16},{24,28},{28,24},{1,5},{5... | collective-permute-start | bytes 49160 | tf_op jit(solution)/shard_map/ppermute | solution.py:24
  (10 other events, 86.5 us)

commit v7 on v6

--- a/solution.py
+++ b/solution.py
@@ -245,7 +245,10 @@
     )(buffer, piece, *after)
 
 
-def finish_rows_kernel(cached_ref, weight_ref, base_ref, own_ref, mate_ref, attended_ref, fresh_ref):
+def finish_rows_kernel(
+    cached_ref, weight_ref, base_ref, own_ref, mate_ref, attended_ref, fresh_ref, token_ref
+):
+    token_ref[...] = jnp.zeros_like(token_ref)
     delta = own_ref[...].astype(jnp.float32) + mate_ref[...].astype(jnp.float32)
     fresh = (base_ref[...] + delta).astype(jnp.bfloat16)
     fresh_ref[...] = fresh
@@ -264,6 +267,7 @@
         out_shape=[
             jax.ShapeDtypeStruct((row_count, heads * size), jnp.bfloat16),
             jax.ShapeDtypeStruct(base_values.shape, jnp.bfloat16),
+            TOKEN,
         ],
         compiler_params=pltpu.CompilerParams(vmem_limit_bytes=VMEM_LIMIT),
         cost_estimate=SHORT,
@@ -409,32 +413,18 @@
     group = heads // kv_local
     first_row = pl.program_id(0) * block
     inverse = 1.0 / math.sqrt(size)
-    head_of = lax.broadcasted_iota(jnp.int32, (heads, slots), 0) // group
+    head_of = lax.broadcasted_iota(jnp.int32, (heads, size), 0) // group
     slot = lax.broadcasted_iota(jnp.int32, (heads, slots), 1)
-
-    def by_head(pieces):
-        chosen = pieces[0]
-        for h, piece in enumerate(pieces[1:], 1):
-            chosen = jnp.where(head_of[:, : piece.shape[1]] == h, piece, chosen)
-        return chosen
 
     scores, own_scores = [], []
     for r in range(block):
-        queries = queries_ref[r]
-        products = by_head(
-            [
-                times_transposed(queries, keys_ref[r, :, h * size : (h + 1) * size])
-                for h in range(kv_local)
-            ]
+        queries = queries_ref[r].astype(jnp.float32)
+        spread_queries = jnp.concatenate(
+            [jnp.where(head_of == h, queries, 0.0) for h in range(kv_local)], axis=1
         )
+        products = times_transposed(spread_queries.astype(jnp.bfloat16), keys_ref[r])
         scores.append(jnp.where(slot < lengths_ref[first_row + r], inverse * products, NEG_FILL))
-        fresh = by_head(
-            [
-                jnp.broadcast_to(fresh_ref[r : r + 1, h * size : (h + 1) * size], (heads, size))
-                for h in range(kv_local)
-            ]
-        )
-        own_scores.append(queries.astype(jnp.float32) * fresh)
+        own_scores.append(spread_queries * fresh_ref[r : r + 1, :])
     scores = jnp.concatenate(scores)
     own_score = inverse * jnp.sum(jnp.concatenate(own_scores), axis=1, keepdims=True)
     highest = jnp.maximum(jnp.max(scores, axis=1, keepdims=True), own_score)
@@ -445,17 +435,13 @@
     own_weight = (own_exp / denominator).astype(jnp.bfloat16).astype(jnp.float32)
     for r in range(block):
         mine = slice(r * heads, (r + 1) * heads)
-        row_weights = weights[mine].astype(jnp.bfloat16)
-        out_ref[r] = by_head(
-            [
-                jnp.dot(
-                    row_weights,
-                    values_ref[r, :, h * size : (h + 1) * size],
-                    preferred_element_type=jnp.float32,
-                )
-                for h in range(kv_local)
-            ]
+        summed = jnp.dot(
+            weights[mine].astype(jnp.bfloat16), values_ref[r], preferred_element_type=jnp.float32
         )
+        chosen = summed[:, :size]
+        for h in range(1, kv_local):
+            chosen = jnp.where(head_of == h, summed[:, h * size : (h + 1) * size], chosen)
+        out_ref[r] = chosen
         own_ref[r] = jnp.broadcast_to(own_weight[mine], (heads, size))
 
 
@@ -691,10 +677,10 @@
     mate_delta = wait_for(mate_delta, *[came for part in last_down for came, _ in part])
     came_up = [(swap(result, "wide", m), 0) for m, result in zip(masks[1:], up_results)]
     grad_down, token = add_arrived([(own_down, last_down)], (), jnp.float32)
-    attended, fresh_values = finish_rows(
+    attended, fresh_values, rows_token = finish_rows(
         cached, own_weight, base_values, own_delta, swap(mate_delta, "wide", core_bit)
     )
-    grad_up, _ = add_arrived([(own_up, [came_up])], (token,), jnp.float32)
+    grad_up, _ = add_arrived([(own_up, [came_up])], (token, rows_token), jnp.float32)
     return (
         attended,
         fresh_values,

time: 98.9 us -> 98 us (level)
  transfers between devices with their start and end apart: 25 -> 25, of which waited for: 8 -> 8; matrix products, arithmetic and copies ran while one was open for 5% -> 5% of each run, Pallas kernels for 47% -> 48%
where the time goes in v7:
time: 98 us; the launch traced here: 97.7 us
  Pallas kernels  47.5 us (48%)
  starting transfers between devices  28.4 us (29%)
  waiting for transfers between devices  15.2 us (16%)
  matrix products  3.84 us (4%)
  local copies, waits for them, and re-layouts  1 us (1%)
    ppermute x25, starting transfers between devices, swap(): return lax.ppermute(array, axis, [(i, i ^ mask) for i in range(count)])  28.4 us
    ppermute x25, waiting for transfers between devices, swap(): return lax.ppermute(array, axis, [(i, i ^ mask) for i in range(count)])  15.2 us
    pallas_call x2, Pallas kernels, project_tokens(): pl.pallas_call(functools.partial(token_kernel, code_list([(bases, chunk.s...  15.1 us
    pallas_call x2, Pallas kernels, gradient_chunks(): pl.pallas_call(functools.partial(gradient_kernel, code_list([(chunk[0], r...  14.8 us
    pallas_call x1, Pallas kernels, attend_cached(): pl.pallas_call(functools.partial(attend_kernel, kv_width // HEAD_SIZE), g...  6.1 us
    pallas_call x4, Pallas kernels, add_arrived(): pl.pallas_call(functools.partial(add_kernel, [[[k for _, k in arrived] fo...  4.29 us
    dot_general x1, matrix products, per_device(): jnp.dot(hidden_rows, key_matrix, preferred_element_type=jnp.float32)  3.01 us
    pallas_call x1, Pallas kernels, cut(): pl.pallas_call(cut_kernel, out_shape=[SENT((rows, width), maps.dtype)] *...  2.95 us
  transfers between devices with their start and end apart: 25, of which 8 were waited for; matrix products, arithmetic and copies ran while one was open for 5% of the time, Pallas kernels for 48%

profile of v7, /device:TPU:0, one launch (start us, length us, event | category | flops | bytes accessed | tf_op | source)
XLA Modules:
  0.0 97.7 jit_solution(3777173331966870479)
XLA Ops:
  3.1 3.0 %shard_map.165 = (bf16[128,2048]{1,0:T(8,128)(2,1)}, bf16[128,2048]{1,0:T(8,128)(2,1)}, bf16[256,2048]{1,0:T(8,128)(2,1)}, bf16[256,2048]{1,0:T(8,128)(2,1)}) custom-call(bf16[256,2048]{1,0:T(8,128)(2,1)} %bitcast.16), custom_call_target="tpu_custom_call" | custom-call | flops 1 | bytes 1 | tf_op jit(solution)/shard_map/pallas_call | solution.py:216
  6.0 2.7 %collective-permute-start.2 = (bf16[256,256]{1,0:T(8,128)(2,1)}, bf16[256,256]{1,0:T(8,128)(2,1)S(1)}, u32[]{:S(2)}, u32[]{:S(2)}) collective-permute-start(bf16[256,256]{1,0:T(8,128)(2,1)} %bitcast.19), channel_id=1, source_target_pairs={{0,16},{4,20},{8,24},{12,28},{16,0},{20,4},{24,8},{28,12},{1,17},{... | collective-permute-start | bytes 393224 | tf_op jit(solution)/shard_map/ppermute | solution.py:24
  8.7 1.5 %collective-permute-start.1 = (bf16[256,256]{1,0:T(8,128)(2,1)}, bf16[256,256]{1,0:T(8,128)(2,1)S(1)}, u32[]{:S(2)}, u32[]{:S(2)}) collective-permute-start(bf16[256,256]{1,0:T(8,128)(2,1)} %bitcast.20), channel_id=1, source_target_pairs={{0,8},{4,12},{8,0},{12,4},{16,24},{20,28},{24,16},{28,20},{1,9},{5... | collective-permute-start | bytes 393224 | tf_op jit(solution)/shard_map/ppermute | solution.py:24
  12.9 3.2 %collective-permute-start.10 = (bf16[256,256]{1,0:T(8,128)(2,1)}, bf16[256,256]{1,0:T(8,128)(2,1)S(1)}, u32[]{:S(2)}, u32[]{:S(2)}) collective-permute-start(bf16[256,256]{1,0:T(8,128)(2,1)} %bitcast.21), channel_id=1, source_target_pairs={{0,24},{4,28},{8,16},{12,20},{16,8},{20,12},{24,0},{28,4},{1,25},{... | collective-permute-start | bytes 393224 | tf_op jit(solution)/shard_map/ppermute | solution.py:24
  16.2 3.0 %fusion.fresh_ref = f32[32,256]{1,0:T(8,128)S(1)} fusion(bf16[32,8192]{1,0:T(8,128)(2,1)S(1)} %copy-done, bf16[8192,256]{1,0:T(8,128)(2,1)} %param.20), kind=kOutput, calls=%fused_computation.1 | convolution fusion | flops 134234112 | bytes 4751360 | tf_op jit(solution)/shard_map/dot_general | solution.py:552
  19.2 6.1 %shard_map.166 = (f32[32,16,128]{2,1,0:T(8,128)S(1)}, f32[32,16,128]{2,1,0:T(8,128)S(1)}) custom-call(s32[32]{0:T(128)S(1)} %copy-done.4, bf16[32,16,128]{2,1,0:T(8,128)(2,1)S(1)} %bitcast.18, bf16[32,256,256]{2,1,0:T(8,128)(2,1)} %keys_ref.1, bf16[32,256,256]{2,1,0:T(8,128)(2,1)} %values_ref.1, f32[32,256]{1,0:T(8,128)S(1)} %fusion.fresh_ref), custom_call_target="tpu_custom_call" | custom-call | flops 1 | bytes 1 | tf_op jit(solution)/shard_map/pallas_call | solution.py:456
  29.3 1.6 %shard_map.169 = (f32[16,2048]{1,0:T(8,128)S(1)}, bf16[16,2048]{1,0:T(8,128)(2,1)S(1)}) custom-call(s32[1,2560]{1,0:T(1,128)S(1)} %fusion.1.codes_ref, bf16[1024,256]{1,0:T(8,128)(2,1)S(1)} %copy-done.2, bf16[1024,256]{1,0:T(8,128)(2,1)S(1)} %collective-permute-done.4.refs_1_.mate_ref, bf16[256,256]{1,0:T(8,128)(2,1)S(1)} %bitcast.22, ...), custom_call_target="tpu_custom_call" | custom-call | flops 1 | bytes 1 | tf_op jit(solution)/shard_map/pallas_call | solution.py:133
  30.9 1.6 %collective-permute-start.11 = (bf16[16,2048]{1,0:T(8,128)(2,1)S(1)}, bf16[16,2048]{1,0:T(8,128)(2,1)S(1)}, u32[]{:S(2)}, u32[]{:S(2)}) collective-permute-start(bf16[16,2048]{1,0:T(8,128)(2,1)S(1)} %get-tuple-element.80), channel_id=1, source_target_pairs={{0,1},{1,0},{2,3},{3,2},{4,5},{5,4},{6,7},{7,6},{8,9},{9,8},{10,11... | collective-permute-start | bytes 196616 | tf_op jit(solution)/shard_map/ppermute | solution.py:24
  32.6 2.6 %collective-permute-done.11.came_ref = bf16[16,2048]{1,0:T(8,128)(2,1)S(1)} collective-permute-done((bf16[16,2048]{1,0:T(8,128)(2,1)S(1)}, bf16[16,2048]{1,0:T(8,128)(2,1)S(1)}, u32[]{:S(2)}, u32[]{:S(2)}) %collective-permute-start.11) | collective-permute-done | bytes 65568 | tf_op jit(solution)/shard_map/ppermute | solution.py:24
  35.2 2.7 %collective-permute-start.12 = (bf16[16,2048]{1,0:T(8,128)(2,1)S(1)}, bf16[16,2048]{1,0:T(8,128)(2,1)S(1)}, u32[]{:S(2)}, u32[]{:S(2)}) collective-permute-start(bf16[16,2048]{1,0:T(8,128)(2,1)S(1)} %get-tuple-element.82), channel_id=1, source_target_pairs={{0,2},{1,3},{2,0},{3,1},{4,6},{5,7},{6,4},{7,5},{8,10},{9,11},{10,... | collective-permute-start | bytes 196616 | tf_op jit(solution)/shard_map/ppermute | solution.py:24
  37.9 2.6 %collective-permute-done.12.came_ref = bf16[16,2048]{1,0:T(8,128)(2,1)S(1)} collective-permute-done((bf16[16,2048]{1,0:T(8,128)(2,1)S(1)}, bf16[16,2048]{1,0:T(8,128)(2,1)S(1)}, u32[]{:S(2)}, u32[]{:S(2)}) %collective-permute-start.12) | collective-permute-done | bytes 65568 | tf_op jit(solution)/shard_map/ppermute | solution.py:24
  41.1 12.9 %shard_map.172 = (f32[256,2048]{1,0:T(8,128)S(1)}, bf16[128,2048]{1,0:T(8,128)(2,1)}, bf16[128,2048]{1,0:T(8,128)(2,1)}, bf16[128,2048]{1,0:T(8,128)(2,1)}, bf16...) custom-call(s32[1,2048]{1,0:T(1,128)S(1)} %fusion.2.codes_ref, ...), custom_call_target="tpu_custom_call" | custom-call | flops 1 | bytes 1 | tf_op jit(solution)/shard_map/pallas_call | solution.py:312
  54.0 1.4 %collective-permute-start.15 = (bf16[128,2048]{1,0:T(8,128)(2,1)}, bf16[128,2048]{1,0:T(8,128)(2,1)S(1)}, u32[]{:S(2)}, u32[]{:S(2)}) collective-permute-start(bf16[128,2048]{1,0:T(8,128)(2,1)} %get-tuple-element.92), channel_id=1, source_target_pairs={{0,8},{4,12},{8,0},{12,4},{16,24},{20,28},{24,16},{28,20},{1,9},{5... | collective-permute-start | bytes 1572872 | tf_op jit(solution)/shard_map/ppermute | solution.py:24
  55.4 1.5 %collective-permute-start.14 = (bf16[128,2048]{1,0:T(8,128)(2,1)}, bf16[128,2048]{1,0:T(8,128)(2,1)S(1)}, u32[]{:S(2)}, u32[]{:S(2)}) collective-permute-start(bf16[128,2048]{1,0:T(8,128)(2,1)} %get-tuple-element.90), channel_id=1, source_target_pairs={{0,16},{4,20},{8,24},{12,28},{16,0},{20,4},{24,8},{28,12},{1,17},{... | collective-permute-start | bytes 1572872 | tf_op jit(solution)/shard_map/ppermute | solution.py:24
  58.1 13.5 %shard_map.173 = (f32[16,2560]{1,0:T(8,128)S(1)}, bf16[16,2560]{1,0:T(8,128)(2,1)S(1)}) custom-call(s32[1,2560]{1,0:T(1,128)S(1)} %fusion.1.codes_ref, bf16[1024,2048]{1,0:T(8,128)(2,1)} %refs_0_.3, bf16[1024,2048]{1,0:T(8,128)(2,1)} %collective-permute-done.3.mate_ref.refs_1_, bf16[32,2048]{1,0:T(8,128)(2,1)S(1)} %constant_dynamic-slice_fusion.refs_2_, ...), custom_call_target="tpu_custom_call" | custom-call | flops 1 | bytes 1 | tf_op jit(solution)/shard_map/pallas_call | solution.py:133
  73.0 1.5 %collective-permute-start.20 = (bf16[128,2048]{1,0:T(8,128)(2,1)}, bf16[128,2048]{1,0:T(8,128)(2,1)S(1)}, u32[]{:S(2)}, u32[]{:S(2)}) collective-permute-start(bf16[128,2048]{1,0:T(8,128)(2,1)} %get-tuple-element.109), channel_id=1, source_target_pairs={{0,16},{4,20},{8,24},{12,28},{16,0},{20,4},{24,8},{28,12},{1,17},{... | collective-permute-start | bytes 1572872 | tf_op jit(solution)/shard_map/ppermute | solution.py:24
  74.4 1.4 %collective-permute-start.19 = (bf16[128,2048]{1,0:T(8,128)(2,1)}, bf16[128,2048]{1,0:T(8,128)(2,1)S(1)}, u32[]{:S(2)}, u32[]{:S(2)}) collective-permute-start(bf16[128,2048]{1,0:T(8,128)(2,1)} %get-tuple-element.107), channel_id=1, source_target_pairs={{0,8},{4,12},{8,0},{12,4},{16,24},{20,28},{24,16},{28,20},{1,9},{5... | collective-permute-start | bytes 1572872 | tf_op jit(solution)/shard_map/ppermute | solution.py:24
  75.8 1.6 %collective-permute-start.13 = (bf16[16,2560]{1,0:T(8,128)(2,1)S(1)}, bf16[16,2560]{1,0:T(8,128)(2,1)S(1)}, u32[]{:S(2)}, u32[]{:S(2)}) collective-permute-start(bf16[16,2560]{1,0:T(8,128)(2,1)S(1)} %get-tuple-element.86.refs_4_), channel_id=1, source_target_pairs={{0,1},{1,0},{2,3},{3,2},{4,5},{5,4},{6,7},{7,6},{8,9},{9,8},{10,11... | collective-permute-start | bytes 245768 | tf_op jit(solution)/shard_map/ppermute | solution.py:24
  77.4 3.7 %collective-permute-done.13.came_ref = bf16[16,2560]{1,0:T(8,128)(2,1)S(1)} collective-permute-done((bf16[16,2560]{1,0:T(8,128)(2,1)S(1)}, bf16[16,2560]{1,0:T(8,128)(2,1)S(1)}, u32[]{:S(2)}, u32[]{:S(2)}) %collective-permute-start.13) | collective-permute-done | bytes 81952 | tf_op jit(solution)/shard_map/ppermute | solution.py:24
  81.2 2.1 %collective-permute-start.16 = (bf16[16,2560]{1,0:T(8,128)(2,1)S(1)}, bf16[16,2560]{1,0:T(8,128)(2,1)S(1)}, u32[]{:S(2)}, u32[]{:S(2)}) collective-permute-start(bf16[16,2560]{1,0:T(8,128)(2,1)S(1)} %get-tuple-element.95), channel_id=1, source_target_pairs={{0,2},{1,3},{2,0},{3,1},{4,6},{5,7},{6,4},{7,5},{8,10},{9,11},{10,... | collective-permute-start | bytes 245768 | tf_op jit(solution)/shard_map/ppermute | solution.py:24
  83.8 2.7 %collective-permute-done.16.came_ref = bf16[16,2560]{1,0:T(8,128)(2,1)S(1)} collective-permute-done((bf16[16,2560]{1,0:T(8,128)(2,1)S(1)}, bf16[16,2560]{1,0:T(8,128)(2,1)S(1)}, u32[]{:S(2)}, u32[]{:S(2)}) %collective-permute-start.16) | collective-permute-done | bytes 81952 | tf_op jit(solution)/shard_map/ppermute | solution.py:24
  87.2 1.9 %shard_map.178 = (f32[256,256]{1,0:T(8,128)S(1)}, bf16[256,256]{1,0:T(8,128)(2,1)}, bf16[256,256]{1,0:T(8,128)(2,1)}, bf16[256,256]{1,0:T(8,128)(2,1)}, f32[8,128]{1,0:T(8,128)S(1)}) custom-call(s32[1,2048]{1,0:T(1,128)S(1)} %fusion.2.codes_ref, s32[1,2048]{1,0:T(1,128)S(1)} %bitcast.25, f32[16,2560]{1,0:T(8,128)S(1)} %get-tuple-element.102.factor_ref.rank_ref, ...), custom_call_target="tpu_custom_call" | custom-call | flops 1 | bytes 1 | tf_op jit(solution)/shard_map/pallas_call | solution.py:312
  90.9 1.8 %collective-permute-start.24 = (bf16[256,256]{1,0:T(8,128)(2,1)}, bf16[256,256]{1,0:T(8,128)(2,1)S(1)}, u32[]{:S(2)}, u32[]{:S(2)}) collective-permute-start(bf16[256,256]{1,0:T(8,128)(2,1)} %get-tuple-element.118), channel_id=1, source_target_pairs={{0,24},{4,28},{8,16},{12,20},{16,8},{20,12},{24,0},{28,4},{1,25},{... | collective-permute-start | bytes 393224 | tf_op jit(solution)/shard_map/ppermute | solution.py:24
  93.9 1.6 %shard_map.181 = (f32[256,2048]{1,0:T(8,128)}, f32[8,128]{1,0:T(8,128)S(1)}) custom-call(f32[256,2048]{1,0:T(8,128)S(1)} %get-tuple-element.113.refs_0_, bf16[128,2048]{1,0:T(8,128)(2,1)S(1)} %collective-permute-done.19.refs_1_, bf16[128,2048]{1,0:T(8,128)(2,1)S(1)} %collective-permute-done.20.refs_2_), custom_call_target="tpu_custom_call" | custom-call | flops 1 | bytes 1 | tf_op jit(solution)/shard_map/pallas_call | solution.py:361
  (73 shorter events, 18.7 us)
Async XLA Ops:
  2.7 38.4 %collective-permute-start.3 = (bf16[1024,2048]{1,0:T(8,128)(2,1)}, bf16[1024,2048]{1,0:T(8,128)(2,1)}, u32[]{:S(2)}, u32[]{:S(2)}) collective-permute-start(bf16[1024,2048]{1,0:T(8,128)(2,1)} %refs_0_.3), channel_id=1, source_target_pairs={{0,4},{4,0},{8,12},{12,8},{16,20},{20,16},{24,28},{28,24},{1,5},{5... | collective-permute-start | bytes 12582920 | tf_op jit(solution)/shard_map/ppermute | solution.py:24
  6.0 6.9 %collective-permute-start.2 = (bf16[256,256]{1,0:T(8,128)(2,1)}, bf16[256,256]{1,0:T(8,128)(2,1)S(1)}, u32[]{:S(2)}, u32[]{:S(2)}) collective-permute-start(bf16[256,256]{1,0:T(8,128)(2,1)} %bitcast.19), channel_id=1, source_target_pairs={{0,16},{4,20},{8,24},{12,28},{16,0},{20,4},{24,8},{28,12},{1,17},{... | collective-permute-start | bytes 393224 | tf_op jit(solution)/shard_map/ppermute | solution.py:24
  8.7 7.5 %collective-permute-start.1 = (bf16[256,256]{1,0:T(8,128)(2,1)}, bf16[256,256]{1,0:T(8,128)(2,1)S(1)}, u32[]{:S(2)}, u32[]{:S(2)}) collective-permute-start(bf16[256,256]{1,0:T(8,128)(2,1)} %bitcast.20), channel_id=1, source_target_pairs={{0,8},{4,12},{8,0},{12,4},{16,24},{20,28},{24,16},{28,20},{1,9},{5... | collective-permute-start | bytes 393224 | tf_op jit(solution)/shard_map/ppermute | solution.py:24
  10.2 17.5 %collective-permute-start.6 = (bf16[128,2048]{1,0:T(8,128)(2,1)}, bf16[128,2048]{1,0:T(8,128)(2,1)S(1)}, u32[]{:S(2)}, u32[]{:S(2)}) collective-permute-start(bf16[128,2048]{1,0:T(8,128)(2,1)} %get-tuple-element.63), channel_id=1, source_target_pairs={{0,8},{4,12},{8,0},{12,4},{16,24},{20,28},{24,16},{28,20},{1,9},{5... | collective-permute-start | bytes 1572872 | tf_op jit(solution)/shard_map/ppermute | solution.py:24
  10.7 15.5 %collective-permute-start.8 = (bf16[128,2048]{1,0:T(8,128)(2,1)}, bf16[128,2048]{1,0:T(8,128)(2,1)S(1)}, u32[]{:S(2)}, u32[]{:S(2)}) collective-permute-start(bf16[128,2048]{1,0:T(8,128)(2,1)} %get-tuple-element.64), channel_id=1, source_target_pairs={{0,16},{4,20},{8,24},{12,28},{16,0},{20,4},{24,8},{28,12},{1,17},{... | collective-permute-start | bytes 1572872 | tf_op jit(solution)/shard_map/ppermute | solution.py:24
  12.9 16.3 %collective-permute-start.10 = (bf16[256,256]{1,0:T(8,128)(2,1)}, bf16[256,256]{1,0:T(8,128)(2,1)S(1)}, u32[]{:S(2)}, u32[]{:S(2)}) collective-permute-start(bf16[256,256]{1,0:T(8,128)(2,1)} %bitcast.21), channel_id=1, source_target_pairs={{0,24},{4,28},{8,16},{12,20},{16,8},{20,12},{24,0},{28,4},{1,25},{... | collective-permute-start | bytes 393224 | tf_op jit(solution)/shard_map/ppermute | solution.py:24
  16.2 13.1 %collective-permute-start.4 = (bf16[1024,256]{1,0:T(8,128)(2,1)}, bf16[1024,256]{1,0:T(8,128)(2,1)S(1)}, u32[]{:S(2)}, u32[]{:S(2)}) collective-permute-start(bf16[1024,256]{1,0:T(8,128)(2,1)} %own_ref.3), channel_id=1, source_target_pairs={{0,4},{4,0},{8,12},{12,8},{16,20},{20,16},{24,28},{28,24},{1,5},{5... | collective-permute-start | bytes 1572872 | tf_op jit(solution)/shard_map/ppermute | solution.py:24
  27.1 26.9 %collective-permute-start.9 = (bf16[256,2048]{1,0:T(8,128)(2,1)}, bf16[256,2048]{1,0:T(8,128)(2,1)S(1)}, u32[]{:S(2)}, u32[]{:S(2)}) collective-permute-start(bf16[256,2048]{1,0:T(8,128)(2,1)} %get-tuple-element.75), channel_id=1, source_target_pairs={{0,8},{4,12},{8,0},{12,4},{16,24},{20,28},{24,16},{28,20},{1,9},{5... | collective-permute-start | bytes 3145736 | tf_op jit(solution)/shard_map/ppermute | solution.py:24
  28.5 25.5 %collective-permute-start.7 = (bf16[256,2048]{1,0:T(8,128)(2,1)}, bf16[256,2048]{1,0:T(8,128)(2,1)S(1)}, u32[]{:S(2)}, u32[]{:S(2)}) collective-permute-start(bf16[256,2048]{1,0:T(8,128)(2,1)} %get-tuple-element.73), channel_id=1, source_target_pairs={{0,16},{4,20},{8,24},{12,28},{16,0},{20,4},{24,8},{28,12},{1,17},{... | collective-permute-start | bytes 3145736 | tf_op jit(solution)/shard_map/ppermute | solution.py:24
  30.9 4.3 %collective-permute-start.11 = (bf16[16,2048]{1,0:T(8,128)(2,1)S(1)}, bf16[16,2048]{1,0:T(8,128)(2,1)S(1)}, u32[]{:S(2)}, u32[]{:S(2)}) collective-permute-start(bf16[16,2048]{1,0:T(8,128)(2,1)S(1)} %get-tuple-element.80), channel_id=1, source_target_pairs={{0,1},{1,0},{2,3},{3,2},{4,5},{5,4},{6,7},{7,6},{8,9},{9,8},{10,11... | collective-permute-start | bytes 196616 | tf_op jit(solution)/shard_map/ppermute | solution.py:24
  32.5 8.6 %collective-permute-start.5 = (bf16[32,2048]{1,0:T(8,128)(2,1)S(1)}, bf16[32,2048]{1,0:T(8,128)(2,1)S(1)}, u32[]{:S(2)}, u32[]{:S(2)}) collective-permute-start(bf16[32,2048]{1,0:T(8,128)(2,1)S(1)} %constant_dynamic-slice_fusion.refs_2_), channel_id=1, source_target_pairs={{0,4},{4,0},{8,12},{12,8},{16,20},{20,16},{24,28},{28,24},{1,5},{5... | collective-permute-start | bytes 393224 | tf_op jit(solution)/shard_map/ppermute | solution.py:24
  35.2 5.2 %collective-permute-start.12 = (bf16[16,2048]{1,0:T(8,128)(2,1)S(1)}, bf16[16,2048]{1,0:T(8,128)(2,1)S(1)}, u32[]{:S(2)}, u32[]{:S(2)}) collective-permute-start(bf16[16,2048]{1,0:T(8,128)(2,1)S(1)} %get-tuple-element.82), channel_id=1, source_target_pairs={{0,2},{1,3},{2,0},{3,1},{4,6},{5,7},{6,4},{7,5},{8,10},{9,11},{10,... | collective-permute-start | bytes 196616 | tf_op jit(solution)/shard_map/ppermute | solution.py:24
  54.0 17.6 %collective-permute-start.15 = (bf16[128,2048]{1,0:T(8,128)(2,1)}, bf16[128,2048]{1,0:T(8,128)(2,1)S(1)}, u32[]{:S(2)}, u32[]{:S(2)}) collective-permute-start(bf16[128,2048]{1,0:T(8,128)(2,1)} %get-tuple-element.92), channel_id=1, source_target_pairs={{0,8},{4,12},{8,0},{12,4},{16,24},{20,28},{24,16},{28,20},{1,9},{5... | collective-permute-start | bytes 1572872 | tf_op jit(solution)/shard_map/ppermute | solution.py:24
  55.4 16.2 %collective-permute-start.14 = (bf16[128,2048]{1,0:T(8,128)(2,1)}, bf16[128,2048]{1,0:T(8,128)(2,1)S(1)}, u32[]{:S(2)}, u32[]{:S(2)}) collective-permute-start(bf16[128,2048]{1,0:T(8,128)(2,1)} %get-tuple-element.90), channel_id=1, source_target_pairs={{0,16},{4,20},{8,24},{12,28},{16,0},{20,4},{24,8},{28,12},{1,17},{... | collective-permute-start | bytes 1572872 | tf_op jit(solution)/shard_map/ppermute | solution.py:24
  56.9 26.3 %collective-permute-start.18 = (bf16[128,2048]{1,0:T(8,128)(2,1)}, bf16[128,2048]{1,0:T(8,128)(2,1)S(1)}, u32[]{:S(2)}, u32[]{:S(2)}) collective-permute-start(bf16[128,2048]{1,0:T(8,128)(2,1)} %get-tuple-element.100), channel_id=1, source_target_pairs={{0,8},{4,12},{8,0},{12,4},{16,24},{20,28},{24,16},{28,20},{1,9},{5... | collective-permute-start | bytes 1572872 | tf_op jit(solution)/shard_map/ppermute | solution.py:24
  57.5 25.7 %collective-permute-start.17 = (bf16[128,2048]{1,0:T(8,128)(2,1)}, bf16[128,2048]{1,0:T(8,128)(2,1)S(1)}, u32[]{:S(2)}, u32[]{:S(2)}) collective-permute-start(bf16[128,2048]{1,0:T(8,128)(2,1)} %get-tuple-element.98), channel_id=1, source_target_pairs={{0,16},{4,20},{8,24},{12,28},{16,0},{20,4},{24,8},{28,12},{1,17},{... | collective-permute-start | bytes 1572872 | tf_op jit(solution)/shard_map/ppermute | solution.py:24
  73.0 20.9 %collective-permute-start.20 = (bf16[128,2048]{1,0:T(8,128)(2,1)}, bf16[128,2048]{1,0:T(8,128)(2,1)S(1)}, u32[]{:S(2)}, u32[]{:S(2)}) collective-permute-start(bf16[128,2048]{1,0:T(8,128)(2,1)} %get-tuple-element.109), channel_id=1, source_target_pairs={{0,16},{4,20},{8,24},{12,28},{16,0},{20,4},{24,8},{28,12},{1,17},{... | collective-permute-start | bytes 1572872 | tf_op jit(solution)/shard_map/ppermute | solution.py:24
  74.4 19.5 %collective-permute-start.19 = (bf16[128,2048]{1,0:T(8,128)(2,1)}, bf16[128,2048]{1,0:T(8,128)(2,1)S(1)}, u32[]{:S(2)}, u32[]{:S(2)}) collective-permute-start(bf16[128,2048]{1,0:T(8,128)(2,1)} %get-tuple-element.107), channel_id=1, source_target_pairs={{0,8},{4,12},{8,0},{12,4},{16,24},{20,28},{24,16},{28,20},{1,9},{5... | collective-permute-start | bytes 1572872 | tf_op jit(solution)/shard_map/ppermute | solution.py:24
  75.8 5.3 %collective-permute-start.13 = (bf16[16,2560]{1,0:T(8,128)(2,1)S(1)}, bf16[16,2560]{1,0:T(8,128)(2,1)S(1)}, u32[]{:S(2)}, u32[]{:S(2)}) collective-permute-start(bf16[16,2560]{1,0:T(8,128)(2,1)S(1)} %get-tuple-element.86.refs_4_), channel_id=1, source_target_pairs={{0,1},{1,0},{2,3},{3,2},{4,5},{5,4},{6,7},{7,6},{8,9},{9,8},{10,11... | collective-permute-start | bytes 245768 | tf_op jit(solution)/shard_map/ppermute | solution.py:24
  81.2 5.4 %collective-permute-start.16 = (bf16[16,2560]{1,0:T(8,128)(2,1)S(1)}, bf16[16,2560]{1,0:T(8,128)(2,1)S(1)}, u32[]{:S(2)}, u32[]{:S(2)}) collective-permute-start(bf16[16,2560]{1,0:T(8,128)(2,1)S(1)} %get-tuple-element.95), channel_id=1, source_target_pairs={{0,2},{1,3},{2,0},{3,1},{4,6},{5,7},{6,4},{7,5},{8,10},{9,11},{10,... | collective-permute-start | bytes 245768 | tf_op jit(solution)/shard_map/ppermute | solution.py:24
  89.1 7.3 %collective-permute-start.22 = (bf16[256,256]{1,0:T(8,128)(2,1)}, bf16[256,256]{1,0:T(8,128)(2,1)S(1)}, u32[]{:S(2)}, u32[]{:S(2)}) collective-permute-start(bf16[256,256]{1,0:T(8,128)(2,1)} %get-tuple-element.116), channel_id=1, source_target_pairs={{0,8},{4,12},{8,0},{12,4},{16,24},{20,28},{24,16},{28,20},{1,9},{5... | collective-permute-start | bytes 393224 | tf_op jit(solution)/shard_map/ppermute | solution.py:24
  89.7 6.7 %collective-permute-start.23 = (bf16[256,256]{1,0:T(8,128)(2,1)}, bf16[256,256]{1,0:T(8,128)(2,1)S(1)}, u32[]{:S(2)}, u32[]{:S(2)}) collective-permute-start(bf16[256,256]{1,0:T(8,128)(2,1)} %get-tuple-element.117), channel_id=1, source_target_pairs={{0,16},{4,20},{8,24},{12,28},{16,0},{20,4},{24,8},{28,12},{1,17},{... | collective-permute-start | bytes 393224 | tf_op jit(solution)/shard_map/ppermute | solution.py:24
  90.9 6.1 %collective-permute-start.24 = (bf16[256,256]{1,0:T(8,128)(2,1)}, bf16[256,256]{1,0:T(8,128)(2,1)S(1)}, u32[]{:S(2)}, u32[]{:S(2)}) collective-permute-start(bf16[256,256]{1,0:T(8,128)(2,1)} %get-tuple-element.118), channel_id=1, source_target_pairs={{0,24},{4,28},{8,16},{12,20},{16,8},{20,12},{24,0},{28,4},{1,25},{... | collective-permute-start | bytes 393224 | tf_op jit(solution)/shard_map/ppermute | solution.py:24
  93.9 1.6 %collective-permute-start.21 = (bf16[32,256]{1,0:T(8,128)(2,1)S(1)}, bf16[32,256]{1,0:T(8,128)(2,1)S(1)}, u32[]{:S(2)}, u32[]{:S(2)}) collective-permute-start(bf16[32,256]{1,0:T(8,128)(2,1)S(1)} %get-tuple-element.110), channel_id=1, source_target_pairs={{0,4},{4,0},{8,12},{12,8},{16,20},{20,16},{24,28},{28,24},{1,5},{5... | collective-permute-start | bytes 49160 | tf_op jit(solution)/shard_map/ppermute | solution.py:24
  (10 other events, 86.5 us)

commit v8 on v7

--- a/solution.py
+++ b/solution.py
@@ -12,7 +12,7 @@
 
 ADAPTER_SCALE = 2.0
 NEG_FILL = -1e30
-VMEM_LIMIT = 48 * 1024 * 1024
+VMEM_LIMIT = 40 * 1024 * 1024
 TOKEN = jax.ShapeDtypeStruct((8, 128), jnp.float32)
 TOKEN_SPEC = pl.BlockSpec(TOKEN.shape, lambda *_: (0, 0))
 SENT = pltpu.HBM
@@ -569,7 +569,7 @@
                 if len(held) > 2:
                     sent = jnp.pad(sent, ((0, (len(held) - 2) * part_rows), (0, 0)))
                 for k, m in enumerate(held[1:], 1):
-                    sent, token = place(sent, down_parts[m, p], k, (cached, base_values))
+                    sent, token = place(sent, down_parts[m, p], k, (cached,))
                     second_sent.append(token)
             came = swap(sent, "wide", bit)
             for k, m in enumerate(held):
@@ -597,7 +597,7 @@
         rank,
         after=second_sent,
     )
-    back = sum_over("narrow", part_back, sent_back)
+    back = sum_over("narrow", part_back, sent_back, [(), (base_values,)])
 
     groups = {}
     for m in far + near:

time: 98 us -> 96.7 us (0.987)
  Pallas kernels: 47.5 us -> 46.5 us
  transfers between devices with their start and end apart: 25 -> 25, of which waited for: 8 -> 8; matrix products, arithmetic and copies ran while one was open for 5% -> 5% of each run, Pallas kernels for 48% -> 47%
where the time goes in v8:
time: 96.7 us; the launch traced here: 96.4 us
  Pallas kernels  46.5 us (48%)
  starting transfers between devices  28.9 us (30%)
  waiting for transfers between devices  14.4 us (15%)
  matrix products  3.83 us (4%)
  local copies, waits for them, and re-layouts  1.02 us (1%)
    ppermute x25, starting transfers between devices, swap(): return lax.ppermute(array, axis, [(i, i ^ mask) for i in range(count)])  28.9 us
    pallas_call x2, Pallas kernels, gradient_chunks(): pl.pallas_call(functools.partial(gradient_kernel, code_list([(chunk[0], r...  14.7 us
    pallas_call x2, Pallas kernels, project_tokens(): pl.pallas_call(functools.partial(token_kernel, code_list([(bases, chunk.s...  14.4 us
    ppermute x25, waiting for transfers between devices, swap(): return lax.ppermute(array, axis, [(i, i ^ mask) for i in range(count)])  14.4 us
    pallas_call x1, Pallas kernels, attend_cached(): pl.pallas_call(functools.partial(attend_kernel, kv_width // HEAD_SIZE), g...  5.82 us
    pallas_call x4, Pallas kernels, add_arrived(): pl.pallas_call(functools.partial(add_kernel, [[[k for _, k in arrived] fo...  4.26 us
    dot_general x1, matrix products, per_device(): jnp.dot(hidden_rows, key_matrix, preferred_element_type=jnp.float32)  3 us
    pallas_call x1, Pallas kernels, cut(): pl.pallas_call(cut_kernel, out_shape=[SENT((rows, width), maps.dtype)] *...  2.95 us
  transfers between devices with their start and end apart: 25, of which 8 were waited for; matrix products, arithmetic and copies ran while one was open for 5% of the time, Pallas kernels for 47%

profile of v8, /device:TPU:0, one launch (start us, length us, event | category | flops | bytes accessed | tf_op | source)
XLA Modules:
  0.0 96.4 jit_solution(5432207896724556794)
XLA Ops:
  3.1 3.0 %shard_map.165 = (bf16[128,2048]{1,0:T(8,128)(2,1)}, bf16[128,2048]{1,0:T(8,128)(2,1)}, bf16[256,2048]{1,0:T(8,128)(2,1)}, bf16[256,2048]{1,0:T(8,128)(2,1)}) custom-call(bf16[256,2048]{1,0:T(8,128)(2,1)} %bitcast.16), custom_call_target="tpu_custom_call" | custom-call | flops 1 | bytes 1 | tf_op jit(solution)/shard_map/pallas_call | solution.py:216
  6.0 2.7 %collective-permute-start.2 = (bf16[256,256]{1,0:T(8,128)(2,1)}, bf16[256,256]{1,0:T(8,128)(2,1)S(1)}, u32[]{:S(2)}, u32[]{:S(2)}) collective-permute-start(bf16[256,256]{1,0:T(8,128)(2,1)} %bitcast.19), channel_id=1, source_target_pairs={{0,16},{4,20},{8,24},{12,28},{16,0},{20,4},{24,8},{28,12},{1,17},{... | collective-permute-start | bytes 393224 | tf_op jit(solution)/shard_map/ppermute | solution.py:24
  8.7 1.5 %collective-permute-start.1 = (bf16[256,256]{1,0:T(8,128)(2,1)}, bf16[256,256]{1,0:T(8,128)(2,1)S(1)}, u32[]{:S(2)}, u32[]{:S(2)}) collective-permute-start(bf16[256,256]{1,0:T(8,128)(2,1)} %bitcast.20), channel_id=1, source_target_pairs={{0,8},{4,12},{8,0},{12,4},{16,24},{20,28},{24,16},{28,20},{1,9},{5... | collective-permute-start | bytes 393224 | tf_op jit(solution)/shard_map/ppermute | solution.py:24
  12.9 3.2 %collective-permute-start.10 = (bf16[256,256]{1,0:T(8,128)(2,1)}, bf16[256,256]{1,0:T(8,128)(2,1)S(1)}, u32[]{:S(2)}, u32[]{:S(2)}) collective-permute-start(bf16[256,256]{1,0:T(8,128)(2,1)} %bitcast.21), channel_id=1, source_target_pairs={{0,24},{4,28},{8,16},{12,20},{16,8},{20,12},{24,0},{28,4},{1,25},{... | collective-permute-start | bytes 393224 | tf_op jit(solution)/shard_map/ppermute | solution.py:24
  16.2 3.0 %fusion.fresh_ref = f32[32,256]{1,0:T(8,128)S(1)} fusion(bf16[32,8192]{1,0:T(8,128)(2,1)S(1)} %copy-done, bf16[8192,256]{1,0:T(8,128)(2,1)} %param.20), kind=kOutput, calls=%fused_computation.1 | convolution fusion | flops 134234112 | bytes 4751360 | tf_op jit(solution)/shard_map/dot_general | solution.py:552
  19.2 5.8 %shard_map.166 = (f32[32,16,128]{2,1,0:T(8,128)S(1)}, f32[32,16,128]{2,1,0:T(8,128)S(1)}) custom-call(s32[32]{0:T(128)S(1)} %copy-done.5, bf16[32,16,128]{2,1,0:T(8,128)(2,1)S(1)} %bitcast.18, bf16[32,256,256]{2,1,0:T(8,128)(2,1)} %keys_ref.1, bf16[32,256,256]{2,1,0:T(8,128)(2,1)} %values_ref.1, f32[32,256]{1,0:T(8,128)S(1)} %fusion.fresh_ref), custom_call_target="tpu_custom_call" | custom-call | flops 1 | bytes 1 | tf_op jit(solution)/shard_map/pallas_call | solution.py:456
  27.5 1.5 %collective-permute-start.7 = (bf16[256,2048]{1,0:T(8,128)(2,1)}, bf16[256,2048]{1,0:T(8,128)(2,1)S(1)}, u32[]{:S(2)}, u32[]{:S(2)}) collective-permute-start(bf16[256,2048]{1,0:T(8,128)(2,1)} %get-tuple-element.73), channel_id=1, source_target_pairs={{0,16},{4,20},{8,24},{12,28},{16,0},{20,4},{24,8},{28,12},{1,17},{... | collective-permute-start | bytes 3145736 | tf_op jit(solution)/shard_map/ppermute | solution.py:24
  29.3 1.6 %shard_map.169 = (f32[16,2048]{1,0:T(8,128)S(1)}, bf16[16,2048]{1,0:T(8,128)(2,1)S(1)}) custom-call(s32[1,2560]{1,0:T(1,128)S(1)} %fusion.1.codes_ref, bf16[1024,256]{1,0:T(8,128)(2,1)S(1)} %copy-done.3, bf16[1024,256]{1,0:T(8,128)(2,1)S(1)} %collective-permute-done.4.refs_1_.mate_ref, bf16[256,256]{1,0:T(8,128)(2,1)S(1)} %bitcast.22, ...), custom_call_target="tpu_custom_call" | custom-call | flops 1 | bytes 1 | tf_op jit(solution)/shard_map/pallas_call | solution.py:133
  30.9 1.6 %collective-permute-start.11 = (bf16[16,2048]{1,0:T(8,128)(2,1)S(1)}, bf16[16,2048]{1,0:T(8,128)(2,1)S(1)}, u32[]{:S(2)}, u32[]{:S(2)}) collective-permute-start(bf16[16,2048]{1,0:T(8,128)(2,1)S(1)} %get-tuple-element.80), channel_id=1, source_target_pairs={{0,1},{1,0},{2,3},{3,2},{4,5},{5,4},{6,7},{7,6},{8,9},{9,8},{10,11... | collective-permute-start | bytes 196616 | tf_op jit(solution)/shard_map/ppermute | solution.py:24
  32.5 2.7 %collective-permute-done.11.came_ref = bf16[16,2048]{1,0:T(8,128)(2,1)S(1)} collective-permute-done((bf16[16,2048]{1,0:T(8,128)(2,1)S(1)}, bf16[16,2048]{1,0:T(8,128)(2,1)S(1)}, u32[]{:S(2)}, u32[]{:S(2)}) %collective-permute-start.11) | collective-permute-done | bytes 65568 | tf_op jit(solution)/shard_map/ppermute | solution.py:24
  35.2 2.6 %collective-permute-start.12 = (bf16[16,2048]{1,0:T(8,128)(2,1)S(1)}, bf16[16,2048]{1,0:T(8,128)(2,1)S(1)}, u32[]{:S(2)}, u32[]{:S(2)}) collective-permute-start(bf16[16,2048]{1,0:T(8,128)(2,1)S(1)} %get-tuple-element.82), channel_id=1, source_target_pairs={{0,2},{1,3},{2,0},{3,1},{4,6},{5,7},{6,4},{7,5},{8,10},{9,11},{10,... | collective-permute-start | bytes 196616 | tf_op jit(solution)/shard_map/ppermute | solution.py:24
  38.7 1.8 %collective-permute-done.12.came_ref = bf16[16,2048]{1,0:T(8,128)(2,1)S(1)} collective-permute-done((bf16[16,2048]{1,0:T(8,128)(2,1)S(1)}, bf16[16,2048]{1,0:T(8,128)(2,1)S(1)}, u32[]{:S(2)}, u32[]{:S(2)}) %collective-permute-start.12) | collective-permute-done | bytes 65568 | tf_op jit(solution)/shard_map/ppermute | solution.py:24
  41.1 12.8 %shard_map.172 = (f32[256,2048]{1,0:T(8,128)S(1)}, bf16[128,2048]{1,0:T(8,128)(2,1)}, bf16[128,2048]{1,0:T(8,128)(2,1)}, bf16[128,2048]{1,0:T(8,128)(2,1)}, bf16...) custom-call(s32[1,2048]{1,0:T(1,128)S(1)} %fusion.2.codes_ref, ...), custom_call_target="tpu_custom_call" | custom-call | flops 1 | bytes 1 | tf_op jit(solution)/shard_map/pallas_call | solution.py:312
  54.6 1.5 %collective-permute-start.14 = (bf16[128,2048]{1,0:T(8,128)(2,1)}, bf16[128,2048]{1,0:T(8,128)(2,1)S(1)}, u32[]{:S(2)}, u32[]{:S(2)}) collective-permute-start(bf16[128,2048]{1,0:T(8,128)(2,1)} %get-tuple-element.90), channel_id=1, source_target_pairs={{0,16},{4,20},{8,24},{12,28},{16,0},{20,4},{24,8},{28,12},{1,17},{... | collective-permute-start | bytes 1572872 | tf_op jit(solution)/shard_map/ppermute | solution.py:24
  56.7 1.4 %collective-permute-start.17 = (bf16[128,2048]{1,0:T(8,128)(2,1)}, bf16[128,2048]{1,0:T(8,128)(2,1)S(1)}, u32[]{:S(2)}, u32[]{:S(2)}) collective-permute-start(bf16[128,2048]{1,0:T(8,128)(2,1)} %get-tuple-element.98), channel_id=1, source_target_pairs={{0,16},{4,20},{8,24},{12,28},{16,0},{20,4},{24,8},{28,12},{1,17},{... | collective-permute-start | bytes 1572872 | tf_op jit(solution)/shard_map/ppermute | solution.py:24
  58.1 12.9 %shard_map.173 = (f32[16,2560]{1,0:T(8,128)S(1)}, bf16[16,2560]{1,0:T(8,128)(2,1)S(1)}) custom-call(s32[1,2560]{1,0:T(1,128)S(1)} %fusion.1.codes_ref, bf16[1024,2048]{1,0:T(8,128)(2,1)S(1)} %copy-done.1, bf16[1024,2048]{1,0:T(8,128)(2,1)} %collective-permute-done.3.mate_ref.refs_1_, bf16[32,2048]{1,0:T(8,128)(2,1)S(1)} %constant_dynamic-slice_fusion.refs_2_, ...), custom_call_target="tpu_custom_call" | custom-call | flops 1 | bytes 1 | tf_op jit(solution)/shard_map/pallas_call | solution.py:133
  72.8 1.5 %collective-permute-start.19 = (bf16[128,2048]{1,0:T(8,128)(2,1)}, bf16[128,2048]{1,0:T(8,128)(2,1)S(1)}, u32[]{:S(2)}, u32[]{:S(2)}) collective-permute-start(bf16[128,2048]{1,0:T(8,128)(2,1)} %get-tuple-element.107), channel_id=1, source_target_pairs={{0,8},{4,12},{8,0},{12,4},{16,24},{20,28},{24,16},{28,20},{1,9},{5... | collective-permute-start | bytes 1572872 | tf_op jit(solution)/shard_map/ppermute | solution.py:24
  74.3 1.6 %collective-permute-start.13 = (bf16[16,2560]{1,0:T(8,128)(2,1)S(1)}, bf16[16,2560]{1,0:T(8,128)(2,1)S(1)}, u32[]{:S(2)}, u32[]{:S(2)}) collective-permute-start(bf16[16,2560]{1,0:T(8,128)(2,1)S(1)} %get-tuple-element.86.refs_4_), channel_id=1, source_target_pairs={{0,1},{1,0},{2,3},{3,2},{4,5},{5,4},{6,7},{7,6},{8,9},{9,8},{10,11... | collective-permute-start | bytes 245768 | tf_op jit(solution)/shard_map/ppermute | solution.py:24
  75.9 3.6 %collective-permute-done.13.came_ref = bf16[16,2560]{1,0:T(8,128)(2,1)S(1)} collective-permute-done((bf16[16,2560]{1,0:T(8,128)(2,1)S(1)}, bf16[16,2560]{1,0:T(8,128)(2,1)S(1)}, u32[]{:S(2)}, u32[]{:S(2)}) %collective-permute-start.13) | collective-permute-done | bytes 81952 | tf_op jit(solution)/shard_map/ppermute | solution.py:24
  79.6 2.2 %collective-permute-start.16 = (bf16[16,2560]{1,0:T(8,128)(2,1)S(1)}, bf16[16,2560]{1,0:T(8,128)(2,1)S(1)}, u32[]{:S(2)}, u32[]{:S(2)}) collective-permute-start(bf16[16,2560]{1,0:T(8,128)(2,1)S(1)} %get-tuple-element.95), channel_id=1, source_target_pairs={{0,2},{1,3},{2,0},{3,1},{4,6},{5,7},{6,4},{7,5},{8,10},{9,11},{10,... | collective-permute-start | bytes 245768 | tf_op jit(solution)/shard_map/ppermute | solution.py:24
  82.4 2.6 %collective-permute-done.16.came_ref = bf16[16,2560]{1,0:T(8,128)(2,1)S(1)} collective-permute-done((bf16[16,2560]{1,0:T(8,128)(2,1)S(1)}, bf16[16,2560]{1,0:T(8,128)(2,1)S(1)}, u32[]{:S(2)}, u32[]{:S(2)}) %collective-permute-start.16) | collective-permute-done | bytes 81952 | tf_op jit(solution)/shard_map/ppermute | solution.py:24
  85.6 1.9 %shard_map.178 = (f32[256,256]{1,0:T(8,128)S(1)}, bf16[256,256]{1,0:T(8,128)(2,1)}, bf16[256,256]{1,0:T(8,128)(2,1)}, bf16[256,256]{1,0:T(8,128)(2,1)}, f32[8,128]{1,0:T(8,128)S(1)}) custom-call(s32[1,2048]{1,0:T(1,128)S(1)} %fusion.2.codes_ref, s32[1,2048]{1,0:T(1,128)S(1)} %bitcast.25, f32[16,2560]{1,0:T(8,128)S(1)} %get-tuple-element.102.factor_ref.rank_ref, ...), custom_call_target="tpu_custom_call" | custom-call | flops 1 | bytes 1 | tf_op jit(solution)/shard_map/pallas_call | solution.py:312
  89.5 1.5 %collective-permute-start.24 = (bf16[256,256]{1,0:T(8,128)(2,1)}, bf16[256,256]{1,0:T(8,128)(2,1)S(1)}, u32[]{:S(2)}, u32[]{:S(2)}) collective-permute-start(bf16[256,256]{1,0:T(8,128)(2,1)} %get-tuple-element.118), channel_id=1, source_target_pairs={{0,24},{4,28},{8,16},{12,20},{16,8},{20,12},{24,0},{28,4},{1,25},{... | collective-permute-start | bytes 393224 | tf_op jit(solution)/shard_map/ppermute | solution.py:24
  92.7 1.6 %shard_map.181 = (f32[256,2048]{1,0:T(8,128)}, f32[8,128]{1,0:T(8,128)S(1)}) custom-call(f32[256,2048]{1,0:T(8,128)S(1)} %get-tuple-element.113.refs_0_, bf16[128,2048]{1,0:T(8,128)(2,1)S(1)} %collective-permute-done.19.refs_1_, bf16[128,2048]{1,0:T(8,128)(2,1)S(1)} %collective-permute-done.20.refs_2_), custom_call_target="tpu_custom_call" | custom-call | flops 1 | bytes 1 | tf_op jit(solution)/shard_map/pallas_call | solution.py:361
  (75 shorter events, 19.3 us)
Async XLA Ops:
  2.7 38.4 %collective-permute-start.3 = (bf16[1024,2048]{1,0:T(8,128)(2,1)}, bf16[1024,2048]{1,0:T(8,128)(2,1)}, u32[]{:S(2)}, u32[]{:S(2)}) collective-permute-start(bf16[1024,2048]{1,0:T(8,128)(2,1)} %refs_0_.3), channel_id=1, source_target_pairs={{0,4},{4,0},{8,12},{12,8},{16,20},{20,16},{24,28},{28,24},{1,5},{5... | collective-permute-start | bytes 12582920 | tf_op jit(solution)/shard_map/ppermute | solution.py:24
  6.0 6.9 %collective-permute-start.2 = (bf16[256,256]{1,0:T(8,128)(2,1)}, bf16[256,256]{1,0:T(8,128)(2,1)S(1)}, u32[]{:S(2)}, u32[]{:S(2)}) collective-permute-start(bf16[256,256]{1,0:T(8,128)(2,1)} %bitcast.19), channel_id=1, source_target_pairs={{0,16},{4,20},{8,24},{12,28},{16,0},{20,4},{24,8},{28,12},{1,17},{... | collective-permute-start | bytes 393224 | tf_op jit(solution)/shard_map/ppermute | solution.py:24
  8.7 7.5 %collective-permute-start.1 = (bf16[256,256]{1,0:T(8,128)(2,1)}, bf16[256,256]{1,0:T(8,128)(2,1)S(1)}, u32[]{:S(2)}, u32[]{:S(2)}) collective-permute-start(bf16[256,256]{1,0:T(8,128)(2,1)} %bitcast.20), channel_id=1, source_target_pairs={{0,8},{4,12},{8,0},{12,4},{16,24},{20,28},{24,16},{28,20},{1,9},{5... | collective-permute-start | bytes 393224 | tf_op jit(solution)/shard_map/ppermute | solution.py:24
  10.2 16.5 %collective-permute-start.6 = (bf16[128,2048]{1,0:T(8,128)(2,1)}, bf16[128,2048]{1,0:T(8,128)(2,1)S(1)}, u32[]{:S(2)}, u32[]{:S(2)}) collective-permute-start(bf16[128,2048]{1,0:T(8,128)(2,1)} %get-tuple-element.63), channel_id=1, source_target_pairs={{0,8},{4,12},{8,0},{12,4},{16,24},{20,28},{24,16},{28,20},{1,9},{5... | collective-permute-start | bytes 1572872 | tf_op jit(solution)/shard_map/ppermute | solution.py:24
  10.7 14.3 %collective-permute-start.8 = (bf16[128,2048]{1,0:T(8,128)(2,1)}, bf16[128,2048]{1,0:T(8,128)(2,1)S(1)}, u32[]{:S(2)}, u32[]{:S(2)}) collective-permute-start(bf16[128,2048]{1,0:T(8,128)(2,1)} %get-tuple-element.64), channel_id=1, source_target_pairs={{0,16},{4,20},{8,24},{12,28},{16,0},{20,4},{24,8},{28,12},{1,17},{... | collective-permute-start | bytes 1572872 | tf_op jit(solution)/shard_map/ppermute | solution.py:24
  12.9 16.3 %collective-permute-start.10 = (bf16[256,256]{1,0:T(8,128)(2,1)}, bf16[256,256]{1,0:T(8,128)(2,1)S(1)}, u32[]{:S(2)}, u32[]{:S(2)}) collective-permute-start(bf16[256,256]{1,0:T(8,128)(2,1)} %bitcast.21), channel_id=1, source_target_pairs={{0,24},{4,28},{8,16},{12,20},{16,8},{20,12},{24,0},{28,4},{1,25},{... | collective-permute-start | bytes 393224 | tf_op jit(solution)/shard_map/ppermute | solution.py:24
  16.2 13.1 %collective-permute-start.4 = (bf16[1024,256]{1,0:T(8,128)(2,1)}, bf16[1024,256]{1,0:T(8,128)(2,1)S(1)}, u32[]{:S(2)}, u32[]{:S(2)}) collective-permute-start(bf16[1024,256]{1,0:T(8,128)(2,1)} %own_ref.3), channel_id=1, source_target_pairs={{0,4},{4,0},{8,12},{12,8},{16,20},{20,16},{24,28},{28,24},{1,5},{5... | collective-permute-start | bytes 1572872 | tf_op jit(solution)/shard_map/ppermute | solution.py:24
  25.9 28.0 %collective-permute-start.9 = (bf16[256,2048]{1,0:T(8,128)(2,1)}, bf16[256,2048]{1,0:T(8,128)(2,1)S(1)}, u32[]{:S(2)}, u32[]{:S(2)}) collective-permute-start(bf16[256,2048]{1,0:T(8,128)(2,1)} %get-tuple-element.75), channel_id=1, source_target_pairs={{0,8},{4,12},{8,0},{12,4},{16,24},{20,28},{24,16},{28,20},{1,9},{5... | collective-permute-start | bytes 3145736 | tf_op jit(solution)/shard_map/ppermute | solution.py:24
  27.5 26.4 %collective-permute-start.7 = (bf16[256,2048]{1,0:T(8,128)(2,1)}, bf16[256,2048]{1,0:T(8,128)(2,1)S(1)}, u32[]{:S(2)}, u32[]{:S(2)}) collective-permute-start(bf16[256,2048]{1,0:T(8,128)(2,1)} %get-tuple-element.73), channel_id=1, source_target_pairs={{0,16},{4,20},{8,24},{12,28},{16,0},{20,4},{24,8},{28,12},{1,17},{... | collective-permute-start | bytes 3145736 | tf_op jit(solution)/shard_map/ppermute | solution.py:24
  30.9 4.3 %collective-permute-start.11 = (bf16[16,2048]{1,0:T(8,128)(2,1)S(1)}, bf16[16,2048]{1,0:T(8,128)(2,1)S(1)}, u32[]{:S(2)}, u32[]{:S(2)}) collective-permute-start(bf16[16,2048]{1,0:T(8,128)(2,1)S(1)} %get-tuple-element.80), channel_id=1, source_target_pairs={{0,1},{1,0},{2,3},{3,2},{4,5},{5,4},{6,7},{7,6},{8,9},{9,8},{10,11... | collective-permute-start | bytes 196616 | tf_op jit(solution)/shard_map/ppermute | solution.py:24
  32.5 8.6 %collective-permute-start.5 = (bf16[32,2048]{1,0:T(8,128)(2,1)S(1)}, bf16[32,2048]{1,0:T(8,128)(2,1)S(1)}, u32[]{:S(2)}, u32[]{:S(2)}) collective-permute-start(bf16[32,2048]{1,0:T(8,128)(2,1)S(1)} %constant_dynamic-slice_fusion.refs_2_), channel_id=1, source_target_pairs={{0,4},{4,0},{8,12},{12,8},{16,20},{20,16},{24,28},{28,24},{1,5},{5... | collective-permute-start | bytes 393224 | tf_op jit(solution)/shard_map/ppermute | solution.py:24
  35.2 5.2 %collective-permute-start.12 = (bf16[16,2048]{1,0:T(8,128)(2,1)S(1)}, bf16[16,2048]{1,0:T(8,128)(2,1)S(1)}, u32[]{:S(2)}, u32[]{:S(2)}) collective-permute-start(bf16[16,2048]{1,0:T(8,128)(2,1)S(1)} %get-tuple-element.82), channel_id=1, source_target_pairs={{0,2},{1,3},{2,0},{3,1},{4,6},{5,7},{6,4},{7,5},{8,10},{9,11},{10,... | collective-permute-start | bytes 196616 | tf_op jit(solution)/shard_map/ppermute | solution.py:24
  54.0 17.0 %collective-permute-start.15 = (bf16[128,2048]{1,0:T(8,128)(2,1)}, bf16[128,2048]{1,0:T(8,128)(2,1)S(1)}, u32[]{:S(2)}, u32[]{:S(2)}) collective-permute-start(bf16[128,2048]{1,0:T(8,128)(2,1)} %get-tuple-element.92), channel_id=1, source_target_pairs={{0,8},{4,12},{8,0},{12,4},{16,24},{20,28},{24,16},{28,20},{1,9},{5... | collective-permute-start | bytes 1572872 | tf_op jit(solution)/shard_map/ppermute | solution.py:24
  54.6 16.4 %collective-permute-start.14 = (bf16[128,2048]{1,0:T(8,128)(2,1)}, bf16[128,2048]{1,0:T(8,128)(2,1)S(1)}, u32[]{:S(2)}, u32[]{:S(2)}) collective-permute-start(bf16[128,2048]{1,0:T(8,128)(2,1)} %get-tuple-element.90), channel_id=1, source_target_pairs={{0,16},{4,20},{8,24},{12,28},{16,0},{20,4},{24,8},{28,12},{1,17},{... | collective-permute-start | bytes 1572872 | tf_op jit(solution)/shard_map/ppermute | solution.py:24
  56.1 25.7 %collective-permute-start.18 = (bf16[128,2048]{1,0:T(8,128)(2,1)}, bf16[128,2048]{1,0:T(8,128)(2,1)S(1)}, u32[]{:S(2)}, u32[]{:S(2)}) collective-permute-start(bf16[128,2048]{1,0:T(8,128)(2,1)} %get-tuple-element.100), channel_id=1, source_target_pairs={{0,8},{4,12},{8,0},{12,4},{16,24},{20,28},{24,16},{28,20},{1,9},{5... | collective-permute-start | bytes 1572872 | tf_op jit(solution)/shard_map/ppermute | solution.py:24
  56.7 25.2 %collective-permute-start.17 = (bf16[128,2048]{1,0:T(8,128)(2,1)}, bf16[128,2048]{1,0:T(8,128)(2,1)S(1)}, u32[]{:S(2)}, u32[]{:S(2)}) collective-permute-start(bf16[128,2048]{1,0:T(8,128)(2,1)} %get-tuple-element.98), channel_id=1, source_target_pairs={{0,16},{4,20},{8,24},{12,28},{16,0},{20,4},{24,8},{28,12},{1,17},{... | collective-permute-start | bytes 1572872 | tf_op jit(solution)/shard_map/ppermute | solution.py:24
  72.2 20.5 %collective-permute-start.20 = (bf16[128,2048]{1,0:T(8,128)(2,1)}, bf16[128,2048]{1,0:T(8,128)(2,1)S(1)}, u32[]{:S(2)}, u32[]{:S(2)}) collective-permute-start(bf16[128,2048]{1,0:T(8,128)(2,1)} %get-tuple-element.109), channel_id=1, source_target_pairs={{0,16},{4,20},{8,24},{12,28},{16,0},{20,4},{24,8},{28,12},{1,17},{... | collective-permute-start | bytes 1572872 | tf_op jit(solution)/shard_map/ppermute | solution.py:24
  72.8 19.9 %collective-permute-start.19 = (bf16[128,2048]{1,0:T(8,128)(2,1)}, bf16[128,2048]{1,0:T(8,128)(2,1)S(1)}, u32[]{:S(2)}, u32[]{:S(2)}) collective-permute-start(bf16[128,2048]{1,0:T(8,128)(2,1)} %get-tuple-element.107), channel_id=1, source_target_pairs={{0,8},{4,12},{8,0},{12,4},{16,24},{20,28},{24,16},{28,20},{1,9},{5... | collective-permute-start | bytes 1572872 | tf_op jit(solution)/shard_map/ppermute | solution.py:24
  74.3 5.2 %collective-permute-start.13 = (bf16[16,2560]{1,0:T(8,128)(2,1)S(1)}, bf16[16,2560]{1,0:T(8,128)(2,1)S(1)}, u32[]{:S(2)}, u32[]{:S(2)}) collective-permute-start(bf16[16,2560]{1,0:T(8,128)(2,1)S(1)} %get-tuple-element.86.refs_4_), channel_id=1, source_target_pairs={{0,1},{1,0},{2,3},{3,2},{4,5},{5,4},{6,7},{7,6},{8,9},{9,8},{10,11... | collective-permute-start | bytes 245768 | tf_op jit(solution)/shard_map/ppermute | solution.py:24
  79.6 5.4 %collective-permute-start.16 = (bf16[16,2560]{1,0:T(8,128)(2,1)S(1)}, bf16[16,2560]{1,0:T(8,128)(2,1)S(1)}, u32[]{:S(2)}, u32[]{:S(2)}) collective-permute-start(bf16[16,2560]{1,0:T(8,128)(2,1)S(1)} %get-tuple-element.95), channel_id=1, source_target_pairs={{0,2},{1,3},{2,0},{3,1},{4,6},{5,7},{6,4},{7,5},{8,10},{9,11},{10,... | collective-permute-start | bytes 245768 | tf_op jit(solution)/shard_map/ppermute | solution.py:24
  87.5 7.8 %collective-permute-start.22 = (bf16[256,256]{1,0:T(8,128)(2,1)}, bf16[256,256]{1,0:T(8,128)(2,1)S(1)}, u32[]{:S(2)}, u32[]{:S(2)}) collective-permute-start(bf16[256,256]{1,0:T(8,128)(2,1)} %get-tuple-element.116), channel_id=1, source_target_pairs={{0,8},{4,12},{8,0},{12,4},{16,24},{20,28},{24,16},{28,20},{1,9},{5... | collective-permute-start | bytes 393224 | tf_op jit(solution)/shard_map/ppermute | solution.py:24
  88.1 7.2 %collective-permute-start.23 = (bf16[256,256]{1,0:T(8,128)(2,1)}, bf16[256,256]{1,0:T(8,128)(2,1)S(1)}, u32[]{:S(2)}, u32[]{:S(2)}) collective-permute-start(bf16[256,256]{1,0:T(8,128)(2,1)} %get-tuple-element.117), channel_id=1, source_target_pairs={{0,16},{4,20},{8,24},{12,28},{16,0},{20,4},{24,8},{28,12},{1,17},{... | collective-permute-start | bytes 393224 | tf_op jit(solution)/shard_map/ppermute | solution.py:24
  89.5 6.1 %collective-permute-start.24 = (bf16[256,256]{1,0:T(8,128)(2,1)}, bf16[256,256]{1,0:T(8,128)(2,1)S(1)}, u32[]{:S(2)}, u32[]{:S(2)}) collective-permute-start(bf16[256,256]{1,0:T(8,128)(2,1)} %get-tuple-element.118), channel_id=1, source_target_pairs={{0,24},{4,28},{8,16},{12,20},{16,8},{20,12},{24,0},{28,4},{1,25},{... | collective-permute-start | bytes 393224 | tf_op jit(solution)/shard_map/ppermute | solution.py:24
  92.7 1.6 %collective-permute-start.21 = (bf16[32,256]{1,0:T(8,128)(2,1)S(1)}, bf16[32,256]{1,0:T(8,128)(2,1)S(1)}, u32[]{:S(2)}, u32[]{:S(2)}) collective-permute-start(bf16[32,256]{1,0:T(8,128)(2,1)S(1)} %get-tuple-element.110), channel_id=1, source_target_pairs={{0,4},{4,0},{8,12},{12,8},{16,20},{20,16},{24,28},{28,24},{1,5},{5... | collective-permute-start | bytes 49160 | tf_op jit(solution)/shard_map/ppermute | solution.py:24
  (11 other events, 122.5 us)
